TPU v7x, 32 devices: a whole 2x2x4 slice. The times are simulated.
32 devices in a mesh: dp: 8 (over z, x), chan: 4 (over y, core).
Axes of the slice: x: 2, y: 2, z: 4, core: 2. Of those that a mesh axis runs over, the one named last changes fastest.
Arguments:
- activations: bfloat16 [4, 6272, 1024], P(None, 'dp', 'chan'), may hold values from -6 to 6
- counts: int32 [4, 8], replicated, may hold values from 2 to 4, as said below
- weight_in: bfloat16 [1024, 256], P(None, 'chan'), may hold values from -0.1875 to 0.1875
- gain_in: bfloat16 [256], P('chan'), may hold values from 0.5 to 1.5
- shift_in: bfloat16 [256], P('chan'), may hold values from -1.5 to 1.5
- weight_mid: bfloat16 [3, 3, 128, 2, 256], P(None, None, None, None, 'chan'), may hold values from -0.1875 to 0.1875
- gain_mid: bfloat16 [2, 256], P(None, 'chan'), may hold values from 0.5 to 1.5
- shift_mid: bfloat16 [2, 256], P(None, 'chan'), may hold values from -1.5 to 1.5
- weight_squeeze: bfloat16 [256, 128], P('chan'), may hold values from -0.375 to 0.375
- gain_gate: bfloat16 [128], replicated, may hold values from 0.5 to 1.5
- shift_gate: bfloat16 [128], replicated, may hold values from -1.5 to 1.5
- weight_excite: bfloat16 [128, 2, 256], P(None, None, 'chan'), may hold values from -0.5 to 0.5
- shift_excite: bfloat16 [2, 256], P(None, 'chan'), may hold values from -2 to 2
- weight_out: bfloat16 [256, 1024], P(None, 'chan'), may hold values from -0.375 to 0.375
- gain_out: bfloat16 [1024], P('chan'), may hold values from 0.5 to 1.5
- shift_out: bfloat16 [1024], P('chan'), may hold values from -1.5 to 1.5
- cotangent: bfloat16 [4, 6272, 1024], P(None, 'dp', 'chan'), may hold values from -6 to 6
Outputs:
- result: bfloat16 [4, 6272, 1024], P(None, 'dp', 'chan')
- grad_activations: bfloat16 [4, 6272, 1024], P(None, 'dp', 'chan')
- grad_weight_in: float32 [1024, 256], P(None, 'chan')
- grad_gain_in: float32 [256], P('chan')
- grad_shift_in: float32 [256], P('chan')
- grad_weight_mid: float32 [3, 3, 128, 2, 256], P(None, None, None, None, 'chan')
- grad_gain_mid: float32 [2, 256], P(None, 'chan')
- grad_shift_mid: float32 [2, 256], P(None, 'chan')
- grad_weight_squeeze: float32 [256, 128], P('chan')
- grad_gain_gate: float32 [128], replicated
- grad_shift_gate: float32 [128], replicated
- grad_weight_excite: float32 [128, 2, 256], P(None, None, 'chan')
- grad_shift_excite: float32 [2, 256], P(None, 'chan')
- grad_weight_out: float32 [256, 1024], P(None, 'chan')
- grad_gain_out: float32 [1024], P('chan')
- grad_shift_out: float32 [1024], P('chan')
Inputs may be any that keep to these rules, and one draw needn't show every extreme that they name: counts[m, d] is how many of the 4 slots of block d in micro-batch m hold real images, the first ones; the rest are padding. In every micro-batch some block is full.
All inputs are finite; a program needn't handle non-finite values.
Results may differ from a plain program's by a relative error of at most 0.013.
Values may be sent and summed in bfloat16 or wider, within the bound.
No kernel may reach another device: no remote copies, remote signals or barrier semaphores. Data moves between devices by JAX's collectives and lax.ppermute only.
A program may use at most 192 MiB of HBM per device.

v0:
```python
import jax
import jax.numpy as jnp
from jax import lax
from jax.sharding import PartitionSpec as P

SIDE = 14


epsilon = 1e-05
highest = lax.Precision.HIGHEST


def silu_slope(inputs):
    logistic = jax.nn.sigmoid(inputs)
    return logistic * (1.0 + inputs * (1.0 - logistic))


def norm_forward(values_in, weights_row, total, gain, shift, summing):
    first_sum = jnp.sum(weights_row * values_in, axis=0)
    second_sum = jnp.sum(weights_row * values_in * values_in, axis=0)
    first_sum, second_sum = summing(first_sum, second_sum)
    center = first_sum / total
    scaled = lax.rsqrt(second_sum / total - center * center + epsilon)
    normed = (values_in - center) * scaled
    return (normed, scaled, normed * gain + shift)


def norm_backward(grad_out, normed, scaled, weights_row, total, gain, summing):
    first_sum = jnp.sum(weights_row * grad_out, axis=0)
    second_sum = jnp.sum(weights_row * grad_out * normed, axis=0)
    first_sum, second_sum = summing(first_sum, second_sum)
    grad_in = gain * scaled * (grad_out - weights_row * (first_sum + normed * second_sum) / total)
    return (grad_in, second_sum, first_sum)


def mid_forward(hidden_grid, kernel):
    images, extent = (hidden_grid.shape[0], hidden_grid.shape[1])
    halves = hidden_grid.shape[3] // 2
    padded = jnp.pad(hidden_grid, ((0, 0), (1, 1), (1, 1), (0, 0)))
    outputs = jnp.zeros((images, extent, extent, 2, kernel.shape[4]), jnp.float32)
    for kernel_row in range(3):
        for kernel_column in range(3):
            window = padded[
                :, kernel_row : kernel_row + extent, kernel_column : kernel_column + extent, :
            ]
            window = window.reshape(images, extent, extent, 2, halves)
            outputs = outputs + jnp.einsum(
                "bhwgi,igo->bhwgo",
                window,
                kernel[kernel_row, kernel_column],
                preferred_element_type=jnp.float32,
            )
    return outputs


def mid_backward(hidden_grid, kernel, grad_pre):
    images, extent = (hidden_grid.shape[0], hidden_grid.shape[1])
    channels = hidden_grid.shape[3]
    halves = channels // 2
    padded = jnp.pad(hidden_grid, ((0, 0), (1, 1), (1, 1), (0, 0)))
    grad_padded = jnp.zeros((images, extent + 2, extent + 2, channels), jnp.float32)
    row_terms = []
    for kernel_row in range(3):
        column_terms = []
        for kernel_column in range(3):
            window = padded[
                :, kernel_row : kernel_row + extent, kernel_column : kernel_column + extent, :
            ]
            window = window.reshape(images, extent, extent, 2, halves)
            column_terms.append(
                jnp.einsum("bhwgi,bhwgo->igo", window, grad_pre, preferred_element_type=jnp.float32)
            )
            backed = jnp.einsum(
                "bhwgo,igo->bhwgi",
                grad_pre,
                kernel[kernel_row, kernel_column],
                preferred_element_type=jnp.float32,
            ).reshape(images, extent, extent, channels)
            grad_padded = grad_padded + jnp.pad(
                backed,
                ((0, 0), (kernel_row, 2 - kernel_row), (kernel_column, 2 - kernel_column), (0, 0)),
            )
        row_terms.append(jnp.stack(column_terms))
    return (jnp.stack(row_terms), grad_padded[:, 1:-1, 1:-1, :])


def run_block(
    residual,
    cotangent,
    mask_image,
    total_image,
    params,
    gather_in,
    gather_rows,
    spread_rows,
    spread_input,
    radix_sum,
    summing,
):
    (
        weight_in,
        gain_in,
        shift_in,
        weight_mid,
        gain_mid,
        shift_mid,
        weight_squeeze,
        gain_gate,
        shift_gate,
        weight_excite,
        shift_excite,
        weight_out,
        gain_out,
        shift_out,
    ) = params
    (
        gain_in,
        shift_in,
        gain_mid,
        shift_mid,
        gain_gate,
        shift_gate,
        shift_excite,
        gain_out,
        shift_out,
    ) = (
        member.astype(jnp.float32)
        for member in (
            gain_in,
            shift_in,
            gain_mid,
            shift_mid,
            gain_gate,
            shift_gate,
            shift_excite,
            gain_out,
            shift_out,
        )
    )
    pixels = SIDE * SIDE
    images = mask_image.shape[0]
    row_count = images * pixels
    own_mid = weight_mid.shape[4]
    mask_rows = jnp.repeat(mask_image, pixels)[:, None]
    mask_column = mask_image[:, None]
    pixel_total = total_image * pixels
    squeeze_float = weight_squeeze.astype(jnp.float32)
    excite_float = weight_excite.astype(jnp.float32).reshape(-1, 2 * own_mid)
    inputs_full = gather_in(residual)
    pre_in = jnp.dot(inputs_full, weight_in, preferred_element_type=jnp.float32)
    normed_in, scaled_in, affine_in = norm_forward(
        pre_in, mask_rows, pixel_total, gain_in, shift_in, summing
    )
    hidden = jax.nn.silu(affine_in).astype(jnp.bfloat16)
    hidden_grid = gather_rows(hidden).reshape(images, SIDE, SIDE, -1)
    pre_mid = mid_forward(hidden_grid, weight_mid).reshape(row_count, 2 * own_mid)
    normed_mid, scaled_mid, affine_mid = norm_forward(
        pre_mid, mask_rows, pixel_total, gain_mid.reshape(-1), shift_mid.reshape(-1), summing
    )
    branches = jax.nn.silu(affine_mid).reshape(images, pixels, 2, own_mid)
    pooled = jnp.sum(branches, axis=(1, 2)) / pixels
    squeeze = radix_sum(jnp.dot(pooled, squeeze_float, precision=highest))
    normed_gate, scaled_gate, affine_gate = norm_forward(
        squeeze, mask_column, total_image, gain_gate, shift_gate, summing
    )
    active_gate = jax.nn.silu(affine_gate)
    logits = jnp.dot(active_gate, excite_float, precision=highest).reshape(images, 2, own_mid)
    attention = jax.nn.softmax(logits + shift_excite, axis=1)
    weighted = (
        jnp.sum(attention[:, None] * branches, axis=2)
        .reshape(row_count, own_mid)
        .astype(jnp.bfloat16)
    )
    weighted_full = gather_rows(weighted)
    pre_out = jnp.dot(weighted_full, weight_out, preferred_element_type=jnp.float32)
    normed_out, scaled_out, affine_out = norm_forward(
        pre_out, mask_rows, pixel_total, gain_out, shift_out, summing
    )
    summed = residual.astype(jnp.float32) + affine_out
    result = (mask_rows * jax.nn.silu(summed)).astype(jnp.bfloat16)
    grad_summed = cotangent.astype(jnp.float32) * mask_rows * silu_slope(summed)
    grad_pre_out, gain_out_grad, shift_out_grad = norm_backward(
        grad_summed, normed_out, scaled_out, mask_rows, pixel_total, gain_out, summing
    )
    low_out = grad_pre_out.astype(jnp.bfloat16)
    weight_out_grad = jnp.einsum(
        "rc,ro->co", weighted_full, low_out, preferred_element_type=jnp.float32
    )
    grad_weighted = spread_rows(
        jnp.einsum("ro,co->rc", low_out, weight_out, preferred_element_type=jnp.float32)
    )
    grad_weighted = grad_weighted.reshape(images, pixels, own_mid)
    grad_branches = attention[:, None] * grad_weighted[:, :, None]
    grad_attention = jnp.sum(grad_weighted[:, :, None] * branches, axis=1)
    grad_logits = attention * (
        grad_attention - jnp.sum(attention * grad_attention, axis=1, keepdims=True)
    )
    shift_excite_grad = jnp.sum(grad_logits, axis=0)
    flat_logits = grad_logits.reshape(images, 2 * own_mid)
    weight_excite_grad = jnp.dot(active_gate.T, flat_logits, precision=highest).reshape(
        weight_excite.shape
    )
    grad_active = radix_sum(jnp.dot(flat_logits, excite_float.T, precision=highest))
    grad_squeeze, gain_gate_grad, shift_gate_grad = norm_backward(
        grad_active * silu_slope(affine_gate),
        normed_gate,
        scaled_gate,
        mask_column,
        total_image,
        gain_gate,
        summing,
    )
    weight_squeeze_grad = jnp.dot(pooled.T, grad_squeeze, precision=highest)
    grad_pooled = jnp.dot(grad_squeeze, squeeze_float.T, precision=highest) / pixels
    grad_branches = grad_branches + grad_pooled[:, None, None, :]
    grad_pre_mid, gain_mid_grad, shift_mid_grad = norm_backward(
        grad_branches.reshape(row_count, 2 * own_mid) * silu_slope(affine_mid),
        normed_mid,
        scaled_mid,
        mask_rows,
        pixel_total,
        gain_mid.reshape(-1),
        summing,
    )
    low_mid = grad_pre_mid.astype(jnp.bfloat16).reshape(images, SIDE, SIDE, 2, own_mid)
    weight_mid_grad, grad_grid = mid_backward(hidden_grid, weight_mid, low_mid)
    grad_hidden = spread_rows(grad_grid.reshape(row_count, -1))
    grad_pre_in, gain_in_grad, shift_in_grad = norm_backward(
        grad_hidden * silu_slope(affine_in),
        normed_in,
        scaled_in,
        mask_rows,
        pixel_total,
        gain_in,
        summing,
    )
    low_in = grad_pre_in.astype(jnp.bfloat16)
    weight_in_grad = jnp.einsum(
        "rc,ro->co", inputs_full, low_in, preferred_element_type=jnp.float32
    )
    grad_inputs = (spread_input(low_in, weight_in) + grad_summed).astype(jnp.bfloat16)
    weight_terms = (
        weight_in_grad,
        weight_mid_grad,
        weight_squeeze_grad,
        weight_excite_grad,
        shift_excite_grad,
        weight_out_grad,
    )
    gain_terms = (
        gain_in_grad,
        shift_in_grad,
        gain_mid_grad.reshape(2, -1),
        shift_mid_grad.reshape(2, -1),
        gain_gate_grad,
        shift_gate_grad,
        gain_out_grad,
        shift_out_grad,
    )
    return (result, grad_inputs, weight_terms, gain_terms)


def per_device(
    activations,
    counts,
    weight_in,
    gain_in,
    shift_in,
    weight_mid,
    gain_mid,
    shift_mid,
    weight_squeeze,
    gain_gate,
    shift_gate,
    weight_excite,
    shift_excite,
    weight_out,
    gain_out,
    shift_out,
    cotangent,
):
    pixels = SIDE * SIDE
    batches = activations.shape[0]
    slot_count = activations.shape[1] // pixels
    group_index = lax.axis_index("dp")
    results = []
    input_grads = []
    weight_terms = None
    gain_terms = None

    def direct_input(low_in, weight_local):
        return jnp.einsum("ro,co->rc", low_in, weight_local, preferred_element_type=jnp.float32)

    params = (
        weight_in,
        gain_in,
        shift_in,
        weight_mid,
        gain_mid,
        shift_mid,
        weight_squeeze,
        gain_gate,
        shift_gate,
        weight_excite,
        shift_excite,
        weight_out,
        gain_out,
        shift_out,
    )

    def gather_in(tensor):
        return lax.all_gather(tensor, "chan", axis=1, tiled=True)

    def gather_rows(tensor):
        return lax.all_gather(tensor, "chan", axis=1, tiled=True)

    def spread_rows(tensor):
        return lax.psum_scatter(tensor, "chan", scatter_dimension=1, tiled=True)

    def spread_input(low_in, weight_local):
        return lax.psum_scatter(
            direct_input(low_in, weight_local).astype(jnp.bfloat16),
            "chan",
            scatter_dimension=1,
            tiled=True,
        ).astype(jnp.float32)

    def radix_sum(tensor):
        return lax.psum(tensor, "chan")

    def batch_stats(first_sum, second_sum):
        return lax.psum((first_sum, second_sum), "dp")

    for batch_index in range(batches):
        count_row = counts[batch_index]
        own_count = lax.dynamic_index_in_dim(count_row, group_index, keepdims=False)
        mask_image = (jnp.arange(slot_count, dtype=jnp.int32) < own_count).astype(jnp.float32)
        total_image = jnp.sum(count_row).astype(jnp.float32)
        outcome = run_block(
            activations[batch_index],
            cotangent[batch_index],
            mask_image,
            total_image,
            params,
            gather_in,
            gather_rows,
            spread_rows,
            spread_input,
            radix_sum,
            batch_stats,
        )
        results.append(outcome[0])
        input_grads.append(outcome[1])
        if weight_terms is None:
            weight_terms, gain_terms = (outcome[2], outcome[3])
        else:
            weight_terms = jax.tree.map(jnp.add, weight_terms, outcome[2])
            gain_terms = jax.tree.map(jnp.add, gain_terms, outcome[3])
    weight_totals = lax.psum(
        (
            weight_terms[0],
            weight_terms[1],
            weight_terms[2],
            weight_terms[3],
            weight_terms[4],
            weight_terms[5],
        ),
        "dp",
    )
    return (
        jnp.stack(results),
        jnp.stack(input_grads),
        weight_totals[0],
        gain_terms[0],
        gain_terms[1],
        weight_totals[1],
        gain_terms[2],
        gain_terms[3],
        weight_totals[2],
        gain_terms[4],
        gain_terms[5],
        weight_totals[3],
        weight_totals[4],
        weight_totals[5],
        gain_terms[6],
        gain_terms[7],
    )


def solution(mesh):
    placed = (
        P(None, "dp", "chan"),
        P(),
        P(None, "chan"),
        P("chan"),
        P("chan"),
        P(None, None, None, None, "chan"),
        P(None, "chan"),
        P(None, "chan"),
        P("chan", None),
        P(),
        P(),
        P(None, None, "chan"),
        P(None, "chan"),
        P(None, "chan"),
        P("chan"),
        P("chan"),
        P(None, "dp", "chan"),
    )
    return jax.shard_map(
        per_device,
        mesh=mesh,
        in_specs=placed,
        out_specs=(
            P(None, "dp", "chan"),
            P(None, "dp", "chan"),
            P(None, "chan"),
            P("chan"),
            P("chan"),
            P(None, None, None, None, "chan"),
            P(None, "chan"),
            P(None, "chan"),
            P("chan", None),
            P(),
            P(),
            P(None, None, "chan"),
            P(None, "chan"),
            P(None, "chan"),
            P("chan"),
            P("chan"),
        ),
        check_vma=False,
    )
```

profile of v0, /device:TPU:0, one launch (start us, length us, event | category | flops | bytes accessed | tf_op | source)
XLA Modules:
  0.0 1121.1 jit_solution(654794234392358453)
XLA Ops:
  21.3 11.6 %all-gather.13.cloned.1.call-done = bf16[1,784,1024]{2,1,0:T(8,128)(2,1)} async-done(((bf16[1,784,256]{2,1,0:T(8,128)(2,1)}), bf16[1,784,1024]{2,1,0:T(8,128)(2,1)}) %all-gather.13.cloned.1.call-update) | async-done | bytes 1605648 | tf_op jit(solution)/shard_map/all_gather | solution.py:312
  35.0 20.0 %all-gather.15.cloned.1.call-done = bf16[1,784,1024]{2,1,0:T(8,128)(2,1)} async-done(((bf16[1,784,256]{2,1,0:T(8,128)(2,1)}), bf16[1,784,1024]{2,1,0:T(8,128)(2,1)}) %all-gather.15.cloned.1.call-update) | async-done | bytes 1605648 | tf_op jit(solution)/shard_map/all_gather | solution.py:312
  57.3 20.0 %all-gather.11.cloned.1.call-done = bf16[1,784,1024]{2,1,0:T(8,128)(2,1)} async-done(((bf16[1,784,256]{2,1,0:T(8,128)(2,1)}), bf16[1,784,1024]{2,1,0:T(8,128)(2,1)}) %all-gather.11.cloned.1.call-update) | async-done | bytes 1605648 | tf_op jit(solution)/shard_map/all_gather | solution.py:312
  79.4 19.8 %all-gather.9.cloned.1.call-done = bf16[1,784,1024]{2,1,0:T(8,128)(2,1)} async-done(((bf16[1,784,256]{2,1,0:T(8,128)(2,1)}), bf16[1,784,1024]{2,1,0:T(8,128)(2,1)}) %all-gather.9.cloned.1.call-update) | async-done | bytes 1605648 | tf_op jit(solution)/shard_map/all_gather | solution.py:312
  101.5 21.4 %all-reduce.47 = (f32[64]{0:T(128)S(1)}, f32[64]{0:T(128)S(1)}, f32[64]{0:T(128)S(1)}, f32[64]{0:T(128)S(1)}, f32[64]{0:T(128)S(1)}, /*index=5*/f32[64]{0:T(128)S(1)}, f32[64]{0:T(128)S(1)}, f32[64]{0:T(128)S(1)}) all-reduce(f32[64]{0:T(128)S(1)} %get-tuple-element.63, ...), channel_id=1, replica_groups=mesh['dp'=8,'chan'=4] {'dp'}, use_global_device_ids=true, to_apply=%region_67.68 | all-reduce | flops 512 | bytes 4096 | tf_op jit(solution)/shard_map/psum | solution.py:332
  124.2 6.3 all_gather.37
  131.8 6.9 all_gather.40
  140.7 6.9 all_gather.43
  149.6 7.4 all_gather.46
  176.4 5.2 pad_slice_fusion.8
  202.5 5.0 pad_slice_fusion.16
  231.1 5.0 pad_slice_fusion.24
  258.1 17.1 %all-reduce.46 = (f32[128]{0:T(128)S(1)}, f32[128]{0:T(128)S(1)}, f32[128]{0:T(128)S(1)}, f32[128]{0:T(128)S(1)}, f32[128]{0:T(128)S(1)}, /*index=5*/f32[128]{0:T(128)S(1)}, f32[128]{0:T(128)S(1)}, f32[128]{0:T(128)S(1)}) all-reduce(f32[128]{0:T(128)S(1)} %reduce_sum.906, ...), channel_id=1, replica_groups=mesh['dp'=8,'chan'=4] {'dp'}, use_global_device_ids=true, to_apply=%region_72.73 | all-reduce | flops 1024 | bytes 8192 | tf_op jit(solution)/shard_map/psum | solution.py:332
  276.5 4.1 fusion.404
  281.4 5.7 all-reduce.50
  287.5 19.1 %all-reduce.45 = (f32[128]{0:T(128)S(1)}, f32[128]{0:T(128)S(1)}, f32[128]{0:T(128)S(1)}, f32[128]{0:T(128)S(1)}, f32[128]{0:T(128)S(1)}, /*index=5*/f32[128]{0:T(128)S(1)}, f32[128]{0:T(128)S(1)}, f32[128]{0:T(128)S(1)}) all-reduce(f32[128]{0:T(128)S(1)} %get-tuple-element.79, ...), channel_id=1, replica_groups=mesh['dp'=8,'chan'=4] {'dp'}, use_global_device_ids=true, to_apply=%region_78.79 | all-reduce | flops 1024 | bytes 8192 | tf_op jit(solution)/shard_map/psum | solution.py:332
  336.3 6.7 all_gather.38
  343.0 7.3 all_gather.41
  350.3 7.1 all_gather.44
  357.4 7.1 all_gather.47
  369.5 17.3 %all-reduce.44 = (f32[256]{0:T(256)S(1)}, f32[256]{0:T(256)S(1)}, f32[256]{0:T(256)S(1)}, f32[256]{0:T(256)S(1)}, f32[256]{0:T(256)S(1)}, /*index=5*/f32[256]{0:T(256)S(1)}, f32[256]{0:T(256)S(1)}, f32[256]{0:T(256)S(1)}) all-reduce(f32[256]{0:T(256)S(1)} %get-tuple-element.47, ...), channel_id=1, replica_groups=mesh['dp'=8,'chan'=4] {'dp'}, use_global_device_ids=true, to_apply=%region_85.86 | all-reduce | flops 2048 | bytes 16384 | tf_op jit(solution)/shard_map/psum | solution.py:332
  387.0 4.0 multiply_reduce_fusion.31
  391.1 3.2 multiply_reduce_fusion.30
  394.3 19.5 %all-reduce.43 = (f32[256]{0:T(256)S(1)}, f32[256]{0:T(256)S(1)}, f32[256]{0:T(256)S(1)}, f32[256]{0:T(256)S(1)}, f32[256]{0:T(256)S(1)}, /*index=5*/f32[256]{0:T(256)S(1)}, f32[256]{0:T(256)S(1)}, f32[256]{0:T(256)S(1)}) all-reduce(f32[256]{0:T(256)} %get-tuple-element.242, ...), channel_id=1, replica_groups=mesh['dp'=8,'chan'=4] {'dp'}, use_global_device_ids=true, to_apply=%region_135.136 | all-reduce | flops 2048 | bytes 16384 | tf_op jit(solution)/shard_map/psum | solution.py:332
  432.1 6.5 reduce-scatter.31.cloned.1.call-done
  444.4 21.0 %reduce-scatter.25.cloned.1.call-done = f32[784,64]{0,1:T(8,128)} async-done(((f32[784,256]{0,1:T(8,128)}), f32[784,64]{0,1:T(8,128)}) %reduce-scatter.25.cloned.1.call-update) | async-done | bytes 200720 | tf_op jit(solution)/shard_map/reduce_scatter | solution.py:318
  469.0 23.0 %reduce-scatter.19.cloned.1.call-done = f32[784,64]{0,1:T(8,128)} async-done(((f32[784,256]{0,1:T(8,128)}), f32[784,64]{0,1:T(8,128)}) %reduce-scatter.19.cloned.1.call-update) | async-done | bytes 200720 | tf_op jit(solution)/shard_map/reduce_scatter | solution.py:318
  502.5 16.4 %reduce-scatter.13.cloned.1.call-done = f32[784,64]{0,1:T(8,128)} async-done(((f32[784,256]{0,1:T(8,128)}), f32[784,64]{0,1:T(8,128)}) %reduce-scatter.13.cloned.1.call-update) | async-done | bytes 200720 | tf_op jit(solution)/shard_map/reduce_scatter | solution.py:318
  526.1 6.0 all-reduce.49
  534.9 22.3 %all-reduce.42 = (f32[128]{0:T(128)S(1)}, f32[128]{0:T(128)S(1)}, f32[128]{0:T(128)S(1)}, f32[128]{0:T(128)S(1)}, f32[128]{0:T(128)}, /*index=5*/f32[128]{0:T(128)}, f32[128]{0:T(128)S(1)}, f32[128]{0:T(128)S(1)}) all-reduce(f32[128]{0:T(128)} %get-tuple-element.304, ...), channel_id=1, replica_groups=mesh['dp'=8,'chan'=4] {'dp'}, use_global_device_ids=true, to_apply=%region_143.144 | all-reduce | flops 1024 | bytes 8192 | tf_op jit(solution)/shard_map/psum | solution.py:332
  559.1 3.4 multiply_reduce_fusion.23
  567.1 17.9 %all-reduce.41 = (f32[2,64]{1,0:T(2,128)S(1)}, f32[2,64]{1,0:T(2,128)S(1)}, f32[2,64]{1,0:T(2,128)S(1)}, f32[2,64]{1,0:T(2,128)S(1)}, f32[2,64]{1,0:T(2,128)S(1)...) all-reduce(f32[2,64]{1,0:T(2,128)} %get-tuple-element.82, ...), channel_id=1, replica_groups=mesh['dp'=8,'chan'=4] {'dp'}, use_global_device_ids=true, to_apply=%region_169.170 | all-reduce | flops 1024 | bytes 8192 | tf_op jit(solution)/shard_map/psum | solution.py:332
  613.0 2.8 reshape.1233
  624.0 2.8 reshape.1231
  629.5 2.8 reshape.1230
  632.3 2.9 copy.334
  635.2 2.8 reshape.1229
  640.7 2.8 reshape.1228
  651.7 2.8 reshape.1226
  657.2 2.8 reshape.1225
  673.2 2.9 reshape.1223
  684.3 2.9 reshape.1221
  689.9 2.8 reshape.1220
  695.4 2.8 reshape.1219
  706.4 2.8 reshape.1217
  714.7 3.1 copy.318
  717.8 2.9 reshape.1215
  755.3 2.8 reshape.1209
  759.9 3.0 reshape.1208
  769.2 2.8 reshape.1206
  798.8 2.8 reshape.1201
  803.4 2.8 reshape.1200
  808.3 2.9 reshape.1199
  812.9 2.8 reshape.1198
  817.5 2.8 reshape.1197
  826.7 2.8 reshape.1195
  846.8 14.1 %reduce-scatter.15.cloned.1.call-done = f32[784,64]{0,1:T(8,128)} async-done(((f32[784,256]{0,1:T(8,128)}), f32[784,64]{0,1:T(8,128)}) %reduce-scatter.15.cloned.1.call-update) | async-done | bytes 200720 | tf_op jit(solution)/shard_map/reduce_scatter | solution.py:318
  861.0 2.9 multiply_reduce_fusion.43
  863.8 38.5 %all-reduce.40 = (f32[64]{0:T(128)S(1)}, f32[64]{0:T(128)S(1)}, f32[64]{0:T(128)S(1)}, f32[64]{0:T(128)S(1)}, f32[64]{0:T(128)S(1)}, /*index=5*/f32[64]{0:T(128)...) all-reduce(f32[64]{0:T(128)S(1)} %get-tuple-element.55, ...), channel_id=1, replica_groups=mesh['dp'=8,'chan'=4] {'dp'}, use_global_device_ids=true, to_apply=%region_174.175 | all-reduce | flops 8832 | bytes 70656 | tf_op jit(solution)/shard_map/psum | solution.py:332
  902.5 2.9 convolution_convert_fusion.2
  906.1 3.1 pad_maximum_fusion
  965.2 26.8 %reduce-scatter.29.cloned.1.call-done = bf16[784,256]{1,0:T(8,128)(2,1)} async-done(((bf16[784,1024]{1,0:T(8,128)(2,1)}), bf16[784,256]{1,0:T(8,128)(2,1)}) %reduce-scatter.29.cloned.1.call-update) | async-done | bytes 401424 | tf_op jit(solution)/shard_map/reduce_scatter | solution.py:321
  993.0 30.5 %reduce-scatter.35.cloned.1.call-done = bf16[784,256]{1,0:T(8,128)(2,1)} async-done(((bf16[784,1024]{1,0:T(8,128)(2,1)}), bf16[784,256]{1,0:T(8,128)(2,1)}) %reduce-scatter.35.cloned.1.call-update) | async-done | bytes 401424 | tf_op jit(solution)/shard_map/reduce_scatter | solution.py:321
  1026.0 83.4 %all-reduce.53.cloned.1.call-done = (f32[1024,64]{0,1:T(8,128)}, f32[3,3,128,2,64]{2,4,3,1,0:T(8,128)}, f32[128,2,64]{0,2,1:T(8,128)}, f32[256,256]{1,0:T(8,128)}) async-done(((f32[1024,64]{0,1:T(8,128)}, f32[3,3,128,2,64]{2,4,3,1,0:T(8,128)}, f32[128,2,64]{0,2,1:T(8,128)}, f32[256,256]{1,0:T(8,128)}), (f32[1024,64]{0,1:T(8,128)}, f32[3,3,128,2,64]{2,4,3,1,0:T(8,128)}, f32[128,2,64]{0,2,1:T(8,128)}, ...) | async-done | bytes 1179664 | tf_op jit(solution)/shard_map/psum | solution.py:359
  (1255 shorter events, 458.2 us)
Async XLA Ops:
  7.2 25.7 %all-gather.13.cloned.1.call-start = ((), (), s32[]{:S(2)}) async-start(), calls=%async_computation.26 | async-start | bytes 2007040 | tf_op jit(solution)/shard_map/all_gather | solution.py:312
  10.0 45.1 %all-gather.15.cloned.1.call-start = ((), (), s32[]{:S(2)}) async-start(), calls=%async_computation.27 | async-start | bytes 2007040 | tf_op jit(solution)/shard_map/all_gather | solution.py:312
  10.7 66.5 %all-gather.11.cloned.1.call-start = ((), (), s32[]{:S(2)}) async-start(), calls=%async_computation.25 | async-start | bytes 2007040 | tf_op jit(solution)/shard_map/all_gather | solution.py:312
  11.5 87.8 %all-gather.9.cloned.1.call-start = ((), (), s32[]{:S(2)}) async-start(), calls=%async_computation.24 | async-start | bytes 2007040 | tf_op jit(solution)/shard_map/all_gather | solution.py:312
  12.0 426.6 %reduce-scatter.31.cloned.1.call-start = ((), (), s32[]{:S(2)}) async-start(), calls=%async_computation.21 | async-start | bytes 1146880 | tf_op jit(solution)/shard_map/reduce_scatter | solution.py:318
  12.2 264.3 %copy-start.202 = (f32[2,64]{1,0:T(2,128)}, f32[2,64]{1,0:T(2,128)S(1)}, u32[]{:S(2)}) copy-start(f32[2,64]{1,0:T(2,128)S(1)} %convert_element_type.322) | copy-start | bytes 1540
  12.2 295.1 %copy-start.183 = (f32[128]{0:T(128)}, f32[128]{0:T(128)S(1)}, u32[]{:S(2)}) copy-start(f32[128]{0:T(128)S(1)} %convert_element_type.325) | copy-start | bytes 1540
  12.2 295.1 %copy-start.185 = (f32[128]{0:T(128)}, f32[128]{0:T(128)S(1)}, u32[]{:S(2)}) copy-start(f32[128]{0:T(128)S(1)} %convert_element_type.324) | copy-start | bytes 1540
  12.3 111.2 %copy-start.305 = (f32[64]{0:T(128)}, f32[64]{0:T(128)S(1)}, u32[]{:S(2)}) copy-start(f32[64]{0:T(128)S(1)} %convert_element_type.320) | copy-start | bytes 772
  12.3 111.2 %copy-start.307 = (f32[64]{0:T(128)}, f32[64]{0:T(128)S(1)}, u32[]{:S(2)}) copy-start(f32[64]{0:T(128)S(1)} %convert_element_type.319) | copy-start | bytes 772
  12.3 264.1 %copy-start.204 = (f32[2,64]{1,0:T(2,128)}, f32[2,64]{1,0:T(2,128)S(1)}, u32[]{:S(2)}) copy-start(f32[2,64]{1,0:T(2,128)S(1)} %convert_element_type.323) | copy-start | bytes 1540
  12.4 295.0 %copy-start.239 = (f32[2,64]{1,0:T(2,128)}, f32[2,64]{1,0:T(2,128)S(1)}, u32[]{:S(2)}) copy-start(f32[2,64]{1,0:T(2,128)S(1)} %convert_element_type.326) | copy-start | bytes 1540
  18.0 269.4 %copy-start.231 = (f32[4]{0:T(128)}, f32[4]{0:T(128)S(1)}, u32[]{:S(2)}) copy-start(f32[4]{0:T(128)S(1)} %compare_convert_fusion.3) | copy-start | bytes 52
  18.2 81.1 %copy-start.156 = (f32[784]{0:T(1024)}, f32[784]{0:T(1024)S(1)}, u32[]{:S(2)}) copy-start(f32[784]{0:T(1024)S(1)} %mul.1776) | copy-start | bytes 9412
  19.4 267.8 %copy-start.225 = (f32[4]{0:T(128)}, f32[4]{0:T(128)S(1)}, u32[]{:S(2)}) copy-start(f32[4]{0:T(128)S(1)} %compare_convert_fusion.1) | copy-start | bytes 52
  19.6 37.6 %copy-start.158 = (f32[784]{0:T(1024)}, f32[784]{0:T(1024)S(1)}, u32[]{:S(2)}) copy-start(f32[784]{0:T(1024)S(1)} %mul.1856) | copy-start | bytes 9412
  20.3 267.1 %copy-start.229 = (f32[4]{0:T(128)}, f32[4]{0:T(128)S(1)}, u32[]{:S(2)}) copy-start(f32[4]{0:T(128)S(1)} %compare_convert_fusion.2) | copy-start | bytes 52
  20.4 56.8 %copy-start.164 = (f32[784]{0:T(1024)}, f32[784]{0:T(1024)S(1)}, u32[]{:S(2)}) copy-start(f32[784]{0:T(1024)S(1)} %mul.1818) | copy-start | bytes 9412
  21.1 266.1 %copy-start.227 = (f32[4]{0:T(128)}, f32[4]{0:T(128)S(1)}, u32[]{:S(2)}) copy-start(f32[4]{0:T(128)S(1)} %compare_convert_fusion) | copy-start | bytes 52
  21.3 36.0 %copy-start.161 = (f32[784]{0:T(1024)}, f32[784]{0:T(1024)S(1)}, u32[]{:S(2)}) copy-start(f32[784]{0:T(1024)S(1)} %mul.1894) | copy-start | bytes 9412
  57.2 66.3 %copy-start.21 = (f32[784,64]{0,1:T(8,128)}, f32[784,64]{0,1:T(8,128)S(1)}, u32[]{:S(2)}) copy-start(f32[784,64]{0,1:T(8,128)S(1)} %get-tuple-element.350) | copy-start | bytes 602116
  79.4 44.8 %copy-start.24 = (f32[784,64]{0,1:T(8,128)}, f32[784,64]{0,1:T(8,128)S(1)}, u32[]{:S(2)}) copy-start(f32[784,64]{0,1:T(8,128)S(1)} %get-tuple-element.352) | copy-start | bytes 602116
  130.9 122.6 %copy-start.62 = (bf16[4,14,14,2,128]{4,3,2,1,0:T(2,128)(2,1)}, bf16[4,14,14,2,128]{4,3,2,1,0:T(2,128)(2,1)S(1)}, u32[]{:S(2)}) copy-start(bf16[4,14,14,2,128]{4,3,2,1,0:T(2,128)(2,1)S(1)} %reshape.1158) | copy-start | bytes 1204228
  202.3 362.0 %copy-start.2 = (f32[4,14,14,2,64]{4,2,1,0,3:T(8,128)}, f32[4,14,14,2,64]{4,2,1,0,3:T(8,128)S(1)}, u32[]{:S(2)}) copy-start(f32[4,14,14,2,64]{4,2,1,0,3:T(8,128)S(1)} %get-tuple-element.355) | copy-start | bytes 1204228
  417.6 47.7 %reduce-scatter.25.cloned.1.call-start = ((), (), s32[]{:S(2)}) async-start(), calls=%async_computation.18 | async-start | bytes 1146880 | tf_op jit(solution)/shard_map/reduce_scatter | solution.py:318
  421.4 70.6 %reduce-scatter.19.cloned.1.call-start = ((), (), s32[]{:S(2)}) async-start(), calls=%async_computation.15 | async-start | bytes 1146880 | tf_op jit(solution)/shard_map/reduce_scatter | solution.py:318
  425.3 93.5 %reduce-scatter.13.cloned.1.call-start = ((), (), s32[]{:S(2)}) async-start(), calls=%async_computation.12 | async-start | bytes 1146880 | tf_op jit(solution)/shard_map/reduce_scatter | solution.py:318
  432.1 412.7 %reduce-scatter.33.cloned.1.call-start = ((), (), s32[]{:S(2)}) async-start(), calls=%async_computation.22 | async-start | bytes 1146880 | tf_op jit(solution)/shard_map/reduce_scatter | solution.py:318
  497.6 34.6 %copy-start.184 = (f32[128]{0:T(128)S(1)}, f32[128]{0:T(128)}, u32[]{:S(2)}) copy-start(f32[128]{0:T(128)} %copy-done.183) | copy-start | bytes 1540
  497.6 34.6 %copy-start.186 = (f32[128]{0:T(128)S(1)}, f32[128]{0:T(128)}, u32[]{:S(2)}) copy-start(f32[128]{0:T(128)} %copy-done.185) | copy-start | bytes 1540
  497.6 34.6 %copy-start.215 = (f32[4,128]{1,0:T(4,128)S(1)}, f32[4,128]{1,0:T(4,128)}, u32[]{:S(2)}) copy-start(f32[4,128]{1,0:T(4,128)} %copy-done.214) | copy-start | bytes 6148
  497.6 35.9 %copy-start.188 = (f32[4,128]{1,0:T(4,128)S(1)}, f32[4,128]{1,0:T(4,128)}, u32[]{:S(2)}) copy-start(f32[4,128]{1,0:T(4,128)} %copy-done.187) | copy-start | bytes 6148
  497.6 35.9 %copy-start.190 = (f32[4,128]{1,0:T(4,128)S(1)}, f32[4,128]{1,0:T(4,128)}, u32[]{:S(2)}) copy-start(f32[4,128]{1,0:T(4,128)} %copy-done.189) | copy-start | bytes 6148
  497.6 35.9 %copy-start.192 = (f32[4,128]{1,0:T(4,128)S(1)}, f32[4,128]{1,0:T(4,128)}, u32[]{:S(2)}) copy-start(f32[4,128]{1,0:T(4,128)} %copy-done.191) | copy-start | bytes 6148
  497.6 59.6 %copy-start.154 = (bf16[64,128]{1,0:T(8,128)(2,1)S(1)}, bf16[64,128]{1,0:T(8,128)(2,1)}, u32[]{:S(2)}) copy-start(bf16[64,128]{1,0:T(8,128)(2,1)} %param.25) | copy-start | bytes 49156
  498.3 59.9 %copy-start.206 = (f32[4,2,64]{2,0,1:T(4,128)}, f32[4,2,64]{2,0,1:T(4,128)S(1)}, u32[]{:S(2)}) copy-start(f32[4,2,64]{2,0,1:T(4,128)S(1)} %get-tuple-element.185) | copy-start | bytes 6148
  499.6 58.6 %copy-start.230 = (f32[4]{0:T(128)S(1)}, f32[4]{0:T(128)}, u32[]{:S(2)}) copy-start(f32[4]{0:T(128)} %copy-done.229) | copy-start | bytes 52
  501.0 58.1 %copy-start.175 = (f32[8,1,64]{2,0,1:T(8,128)S(1)}, f32[8,1,64]{2,0,1:T(8,128)}, u32[]{:S(2)}) copy-start(f32[8,1,64]{2,0,1:T(8,128)} %copy-done.174) | copy-start | bytes 6148
  501.0 58.1 %copy-start.177 = (f32[8,1,64]{2,0,1:T(8,128)S(1)}, f32[8,1,64]{2,0,1:T(8,128)}, u32[]{:S(2)}) copy-start(f32[8,1,64]{2,0,1:T(8,128)} %copy-done.176) | copy-start | bytes 6148
  501.0 58.1 %copy-start.203 = (f32[2,64]{1,0:T(2,128)S(1)}, f32[2,64]{1,0:T(2,128)}, u32[]{:S(2)}) copy-start(f32[2,64]{1,0:T(2,128)} %copy-done.202) | copy-start | bytes 1540
  501.0 58.1 %copy-start.205 = (f32[2,64]{1,0:T(2,128)S(1)}, f32[2,64]{1,0:T(2,128)}, u32[]{:S(2)}) copy-start(f32[2,64]{1,0:T(2,128)} %copy-done.204) | copy-start | bytes 1540
  524.0 38.6 %copy-start.226 = (f32[4]{0:T(128)S(1)}, f32[4]{0:T(128)}, u32[]{:S(2)}) copy-start(f32[4]{0:T(128)} %copy-done.225) | copy-start | bytes 52
  524.0 39.5 %copy-start.228 = (f32[4]{0:T(128)S(1)}, f32[4]{0:T(128)}, u32[]{:S(2)}) copy-start(f32[4]{0:T(128)} %copy-done.227) | copy-start | bytes 52
  524.0 40.4 %copy-start.179 = (f32[8,1,64]{2,0,1:T(8,128)S(1)}, f32[8,1,64]{2,0,1:T(8,128)}, u32[]{:S(2)}) copy-start(f32[8,1,64]{2,0,1:T(8,128)} %copy-done.178) | copy-start | bytes 6148
  524.0 40.4 %copy-start.181 = (f32[8,1,64]{2,0,1:T(8,128)S(1)}, f32[8,1,64]{2,0,1:T(8,128)}, u32[]{:S(2)}) copy-start(f32[8,1,64]{2,0,1:T(8,128)} %copy-done.180) | copy-start | bytes 6148
  526.0 41.1 %copy-start.212 = (f32[4,2,64]{2,0,1:T(4,128)}, f32[4,2,64]{2,0,1:T(4,128)S(1)}, u32[]{:S(2)}) copy-start(f32[4,2,64]{2,0,1:T(4,128)S(1)} %get-tuple-element.181) | copy-start | bytes 6148
  534.9 32.2 %copy-start.297 = (f32[4,128]{1,0:T(4,128)}, f32[4,128]{1,0:T(4,128)S(1)}, u32[]{:S(2)}) copy-start(f32[4,128]{1,0:T(4,128)S(1)} %get-tuple-element.309) | copy-start | bytes 6148
  534.9 32.2 %copy-start.299 = (f32[4,128]{1,0:T(4,128)}, f32[4,128]{1,0:T(4,128)S(1)}, u32[]{:S(2)}) copy-start(f32[4,128]{1,0:T(4,128)S(1)} %get-tuple-element.306) | copy-start | bytes 6148
  585.1 202.0 %copy-start.341 = (f32[2,64]{1,0:T(2,128)}, f32[2,64]{1,0:T(2,128)S(1)}, u32[]{:S(2)}) copy-start(f32[2,64]{1,0:T(2,128)S(1)} %get-tuple-element.104) | copy-start | bytes 1540
  585.1 202.0 %copy-start.345 = (f32[2,64]{1,0:T(2,128)}, f32[2,64]{1,0:T(2,128)S(1)}, u32[]{:S(2)}) copy-start(f32[2,64]{1,0:T(2,128)S(1)} %get-tuple-element.105) | copy-start | bytes 1540
  670.3 176.5 %reduce-scatter.27.cloned.1.call-start = ((), (), s32[]{:S(2)}) async-start(), calls=%async_computation.19 | async-start | bytes 1146880 | tf_op jit(solution)/shard_map/reduce_scatter | solution.py:318
  776.7 70.1 %reduce-scatter.21.cloned.1.call-start = ((), (), s32[]{:S(2)}) async-start(), calls=%async_computation.16 | async-start | bytes 1146880 | tf_op jit(solution)/shard_map/reduce_scatter | solution.py:318
  806.3 54.6 %reduce-scatter.15.cloned.1.call-start = ((), (), s32[]{:S(2)}) async-start(), calls=%async_computation.13 | async-start | bytes 1146880 | tf_op jit(solution)/shard_map/reduce_scatter | solution.py:318
  837.9 124.2 %reduce-scatter.23.cloned.1.call-start = ((), (), s32[]{:S(2)}) async-start(), calls=%async_computation.17 | async-start | bytes 2007040 | tf_op jit(solution)/shard_map/reduce_scatter | solution.py:321
  840.7 61.7 %copy-start.361 = (f32[64]{0:T(128)S(1)}, f32[64]{0:T(128)}, u32[]{:S(2)}) copy-start(f32[64]{0:T(128)} %get-tuple-element.341) | copy-start | bytes 772
  863.8 66.7 %copy-start.57 = (f32[784,64]{0,1:T(8,128)}, f32[784,64]{0,1:T(8,128)S(1)}, u32[]{:S(2)}) copy-start(f32[784,64]{0,1:T(8,128)S(1)} %get-tuple-element.303) | copy-start | bytes 602116
  902.4 39.9 %copy-start.313 = (f32[64]{0:T(128)}, f32[64]{0:T(128)S(1)}, u32[]{:S(2)}) copy-start(f32[64]{0:T(128)S(1)} %get-tuple-element.88) | copy-start | bytes 772
  902.4 39.9 %copy-start.315 = (f32[64]{0:T(128)}, f32[64]{0:T(128)S(1)}, u32[]{:S(2)}) copy-start(f32[64]{0:T(128)S(1)} %get-tuple-element.89) | copy-start | bytes 772
  905.4 57.9 %reduce-scatter.17.cloned.1.call-start = ((), (), s32[]{:S(2)}) async-start(), calls=%async_computation.14 | async-start | bytes 2007040 | tf_op jit(solution)/shard_map/reduce_scatter | solution.py:321
  920.4 71.5 %reduce-scatter.29.cloned.1.call-start = ((), (), s32[]{:S(2)}) async-start(), calls=%async_computation.20 | async-start | bytes 2007040 | tf_op jit(solution)/shard_map/reduce_scatter | solution.py:321
  932.6 90.9 %reduce-scatter.35.cloned.1.call-start = ((), (), s32[]{:S(2)}) async-start(), calls=%async_computation.23 | async-start | bytes 2007040 | tf_op jit(solution)/shard_map/reduce_scatter | solution.py:321
  944.5 164.9 %all-reduce.53.cloned.1.call-start = ((), (), s32[]{:S(2)}) async-start(), calls=%async_computation.28 | async-start | bytes 2359296 | tf_op jit(solution)/shard_map/psum | solution.py:359
  963.2 60.3 %copy-start.11 = (f32[784,256]{1,0:T(8,128)S(1)}, f32[784,256]{1,0:T(8,128)}, u32[]{:S(2)}) copy-start(f32[784,256]{1,0:T(8,128)} %get-tuple-element.247) | copy-start | bytes 2408452
  965.2 59.4 %copy-start.140 = (bf16[1,784,256]{2,1,0:T(8,128)(2,1)S(1)}, bf16[1,784,256]{2,1,0:T(8,128)(2,1)}, u32[]{:S(2)}) copy-start(bf16[1,784,256]{2,1,0:T(8,128)(2,1)} %fusion.126) | copy-start | bytes 1204228
  (348 other events, 2145.5 us)
Sparse Core Ops, SparseCore 0:
  10.1 22.7 all-gather.12
  35.0 20.0 all-gather.14
  57.2 20.0 all-gather.10
  79.2 20.0 all-gather.8
  417.8 20.8 reduce-scatter.30
  441.2 24.0 reduce-scatter.24
  467.9 24.0 reduce-scatter.18
  494.7 24.1 reduce-scatter.12
  670.4 22.7 reduce-scatter.32
  776.8 22.7 reduce-scatter.26
  806.4 22.8 reduce-scatter.20
  838.0 22.9 reduce-scatter.14
  905.5 24.7 reduce-scatter.22
  932.8 28.4 reduce-scatter.16
  963.7 28.2 reduce-scatter.28
  995.1 28.3 reduce-scatter.34
  1028.4 81.0 all-reduce.52
where the time goes:
time: 1130 us; the launch traced here: 1120 us
  local copies, waits for them, and re-layouts  351 us (31%)
  waiting for transfers between devices  295 us (26%)
  blocking collectives  241 us (21%)
  other arithmetic  106 us (9%)
  matrix products  106 us (9%)
  between operations  21.8 us (2%)
    psum x8, blocking collectives, batch_stats(): return lax.psum((first_sum, second_sum), 'dp')  173 us
    reshape x36, local copies, waits for them, and re-layouts, mid_backward(): backed = jnp.einsum('bhwgo,igo->bhwgi', grad_pre, kernel[kernel_row, kern...  101 us
    psum x1, waiting for transfers between devices, per_device(): lax.psum((weight_terms[0], weight_terms[1], weight_terms[2], weight_terms...  83.4 us
    reduce_scatter x8, waiting for transfers between devices, spread_rows(): return lax.psum_scatter(tensor, 'chan', scatter_dimension=1, tiled=True)  81.1 us
    transpose x36, local copies, waits for them, and re-layouts, mid_backward(): jnp.einsum('bhwgo,igo->bhwgi', grad_pre, kernel[kernel_row, kernel_column...  78.6 us
    all_gather x4, waiting for transfers between devices, gather_in(): return lax.all_gather(tensor, 'chan', axis=1, tiled=True)  71.4 us
    reduce_scatter x4, waiting for transfers between devices, spread_input(): lax.psum_scatter(direct_input(low_in, weight_local).astype(jnp.bfloat16),...  57.3 us
    reshape x36, local copies, waits for them, and re-layouts, mid_forward(): window = window.reshape(images, extent, extent, 2, halves)  55.9 us
  transfers between devices with their start and end apart: 17, of which 12 were waited for; matrix products, arithmetic and copies ran while one was open for 24% of the time, Pallas kernels for 0%

commit v1 on v0

v1 whole, which is shorter than its diff:
```python
import functools

import jax
import jax.numpy as jnp
from jax import lax
from jax.experimental import pallas as pl
from jax.experimental.pallas import tpu as pltpu
from jax.sharding import PartitionSpec as P

SIDE = 14
PIXELS = SIDE * SIDE
WIDE = 16
PADDED = SIDE * WIDE
STRIDE = PADDED + WIDE
CHUNK = 16
UNROLL = 2
EPSILON = 1e-05
HIGHEST = lax.Precision.HIGHEST
F32 = jnp.float32
BF16 = jnp.bfloat16


def dot_nn(left, right):
    return lax.dot_general(left, right, (((1,), (0,)), ((), ())), preferred_element_type=F32)


def dot_nt(left, right, precision=None):
    return lax.dot_general(
        left, right, (((1,), (1,)), ((), ())), preferred_element_type=F32, precision=precision
    )


def dot_tn(left, right):
    return lax.dot_general(left, right, (((0,), (0,)), ((), ())), preferred_element_type=F32)


def logistic(value):
    return 0.5 + 0.5 * jnp.tanh(0.5 * value)


def silu(value):
    return value * logistic(value)


def slope(value):
    share = logistic(value)
    return share * (1.0 + value * (1.0 - share))


def moments(first, second, total):
    center = first / total
    return center, lax.rsqrt(second / total - center * center + EPSILON)


def fold(value):
    return jnp.sum(value.reshape(-1, 8, value.shape[-1]), axis=0)


def total_of(value):
    return jnp.sum(value, axis=0, keepdims=True)


def columns_real(rows):
    spot = lax.broadcasted_iota(jnp.int32, (rows, 1), 0)
    return (lax.rem(spot, WIDE) < SIDE).astype(F32)


def real_image(count_ref, image):
    return jnp.where(count_ref[0] > image, 1.0, 0.0).astype(F32)


def spread_map_rows(flat_ref, wide_ref):
    for line in range(flat_ref.shape[0] // SIDE):
        wide_ref[line * WIDE : line * WIDE + SIDE, :] = flat_ref[line * SIDE : (line + 1) * SIDE, :]
        wide_ref[line * WIDE + SIDE : (line + 1) * WIDE, :] = jnp.zeros(
            (WIDE - SIDE, wide_ref.shape[1]), wide_ref.dtype
        )


def pack_map_rows(wide_ref, flat_ref):
    for line in range(flat_ref.shape[0] // SIDE):
        flat_ref[line * SIDE : (line + 1) * SIDE, :] = wide_ref[line * WIDE : line * WIDE + SIDE, :]


def clear_gaps(taps_ref, images):
    for gap in range(images + 1):
        taps_ref[:, gap * STRIDE : gap * STRIDE + WIDE, :] = jnp.zeros(
            (3, WIDE, taps_ref.shape[2]), taps_ref.dtype
        )


def store_taps(taps_ref, at, value):
    here = pl.ds(pl.multiple_of(at, WIDE), WIDE)
    taps_ref[0, here, :] = pltpu.roll(value, 1, 0).astype(taps_ref.dtype)
    taps_ref[1, here, :] = value.astype(taps_ref.dtype)
    taps_ref[2, here, :] = pltpu.roll(value, WIDE - 1, 0).astype(taps_ref.dtype)


def call(body, outs, scratch, flops, *args, smem=1):
    specs = [pl.BlockSpec(memory_space=pltpu.SMEM)] * smem + [
        pl.BlockSpec(memory_space=pltpu.VMEM)
    ] * (len(args) - smem)
    moved = sum(a.size * a.dtype.itemsize for a in args) + sum(
        o.size * o.dtype.itemsize for o in outs
    )
    return pl.pallas_call(
        body,
        out_shape=outs,
        in_specs=specs,
        out_specs=[pl.BlockSpec(memory_space=pltpu.VMEM)] * len(outs),
        scratch_shapes=scratch,
        compiler_params=pltpu.CompilerParams(vmem_limit_bytes=50 * 2**20),
        cost_estimate=pl.CostEstimate(flops=flops, bytes_accessed=moved, transcendentals=0),
        name=body.func.__name__ if isinstance(body, functools.partial) else body.__name__,
    )(*args)


def shape(dims, kind=F32):
    return jax.ShapeDtypeStruct(dims, kind)


def reduce_in(count_ref, x_ref, w_ref, pre_ref, msg_ref, flat_ref):
    parts = [dot_nn(x_ref[k], w_ref[k]) for k in range(x_ref.shape[0])]
    flat_ref[...] = functools.reduce(jnp.add, parts)
    spread_map_rows(flat_ref, pre_ref)
    first = jnp.zeros((1, pre_ref.shape[1]), F32)
    second = jnp.zeros((1, pre_ref.shape[1]), F32)
    for image in range(pre_ref.shape[0] // PADDED):
        real = real_image(count_ref, image)
        value = pre_ref[image * PADDED : (image + 1) * PADDED, :]
        first = first + real * total_of(value)
        second = second + real * total_of(value * value)
    sums = jnp.concatenate([first, second], axis=0)
    msg_ref[...] = jnp.broadcast_to(sums[None], msg_ref.shape)


def conv_mid(
    count_ref, total_ref, pre_ref, sums_ref, affine_ref, w_ref, taps_ref, mid_ref, msg_ref
):
    images = pre_ref.shape[0] // PADDED
    total = total_ref[0] * PIXELS
    sums = jnp.sum(sums_ref[...], axis=0)
    center, scale = moments(sums[0:1], sums[1:2], total)
    gain = affine_ref[0:1, :] * scale
    shift = affine_ref[1:2, :]
    clear_gaps(taps_ref, images)
    keep = columns_real(WIDE)
    for image in range(images):

        def normalize(step, carry, image=image):
            rows = pl.multiple_of(step * WIDE, WIDE)
            value = pre_ref[pl.ds(image * PADDED + rows, WIDE), :]
            value = silu((value - center) * gain + shift) * keep
            store_taps(taps_ref, image * STRIDE + WIDE + rows, value)
            return carry

        lax.fori_loop(0, SIDE, normalize, 0, unroll=UNROLL)
    half = pre_ref.shape[1] // 2
    width = pre_ref.shape[1]
    keep = columns_real(PADDED)
    firsts = [jnp.zeros((1, width), F32) for _ in range(2)]
    seconds = [jnp.zeros((1, width), F32) for _ in range(2)]
    for image in range(images):
        real = real_image(count_ref, image)
        for r in range(2):
            left = jnp.concatenate(
                [
                    taps_ref[
                        b,
                        image * STRIDE + a * WIDE : image * STRIDE + a * WIDE + PADDED,
                        r * half : (r + 1) * half,
                    ]
                    for a in range(3)
                    for b in range(3)
                ],
                axis=1,
            )
            value = dot_nn(left, w_ref[r])
            mid_ref[image * PADDED : (image + 1) * PADDED, r * width : (r + 1) * width] = value
            held = value * keep
            firsts[r] = firsts[r] + real * total_of(held)
            seconds[r] = seconds[r] + real * total_of(held * held)
    sums = jnp.concatenate(
        [jnp.concatenate(firsts, axis=1), jnp.concatenate(seconds, axis=1)], axis=0
    )
    msg_ref[...] = jnp.broadcast_to(sums[None], msg_ref.shape)


def mid_norm(total_ref, sums_ref, affine_ref):
    sums = jnp.sum(sums_ref[...], axis=0)
    center, scale = moments(sums[0:1], sums[1:2], total_ref[0] * PIXELS)
    return center, scale, affine_ref[0:1, :], affine_ref[1:2, :]


def pool(count_ref, total_ref, mid_ref, sums_ref, affine_ref, squeeze_ref, pooled_ref, msg_ref):
    images = mid_ref.shape[0] // PADDED
    width = mid_ref.shape[1] // 2
    center, scale, gain, shift = mid_norm(total_ref, sums_ref, affine_ref)
    keep = columns_real(CHUNK)
    for image in range(images):

        def gather(step, carry, image=image):
            active, rise, lean = carry
            at = pl.multiple_of(image * PADDED + step * CHUNK, CHUNK)
            normed = (mid_ref[pl.ds(at, CHUNK), :] - center) * scale
            value = normed * gain + shift
            share = logistic(value)
            active = active + fold(value * share * keep)
            inclined = share * (1.0 + value * (1.0 - share)) * keep
            return active, rise + fold(inclined), lean + fold(inclined * normed)

        nothing = jnp.zeros((8, 2 * width), F32)
        active, rise, lean = lax.fori_loop(
            0, PADDED // CHUNK, gather, (nothing, nothing, nothing), unroll=UNROLL
        )
        active = total_of(active)
        pooled_ref[image : image + 1, :] = (active[:, :width] + active[:, width:]) / PIXELS
        rise, lean = total_of(rise), total_of(lean)
        lanes = msg_ref.shape[2]
        for t, row in enumerate((rise, lean)):
            for q in range(2 * width // lanes):
                at = images + (t * images + image) * (2 * width // lanes) + q
                msg_ref[:, at : at + 1, :] = jnp.broadcast_to(
                    row[:, q * lanes : (q + 1) * lanes][None], (msg_ref.shape[0], 1, lanes)
                )
    squeezed = lax.dot_general(
        pooled_ref[...],
        squeeze_ref[...].astype(F32),
        (((1,), (0,)), ((), ())),
        preferred_element_type=F32,
        precision=HIGHEST,
    )
    msg_ref[:, 0:images, :] = jnp.broadcast_to(
        squeezed[None], (msg_ref.shape[0],) + squeezed.shape
    )
    real = [real_image(count_ref, image) * pooled_ref[image : image + 1, :] for image in range(images)]
    real = functools.reduce(jnp.add, real)
    for q in range(width // lanes):
        at = images + 2 * images * (2 * width // lanes) + q
        msg_ref[:, at : at + 1, :] = jnp.broadcast_to(
            real[:, q * lanes : (q + 1) * lanes][None], (msg_ref.shape[0], 1, lanes)
        )


def gate_norm(total_ref, pooled_ref, wall_ref):
    images = wall_ref.shape[1]
    rows = pooled_ref[:, 0:images, :]
    wall = wall_ref[...]
    first = jnp.sum(jnp.sum(wall * rows, axis=0), axis=0, keepdims=True)
    second = jnp.sum(jnp.sum(wall * rows * rows, axis=0), axis=0, keepdims=True)
    return moments(first, second, total_ref[0])


def attend(
    count_ref,
    total_ref,
    pooled_ref,
    wall_ref,
    gate_affine_ref,
    excite_ref,
    bias_ref,
    mid_ref,
    mid_sums_ref,
    mid_affine_ref,
    w_out_ref,
    gate_ref,
    attention_ref,
    weighted_ref,
    out_ref,
    msg_ref,
    wide_ref,
    flat_ref,
):
    images = mid_ref.shape[0] // PADDED
    width = mid_ref.shape[1] // 2
    center, scale = gate_norm(total_ref, pooled_ref, wall_ref)
    own = pooled_ref[count_ref[1], 0:images, :]
    normed = (own - center) * scale
    gate_pre = normed * gate_affine_ref[0:1, :] + gate_affine_ref[1:2, :]
    gate = silu(gate_pre)
    gate_ref[0] = gate
    gate_ref[1] = slope(gate_pre)
    logits = (
        lax.dot_general(
            gate,
            excite_ref[...].astype(F32),
            (((1,), (0,)), ((), ())),
            preferred_element_type=F32,
            precision=HIGHEST,
        )
        + bias_ref[...]
    )
    lean = 0.5 * jnp.tanh(0.5 * (logits[:, :width] - logits[:, width:]))
    attention_ref[:, :width] = 0.5 + lean
    attention_ref[:, width:] = 0.5 - lean
    center, scale, gain, shift = mid_norm(total_ref, mid_sums_ref, mid_affine_ref)
    for image in range(images):
        share = attention_ref[image : image + 1, :]

        def weigh(step, carry, image=image, share=share):
            at = pl.multiple_of(image * PADDED + step * CHUNK, CHUNK)
            normed = (mid_ref[pl.ds(at, CHUNK), :] - center) * scale
            value = share * silu(normed * gain + shift)
            wide_ref[pl.ds(at, CHUNK), :] = value[:, :width] + value[:, width:]
            return carry

        lax.fori_loop(0, PADDED // CHUNK, weigh, 0, unroll=UNROLL)
    pack_map_rows(wide_ref, flat_ref)
    weighted_ref[...] = flat_ref[...].astype(BF16)
    spot = lax.broadcasted_iota(jnp.int32, (flat_ref.shape[0], 1), 0)
    real = (spot < count_ref[0] * PIXELS).astype(F32)
    blocks = w_out_ref.shape[0]
    for k in range(blocks):
        value = dot_nn(weighted_ref[...], w_out_ref[k])
        out_ref[k] = value
        held = value * real
        for t, row in enumerate((total_of(held), total_of(held * value))):
            msg_ref[:, t * blocks + k : t * blocks + k + 1, :] = jnp.broadcast_to(
                row[None], (msg_ref.shape[0], 1, row.shape[1])
            )


def finish(
    count_ref, total_ref, out_ref, sums_ref, affine_ref, x_ref, cot_ref, result_ref, grad_ref, msg_ref
):
    blocks, rows, lanes = out_ref.shape
    sums = jnp.sum(sums_ref[...], axis=0)
    center, scale = moments(sums[:blocks], sums[blocks:], total_ref[0] * PIXELS)
    limit = count_ref[0] * PIXELS
    for k in range(blocks):
        mu, r = center[k : k + 1], scale[k : k + 1]
        gain, shift = affine_ref[0, k : k + 1, :], affine_ref[1, k : k + 1, :]

        def chunk(step, carry, k=k, mu=mu, r=r, gain=gain, shift=shift):
            first, second = carry
            at = pl.multiple_of(step * CHUNK, CHUNK)
            here = pl.ds(at, CHUNK)
            spot = lax.broadcasted_iota(jnp.int32, (CHUNK, 1), 0) + at
            real = (spot < limit).astype(F32)
            normed = (out_ref[k, here, :] - mu) * r
            summed = x_ref[k, here, :].astype(F32) + (normed * gain + shift)
            share = logistic(summed) * real
            result_ref[k, here, :] = (summed * share).astype(BF16)
            upstream = cot_ref[k, here, :].astype(F32)
            grad = upstream * share * (1.0 + summed * (1.0 - share))
            grad_ref[k, here, :] = grad
            return first + fold(grad), second + fold(grad * normed)

        nothing = jnp.zeros((8, lanes), F32)
        first, second = lax.fori_loop(
            0, rows // CHUNK, chunk, (nothing, nothing), unroll=UNROLL
        )
        for t, row in enumerate((total_of(first), total_of(second))):
            msg_ref[:, t * blocks + k : t * blocks + k + 1, :] = jnp.broadcast_to(
                row[None], (msg_ref.shape[0], 1, lanes)
            )


def back_out(
    count_ref,
    total_ref,
    grad_ref,
    out_ref,
    sums_ref,
    back_ref,
    affine_ref,
    w_out_ref,
    mid_ref,
    mid_sums_ref,
    mid_affine_ref,
    attention_ref,
    gate_ref,
    excite_ref,
    low_ref,
    gw_ref,
    logits_ref,
    msg_ref,
    flat_ref,
):
    blocks, rows, lanes = out_ref.shape
    images = attention_ref.shape[0]
    width = attention_ref.shape[1] // 2
    total = total_ref[0] * PIXELS
    sums = jnp.sum(sums_ref[...], axis=0)
    center, scale = moments(sums[:blocks], sums[blocks:], total)
    back = jnp.sum(back_ref[...], axis=0) / total
    limit = count_ref[0] * PIXELS
    for k in range(blocks):
        mu, r = center[k : k + 1], scale[k : k + 1]
        gain = affine_ref[0, k : k + 1, :] * r
        first, second = back[k : k + 1], back[blocks + k : blocks + k + 1]

        def chunk(step, carry, k=k, mu=mu, r=r, gain=gain, first=first, second=second):
            at = pl.multiple_of(step * CHUNK, CHUNK)
            here = pl.ds(at, CHUNK)
            spot = lax.broadcasted_iota(jnp.int32, (CHUNK, 1), 0) + at
            real = (spot < limit).astype(F32)
            normed = (out_ref[k, here, :] - mu) * r
            value = gain * (grad_ref[k, here, :] - real * (first + normed * second))
            low_ref[k, here, :] = value.astype(BF16)
            return carry

        lax.fori_loop(0, rows // CHUNK, chunk, 0, unroll=UNROLL)
    parts = [dot_nt(low_ref[k], w_out_ref[k]) for k in range(blocks)]
    flat_ref[...] = functools.reduce(jnp.add, parts)
    spread_map_rows(flat_ref, gw_ref)
    center, scale, gain, shift = mid_norm(total_ref, mid_sums_ref, mid_affine_ref)
    rises, leans, attended = [], [], []
    for image in range(images):

        def gather(step, carry, image=image):
            attended, rise, lean = carry
            at = pl.multiple_of(image * PADDED + step * CHUNK, CHUNK)
            normed = (mid_ref[pl.ds(at, CHUNK), :] - center) * scale
            value = normed * gain + shift
            share = logistic(value)
            grad = gw_ref[pl.ds(at, CHUNK), :]
            grad = jnp.concatenate([grad, grad], axis=1)
            active = grad * share
            attended = attended + fold(active * value)
            inclined = active * (1.0 + value * (1.0 - share))
            return attended, rise + fold(inclined), lean + fold(inclined * normed)

        nothing = jnp.zeros((8, 2 * width), F32)
        parts = lax.fori_loop(
            0, PADDED // CHUNK, gather, (nothing, nothing, nothing), unroll=UNROLL
        )
        share = attention_ref[image : image + 1, :]
        attended.append(total_of(parts[0]))
        rises.append(share * total_of(parts[1]))
        leans.append(share * total_of(parts[2]))
    grad = jnp.concatenate(attended, axis=0)
    attention = attention_ref[...]
    inner = attention * grad
    inner = inner[:, :width] + inner[:, width:]
    logits = attention * (grad - jnp.concatenate([inner, inner], axis=1))
    logits_ref[...] = logits
    gate = dot_nt(logits, excite_ref[...].astype(F32), HIGHEST) * gate_ref[1]
    pack = msg_ref.shape[2]
    msg_ref[:, 0:images, :] = jnp.broadcast_to(gate[None], (msg_ref.shape[0],) + gate.shape)
    for t, row in enumerate((functools.reduce(jnp.add, rises), functools.reduce(jnp.add, leans))):
        for q in range(2 * width // pack):
            at = images + t * (2 * width // pack) + q
            msg_ref[:, at : at + 1, :] = jnp.broadcast_to(
                row[:, q * pack : (q + 1) * pack][None], (msg_ref.shape[0], 1, pack)
            )


def back_mid(
    count_ref,
    total_ref,
    back_ref,
    pooled_ref,
    wall_ref,
    gate_affine_ref,
    squeeze_ref,
    attention_ref,
    gw_ref,
    mid_ref,
    mid_sums_ref,
    mid_affine_ref,
    pre_ref,
    sums_ref,
    affine_ref,
    w_ref,
    low_ref,
    grad_ref,
    gate_ref,
    vector_ref,
    msg_ref,
    taps_ref,
):
    images = attention_ref.shape[0]
    width = attention_ref.shape[1] // 2
    groups = wall_ref.shape[0]
    lanes = wall_ref.shape[2]
    pieces = 2 * width // lanes
    total = total_ref[0] * PIXELS
    center, scale = gate_norm(total_ref, pooled_ref, wall_ref)
    gain = gate_affine_ref[0:1, :] * scale
    wall = wall_ref[...]
    normed = (pooled_ref[:, 0:images, :] - center) * scale
    grads = back_ref[:, 0:images, :]
    first = jnp.sum(jnp.sum(wall * grads, axis=0), axis=0, keepdims=True)
    second = jnp.sum(jnp.sum(wall * grads * normed, axis=0), axis=0, keepdims=True)
    vector_ref[0:1, 0:lanes] = second
    vector_ref[0:1, lanes : 2 * lanes] = first
    squeezed = gain * (grads - wall * (first + normed * second) / total_ref[0])
    gate_ref[...] = squeezed
    gate_rows = jnp.concatenate([gate_ref[g] for g in range(groups)], axis=0)
    pooled_grad = dot_nt(gate_rows, squeeze_ref[...].astype(F32), HIGHEST) / PIXELS
    back = []
    for t in range(2):
        row = [
            jnp.sum(back_ref[:, images + t * pieces + q, :], axis=0, keepdims=True)
            for q in range(pieces)
        ]
        for g in range(groups):
            for image in range(images):
                grad = pooled_grad[g * images + image : g * images + image + 1, :]
                for q in range(pieces):
                    at = images + (t * images + image) * pieces + q
                    place = (q * lanes) % width
                    row[q] = row[q] + pooled_ref[g, at : at + 1, :] * grad[:, place : place + lanes]
        back.append(jnp.concatenate(row, axis=1))
    vector_ref[1:2, :] = back[1]
    vector_ref[2:3, :] = back[0]
    first, second = back[0] / total, back[1] / total
    center, scale, gain, shift = mid_norm(total_ref, mid_sums_ref, mid_affine_ref)
    gained = gain * scale
    clear_gaps(taps_ref, images)
    keep = columns_real(WIDE)
    own = dot_nt(gate_ref[count_ref[1]], squeeze_ref[...].astype(F32), HIGHEST) / PIXELS
    own = jnp.concatenate([own, own], axis=1)
    for image in range(images):
        share = attention_ref[image : image + 1, :]
        offset = own[image : image + 1, :]
        real = real_image(count_ref, image)
        lead, lag = real * first, real * second

        def chunk(step, carry, image=image, share=share, offset=offset, lead=lead, lag=lag):
            rows = pl.multiple_of(step * WIDE, WIDE)
            here = pl.ds(image * PADDED + rows, WIDE)
            normed = (mid_ref[here, :] - center) * scale
            grad = gw_ref[here, :]
            grad = jnp.concatenate([grad, grad], axis=1)
            grad = (share * grad + offset) * slope(normed * gain + shift)
            value = gained * (grad - (lead + normed * lag)) * keep
            store_taps(taps_ref, image * STRIDE + WIDE + rows, value)
            return carry

        lax.fori_loop(0, SIDE, chunk, 0, unroll=UNROLL)
    low_ref[...] = taps_ref[1]
    sums = jnp.sum(sums_ref[...], axis=0)
    center, scale = moments(sums[0:1], sums[1:2], total)
    gain, shift = affine_ref[0:1, :], affine_ref[1:2, :]
    half = width // 2
    keep = columns_real(PADDED)
    firsts = [jnp.zeros((1, half), F32) for _ in range(2)]
    seconds = [jnp.zeros((1, half), F32) for _ in range(2)]
    for image in range(images):
        real = real_image(count_ref, image)
        here = slice(image * PADDED, (image + 1) * PADDED)
        for r in range(2):
            left = jnp.concatenate(
                [
                    taps_ref[
                        2 - b,
                        image * STRIDE + (2 - a) * WIDE : image * STRIDE + (2 - a) * WIDE + PADDED,
                        r * width : (r + 1) * width,
                    ]
                    for a in range(3)
                    for b in range(3)
                ],
                axis=1,
            )
            lane = slice(r * half, (r + 1) * half)
            normed = (pre_ref[here, lane] - center[:, lane]) * scale[:, lane]
            value = dot_nn(left, w_ref[r]) * slope(normed * gain[:, lane] + shift[:, lane])
            value = value * (keep * real)
            grad_ref[here, lane] = value
            firsts[r] = firsts[r] + total_of(value)
            seconds[r] = seconds[r] + total_of(value * normed)
    sums = jnp.concatenate(
        [jnp.concatenate(firsts, axis=1), jnp.concatenate(seconds, axis=1)], axis=0
    )
    msg_ref[...] = jnp.broadcast_to(sums[None], msg_ref.shape)


def weight_mid_term(taps_ref, low_ref, out_ref):
    half = taps_ref.shape[2] // 2
    width = low_ref.shape[1] // 2
    rows = low_ref.shape[0] - 2 * WIDE
    for r in range(2):
        right = low_ref[WIDE : WIDE + rows, r * width : (r + 1) * width]
        for a in range(3):
            for b in range(3):
                left = taps_ref[b, a * WIDE : a * WIDE + rows, r * half : (r + 1) * half]
                at = (3 * a + b) * half
                out_ref[r, at : at + half, :] = dot_tn(left, right)


def back_in(
    count_ref,
    total_ref,
    grad_ref,
    pre_ref,
    sums_ref,
    back_ref,
    affine_ref,
    w_ref,
    summed_ref,
    low_ref,
    result_ref,
    vector_ref,
    flat_ref,
):
    images = pre_ref.shape[0] // PADDED
    total = total_ref[0] * PIXELS
    sums = jnp.sum(sums_ref[...], axis=0)
    center, scale = moments(sums[0:1], sums[1:2], total)
    back = jnp.sum(back_ref[...], axis=0)
    vector_ref[0:1, :] = back[1:2]
    vector_ref[1:2, :] = back[0:1]
    first, second = back[0:1] / total, back[1:2] / total
    gain = affine_ref[0:1, :] * scale
    for image in range(images):
        real = real_image(count_ref, image)
        lead, lag = real * first, real * second
        for line in range(SIDE):
            at = image * PADDED + line * WIDE
            normed = (pre_ref[at : at + WIDE, :] - center) * scale
            value = gain * (grad_ref[at : at + WIDE, :] - (lead + normed * lag))
            at = image * PIXELS + line * SIDE
            flat_ref[at : at + SIDE, :] = value[:SIDE]
    low_ref[...] = flat_ref[...].astype(BF16)
    for k in range(w_ref.shape[0]):
        result_ref[k] = (dot_nt(low_ref[...], w_ref[k]) + summed_ref[k]).astype(BF16)


def stack_lanes(value):
    rows = value.shape[-2] // 2
    return jnp.concatenate([value[..., :rows, :], value[..., rows:, :]], axis=-1)


def unstack_lanes(value):
    lanes = value.shape[-1] // 2
    return jnp.concatenate([value[..., :lanes], value[..., lanes:]], axis=-2)


def per_device(
    activations,
    counts,
    weight_in,
    gain_in,
    shift_in,
    weight_mid,
    gain_mid,
    shift_mid,
    weight_squeeze,
    gain_gate,
    shift_gate,
    weight_excite,
    shift_excite,
    weight_out,
    gain_out,
    shift_out,
    cotangent,
    *,
    groups,
    parts,
):
    batches, rows, lanes = activations.shape
    images = rows // PIXELS
    own = weight_in.shape[1]
    width = own * parts
    inter = gain_gate.shape[0]
    wide_rows = images * PADDED
    gap_rows = WIDE + images * STRIDE
    batch = lax.axis_index("chan")
    group = lax.axis_index("dp")

    def over_chan(tensor):
        return lax.all_to_all(tensor, "chan", 0, 0, tiled=False)

    def over_groups(tensor):
        return lax.all_to_all(tensor, "dp", 0, 0, tiled=False)

    x = over_chan(activations)
    cot = over_chan(cotangent)
    count_row = lax.dynamic_index_in_dim(counts, batch, keepdims=False)
    own_count = lax.dynamic_index_in_dim(count_row, group, keepdims=False)
    count = jnp.stack([own_count, group]).astype(jnp.int32)
    total = jnp.sum(count_row).astype(F32).reshape(1)
    slots = jnp.arange(images, dtype=jnp.int32)
    wall = (slots[None, :] < count_row[:, None]).astype(F32)
    wall = jnp.broadcast_to(wall[:, :, None], (groups, images, inter))

    small = jnp.concatenate(
        [
            jnp.concatenate([gain_in, shift_in])[None],
            gain_mid.reshape(1, 2 * own),
            shift_mid.reshape(1, 2 * own),
            shift_excite.reshape(1, 2 * own),
            gain_out.reshape(-1, 2 * own),
            shift_out.reshape(-1, 2 * own),
        ]
    )
    small = jnp.pad(small, ((0, 16 - small.shape[0]), (0, 0)))
    blocks = [
        small,
        stack_lanes(weight_in),
        weight_mid.reshape(-1, 2 * own),
        stack_lanes(weight_squeeze.reshape(-1, 64)),
        weight_excite.reshape(inter, 2 * own),
        jnp.concatenate([weight_out[:, :128], weight_out[:, 128:]]),
    ]
    sizes = [b.shape[0] for b in blocks]
    packed = lax.all_gather(jnp.concatenate(blocks), "chan")
    pieces = []
    at = 0
    for size in sizes:
        pieces.append(packed[:, at : at + size])
        at += size
    small = pieces[0].astype(F32)
    in_affine = jnp.stack([small[:, 0, :own].reshape(-1), small[:, 0, own:].reshape(-1)])

    def halves(value):
        return value.reshape(parts, 2, own).transpose(1, 0, 2).reshape(1, 2 * width)

    mid_affine = jnp.concatenate([halves(small[:, 1]), halves(small[:, 2])])
    bias = halves(small[:, 3])
    outs = lanes // (2 * own)
    out_affine = jnp.stack(
        [small[:, 4 : 4 + outs].reshape(parts, lanes), small[:, 4 + outs : 4 + 2 * outs].reshape(parts, lanes)]
    )
    w_in = unstack_lanes(pieces[1]).transpose(1, 0, 2).reshape(parts, lanes, width)
    w_mid = pieces[2].reshape(parts, -1, 2, own).transpose(2, 1, 0, 3).reshape(2, -1, width)
    w_mid_back = (
        w_mid.reshape(2, 9, width // 2, width).transpose(0, 1, 3, 2).reshape(2, 9 * width, width // 2)
    )
    squeeze = unstack_lanes(pieces[3]).reshape(width, inter)
    excite = pieces[4].reshape(parts, inter, 2, own).transpose(1, 2, 0, 3).reshape(inter, 2 * width)
    w_out = jnp.concatenate(
        [pieces[5][:, :width], pieces[5][:, width:]], axis=-1
    )
    gate_affine = jnp.stack([gain_gate, shift_gate]).astype(F32)

    product = 2 * rows * lanes * parts * width
    pre_in, msg = call(
        reduce_in,
        [shape((wide_rows, width)), shape((groups, 2, width))],
        [pltpu.VMEM((rows, width), F32)],
        product,
        count,
        x,
        w_in,
    )
    in_sums = over_groups(msg)
    conv = 2 * wide_rows * 9 * width * width
    taps, mid, msg = call(
        conv_mid,
        [
            shape((3, gap_rows, width), BF16),
            shape((wide_rows, 2 * width)),
            shape((groups, 2, 2 * width)),
        ],
        [],
        conv,
        count,
        total,
        pre_in,
        in_sums,
        in_affine,
        w_mid,
        smem=2,
    )
    mid_sums = over_groups(msg)
    inclines = 2 * images * 2 * width // inter
    message = -(-(images + inclines + width // inter) // 8) * 8
    pooled, msg = call(
        pool,
        [shape((images, width)), shape((groups, message, inter))],
        [],
        0,
        count,
        total,
        mid,
        mid_sums,
        mid_affine,
        squeeze,
        smem=2,
    )
    gathered = over_groups(msg)
    gate, attention, weighted, out, msg = call(
        attend,
        [
            shape((2, images, inter)),
            shape((images, 2 * width)),
            shape((rows, width), BF16),
            shape((parts, rows, lanes)),
            shape((groups, 2 * parts, lanes)),
        ],
        [pltpu.VMEM((wide_rows, width), F32), pltpu.VMEM((rows, width), F32)],
        product,
        count,
        total,
        gathered,
        wall,
        gate_affine,
        excite,
        bias,
        mid,
        mid_sums,
        mid_affine,
        w_out,
        smem=2,
    )
    out_sums = over_groups(msg)
    result, grad, msg = call(
        finish,
        [
            shape((parts, rows, lanes), BF16),
            shape((parts, rows, lanes)),
            shape((groups, 2 * parts, lanes)),
        ],
        [],
        0,
        count,
        total,
        out,
        out_sums,
        out_affine,
        x,
        cot,
        smem=2,
    )
    out_back = over_groups(msg)
    result = over_chan(result)

    message = -(-(images + 2 * 2 * width // inter) // 8) * 8
    low_out, grad_weighted, grad_logits, msg = call(
        back_out,
        [
            shape((parts, rows, lanes), BF16),
            shape((wide_rows, width)),
            shape((images, 2 * width)),
            shape((groups, message, inter)),
        ],
        [pltpu.VMEM((rows, width), F32)],
        product,
        count,
        total,
        grad,
        out,
        out_sums,
        out_back,
        out_affine,
        w_out,
        mid,
        mid_sums,
        mid_affine,
        attention,
        gate,
        excite,
        smem=2,
    )
    mid_back = over_groups(msg)
    low_mid, grad_hidden, grad_squeeze, vectors, msg = call(
        back_mid,
        [
            shape((gap_rows, 2 * width), BF16),
            shape((wide_rows, width)),
            shape((groups, images, inter)),
            shape((8, 2 * width)),
            shape((groups, 2, width)),
        ],
        [pltpu.VMEM((3, gap_rows, 2 * width), BF16)],
        conv,
        count,
        total,
        mid_back,
        gathered,
        wall,
        gate_affine,
        squeeze,
        attention,
        grad_weighted,
        mid,
        mid_sums,
        mid_affine,
        pre_in,
        in_sums,
        in_affine,
        w_mid_back,
        smem=2,
    )
    in_back = over_groups(msg)
    low_in, grad_x, in_vectors = call(
        back_in,
        [
            shape((rows, width), BF16),
            shape((parts, rows, lanes), BF16),
            shape((8, width)),
        ],
        [pltpu.VMEM((rows, width), F32)],
        product,
        count,
        total,
        grad_hidden,
        pre_in,
        in_sums,
        in_back,
        in_affine,
        w_in,
        grad,
        smem=2,
    )
    grad_x = over_chan(grad_x)

    term_in = jnp.einsum("krc,ro->kco", x, low_in, preferred_element_type=F32)
    term_in = term_in.reshape(parts * lanes, parts, own).transpose(1, 0, 2)
    (term_mid,) = call(
        weight_mid_term, [shape((2, 9 * width // 2, width))], [], conv, taps, low_mid, smem=0
    )
    term_mid = term_mid.reshape(2, -1, parts, own).transpose(2, 1, 0, 3).reshape(parts, -1, 2 * own)
    term_out = jnp.einsum("rc,kro->kco", weighted, low_out, preferred_element_type=F32)
    own_squeeze = lax.dynamic_index_in_dim(grad_squeeze, group, keepdims=False)
    mean = jnp.sum(gathered[:, images + inclines : images + inclines + width // inter], axis=0)
    mean = mean.reshape(1, width) / total
    term_squeeze = jnp.einsum("bc,bk->ck", pooled - mean, own_squeeze, precision=HIGHEST)
    term_excite = jnp.einsum("bk,bo->ko", gate[0], grad_logits, precision=HIGHEST)
    term_excite = term_excite.reshape(inter, 2, parts, own).transpose(2, 0, 1, 3)
    term_bias = jnp.sum(grad_logits, axis=0).reshape(1, 2, parts, own).transpose(2, 0, 1, 3)
    out_vectors = jnp.sum(out_back, axis=0).reshape(2, parts, lanes)

    def piece(row):
        return row.reshape(2, parts, own).transpose(1, 0, 2).reshape(parts, 1, 2 * own)

    everyone = jnp.broadcast_to(vectors[0, : 2 * inter].reshape(1, 2, inter), (parts, 2, inter))
    batch_sums = jnp.concatenate(
        [
            piece(in_vectors[:2].reshape(-1)),
            piece(vectors[1]),
            piece(vectors[2]),
            everyone,
            out_vectors[1].reshape(parts, -1, 2 * own),
            out_vectors[0].reshape(parts, -1, 2 * own),
        ],
        axis=1,
    )
    terms = [
        stack_lanes(term_in),
        term_mid,
        stack_lanes(term_squeeze.reshape(parts, -1, 64)),
        term_excite.reshape(parts, inter, 2 * own),
        jnp.concatenate([term_out[..., :128], term_out[..., 128:]], axis=1),
        term_bias.reshape(parts, 1, 2 * own),
        batch_sums / groups,
    ]
    sizes = [t.shape[1] for t in terms]
    terms = jnp.concatenate(terms, axis=1)
    count_rows = terms.shape[1]
    whole = -(-count_rows // (16 * groups)) * 16 * groups
    terms = jnp.pad(terms, ((0, 0), (0, whole - count_rows), (0, 0)))
    terms = jnp.sum(over_chan(terms.astype(BF16)).astype(F32), axis=0)
    terms = terms.reshape(groups, whole // groups, 2 * own).astype(BF16)
    terms = jnp.sum(over_groups(terms).astype(F32), axis=0).astype(BF16)
    terms = over_groups(jnp.broadcast_to(terms[None], (groups,) + terms.shape))
    terms = terms.reshape(whole, 2 * own).astype(F32)
    pieces = []
    at = 0
    for size in sizes:
        pieces.append(terms[at : at + size])
        at += size
    sums = pieces[6]
    return (
        result,
        grad_x,
        unstack_lanes(pieces[0]),
        sums[0, :own],
        sums[0, own:],
        pieces[1].reshape(weight_mid.shape),
        sums[1].reshape(2, own),
        sums[2].reshape(2, own),
        unstack_lanes(pieces[2]).reshape(weight_squeeze.shape),
        sums[3],
        sums[4],
        pieces[3].reshape(weight_excite.shape),
        pieces[5].reshape(2, own),
        jnp.concatenate([pieces[4][:width], pieces[4][width:]], axis=1),
        sums[5 : 5 + outs].reshape(-1),
        sums[5 + outs : 5 + 2 * outs].reshape(-1),
    )


def solution(mesh):
    placed = (
        P(None, "dp", "chan"),
        P(),
        P(None, "chan"),
        P("chan"),
        P("chan"),
        P(None, None, None, None, "chan"),
        P(None, "chan"),
        P(None, "chan"),
        P("chan", None),
        P(),
        P(),
        P(None, None, "chan"),
        P(None, "chan"),
        P(None, "chan"),
        P("chan"),
        P("chan"),
        P(None, "dp", "chan"),
    )
    return jax.shard_map(
        functools.partial(per_device, groups=mesh.shape["dp"], parts=mesh.shape["chan"]),
        mesh=mesh,
        in_specs=placed,
        out_specs=placed[:1] + placed[:1] + placed[2:16],
        check_vma=False,
    )
```

time: 1130 us -> 386 us (0.34)
  local copies, waits for them, and re-layouts: 351 us -> 90.9 us
  waiting for transfers between devices: 295 us -> 85.3 us
  blocking collectives: 241 us -> 86.1 us
  matrix products: 106 us -> 3.92 us
  other arithmetic: 106 us -> 11.4 us
  starting transfers between devices: 1.3 us -> 47.9 us
  Pallas kernels: 0 us -> 42.6 us
    psum x10 -> x0, blocking collectives: 185 us -> none  [the longest x8 173 us: batch_stats(): return lax.psum((first_sum, second_sum), 'dp')]
    reshape x89 -> x21, local copies, waits for them, and re-layouts: 177 us -> 15.2 us  [the longest x2 3.86 us: per_device(): unstack_lanes(pieces[1]).transpose(1, 0, 2).reshape(parts, lanes, width)]
    reduce_scatter x12 -> x0, waiting for transfers between devices: 138 us -> none  [the longest x8 81.1 us: spread_rows(): return lax.psum_scatter(tensor, 'chan', scatter_dimension=1, tiled=True)]
    dot_general x156 -> x4, matrix products: 106 us -> 3.92 us  [the longest x1 2.18 us: per_device(): jnp.einsum('rc,kro->kco', weighted, low_out, preferred_element_type=F32)]
    all_to_all x0 -> x4, blocking collectives: none -> 86.1 us  [the longest x3 53.2 us: over_groups(): return lax.all_to_all(tensor, 'dp', 0, 0, tiled=False)]
    psum x1 -> x0, waiting for transfers between devices: 83.4 us -> none  [per_device(): lax.psum((weight_terms[0], weight_terms[1], weight_terms[2], weight_terms...]
    transpose x36 -> x7, local copies, waits for them, and re-layouts: 78.6 us -> 10.1 us  [the longest x1 3.03 us: per_device(): w_mid.reshape(2, 9, width // 2, width).transpose(0, 1, 3, 2)]
    all_gather x8 -> x0, blocking collectives: 55.8 us -> none  [gather_rows(): return lax.all_gather(tensor, 'chan', axis=1, tiled=True)]
  transfers between devices with their start and end apart: 17 -> 11, of which waited for: 12 -> 5; matrix products, arithmetic and copies ran while one was open for 24% -> 15% of each run, Pallas kernels for 0% -> 2%
where the time goes in v1:
time: 386 us; the launch traced here: 384 us
  local copies, waits for them, and re-layouts  90.9 us (24%)
  blocking collectives  86.1 us (22%)
  waiting for transfers between devices  85.3 us (22%)
  starting transfers between devices  47.9 us (12%)
  Pallas kernels  42.6 us (11%)
  between operations  15.6 us (4%)
  other arithmetic  11.4 us (3%)
  matrix products  3.92 us (1%)
    all_to_all x3, blocking collectives, over_groups(): return lax.all_to_all(tensor, 'dp', 0, 0, tiled=False)  53.2 us
    pallas_call x9, Pallas kernels, call(): pl.pallas_call(body, out_shape=outs, in_specs=specs, out_specs=[pl.BlockS...  42.6 us
    all_to_all x4, waiting for transfers between devices, over_chan(): return lax.all_to_all(tensor, 'chan', 0, 0, tiled=False)  39.8 us
    all_to_all x1, blocking collectives, over_chan(): return lax.all_to_all(tensor, 'chan', 0, 0, tiled=False)  32.9 us
    all_gather x1, waiting for transfers between devices, per_device(): packed = lax.all_gather(jnp.concatenate(blocks), 'chan')  32.5 us
    all_to_all x6, starting transfers between devices, over_groups(): return lax.all_to_all(tensor, 'dp', 0, 0, tiled=False)  31 us
    unnamed x140, local copies, waits for them, and re-layouts  27.9 us
    all_to_all x4, starting transfers between devices, over_chan(): return lax.all_to_all(tensor, 'chan', 0, 0, tiled=False)  16.9 us
  transfers between devices with their start and end apart: 11, of which 5 were waited for; matrix products, arithmetic and copies ran while one was open for 15% of the time, Pallas kernels for 2%

profile of v1, /device:TPU:0, one launch (start us, length us, event | category | flops | bytes accessed | tf_op | source)
XLA Modules:
  0.0 383.7 jit_solution(8067448019284701530)
XLA Ops:
  12.0 1.2 copy.219
  14.8 1.1 copy.225
  15.9 4.2 %all-to-all-start = ((bf16[4,784,256]{2,1,0:T(8,128)(2,1)}), bf16[4,784,256]{2,1,0:T(8,128)(2,1)S(1)}, u32[]{:S(2)}, u32[]{:S(2)}) async-start(bf16[4,784,256]{2,1,0:T(8,128)(2,1)} %param.17), calls=%async_computation | async-start | bytes 3211264 | tf_op jit(solution)/shard_map/all_to_all | solution.py:664
  22.7 32.5 %all-gather.3.cloned.1.call-done = bf16[9536,128]{1,0:T(8,128)(2,1)} async-done(((bf16[2384,128]{1,0:T(8,128)(2,1)}), bf16[9536,128]{1,0:T(8,128)(2,1)}) %all-gather.3.cloned.1.call-update) | async-done | bytes 2441232 | tf_op jit(solution)/shard_map/all_gather | solution.py:699
  55.2 1.4 fusion.18
  56.8 1.8 copy.264
  58.6 2.1 reshape.239.w_ref
  61.6 1.0 fusion.17
  62.6 1.8 reduce_in.1
  64.4 6.4 %all-to-all-start.1 = ((f32[8,2,256]{2,1,0:T(2,128)}), f32[8,2,256]{2,1,0:T(2,128)S(1)}, u32[]{:S(2)}, u32[]{:S(2)}) async-start(f32[8,2,256]{2,1,0:T(2,128)} %get-tuple-element.44), calls=%async_computation.1 | async-start | bytes 32768 | tf_op jit(solution)/shard_map/all_to_all | solution.py:667
  71.1 2.4 slice.260
  73.5 2.4 copy.228
  75.8 2.4 copy.229
  78.2 2.4 copy.230.w_ref
  81.1 1.3 copy-done.14
  82.4 4.0 %conv_mid.1 = (bf16[3,976,256]{2,1,0:T(8,128)(2,1)S(1)}, f32[896,512]{1,0:T(8,128)}, f32[8,2,512]{2,1,0:T(2,128)}) custom-call(s32[2]{0:T(128)S(1)} %pad_add_fusion.count_ref, f32[1]{0:T(128)} %bitcast.2.total_ref, f32[896,256]{1,0:T(8,128)S(1)} %get-tuple-element.43.pre_ref, f32[8,2,256]{2,1,0:T(2,128)S(1)} %all-to-all-done.1.sums_ref, ...), custom_call_target="tpu_custom_call" | custom-call | flops 1056964608 | bytes 5482508 | tf_op jit(solution)/shard_map/conv_mid/pallas_call | solution.py:106
  86.3 1.1 copy-done.10
  87.4 6.0 %all-to-all-start.2 = ((f32[8,2,512]{2,1,0:T(2,128)}), f32[8,2,512]{2,1,0:T(2,128)S(1)}, u32[]{:S(2)}, u32[]{:S(2)}) async-start(f32[8,2,512]{2,1,0:T(2,128)} %get-tuple-element.46), calls=%async_computation.2 | async-start | bytes 65536 | tf_op jit(solution)/shard_map/all_to_all | solution.py:667
  93.4 6.7 %all-to-all-done.2.sums_ref.mid_sums_ref = f32[8,2,512]{2,1,0:T(2,128)S(1)} async-done(((f32[8,2,512]{2,1,0:T(2,128)}), f32[8,2,512]{2,1,0:T(2,128)S(1)}, u32[]{:S(2)}, u32[]{:S(2)}) %all-to-all-start.2) | async-done | bytes 32800 | tf_op jit(solution)/shard_map/all_to_all | solution.py:667
  100.1 1.5 copy-done
  101.6 2.1 pool.1
  104.4 10.6 %all_to_all.70.pooled_ref = f32[8,40,128]{2,1,0:T(8,128)} all-to-all(f32[8,40,128]{2,1,0:T(8,128)S(1)} %get-tuple-element.47), channel_id=1, replica_groups=mesh['dp'=8,'chan'=4] {'dp'}, dimensions={0} | all-to-all | bytes 327680 | tf_op jit(solution)/shard_map/all_to_all | solution.py:667
  115.0 4.5 %all-to-all-start.5 = ((bf16[4,784,256]{2,1,0:T(8,128)(2,1)}), bf16[4,784,256]{2,1,0:T(8,128)(2,1)}, u32[]{:S(2)}, u32[]{:S(2)}) async-start(bf16[4,784,256]{2,1,0:T(8,128)(2,1)} %param.33), calls=%async_computation.5 | async-start | bytes 3211264 | tf_op jit(solution)/shard_map/all_to_all | solution.py:664
  120.7 1.7 slice.265
  122.4 1.7 copy.233
  124.1 1.6 copy.234
  125.7 1.7 copy.236.excite_ref
  130.1 1.1 fusion.16
  133.4 4.1 %attend.1 = (f32[2,4,128]{2,1,0:T(4,128)S(1)}, f32[4,512]{1,0:T(4,128)S(1)}, bf16[784,256]{1,0:T(8,128)(2,1)S(1)}, f32[4,784,256]{2,1,0:T(8,128)}, f32[8,8,256]{2,1,0:T(8,128)S(1)}) custom-call(s32[2]{0:T(128)S(1)} %copy-done.32, f32[1]{0:T(128)} %bitcast.2.total_ref, f32[8,40,128]{2,1,0:T(8,128)S(1)} %copy-done.8, ...), custom_call_target="tpu_custom_call" | custom-call | flops 411041792 | bytes 6401036 | tf_op jit(solution)/shard_map/attend/pallas_call | solution.py:106
  140.9 3.4 all-to-all-start.4
  144.3 1.3 constant_dynamic-update-slice_fusion.affine_ref
  145.5 3.6 reshape_reshape.6
  149.1 3.0 copy.239
  152.3 8.1 %finish.1 = (bf16[4,784,256]{2,1,0:T(8,128)(2,1)}, f32[4,784,256]{2,1,0:T(8,128)}, f32[8,8,256]{2,1,0:T(8,128)}) custom-call(s32[2]{0:T(128)S(1)} %copy-done.33, f32[1]{0:T(128)} %bitcast.2.total_ref, f32[4,784,256]{2,1,0:T(8,128)} %get-tuple-element.48.out_ref, f32[8,8,256]{2,1,0:T(8,128)S(1)} %all-to-all-done.4.sums_ref, f32[2,4,256]{2,1,0:T(4,128)S(1)} %copy-done.28, ...), custom_call_target="tpu_custom_call" | custom-call | bytes 11378700 | tf_op jit(solution)/shard_map/finish/pallas_call | solution.py:106
  160.4 5.9 %all-to-all-start.7 = ((f32[8,8,256]{2,1,0:T(8,128)}), f32[8,8,256]{2,1,0:T(8,128)S(1)}, u32[]{:S(2)}, u32[]{:S(2)}) async-start(f32[8,8,256]{2,1,0:T(8,128)} %get-tuple-element.52), calls=%async_computation.7 | async-start | bytes 131072 | tf_op jit(solution)/shard_map/all_to_all | solution.py:667
  166.9 6.3 %all-to-all-done.7.back_ref = f32[8,8,256]{2,1,0:T(8,128)S(1)} async-done(((f32[8,8,256]{2,1,0:T(8,128)}), f32[8,8,256]{2,1,0:T(8,128)S(1)}, u32[]{:S(2)}, u32[]{:S(2)}) %all-to-all-start.7) | async-done | bytes 65568 | tf_op jit(solution)/shard_map/all_to_all | solution.py:667
  173.3 8.3 %back_out.1 = (bf16[4,784,256]{2,1,0:T(8,128)(2,1)S(1)}, f32[896,256]{1,0:T(8,128)S(1)}, f32[4,512]{1,0:T(4,128)S(1)}, f32[8,16,128]{2,1,0:T(8,128)}) custom-call(s32[2]{0:T(128)S(1)} %copy-done.33, f32[1]{0:T(128)} %bitcast.2.total_ref, f32[4,784,256]{2,1,0:T(8,128)} %get-tuple-element.51.grad_ref.summed_ref, f32[4,784,256]{2,1,0:T(8,128)} %get-tuple-element.48.out_ref, ...), custom_call_target="tpu_custom_call" | custom-call | flops 411041792 | bytes 11698188 | tf_op jit(solution)/shard_map/back_out/pallas_call | solution.py:106
  182.4 1.2 copy-done.44
  183.6 3.4 all-to-all-start.8
  187.1 2.2 fusion.1
  194.1 1.2 copy-done.17
  195.2 7.4 %back_mid.1 = (bf16[976,512]{1,0:T(8,128)(2,1)}, f32[896,256]{1,0:T(8,128)S(1)}, f32[8,4,128]{2,1,0:T(4,128)S(1)}, f32[8,512]{1,0:T(8,128)S(1)}, f32[8,2,256]{2,1,0:T(2,128)}) custom-call(s32[2]{0:T(128)S(1)} %copy-done.33, f32[1]{0:T(128)} %bitcast.2.total_ref, f32[8,16,128]{2,1,0:T(8,128)S(1)} %all-to-all-done.8.back_ref, f32[8,40,128]{2,1,0:T(8,128)S(1)} %copy-done.9, ...), custom_call_target="tpu_custom_call" | custom-call | flops 1056964608 | bytes 7191564 | tf_op jit(solution)/shard_map/back_mid/pallas_call | solution.py:106
  202.7 0.9 copy-done.18
  203.6 5.9 %all-to-all-start.9 = ((f32[8,2,256]{2,1,0:T(2,128)}), f32[8,2,256]{2,1,0:T(2,128)S(1)}, u32[]{:S(2)}, u32[]{:S(2)}) async-start(f32[8,2,256]{2,1,0:T(2,128)} %get-tuple-element.58), calls=%async_computation.9 | async-start | bytes 32768 | tf_op jit(solution)/shard_map/all_to_all | solution.py:667
  211.0 1.4 copy-done.11
  212.4 1.2 copy-done.15
  213.6 2.9 weight_mid_term.1
  216.5 2.8 convert.46
  219.3 2.4 copy.242
  221.7 2.4 copy.243
  224.5 1.2 copy-done.19
  225.6 3.9 %back_in.1 = (bf16[784,256]{1,0:T(8,128)(2,1)S(1)}, bf16[4,784,256]{2,1,0:T(8,128)(2,1)}, f32[8,256]{1,0:T(8,128)S(1)}) custom-call(s32[2]{0:T(128)S(1)} %copy-done.33, f32[1]{0:T(128)} %bitcast.2.total_ref, f32[896,256]{1,0:T(8,128)S(1)} %copy-done.19, f32[896,256]{1,0:T(8,128)S(1)} %copy-done.7, f32[8,2,256]{2,1,0:T(2,128)S(1)} %copy-done.23, ...), custom_call_target="tpu_custom_call" | custom-call | flops 411041792 | bytes 7620620 | tf_op jit(solution)/shard_map/back_in/pallas_call | solution.py:106
  232.2 4.0 %concatenate.63 = bf16[4,2378,128]{1,2,0:T(8,128)(2,1)S(1)} concatenate(bf16[4,512,128]{1,2,0:T(8,128)(2,1)S(1)} %pad_maximum_fusion.1, bf16[4,1152,128]{1,2,0:T(8,128)(2,1)} %bitcast.117, bf16[4,64,128]{1,2,0:T(8,128)(2,1)} %pad_maximum_fusion.6, bf16[4,128,128]{1,2,0:T(8,128)(2,1)} %bitcast.128, bf16[4,256,128]{1,2,0:T(8,128)(2,1)S(1)} %copy-done.48, ...), dimensions={1} | concatenate | bytes 4870144 | tf_op jit(solution)/shard_map/concatenate | solution.py:942
  236.4 32.9 %all_to_all.71 = bf16[4,2432,128]{1,2,0:T(8,128)(2,1)S(1)} all-to-all(bf16[4,2432,128]{1,2,0:T(8,128)(2,1)S(1)} %pad.10), channel_id=1, replica_groups=mesh['dp'=8,'chan'=4] {'chan'}, dimensions={0} | all-to-all | bytes 4980736 | tf_op jit(solution)/shard_map/all_to_all | solution.py:664
  269.3 4.6 %all-to-all-start.6 = ((bf16[4,784,256]{2,1,0:T(8,128)(2,1)}), bf16[4,784,256]{2,1,0:T(8,128)(2,1)}, u32[]{:S(2)}, u32[]{:S(2)}) async-start(bf16[4,784,256]{2,1,0:T(8,128)(2,1)} %get-tuple-element.50), calls=%async_computation.6 | async-start | bytes 3211264 | tf_op jit(solution)/shard_map/all_to_all | solution.py:664
  274.7 19.5 %all-to-all-done.6 = bf16[4,784,256]{2,1,0:T(8,128)(2,1)} async-done(((bf16[4,784,256]{2,1,0:T(8,128)(2,1)}), bf16[4,784,256]{2,1,0:T(8,128)(2,1)}, u32[]{:S(2)}, u32[]{:S(2)}) %all-to-all-start.6) | async-done | bytes 1605664 | tf_op jit(solution)/shard_map/all_to_all | solution.py:664
  294.2 22.7 %all_to_all.72 = bf16[8,304,128]{2,1,0:T(8,128)(2,1)S(1)} all-to-all(bf16[8,304,128]{2,1,0:T(8,128)(2,1)S(1)} %bitcast.126), channel_id=1, replica_groups=mesh['dp'=8,'chan'=4] {'dp'}, dimensions={0} | all-to-all | bytes 1245184 | tf_op jit(solution)/shard_map/all_to_all | solution.py:667
  316.9 3.6 all-to-all-start.10
  320.6 20.3 %all-to-all-done.10 = bf16[4,784,256]{2,1,0:T(8,128)(2,1)S(1)} async-done(((bf16[4,784,256]{2,1,0:T(8,128)(2,1)}), bf16[4,784,256]{2,1,0:T(8,128)(2,1)S(1)}, u32[]{:S(2)}, u32[]{:S(2)}) %all-to-all-start.10) | async-done | bytes 1605664 | tf_op jit(solution)/shard_map/all_to_all | solution.py:664
  340.9 19.8 %all_to_all.73 = bf16[8,304,128]{2,1,0:T(8,128)(2,1)S(1)} all-to-all(bf16[8,304,128]{2,1,0:T(8,128)(2,1)S(1)} %broadcast_in_dim.28), channel_id=1, replica_groups=mesh['dp'=8,'chan'=4] {'dp'}, dimensions={0} | all-to-all | bytes 1245184 | tf_op jit(solution)/shard_map/all_to_all | solution.py:667
  364.6 1.9 copy.259
  367.2 1.7 copy.260
  373.0 2.7 copy.291
  375.7 1.2 copy.292
  (241 shorter events, 40.5 us)
Async XLA Ops:
  7.2 6.3 %copy-start.57 = (bf16[64,128]{1,0:T(8,128)(2,1)S(1)}, bf16[64,128]{1,0:T(8,128)(2,1)}, u32[]{:S(2)}) copy-start(bf16[64,128]{1,0:T(8,128)(2,1)} %param.25) | copy-start | bytes 49156
  7.2 6.6 %copy-start.52 = (bf16[256,256]{1,0:T(8,128)(2,1)S(1)}, bf16[256,256]{1,0:T(8,128)(2,1)}, u32[]{:S(2)}) copy-start(bf16[256,256]{1,0:T(8,128)(2,1)} %param.30) | copy-start | bytes 393220
  7.2 6.9 %copy-start.54 = (bf16[128,2,64]{0,2,1:T(8,128)(2,1)S(1)}, bf16[128,2,64]{0,2,1:T(8,128)(2,1)}, u32[]{:S(2)}) copy-start(bf16[128,2,64]{0,2,1:T(8,128)(2,1)} %param.28) | copy-start | bytes 98308
  7.2 48.0 %all-gather.3.cloned.1.call-start = ((), (), s32[]{:S(2)}) async-start(), calls=%async_computation.14 | async-start | bytes 3051520 | tf_op jit(solution)/shard_map/all_gather | solution.py:699
  15.9 4.3 %copy-start.59 = (s32[4,8]{1,0:T(4,128)S(1)}, s32[4,8]{1,0:T(4,128)}, u32[]{:S(2)}) copy-start(s32[4,8]{1,0:T(4,128)} %param.18) | copy-start | bytes 388
  15.9 46.7 %all-to-all-start = ((bf16[4,784,256]{2,1,0:T(8,128)(2,1)}), bf16[4,784,256]{2,1,0:T(8,128)(2,1)S(1)}, u32[]{:S(2)}, u32[]{:S(2)}) async-start(bf16[4,784,256]{2,1,0:T(8,128)(2,1)} %param.17), calls=%async_computation | async-start | bytes 3211264 | tf_op jit(solution)/shard_map/all_to_all | solution.py:664
  22.7 77.4 %copy-start.31 = (s32[2]{0:T(128)}, s32[2]{0:T(128)S(1)}, u32[]{:S(2)}) copy-start(s32[2]{0:T(128)S(1)} %pad_add_fusion.count_ref) | copy-start | bytes 28
  60.7 12.8 %copy-start.4 = (bf16[4,256,256]{2,1,0:T(8,128)(2,1)}, bf16[4,256,256]{2,1,0:T(8,128)(2,1)S(1)}, u32[]{:S(2)}) copy-start(bf16[4,256,256]{2,1,0:T(8,128)(2,1)S(1)} %reshape.239.w_ref) | copy-start | bytes 1572868
  61.5 9.6 %copy-start.53 = (f32[4,16,128]{2,1,0:T(8,128)}, f32[4,16,128]{2,1,0:T(8,128)S(1)}, u32[]{:S(2)}) copy-start(f32[4,16,128]{2,1,0:T(8,128)S(1)} %slice_convert_fusion) | copy-start | bytes 98308
  64.4 16.6 %copy-start.6 = (f32[896,256]{1,0:T(8,128)}, f32[896,256]{1,0:T(8,128)S(1)}, u32[]{:S(2)}) copy-start(f32[896,256]{1,0:T(8,128)S(1)} %get-tuple-element.43.pre_ref) | copy-start | bytes 2752516
  64.4 16.6 %all-to-all-start.1 = ((f32[8,2,256]{2,1,0:T(2,128)}), f32[8,2,256]{2,1,0:T(2,128)S(1)}, u32[]{:S(2)}, u32[]{:S(2)}) async-start(f32[8,2,256]{2,1,0:T(2,128)} %get-tuple-element.44), calls=%async_computation.1 | async-start | bytes 32768 | tf_op jit(solution)/shard_map/all_to_all | solution.py:667
  71.1 10.0 %copy-start.34 = (f32[2,256]{1,0:T(2,128)}, f32[2,256]{1,0:T(2,128)S(1)}, u32[]{:S(2)}) copy-start(f32[2,256]{1,0:T(2,128)S(1)} %pad_maximum_fusion.10.affine_ref) | copy-start | bytes 6148
  81.1 5.3 %copy-start.22 = (f32[8,2,256]{2,1,0:T(2,128)}, f32[8,2,256]{2,1,0:T(2,128)S(1)}, u32[]{:S(2)}) copy-start(f32[8,2,256]{2,1,0:T(2,128)S(1)} %all-to-all-done.1.sums_ref) | copy-start | bytes 49156
  81.1 1.3 copy-start.14
  86.3 1.1 copy-start.10
  87.4 12.7 %all-to-all-start.2 = ((f32[8,2,512]{2,1,0:T(2,128)}), f32[8,2,512]{2,1,0:T(2,128)S(1)}, u32[]{:S(2)}, u32[]{:S(2)}) async-start(f32[8,2,512]{2,1,0:T(2,128)} %get-tuple-element.46), calls=%async_computation.2 | async-start | bytes 65536 | tf_op jit(solution)/shard_map/all_to_all | solution.py:667
  93.4 21.6 %copy-start.24 = (f32[2,512]{1,0:T(2,128)}, f32[2,512]{1,0:T(2,128)S(1)}, u32[]{:S(2)}) copy-start(f32[2,512]{1,0:T(2,128)S(1)} %pad_maximum_fusion.9.affine_ref.mid_affine_ref) | copy-start | bytes 12292
  100.1 1.5 copy-start
  115.0 4.5 %copy-start.60 = (bf16[128]{0:T(256)(128)(2,1)S(1)}, bf16[128]{0:T(256)(128)(2,1)}, u32[]{:S(2)}) copy-start(bf16[128]{0:T(256)(128)(2,1)} %param.27) | copy-start | bytes 772
  115.0 4.5 %copy-start.61 = (bf16[128]{0:T(256)(128)(2,1)S(1)}, bf16[128]{0:T(256)(128)(2,1)}, u32[]{:S(2)}) copy-start(bf16[128]{0:T(256)(128)(2,1)} %param.26) | copy-start | bytes 772
  115.0 25.9 %all-to-all-start.5 = ((bf16[4,784,256]{2,1,0:T(8,128)(2,1)}), bf16[4,784,256]{2,1,0:T(8,128)(2,1)}, u32[]{:S(2)}, u32[]{:S(2)}) async-start(bf16[4,784,256]{2,1,0:T(8,128)(2,1)} %param.33), calls=%async_computation.5 | async-start | bytes 3211264 | tf_op jit(solution)/shard_map/all_to_all | solution.py:664
  120.7 10.6 %copy-start.1 = (f32[896,512]{1,0:T(8,128)S(1)}, f32[896,512]{1,0:T(8,128)}, u32[]{:S(2)}) copy-start(f32[896,512]{1,0:T(8,128)} %get-tuple-element.45.mid_ref) | copy-start | bytes 5505028
  129.5 1.8 copy-start.56
  129.5 1.8 copy-start.8
  129.5 1.8 copy-start.12
  129.5 1.8 copy-start.41
  140.9 11.3 %all-to-all-start.4 = ((f32[8,8,256]{2,1,0:T(8,128)}), f32[8,8,256]{2,1,0:T(8,128)S(1)}, u32[]{:S(2)}, u32[]{:S(2)}) async-start(f32[8,8,256]{2,1,0:T(8,128)} %copy-done.27), calls=%async_computation.4 | async-start | bytes 131072 | tf_op jit(solution)/shard_map/all_to_all | solution.py:667
  149.1 3.0 copy-start.9
  149.1 3.1 copy-start.28
  149.1 3.1 copy-start.33
  152.2 21.0 %copy-start.3 = (bf16[4,256,256]{2,1,0:T(8,128)(2,1)S(1)}, bf16[4,256,256]{2,1,0:T(8,128)(2,1)}, u32[]{:S(2)}) copy-start(bf16[4,256,256]{2,1,0:T(8,128)(2,1)} %copy-done.2) | copy-start | bytes 1572868
  152.2 21.0 %copy-start.13 = (bf16[128,512]{1,0:T(8,128)(2,1)S(1)}, bf16[128,512]{1,0:T(8,128)(2,1)}, u32[]{:S(2)}) copy-start(bf16[128,512]{1,0:T(8,128)(2,1)} %copy.236.excite_ref) | copy-start | bytes 393220
  152.2 21.0 %copy-start.26 = (f32[2,512]{1,0:T(2,128)S(1)}, f32[2,512]{1,0:T(2,128)}, u32[]{:S(2)}) copy-start(f32[2,512]{1,0:T(2,128)} %copy-done.24) | copy-start | bytes 12292
  152.2 21.0 %copy-start.30 = (f32[4,512]{1,0:T(4,128)S(1)}, f32[4,512]{1,0:T(4,128)}, u32[]{:S(2)}) copy-start(f32[4,512]{1,0:T(4,128)} %copy-done.29) | copy-start | bytes 24580
  152.3 21.0 %copy-start.37 = (f32[2,4,128]{2,1,0:T(4,128)S(1)}, f32[2,4,128]{2,1,0:T(4,128)}, u32[]{:S(2)}) copy-start(f32[2,4,128]{2,1,0:T(4,128)} %copy-done.36) | copy-start | bytes 12292
  160.4 12.8 %all-to-all-start.7 = ((f32[8,8,256]{2,1,0:T(8,128)}), f32[8,8,256]{2,1,0:T(8,128)S(1)}, u32[]{:S(2)}, u32[]{:S(2)}) async-start(f32[8,8,256]{2,1,0:T(8,128)} %get-tuple-element.52), calls=%async_computation.7 | async-start | bytes 131072 | tf_op jit(solution)/shard_map/all_to_all | solution.py:667
  173.2 8.3 %copy-start.20 = (f32[8,8,256]{2,1,0:T(8,128)}, f32[8,8,256]{2,1,0:T(8,128)S(1)}, u32[]{:S(2)}) copy-start(f32[8,8,256]{2,1,0:T(8,128)S(1)} %all-to-all-done.7.back_ref) | copy-start | bytes 196612
  173.3 13.8 %copy-start.46 = (bf16[784,256]{1,0:T(8,128)(2,1)S(1)}, bf16[784,256]{1,0:T(8,128)(2,1)}, u32[]{:S(2)}) copy-start(bf16[784,256]{1,0:T(8,128)(2,1)} %copy-done.45) | copy-start | bytes 1204228
  182.4 1.2 copy-start.44
  183.6 10.4 %all-to-all-start.8 = ((f32[8,16,128]{2,1,0:T(8,128)}), f32[8,16,128]{2,1,0:T(8,128)S(1)}, u32[]{:S(2)}, u32[]{:S(2)}) async-start(f32[8,16,128]{2,1,0:T(8,128)} %get-tuple-element.55), calls=%async_computation.8 | async-start | bytes 131072 | tf_op jit(solution)/shard_map/all_to_all | solution.py:667
  187.1 2.4 copy-start.38
  189.2 4.2 %copy-start.21 = (f32[8,8,256]{2,1,0:T(8,128)S(1)}, f32[8,8,256]{2,1,0:T(8,128)}, u32[]{:S(2)}) copy-start(f32[8,8,256]{2,1,0:T(8,128)} %copy-done.20) | copy-start | bytes 196612
  189.3 4.8 %copy-start.7 = (f32[896,256]{1,0:T(8,128)S(1)}, f32[896,256]{1,0:T(8,128)}, u32[]{:S(2)}) copy-start(f32[896,256]{1,0:T(8,128)} %copy-done.6) | copy-start | bytes 2752516
  189.3 4.8 %copy-start.23 = (f32[8,2,256]{2,1,0:T(2,128)S(1)}, f32[8,2,256]{2,1,0:T(2,128)}, u32[]{:S(2)}) copy-start(f32[8,2,256]{2,1,0:T(2,128)} %copy-done.22) | copy-start | bytes 49156
  189.3 4.8 %copy-start.35 = (f32[2,256]{1,0:T(2,128)S(1)}, f32[2,256]{1,0:T(2,128)}, u32[]{:S(2)}) copy-start(f32[2,256]{1,0:T(2,128)} %copy-done.34) | copy-start | bytes 6148
  189.3 4.8 %copy-start.40 = (f32[2,128]{1,0:T(2,128)S(1)}, f32[2,128]{1,0:T(2,128)}, u32[]{:S(2)}) copy-start(f32[2,128]{1,0:T(2,128)} %maximum_convert_fusion.gate_affine_ref) | copy-start | bytes 3076
  194.1 1.2 copy-start.17
  195.2 14.3 %copy-start.43 = (f32[4,256]{1,0:T(4,128)S(1)}, f32[4,256]{1,0:T(4,128)}, u32[]{:S(2)}) copy-start(f32[4,256]{1,0:T(4,128)} %copy-done.42) | copy-start | bytes 12292
  195.2 14.3 %copy-start.58 = (f32[256]{0:T(256)S(1)}, f32[256]{0:T(256)}, u32[]{:S(2)}) copy-start(f32[256]{0:T(256)} %divide_bitcast_fusion) | copy-start | bytes 3076
  202.6 0.9 copy-start.18
  203.6 20.9 %all-to-all-start.9 = ((f32[8,2,256]{2,1,0:T(2,128)}), f32[8,2,256]{2,1,0:T(2,128)S(1)}, u32[]{:S(2)}, u32[]{:S(2)}) async-start(f32[8,2,256]{2,1,0:T(2,128)} %get-tuple-element.58), calls=%async_computation.9 | async-start | bytes 32768 | tf_op jit(solution)/shard_map/all_to_all | solution.py:667
  211.0 1.4 copy-start.11
  212.4 1.2 copy-start.15
  221.7 2.8 copy-start.5
  224.5 1.2 copy-start.19
  230.2 1.1 copy-start.55
  230.6 1.5 copy-start.48
  230.7 1.5 copy-start.49
  269.3 24.9 %all-to-all-start.6 = ((bf16[4,784,256]{2,1,0:T(8,128)(2,1)}), bf16[4,784,256]{2,1,0:T(8,128)(2,1)}, u32[]{:S(2)}, u32[]{:S(2)}) async-start(bf16[4,784,256]{2,1,0:T(8,128)(2,1)} %get-tuple-element.50), calls=%async_computation.6 | async-start | bytes 3211264 | tf_op jit(solution)/shard_map/all_to_all | solution.py:664
  316.9 24.0 %all-to-all-start.10 = ((bf16[4,784,256]{2,1,0:T(8,128)(2,1)}), bf16[4,784,256]{2,1,0:T(8,128)(2,1)S(1)}, u32[]{:S(2)}, u32[]{:S(2)}) async-start(bf16[4,784,256]{2,1,0:T(8,128)(2,1)} %get-tuple-element.59), calls=%async_computation.10 | async-start | bytes 3211264 | tf_op jit(solution)/shard_map/all_to_all | solution.py:664
  360.9 3.7 copy-start.47
  366.5 4.4 %slice-start = ((f32[2432,128]{1,0:T(8,128)}), f32[128,128]{1,0:T(8,128)S(1)}, s32[]{:S(2)}) async-start(f32[2432,128]{1,0:T(8,128)} %copy-done.47), calls=%async_computation.15 | async-start | bytes 131072 | tf_op jit(solution)/shard_map/slice | solution.py:954
  367.2 5.1 %copy-start.50 = (f32[256,128]{1,0:T(8,128)S(1)}, f32[256,128]{1,0:T(8,128)}, u32[]{:S(2)}) copy-start(f32[256,128]{1,0:T(8,128)} %get-tuple-element.184) | copy-start | bytes 393220
  367.2 5.1 %copy-start.51 = (f32[256,128]{1,0:T(8,128)S(1)}, f32[256,128]{1,0:T(8,128)}, u32[]{:S(2)}) copy-start(f32[256,128]{1,0:T(8,128)} %get-tuple-element.185) | copy-start | bytes 393220
  (10 other events, 6.9 us)
Sparse Core Ops, SparseCore 0:
  16.0 39.1 all-gather.2

commit v2 on v1

v2 whole, which is shorter than its diff:
```python
import functools

import jax
import jax.numpy as jnp
from jax import lax
from jax.experimental import pallas as pl
from jax.experimental.pallas import tpu as pltpu
from jax.sharding import PartitionSpec as P

SIDE = 14
PIXELS = SIDE * SIDE
WIDE = 16
PADDED = SIDE * WIDE
STRIDE = PADDED + WIDE
CHUNK = 16
UNROLL = 2
VMEM_LIMIT = 24 * 2**20
SLOTS = (0, 1, 2, 3)
ORDER = (0, 2, 1, 3)
EPSILON = 1e-05
HIGHEST = lax.Precision.HIGHEST
F32 = jnp.float32
BF16 = jnp.bfloat16


def dot_nn(left, right, precision=None):
    return lax.dot_general(
        left, right, (((1,), (0,)), ((), ())), preferred_element_type=F32, precision=precision
    )


def dot_nt(left, right, precision=None):
    return lax.dot_general(
        left, right, (((1,), (1,)), ((), ())), preferred_element_type=F32, precision=precision
    )


def dot_tn(left, right, precision=None):
    return lax.dot_general(
        left, right, (((0,), (0,)), ((), ())), preferred_element_type=F32, precision=precision
    )


def logistic(value):
    return 0.5 + 0.5 * jnp.tanh(0.5 * value)


def silu(value):
    return value * logistic(value)


def slope(value):
    share = logistic(value)
    return share * (1.0 + value * (1.0 - share))


def moments(first, second, total):
    center = first / total
    return center, lax.rsqrt(second / total - center * center + EPSILON)


def fold(value):
    return jnp.sum(value.reshape(-1, 8, value.shape[-1]), axis=0)


def total_of(value):
    return jnp.sum(value, axis=0, keepdims=True)


def columns_real(rows):
    spot = lax.broadcasted_iota(jnp.int32, (rows, 1), 0)
    return (lax.rem(spot, WIDE) < SIDE).astype(F32)


def summed_over(refs):
    values = [ref[...] for ref in refs]
    while len(values) > 1:
        values = [left + right for left, right in zip(values[::2], values[1::2])]
    return values[0]


def slot_rows(refs, size, first, count, skip=0):
    return jnp.concatenate(
        [
            ref[at + first : at + first + count, :]
            for ref in refs
            for at in range(skip, ref.shape[0], size)
        ],
        axis=0,
    )


class Place:
    def __init__(self, counts_ref):
        group = lax.axis_index("dp")
        self.chan = lax.axis_index("chan")
        self.parity, self.depth, self.core = group & 1, group >> 1, self.chan & 1
        self.batch = (self.chan & 2) | self.parity
        self.counts = counts_ref
        self.groups = counts_ref.shape[1]

    def images(self, depth, core):
        return self.counts[self.batch, 2 * depth + core]

    def real(self, image):
        return jnp.where(self.images(self.depth, self.core) > image, 1.0, 0.0).astype(F32)

    def total(self):
        every = [self.counts[self.batch, g] for g in range(self.groups)]
        return functools.reduce(jnp.add, every).astype(F32)


def spread_map_rows(flat_ref, wide_ref):
    for line in range(flat_ref.shape[0] // SIDE):
        wide_ref[line * WIDE : line * WIDE + SIDE, :] = flat_ref[line * SIDE : (line + 1) * SIDE, :]
        wide_ref[line * WIDE + SIDE : (line + 1) * WIDE, :] = jnp.zeros(
            (WIDE - SIDE, wide_ref.shape[1]), wide_ref.dtype
        )


def pack_map_rows(wide_ref, flat_ref):
    for line in range(flat_ref.shape[0] // SIDE):
        flat_ref[line * SIDE : (line + 1) * SIDE, :] = wide_ref[line * WIDE : line * WIDE + SIDE, :]


def clear_gaps(taps_ref, images):
    for gap in range(images + 1):
        taps_ref[:, gap * STRIDE : gap * STRIDE + WIDE, :] = jnp.zeros(
            (3, WIDE, taps_ref.shape[2]), taps_ref.dtype
        )


def store_taps(taps_ref, at, value):
    here = pl.ds(pl.multiple_of(at, WIDE), WIDE)
    taps_ref[0, here, :] = pltpu.roll(value, 1, 0).astype(taps_ref.dtype)
    taps_ref[1, here, :] = value.astype(taps_ref.dtype)
    taps_ref[2, here, :] = pltpu.roll(value, WIDE - 1, 0).astype(taps_ref.dtype)


def call(body, outs, scratch, flops, *args, smem=1):
    specs = tuple(
        pl.BlockSpec(memory_space=pltpu.SMEM)
        if place < smem
        else jax.tree.map(lambda _: pl.BlockSpec(memory_space=pltpu.VMEM), arg)
        for place, arg in enumerate(args)
    )
    moved = sum(a.size * a.dtype.itemsize for a in jax.tree.leaves((args, outs)))
    return pl.pallas_call(
        body,
        out_shape=outs,
        in_specs=specs,
        out_specs=[pl.BlockSpec(memory_space=pltpu.VMEM)] * len(outs),
        scratch_shapes=scratch,
        compiler_params=pltpu.CompilerParams(vmem_limit_bytes=VMEM_LIMIT),
        cost_estimate=pl.CostEstimate(flops=flops, bytes_accessed=moved, transcendentals=0),
        name=getattr(body, "func", body).__name__,
    )(*args)


def shape(dims, kind=F32):
    return jax.ShapeDtypeStruct(dims, kind)


def reduce_in(
    counts_ref,
    x0,
    x1,
    x2,
    x3,
    a0,
    a1,
    a2,
    a3,
    pre_ref,
    msg_ref,
    w_ref,
    in_affine_ref,
    mid_affine_ref,
    bias_ref,
    out_affine_ref,
    wall_ref,
    flat_ref,
    small_ref,
):
    place = Place(counts_ref)
    images = wall_ref.shape[0] // place.groups
    spot = lax.broadcasted_iota(jnp.int32, wall_ref.shape, 0)
    real = jnp.zeros(wall_ref.shape, jnp.int32)
    for slot in range(place.groups):
        number = place.images(place.depth ^ (slot >> 1), place.core ^ (slot & 1))
        here = (spot >= slot * images) & (spot < slot * images + number)
        real = jnp.where(here, 1, real)
    wall_ref[...] = real.astype(F32)
    chan, batch = place.chan, place.batch
    own = w_ref.shape[1] // len(SLOTS)
    half = w_ref.shape[2] // 2
    weights = 2 * w_ref.shape[0] * own
    for s, piece in enumerate((a0, a1, a2, a3)):
        here = pl.ds(pl.multiple_of((chan ^ s) * own, own), own)
        for block in range(2 * w_ref.shape[0]):
            lane = slice((block % 2) * half, (block % 2 + 1) * half)
            w_ref[block // 2, here, lane] = piece[block * own : (block + 1) * own, :]
        small = piece[weights:, :].astype(F32)
        small_ref[chan ^ s] = small
        for t in range(2):
            out_affine_ref[t, chan ^ s, :, :half] = small[4 + 2 * t : 5 + 2 * t, :]
            out_affine_ref[t, chan ^ s, :, half:] = small[5 + 2 * t : 6 + 2 * t, :]
    width = own * len(SLOTS)
    for k in range(len(SLOTS)):
        here = slice(k * own, (k + 1) * own)
        there = slice(width + k * own, width + (k + 1) * own)
        in_affine_ref[0:1, here] = small_ref[k, 0:1, :own]
        in_affine_ref[1:2, here] = small_ref[k, 0:1, own:]
        for t in range(2):
            mid_affine_ref[t : t + 1, here] = small_ref[k, 1 + t : 2 + t, :own]
            mid_affine_ref[t : t + 1, there] = small_ref[k, 1 + t : 2 + t, own:]
        bias_ref[0:1, here] = small_ref[k, 3:4, :own]
        bias_ref[0:1, there] = small_ref[k, 3:4, own:]
    parts = [dot_nt(x[...], w_ref[batch ^ s]) for s, x in enumerate((x0, x1, x2, x3))]
    flat_ref[...] = functools.reduce(jnp.add, parts)
    spread_map_rows(flat_ref, pre_ref)
    first = jnp.zeros((1, pre_ref.shape[1]), F32)
    second = jnp.zeros((1, pre_ref.shape[1]), F32)
    for image in range(pre_ref.shape[0] // PADDED):
        real = place.real(image)
        value = pre_ref[image * PADDED : (image + 1) * PADDED, :]
        first = first + real * total_of(value)
        second = second + real * total_of(value * value)
    msg_ref[...] = jnp.concatenate([first, second], axis=0)


def place_mid(counts_ref, b0, b1, b2, b3, w_ref, w_back_ref):
    place = Place(counts_ref)
    width, lanes = w_ref.shape[1], b0.shape[1]
    own = width // len(SLOTS)
    for s, piece in enumerate((b0, b1, b2, b3)):
        at = pl.multiple_of((place.chan ^ s) * own, own)
        for tap in range(9):
            for r in range(2):
                block = piece[(2 * tap + r) * own : (2 * tap + r + 1) * own, :]
                w_ref[r, pl.ds(at, own), tap * lanes : (tap + 1) * lanes] = block
                w_back_ref[r, pl.ds(tap * width + at, own), :] = block


def place_rest(counts_ref, b0, b1, b2, b3, excite_ref, squeeze_ref, w_out_ref):
    place = Place(counts_ref)
    width, lanes = squeeze_ref.shape
    own = width // len(SLOTS)
    for s, piece in enumerate((b0, b1, b2, b3)):
        at = pl.multiple_of((place.chan ^ s) * own, own)
        for r in range(2):
            excite_ref[pl.ds(r * width + at, own), :] = piece[r * own : (r + 1) * own, :]
        squeeze_ref[pl.ds(at, own), :] = piece[2 * own : 3 * own, :]
        row = 3 * own
        w_out_ref[place.chan ^ s, :, :lanes] = piece[row : row + width, :]
        w_out_ref[place.chan ^ s, :, lanes:] = piece[row + width : row + 2 * width, :]


def conv_mid(
    counts_ref,
    pre_ref,
    sums_refs,
    affine_ref,
    w_ref,
    taps_ref,
    mid_ref,
    msg_ref,
):
    place = Place(counts_ref)
    images = pre_ref.shape[0] // PADDED
    total = place.total() * PIXELS
    sums = summed_over(sums_refs)
    center, scale = moments(sums[0:1], sums[1:2], total)
    gain = affine_ref[0:1, :] * scale
    shift = affine_ref[1:2, :]
    clear_gaps(taps_ref, images)
    keep = columns_real(WIDE)
    for image in range(images):

        def normalize(step, carry, image=image):
            rows = pl.multiple_of(step * WIDE, WIDE)
            value = pre_ref[pl.ds(image * PADDED + rows, WIDE), :]
            value = silu((value - center) * gain + shift) * keep
            store_taps(taps_ref, image * STRIDE + WIDE + rows, value)
            return carry

        lax.fori_loop(0, SIDE, normalize, 0, unroll=UNROLL)
    half = pre_ref.shape[1] // 2
    width = pre_ref.shape[1]
    keep = columns_real(PADDED)
    firsts = [jnp.zeros((1, width), F32) for _ in range(2)]
    seconds = [jnp.zeros((1, width), F32) for _ in range(2)]
    for image in range(images):
        real = place.real(image)
        for r in range(2):
            left = jnp.concatenate(
                [
                    taps_ref[
                        b,
                        image * STRIDE + a * WIDE : image * STRIDE + a * WIDE + PADDED,
                        r * half : (r + 1) * half,
                    ]
                    for a in range(3)
                    for b in range(3)
                ],
                axis=1,
            )
            value = dot_nt(left, w_ref[r])
            mid_ref[image * PADDED : (image + 1) * PADDED, r * width : (r + 1) * width] = value
            held = value * keep
            firsts[r] = firsts[r] + real * total_of(held)
            seconds[r] = seconds[r] + real * total_of(held * held)
    sums = jnp.concatenate(
        [jnp.concatenate(firsts, axis=1), jnp.concatenate(seconds, axis=1)], axis=0
    )
    msg_ref[...] = sums


def mid_norm(
    place,
    sums_refs,
    affine_ref,
):
    sums = summed_over(sums_refs)
    center, scale = moments(sums[0:1], sums[1:2], place.total() * PIXELS)
    return center, scale, affine_ref[0:1, :], affine_ref[1:2, :]


def pool(
    counts_ref,
    mid_ref,
    sums_refs,
    affine_ref,
    squeeze_ref,
    pooled_ref,
    msg_ref,
    incline_ref,
):
    place = Place(counts_ref)
    images = mid_ref.shape[0] // PADDED
    width = mid_ref.shape[1] // 2
    lanes = msg_ref.shape[1]
    center, scale, gain, shift = mid_norm(place, sums_refs, affine_ref)
    keep = columns_real(CHUNK)
    inclines = [[], []]
    for image in range(images):

        def gather(step, carry, image=image):
            active, rise, lean = carry
            at = pl.multiple_of(image * PADDED + step * CHUNK, CHUNK)
            normed = (mid_ref[pl.ds(at, CHUNK), :] - center) * scale
            value = normed * gain + shift
            share = logistic(value)
            active = active + fold(value * share * keep)
            inclined = share * (1.0 + value * (1.0 - share)) * keep
            return active, rise + fold(inclined), lean + fold(inclined * normed)

        nothing = jnp.zeros((8, 2 * width), F32)
        active, rise, lean = lax.fori_loop(
            0, PADDED // CHUNK, gather, (nothing, nothing, nothing), unroll=UNROLL
        )
        active = total_of(active)
        pooled_ref[image : image + 1, :] = (active[:, :width] + active[:, width:]) / PIXELS
        inclines[0].append(total_of(rise))
        inclines[1].append(total_of(lean))
    incline_ref[...] = jnp.concatenate(inclines[0] + inclines[1], axis=0)
    msg_ref[...] = jnp.zeros_like(msg_ref)
    msg_ref[0:images, :] = dot_nn(pooled_ref[...], squeeze_ref[...].astype(F32), HIGHEST)
    real = [place.real(image) * pooled_ref[image : image + 1, :] for image in range(images)]
    real = functools.reduce(jnp.add, real)
    for q in range(width // lanes):
        msg_ref[images + q : images + q + 1, :] = real[:, q * lanes : (q + 1) * lanes]


def gate_norm(
    place,
    rows,
    wall,
):
    return moments(total_of(wall * rows), total_of(wall * rows * rows), place.total())


def attend(
    counts_ref,
    gathered_refs,
    wall_ref,
    gate_affine_ref,
    excite_ref,
    bias_ref,
    mid_ref,
    mid_sums_refs,
    mid_affine_ref,
    w_out_ref,
    gate_ref,
    attention_ref,
    weighted_ref,
    out_ref,
    msg_ref,
    wide_ref,
    flat_ref,
):
    place = Place(counts_ref)
    images = mid_ref.shape[0] // PADDED
    width = mid_ref.shape[1] // 2
    rows = slot_rows(gathered_refs, 8, 0, images)
    center, scale = gate_norm(place, rows, wall_ref[...])
    normed = (rows[0:images] - center) * scale
    gate_pre = normed * gate_affine_ref[0:1, :] + gate_affine_ref[1:2, :]
    gate = silu(gate_pre)
    gate_ref[0] = gate
    gate_ref[1] = slope(gate_pre)
    logits = (
        dot_nt(gate, excite_ref[...].astype(F32), HIGHEST) + bias_ref[...]
    )
    lean = 0.5 * jnp.tanh(0.5 * (logits[:, :width] - logits[:, width:]))
    attention_ref[:, :width] = 0.5 + lean
    attention_ref[:, width:] = 0.5 - lean
    center, scale, gain, shift = mid_norm(place, mid_sums_refs, mid_affine_ref)
    for image in range(images):
        share = attention_ref[image : image + 1, :]

        def weigh(step, carry, image=image, share=share):
            at = pl.multiple_of(image * PADDED + step * CHUNK, CHUNK)
            normed = (mid_ref[pl.ds(at, CHUNK), :] - center) * scale
            value = share * silu(normed * gain + shift)
            wide_ref[pl.ds(at, CHUNK), :] = value[:, :width] + value[:, width:]
            return carry

        lax.fori_loop(0, PADDED // CHUNK, weigh, 0, unroll=UNROLL)
    pack_map_rows(wide_ref, flat_ref)
    weighted_ref[...] = flat_ref[...].astype(BF16)
    spot = lax.broadcasted_iota(jnp.int32, (flat_ref.shape[0], 1), 0)
    real = (spot < place.images(place.depth, place.core) * PIXELS).astype(F32)
    blocks = w_out_ref.shape[0]
    for k in range(blocks):
        value = dot_nn(weighted_ref[...], w_out_ref[place.batch ^ k])
        out_ref[k] = value
        held = value * real
        for t, row in enumerate((total_of(held), total_of(held * value))):
            msg_ref[t * blocks + k : t * blocks + k + 1, :] = row


def finish(
    counts_ref,
    out_ref,
    sums_refs,
    affine_ref,
    x0,
    x1,
    x2,
    x3,
    c0,
    c1,
    c2,
    c3,
    r0,
    r1,
    r2,
    r3,
    grad_ref,
    msg_ref,
):
    place = Place(counts_ref)
    blocks, rows, lanes = out_ref.shape
    sums = summed_over(sums_refs)
    center, scale = moments(sums[:blocks], sums[blocks:], place.total() * PIXELS)
    limit = place.images(place.depth, place.core) * PIXELS
    for k in range(blocks):
        mu, r = center[k : k + 1], scale[k : k + 1]
        block = place.batch ^ k
        gain, shift = affine_ref[0, block], affine_ref[1, block]
        x_ref, cot_ref, result_ref = (x0, x1, x2, x3)[k], (c0, c1, c2, c3)[k], (r0, r1, r2, r3)[k]

        def chunk(
            step, carry, k=k, mu=mu, r=r, gain=gain, shift=shift,
            x_ref=x_ref, cot_ref=cot_ref, result_ref=result_ref,
        ):
            first, second = carry
            at = pl.multiple_of(step * CHUNK, CHUNK)
            here = pl.ds(at, CHUNK)
            spot = lax.broadcasted_iota(jnp.int32, (CHUNK, 1), 0) + at
            real = (spot < limit).astype(F32)
            normed = (out_ref[k, here, :] - mu) * r
            summed = x_ref[here, :].astype(F32) + (normed * gain + shift)
            share = logistic(summed) * real
            result_ref[here, :] = (summed * share).astype(BF16)
            upstream = cot_ref[here, :].astype(F32)
            grad = upstream * share * (1.0 + summed * (1.0 - share))
            grad_ref[k, here, :] = grad
            return first + fold(grad), second + fold(grad * normed)

        nothing = jnp.zeros((8, lanes), F32)
        first, second = lax.fori_loop(
            0, rows // CHUNK, chunk, (nothing, nothing), unroll=UNROLL
        )
        for t, row in enumerate((total_of(first), total_of(second))):
            msg_ref[t * blocks + k : t * blocks + k + 1, :] = row


def back_out(
    counts_ref,
    grad_ref,
    out_ref,
    sums_refs,
    back_refs,
    affine_ref,
    w_out_ref,
    mid_ref,
    mid_sums_refs,
    mid_affine_ref,
    attention_ref,
    gate_ref,
    excite_ref,
    low_ref,
    gw_ref,
    logits_ref,
    msg_ref,
    flat_ref,
):
    place = Place(counts_ref)
    blocks, rows, lanes = out_ref.shape
    images = attention_ref.shape[0]
    width = attention_ref.shape[1] // 2
    total = place.total() * PIXELS
    sums = summed_over(sums_refs)
    center, scale = moments(sums[:blocks], sums[blocks:], total)
    back = summed_over(back_refs) / total
    limit = place.images(place.depth, place.core) * PIXELS
    for k in range(blocks):
        mu, r = center[k : k + 1], scale[k : k + 1]
        gain = affine_ref[0, place.batch ^ k] * r
        first, second = back[k : k + 1], back[blocks + k : blocks + k + 1]

        def chunk(step, carry, k=k, mu=mu, r=r, gain=gain, first=first, second=second):
            at = pl.multiple_of(step * CHUNK, CHUNK)
            here = pl.ds(at, CHUNK)
            spot = lax.broadcasted_iota(jnp.int32, (CHUNK, 1), 0) + at
            real = (spot < limit).astype(F32)
            normed = (out_ref[k, here, :] - mu) * r
            value = gain * (grad_ref[k, here, :] - real * (first + normed * second))
            low_ref[k, here, :] = value.astype(BF16)
            return carry

        lax.fori_loop(0, rows // CHUNK, chunk, 0, unroll=UNROLL)
    parts = [dot_nt(low_ref[k], w_out_ref[place.batch ^ k]) for k in range(blocks)]
    flat_ref[...] = functools.reduce(jnp.add, parts)
    spread_map_rows(flat_ref, gw_ref)
    center, scale, gain, shift = mid_norm(place, mid_sums_refs, mid_affine_ref)
    rises, leans, attended = [], [], []
    for image in range(images):

        def gather(step, carry, image=image):
            attended, rise, lean = carry
            at = pl.multiple_of(image * PADDED + step * CHUNK, CHUNK)
            normed = (mid_ref[pl.ds(at, CHUNK), :] - center) * scale
            value = normed * gain + shift
            share = logistic(value)
            grad = gw_ref[pl.ds(at, CHUNK), :]
            grad = jnp.concatenate([grad, grad], axis=1)
            active = grad * share
            attended = attended + fold(active * value)
            inclined = active * (1.0 + value * (1.0 - share))
            return attended, rise + fold(inclined), lean + fold(inclined * normed)

        nothing = jnp.zeros((8, 2 * width), F32)
        parts = lax.fori_loop(
            0, PADDED // CHUNK, gather, (nothing, nothing, nothing), unroll=UNROLL
        )
        share = attention_ref[image : image + 1, :]
        attended.append(total_of(parts[0]))
        rises.append(share * total_of(parts[1]))
        leans.append(share * total_of(parts[2]))
    grad = jnp.concatenate(attended, axis=0)
    attention = attention_ref[...]
    inner = attention * grad
    inner = inner[:, :width] + inner[:, width:]
    logits = attention * (grad - jnp.concatenate([inner, inner], axis=1))
    logits_ref[...] = logits
    gate = dot_nn(logits, excite_ref[...].astype(F32), HIGHEST) * gate_ref[1]
    pack = msg_ref.shape[1]
    pieces = 2 * width // pack
    for t, row in enumerate((functools.reduce(jnp.add, rises), functools.reduce(jnp.add, leans))):
        for q in range(pieces):
            msg_ref[t * pieces + q : t * pieces + q + 1, :] = row[:, q * pack : (q + 1) * pack]
    msg_ref[2 * pieces : 2 * pieces + images, :] = gate


def back_mid(
    counts_ref,
    back_refs,
    gathered_refs,
    incline_refs,
    wall_ref,
    gate_affine_ref,
    squeeze_ref,
    attention_ref,
    gw_ref,
    mid_ref,
    mid_sums_refs,
    mid_affine_ref,
    pre_ref,
    sums_refs,
    affine_ref,
    w_ref,
    low_ref,
    grad_ref,
    gate_ref,
    vector_ref,
    msg_ref,
    taps_ref,
):
    place = Place(counts_ref)
    images = attention_ref.shape[0]
    width = attention_ref.shape[1] // 2
    lanes = wall_ref.shape[1]
    pieces = 2 * width // lanes
    total = place.total() * PIXELS
    wall = wall_ref[...]
    rows = slot_rows(gathered_refs, 8, 0, images)
    center, scale = gate_norm(place, rows, wall)
    gain = gate_affine_ref[0:1, :] * scale
    normed = (rows - center) * scale
    grads = slot_rows(back_refs, images, 0, images, 2 * pieces)
    first, second = total_of(wall * grads), total_of(wall * grads * normed)
    vector_ref[0:1, 0:lanes] = second
    vector_ref[0:1, lanes : 2 * lanes] = first
    squeezed = gain * (grads - wall * (first + normed * second) / place.total())
    gate_ref[...] = squeezed[0:images]
    pooled_grad = dot_nt(squeezed, squeeze_ref[...].astype(F32), HIGHEST) / PIXELS
    pooled_grad = jnp.concatenate([pooled_grad, pooled_grad], axis=1)
    slot = 0
    terms = jnp.zeros((2 * images, 2 * width), F32)
    for ref in incline_refs:
        inclines = ref[...]
        for at in range(0, inclines.shape[0], 2 * images):
            grad = pooled_grad[slot * images : (slot + 1) * images, :]
            terms = terms + inclines[at : at + 2 * images] * jnp.concatenate([grad, grad], axis=0)
            slot += 1
    sums = functools.reduce(jnp.add, [ref[0 : 2 * pieces, :] for ref in back_refs])
    back = []
    for t in range(2):
        row = [sums[t * pieces + q : t * pieces + q + 1, :] for q in range(pieces)]
        back.append(
            jnp.concatenate(row, axis=1) + total_of(terms[t * images : (t + 1) * images])
        )
    vector_ref[1:2, :] = back[1]
    vector_ref[2:3, :] = back[0]
    own = pooled_grad[0:images]
    first, second = back[0] / total, back[1] / total
    center, scale, gain, shift = mid_norm(place, mid_sums_refs, mid_affine_ref)
    gained = gain * scale
    clear_gaps(taps_ref, images)
    keep = columns_real(WIDE)
    for image in range(images):
        share = attention_ref[image : image + 1, :]
        offset = own[image : image + 1, :]
        real = place.real(image)
        lead, lag = real * first, real * second

        def chunk(step, carry, image=image, share=share, offset=offset, lead=lead, lag=lag):
            rows = pl.multiple_of(step * WIDE, WIDE)
            here = pl.ds(image * PADDED + rows, WIDE)
            normed = (mid_ref[here, :] - center) * scale
            grad = gw_ref[here, :]
            grad = jnp.concatenate([grad, grad], axis=1)
            grad = (share * grad + offset) * slope(normed * gain + shift)
            value = gained * (grad - (lead + normed * lag)) * keep
            store_taps(taps_ref, image * STRIDE + WIDE + rows, value)
            return carry

        lax.fori_loop(0, SIDE, chunk, 0, unroll=UNROLL)
    low_ref[...] = taps_ref[1]
    sums = summed_over(sums_refs)
    center, scale = moments(sums[0:1], sums[1:2], total)
    gain, shift = affine_ref[0:1, :], affine_ref[1:2, :]
    half = width // 2
    keep = columns_real(PADDED)
    firsts = [jnp.zeros((1, half), F32) for _ in range(2)]
    seconds = [jnp.zeros((1, half), F32) for _ in range(2)]
    for image in range(images):
        real = place.real(image)
        here = slice(image * PADDED, (image + 1) * PADDED)
        for r in range(2):
            left = jnp.concatenate(
                [
                    taps_ref[
                        2 - b,
                        image * STRIDE + (2 - a) * WIDE : image * STRIDE + (2 - a) * WIDE + PADDED,
                        r * width : (r + 1) * width,
                    ]
                    for a in range(3)
                    for b in range(3)
                ],
                axis=1,
            )
            lane = slice(r * half, (r + 1) * half)
            normed = (pre_ref[here, lane] - center[:, lane]) * scale[:, lane]
            value = dot_nn(left, w_ref[r]) * slope(normed * gain[:, lane] + shift[:, lane])
            value = value * (keep * real)
            grad_ref[here, lane] = value
            firsts[r] = firsts[r] + total_of(value)
            seconds[r] = seconds[r] + total_of(value * normed)
    sums = jnp.concatenate(
        [jnp.concatenate(firsts, axis=1), jnp.concatenate(seconds, axis=1)], axis=0
    )
    msg_ref[...] = sums


def sort_pieces(
    place,
    source_ref,
    keep_ref,
    send_ref,
    row,
):
    for turn, s in enumerate(ORDER):
        target = keep_ref if turn < 2 else send_ref
        rows = source_ref.shape[1]
        target[turn % 2, row : row + rows, :] = source_ref[place.chan ^ s].astype(BF16)


def weight_out_term(
    counts_ref,
    weighted_ref,
    low_ref,
    gate_ref,
    logits_ref,
    keep_ref,
    send_ref,
    wide_ref,
    small_ref,
):
    place = Place(counts_ref)
    width = weighted_ref.shape[1]
    lanes = keep_ref.shape[2]
    own = width // len(SLOTS)
    for turn, s in enumerate(ORDER):
        target = keep_ref if turn < 2 else send_ref
        held = place.batch ^ place.chan ^ s
        term = dot_tn(weighted_ref[...], low_ref[held]).astype(BF16)
        target[turn % 2, 0:width, :] = term[:, :lanes]
        target[turn % 2, width : 2 * width, :] = term[:, lanes:]
    wide_ref[...] = dot_tn(logits_ref[...], gate_ref[0], HIGHEST)
    for turn, s in enumerate(ORDER):
        target = keep_ref if turn < 2 else send_ref
        for r in range(2):
            at = pl.multiple_of(r * width + (place.chan ^ s) * own, own)
            row = 2 * width + r * own
            target[turn % 2, row : row + own, :] = wide_ref[pl.ds(at, own), :].astype(BF16)
    small_ref[...] = jnp.zeros_like(small_ref)
    bias = total_of(logits_ref[...])
    for k in range(len(SLOTS)):
        small_ref[k, 0:1, :own] = bias[:, k * own : (k + 1) * own]
        small_ref[k, 0:1, own:] = bias[:, width + k * own : width + (k + 1) * own]
    sort_pieces(place, small_ref, keep_ref, send_ref, 2 * width + 2 * own)


def weight_mid_term(
    counts_ref,
    taps_ref,
    low_ref,
    pooled_ref,
    gathered_refs,
    squeezed_ref,
    keep_ref,
    send_ref,
    wide_ref,
    narrow_ref,
):
    place = Place(counts_ref)
    half = taps_ref.shape[2] // 2
    width = low_ref.shape[1] // 2
    own = width // len(SLOTS)
    rows = low_ref.shape[0] - 2 * WIDE
    for r in range(2):
        right = jnp.concatenate(
            [
                taps_ref[b, a * WIDE : a * WIDE + rows, r * half : (r + 1) * half]
                for a in range(3)
                for b in range(3)
            ],
            axis=1,
        )
        wide_ref[...] = dot_tn(low_ref[WIDE : WIDE + rows, r * width : (r + 1) * width], right)
        for turn, s in enumerate(ORDER):
            target = keep_ref if turn < 2 else send_ref
            here = pl.ds(pl.multiple_of((place.chan ^ s) * own, own), own)
            for tap in range(9):
                row = (2 * tap + r) * own
                target[turn % 2, row : row + own, :] = wide_ref[
                    here, tap * half : (tap + 1) * half
                ].astype(BF16)
    images, lanes = pooled_ref.shape[0], squeezed_ref.shape[1]
    mean = [
        total_of(slot_rows(gathered_refs, 8, images + q, 1)) for q in range(width // lanes)
    ]
    mean = jnp.concatenate(mean, axis=1) / place.total()
    narrow_ref[...] = dot_tn(pooled_ref[...] - mean, squeezed_ref[...], HIGHEST)
    for turn, s in enumerate(ORDER):
        target = keep_ref if turn < 2 else send_ref
        here = pl.ds(pl.multiple_of((place.chan ^ s) * own, own), own)
        target[turn % 2, 18 * own : 19 * own, :] = narrow_ref[here, :].astype(BF16)


def back_in(
    share,
    counts_ref,
    grad_ref,
    pre_ref,
    sums_refs,
    back_refs,
    affine_ref,
    x0,
    x1,
    x2,
    x3,
    vector_ref,
    out_back_refs,
    low_ref,
    keep_ref,
    send_ref,
    flat_ref,
    wide_ref,
    small_ref,
):
    place = Place(counts_ref)
    images = pre_ref.shape[0] // PADDED
    width = pre_ref.shape[1]
    own = width // len(SLOTS)
    chan, batch = place.chan, place.batch
    total = place.total() * PIXELS
    sums = summed_over(sums_refs)
    center, scale = moments(sums[0:1], sums[1:2], total)
    back = summed_over(back_refs)
    first, second = back[0:1] / total, back[1:2] / total
    gain = affine_ref[0:1, :] * scale
    for image in range(images):
        real = place.real(image)
        lead, lag = real * first, real * second
        for line in range(SIDE):
            at = image * PADDED + line * WIDE
            normed = (pre_ref[at : at + WIDE, :] - center) * scale
            value = gain * (grad_ref[at : at + WIDE, :] - (lead + normed * lag))
            at = image * PIXELS + line * SIDE
            flat_ref[at : at + SIDE, :] = value[:SIDE]
    low_ref[...] = flat_ref[...].astype(BF16)
    lanes = keep_ref.shape[2]
    for k, x in enumerate((x0, x1, x2, x3)):
        wide_ref[...] = dot_tn(low_ref[...], x[...])
        for turn, s in enumerate(ORDER):
            target = keep_ref if turn < 2 else send_ref
            here = pl.ds(pl.multiple_of((chan ^ s) * own, own), own)
            for part in range(wide_ref.shape[1] // lanes):
                at = pl.multiple_of(((batch ^ k) * (wide_ref.shape[1] // lanes) + part) * own, own)
                target[turn % 2, pl.ds(at, own), :] = wide_ref[
                    here, part * lanes : (part + 1) * lanes
                ].astype(BF16)
    small_ref[...] = jnp.zeros_like(small_ref)
    outs = summed_over(out_back_refs)
    for k in range(len(SLOTS)):
        here = slice(k * own, (k + 1) * own)
        there = slice(width + k * own, width + (k + 1) * own)
        small_ref[k, 0:1, :own] = back[1:2, here]
        small_ref[k, 0:1, own:] = back[0:1, here]
        for t in range(2):
            small_ref[k, 1 + t : 2 + t, :own] = vector_ref[1 + t : 2 + t, here]
            small_ref[k, 1 + t : 2 + t, own:] = vector_ref[1 + t : 2 + t, there]
        small_ref[k, 3:4, :] = vector_ref[0:1, 0:lanes]
        small_ref[k, 4:5, :] = vector_ref[0:1, lanes : 2 * lanes]
    for s in SLOTS:
        for t in range(2):
            row = outs[(1 - t) * len(SLOTS) + s : (1 - t) * len(SLOTS) + s + 1, :]
            small_ref[batch ^ s, 5 + 2 * t : 6 + 2 * t, :] = row[:, :lanes]
            small_ref[batch ^ s, 6 + 2 * t : 7 + 2 * t, :] = row[:, lanes:]
    small_ref[...] = small_ref[...] * share
    sort_pieces(place, small_ref, keep_ref, send_ref, keep_ref.shape[1] - small_ref.shape[1])


def grad_input(
    counts_ref,
    low_ref,
    w_ref,
    summed_ref,
    g0,
    g1,
    g2,
    g3,
):
    place = Place(counts_ref)
    for s, target in enumerate((g0, g1, g2, g3)):
        target[...] = (dot_nn(low_ref[...], w_ref[place.batch ^ s]) + summed_ref[s]).astype(BF16)


def add_groups(terms_ref, sum_ref):
    value = jnp.sum(terms_ref[...].astype(F32), axis=0).astype(BF16)
    sum_ref[...] = jnp.broadcast_to(value[None], sum_ref.shape)


def added(left_ref, right_ref):
    return left_ref[...].astype(F32) + right_ref[...].astype(F32)


def add_core(keep_ref, arrived_ref, kept_ref, send_ref):
    value = added(keep_ref, arrived_ref).astype(BF16)
    kept_ref[...] = value[0]
    send_ref[...] = value[1]


def add_chip(counts_ref, keep_refs, arrived_refs, kept_ref, send_ref, whole_ref):
    place = Place(counts_ref)
    at = 0
    for keep_ref, arrived_ref in zip(keep_refs, arrived_refs):
        whole_ref[at : at + keep_ref.shape[0], :] = added(keep_ref, arrived_ref)
        at += keep_ref.shape[0]
    if at < whole_ref.shape[0]:
        whole_ref[at:, :] = jnp.zeros((whole_ref.shape[0] - at, whole_ref.shape[1]), F32)
    rows = kept_ref.shape[0]
    own = place.parity
    kept_ref[...] = whole_ref[pl.ds(pl.multiple_of(own * rows, 16), rows), :]
    send_ref[...] = whole_ref[pl.ds(pl.multiple_of((1 - own) * rows, 16), rows), :].astype(BF16)


def add_parity(
    counts_ref,
    keep_ref,
    arrived_ref,
    kept_ref,
    s1,
    s2,
    s3,
    whole_ref,
):
    place = Place(counts_ref)
    whole_ref[...] = added(keep_ref, arrived_ref)
    rows = kept_ref.shape[0]
    for t, target in enumerate((kept_ref, s1, s2, s3)):
        at = pl.multiple_of((place.depth ^ t) * rows, 16)
        target[...] = whole_ref[pl.ds(at, rows), :].astype(target.dtype)


def add_depth(keep_ref, arrived_refs, sum_ref):
    value = keep_ref[...]
    for ref in arrived_refs:
        value = value + ref[...].astype(F32)
    sum_ref[...] = value.astype(BF16)


def join_depth(
    counts_ref,
    piece_refs,
    whole_ref,
):
    place = Place(counts_ref)
    rows = piece_refs[0].shape[0]
    for t, ref in enumerate(piece_refs):
        whole_ref[pl.ds(pl.multiple_of((place.depth ^ t) * rows, 16), rows), :] = ref[...]


def join_parity(
    place,
    half_refs,
    whole_ref,
):
    rows = half_refs[0].shape[0]
    for t, ref in enumerate(half_refs):
        at = pl.multiple_of((place.parity ^ t) * rows, 16)
        whole_ref[pl.ds(at, rows), :] = ref[...].astype(F32)


def unpack(
    counts_ref,
    half_refs,
    in_ref,
    mid_ref,
    squeeze_ref,
    excite_ref,
    bias_ref,
    out_ref,
    small_ref,
    whole_ref,
):
    join_parity(Place(counts_ref), half_refs, whole_ref)
    own, lanes = squeeze_ref.shape
    width = out_ref.shape[0]
    out_ref[:, :lanes] = whole_ref[0:width, :]
    out_ref[:, lanes:] = whole_ref[width : 2 * width, :]
    row = 2 * width
    for target in (excite_ref, bias_ref, mid_ref, squeeze_ref):
        target[...] = whole_ref[row : row + target.shape[0], :]
        row += target.shape[0]
    for block in range(in_ref.shape[1] // lanes):
        in_ref[:, block * lanes : (block + 1) * lanes] = whole_ref[row : row + own, :]
        row += own
    small_ref[...] = whole_ref[row : row + small_ref.shape[0], :]


def per_device(
    activations,
    counts,
    weight_in,
    gain_in,
    shift_in,
    weight_mid,
    gain_mid,
    shift_mid,
    weight_squeeze,
    gain_gate,
    shift_gate,
    weight_excite,
    shift_excite,
    weight_out,
    gain_out,
    shift_out,
    cotangent,
    *,
    groups,
    parts,
):
    batches, rows, lanes = activations.shape
    images = rows // PIXELS
    own = weight_in.shape[1]
    width = own * parts
    inter = gain_gate.shape[0]
    wide_rows = images * PADDED
    gap_rows = WIDE + images * STRIDE
    chan, group = lax.axis_index("chan"), lax.axis_index("dp")
    depth = groups // 2

    def permute(tensor, to):
        pairs = []
        for index in range(groups * parts):
            z, x, y, c = index // parts // 2, index // parts % 2, index % parts // 2, index % 2
            z, x, y, c = to(z, x, y, c)
            pairs.append((index, (2 * z + x) * parts + 2 * y + c))
        return lax.ppermute(tensor, ("dp", "chan"), pairs)

    def home(tensor, s):
        return permute(tensor, lambda z, x, y, c: (z, c ^ (s & 1), y ^ (s >> 1), x))

    def away(tensor, s):
        return permute(tensor, lambda z, x, y, c: (z, c, y ^ (s >> 1), x ^ (s & 1)))

    def core(tensor):
        return permute(tensor, lambda z, x, y, c: (z, x, y, c ^ 1))

    def across(tensor):
        return permute(tensor, lambda z, x, y, c: (z, x, y ^ 1, c))

    def parity(tensor):
        return permute(tensor, lambda z, x, y, c: (z, x ^ 1, y, c))

    def along(tensor, t):
        return permute(tensor, lambda z, x, y, c: (z ^ t, x, y, c))

    def after(tensor, *others):
        return lax.optimization_barrier((tensor,) + others)[0]

    def after_all(tensors, *others):
        return lax.optimization_barrier(tuple(tensors) + others)[: len(tensors)]

    def exchange(total, gather):
        def merge(mine, other):
            cut = 0 if total is None else total
            joined = [mine[:cut] + other[:cut]] if cut else []
            if gather:
                joined += [mine[cut : cut + gather], other[cut : cut + gather]]
            return jnp.concatenate(joined) if len(joined) > 1 else joined[0]

        def run(mine):
            nonlocal gather
            mine = merge(mine, core(mine))
            gather = 2 * gather
            if depth <= 4:
                return (mine,) + tuple(along(mine, t) for t in range(1, depth))
            step = 1
            while step < depth:
                mine = merge(mine, along(mine, step))
                gather, step = 2 * gather, 2 * step
            return (mine,)

        return run

    def add_over_chan(keep, send):
        rows = keep.shape[1]
        keep, send = call(
            add_core, [shape((rows, 2 * own), BF16)] * 2, [], 0, keep, core(send), smem=0
        )
        return keep, across(send)

    def add_over_dp(keep, arrived):
        rows = sum(k.shape[0] for k in keep)
        if groups != 8:
            whole = -(-rows // (16 * groups)) * 16 * groups
            terms = jnp.concatenate(keep).astype(F32) + jnp.concatenate(arrived).astype(F32)
            terms = jnp.pad(terms.astype(BF16), ((0, whole - rows), (0, 0)))
            terms = lax.all_to_all(terms.reshape(groups, whole // groups, -1), "dp", 0, 0)
            (terms,) = call(add_groups, [shape(terms.shape, BF16)], [], 0, terms, smem=0)
            terms = lax.all_to_all(terms, "dp", 0, 0).reshape(2, whole // 2, -1)
            swap = group % 2 == 1
            return (
                jnp.where(swap, terms[1], terms[0]),
                jnp.where(swap, terms[0], terms[1]),
            )
        piece = -(-rows // (16 * groups)) * 16
        half = piece * depth
        keep, send = call(
            add_chip,
            [shape((half, 2 * own)), shape((half, 2 * own), BF16)],
            [pltpu.VMEM((2 * half, 2 * own), F32)],
            0,
            counts,
            keep,
            arrived,
        )
        keep, *send = call(
            add_parity,
            [shape((piece, 2 * own))] + [shape((piece, 2 * own), BF16)] * (depth - 1),
            [pltpu.VMEM((half, 2 * own), F32)],
            0,
            counts,
            keep,
            parity(send),
        )
        arrived = tuple(along(send[t - 1], t) for t in range(1, depth))
        (mine,) = call(add_depth, [shape((piece, 2 * own), BF16)], [], 0, keep, arrived, smem=0)
        pieces = (mine,) + tuple(along(mine, t) for t in range(1, depth))
        (mine,) = call(join_depth, [shape((half, 2 * own), BF16)], [], 0, counts, pieces)
        return mine, parity(mine)

    def send_home(tensor):
        pieces = [lax.dynamic_index_in_dim(tensor, chan ^ s, 0, keepdims=False) for s in SLOTS]
        return tuple(home(piece, s) for s, piece in enumerate(pieces))

    x = send_home(activations)
    small = jnp.concatenate(
        [
            jnp.concatenate([gain_in, shift_in])[None],
            gain_mid.reshape(1, 2 * own),
            shift_mid.reshape(1, 2 * own),
            shift_excite.reshape(1, 2 * own),
            gain_out.reshape(-1, 2 * own),
            shift_out.reshape(-1, 2 * own),
            jnp.zeros((8, 2 * own), BF16),
        ]
    )

    def lane_blocks(tensor):
        return [tensor[:, at : at + 2 * own] for at in range(0, tensor.shape[1], 2 * own)]

    first = jnp.concatenate(lane_blocks(weight_in.T) + [small])
    second = weight_mid.transpose(0, 1, 3, 4, 2).reshape(-1, 2 * own)
    third = jnp.concatenate(
        [weight_excite.transpose(1, 2, 0).reshape(-1, inter), weight_squeeze]
        + lane_blocks(weight_out)
    )

    def gather_slots(tensor, *others):
        near, other = core(tensor), across(tensor)
        other = after(other, near, *others)
        return tensor, near, other, core(other)

    first = gather_slots(first, x[0], x[1])
    second = gather_slots(after(second, x[2], x[3], first[2]))
    third = gather_slots(after(third, second[2]))
    gate_affine = jnp.stack([gain_gate, shift_gate]).astype(F32)

    product = 2 * rows * lanes * parts * width
    pre_in, msg, w_in, in_affine, mid_affine, bias, out_affine, wall = call(
        reduce_in,
        [
            shape((wide_rows, width)),
            shape((2, width)),
            shape((parts, width, lanes), BF16),
            shape((2, width)),
            shape((2, 2 * width)),
            shape((1, 2 * width)),
            shape((2, parts, 1, lanes)),
            shape((groups * images, inter)),
        ],
        [pltpu.VMEM((rows, width), F32), pltpu.VMEM((parts, 16, 2 * own), F32)],
        product,
        counts,
        *x,
        *first,
    )
    in_sums = exchange(2, 0)(msg)
    w_mid, w_mid_back = call(
        place_mid,
        [shape((2, width, 9 * inter), BF16), shape((2, 9 * width, inter), BF16)],
        [],
        0,
        counts,
        *second,
    )
    excite, squeeze, w_out = call(
        place_rest,
        [
            shape((2 * width, inter), BF16),
            shape((width, inter), BF16),
            shape((parts, width, lanes), BF16),
        ],
        [],
        0,
        counts,
        *third,
    )
    cot = send_home(after(cotangent, third[2]))
    conv = 2 * wide_rows * 9 * width * width
    taps, mid, msg = call(
        conv_mid,
        [
            shape((3, gap_rows, width), BF16),
            shape((wide_rows, 2 * width)),
            shape((2, 2 * width)),
        ],
        [],
        conv,
        counts,
        pre_in,
        in_sums,
        in_affine,
        w_mid,
    )
    mid_sums = exchange(2, 0)(msg)
    pooled, msg, inclines = call(
        pool,
        [shape((images, width)), shape((8, inter)), shape((2 * images, 2 * width))],
        [],
        0,
        counts,
        mid,
        mid_sums,
        mid_affine,
        squeeze,
    )
    gathered = exchange(None, 8)(msg)
    inclines = exchange(None, 2 * images)(inclines)
    gate, attention, weighted, out, msg = call(
        attend,
        [
            shape((2, images, inter)),
            shape((images, 2 * width)),
            shape((rows, width), BF16),
            shape((parts, rows, lanes)),
            shape((2 * parts, lanes)),
        ],
        [pltpu.VMEM((wide_rows, width), F32), pltpu.VMEM((rows, width), F32)],
        product,
        counts,
        gathered,
        wall,
        gate_affine,
        excite,
        bias,
        mid,
        mid_sums,
        mid_affine,
        w_out,
    )
    out_sums = exchange(2 * parts, 0)(msg)
    *result, grad, msg = call(
        finish,
        [shape((rows, lanes), BF16)] * parts
        + [shape((parts, rows, lanes)), shape((2 * parts, lanes))],
        [],
        0,
        counts,
        out,
        out_sums,
        out_affine,
        *x,
        *cot,
    )
    out_back = exchange(2 * parts, 0)(msg)

    def settle(pieces, *others):
        pieces = after_all([away(piece, s) for s, piece in enumerate(pieces)], *others)
        settled = jnp.zeros((batches, rows, lanes), BF16)
        for s, piece in enumerate(pieces):
            settled = lax.dynamic_update_index_in_dim(settled, piece, chan ^ s, 0)
        return settled

    result = settle(result)

    sums_rows = 2 * 2 * width // inter
    low_out, grad_weighted, grad_logits, msg = call(
        back_out,
        [
            shape((parts, rows, lanes), BF16),
            shape((wide_rows, width)),
            shape((images, 2 * width)),
            shape((sums_rows + images, inter)),
        ],
        [pltpu.VMEM((rows, width), F32)],
        product,
        counts,
        grad,
        out,
        out_sums,
        out_back,
        out_affine,
        w_out,
        mid,
        mid_sums,
        mid_affine,
        attention,
        gate,
        excite,
    )
    mid_back = exchange(sums_rows, images)(msg)
    term_rows = 2 * width + 2 * own + 16
    keep, send = call(
        weight_out_term,
        [shape((2, term_rows, 2 * own), BF16)] * 2,
        [pltpu.VMEM((2 * width, inter), F32), pltpu.VMEM((parts, 16, 2 * own), F32)],
        product,
        counts,
        after(weighted, mid_back[0]),
        low_out,
        gate,
        grad_logits,
    )
    mid_back = after_all(mid_back, keep)
    out_keep, out_arrived = add_over_chan(keep, send)
    low_mid, grad_hidden, grad_squeeze, vectors, msg = call(
        back_mid,
        [
            shape((gap_rows, 2 * width), BF16),
            shape((wide_rows, width)),
            shape((images, inter)),
            shape((8, 2 * width)),
            shape((2, width)),
        ],
        [pltpu.VMEM((3, gap_rows, 2 * width), BF16)],
        conv,
        counts,
        mid_back,
        gathered,
        inclines,
        wall,
        gate_affine,
        squeeze,
        attention,
        grad_weighted,
        mid,
        mid_sums,
        mid_affine,
        pre_in,
        in_sums,
        in_affine,
        w_mid_back,
    )
    in_back = exchange(2, 0)(msg)
    keep, send = call(
        weight_mid_term,
        [shape((2, 19 * own, 2 * own), BF16)] * 2,
        [pltpu.VMEM((width, 9 * inter), F32), pltpu.VMEM((width, inter), F32)],
        conv,
        counts,
        after(taps, in_back[0]),
        low_mid,
        pooled,
        gathered,
        grad_squeeze,
    )
    in_back = after_all(in_back, keep)
    mid_keep, mid_arrived = add_over_chan(keep, send)
    in_rows = parts * lanes // (2 * own) * own
    low_in, keep, send = call(
        functools.partial(back_in, 1.0 / groups),
        [shape((rows, width), BF16)] + [shape((2, in_rows + 16, 2 * own), BF16)] * 2,
        [
            pltpu.VMEM((rows, width), F32),
            pltpu.VMEM((width, lanes), F32),
            pltpu.VMEM((parts, 16, 2 * own), F32),
        ],
        product,
        counts,
        grad_hidden,
        pre_in,
        in_sums,
        in_back,
        in_affine,
        *x,
        vectors,
        out_back,
    )
    in_keep, in_arrived = add_over_chan(keep, send)
    low_in = after(low_in, in_arrived)
    grad_x = call(
        grad_input, [shape((rows, lanes), BF16)] * parts, [], product, counts, low_in, w_in, grad
    )
    halves = add_over_dp((out_keep, mid_keep, in_keep), (out_arrived, mid_arrived, in_arrived))
    g_in, g_mid, g_squeeze, g_excite, g_bias, g_out, sums = call(
        unpack,
        [
            shape((own, parts * lanes)),
            shape((18 * own, inter)),
            shape((own, inter)),
            shape((2 * own, inter)),
            shape((16, 2 * own)),
            shape((width, lanes)),
            shape((16, 2 * own)),
        ],
        [pltpu.VMEM((2 * halves[0].shape[0], 2 * own), F32)],
        0,
        counts,
        halves,
    )
    grad_x = settle(grad_x, g_in)
    outs = lanes // (2 * own)
    return (
        result,
        grad_x,
        g_in.T,
        sums[0, :own],
        sums[0, own:],
        g_mid.reshape(3, 3, 2, own, inter).transpose(0, 1, 4, 2, 3),
        sums[1].reshape(2, own),
        sums[2].reshape(2, own),
        g_squeeze,
        sums[3],
        sums[4],
        g_excite.reshape(2, own, inter).transpose(2, 0, 1),
        g_bias[0].reshape(2, own),
        g_out,
        sums[5 : 5 + outs].reshape(-1),
        sums[5 + outs : 5 + 2 * outs].reshape(-1),
    )


def solution(mesh):
    placed = (
        P(None, "dp", "chan"),
        P(),
        P(None, "chan"),
        P("chan"),
        P("chan"),
        P(None, None, None, None, "chan"),
        P(None, "chan"),
        P(None, "chan"),
        P("chan", None),
        P(),
        P(),
        P(None, None, "chan"),
        P(None, "chan"),
        P(None, "chan"),
        P("chan"),
        P("chan"),
        P(None, "dp", "chan"),
    )
    return jax.shard_map(
        functools.partial(per_device, groups=mesh.shape["dp"], parts=mesh.shape["chan"]),
        mesh=mesh,
        in_specs=placed,
        out_specs=placed[:1] + placed[:1] + placed[2:16],
        check_vma=False,
    )
```

time: 386 us -> 245 us (0.63)
  blocking collectives: 86.1 us -> 0 us
  local copies, waits for them, and re-layouts: 90.9 us -> 17.5 us
  waiting for transfers between devices: 85.3 us -> 114 us
  starting transfers between devices: 47.9 us -> 72.8 us
  between operations: 15.6 us -> 1.31 us
  other arithmetic: 11.4 us -> 1.31 us
  Pallas kernels: 42.6 us -> 35.8 us
  matrix products: 3.92 us -> 0 us
    ppermute x0 -> x71, waiting for transfers between devices: none -> 114 us  [permute(): return lax.ppermute(tensor, ('dp', 'chan'), pairs)]
    all_to_all x4 -> x0, blocking collectives: 86.1 us -> none  [the longest x3 53.2 us: over_groups(): return lax.all_to_all(tensor, 'dp', 0, 0, tiled=False)]
    ppermute x0 -> x71, starting transfers between devices: none -> 72.8 us  [permute(): return lax.ppermute(tensor, ('dp', 'chan'), pairs)]
    all_to_all x10 -> x0, waiting for transfers between devices: 52.8 us -> none  [the longest x4 39.8 us: over_chan(): return lax.all_to_all(tensor, 'chan', 0, 0, tiled=False)]
    all_to_all x10 -> x0, starting transfers between devices: 47.9 us -> none  [the longest x6 31 us: over_groups(): return lax.all_to_all(tensor, 'dp', 0, 0, tiled=False)]
    all_gather x1 -> x0, waiting for transfers between devices: 32.5 us -> none  [per_device(): packed = lax.all_gather(jnp.concatenate(blocks), 'chan')]
    unnamed x140 -> x38, local copies, waits for them, and re-layouts: 27.9 us -> 1.64 us
    slice x33 -> x4, local copies, waits for them, and re-layouts: 17.8 us -> 0.04 us  [the longest x2 0.03 us: lane_blocks(): tensor[:, at:at + 2 * own]]
  transfers between devices with their start and end apart: 11 -> 71, of which waited for: 5 -> 34; matrix products, arithmetic and copies ran while one was open for 15% -> 4% of each run, Pallas kernels for 2% -> 7%
where the time goes in v2:
time: 245 us; the launch traced here: 243 us
  waiting for transfers between devices  114 us (47%)
  starting transfers between devices  72.8 us (30%)
  Pallas kernels  35.8 us (15%)
  local copies, waits for them, and re-layouts  17.5 us (7%)
    ppermute x71, waiting for transfers between devices, permute(): return lax.ppermute(tensor, ('dp', 'chan'), pairs)  114 us
    ppermute x71, starting transfers between devices, permute(): return lax.ppermute(tensor, ('dp', 'chan'), pairs)  72.8 us
    pallas_call x21, Pallas kernels, call(): pl.pallas_call(body, out_shape=outs, in_specs=specs, out_specs=[pl.BlockS...  35.8 us
  transfers between devices with their start and end apart: 71, of which 34 were waited for; matrix products, arithmetic and copies ran while one was open for 4% of the time, Pallas kernels for 7%

profile of v2, /device:TPU:0, one launch (start us, length us, event | category | flops | bytes accessed | tf_op | source)
XLA Modules:
  0.0 242.9 jit_solution(6563433481761875063)
XLA Ops:
  0.7 2.3 dynamic-slice_bitcast_fusion.4
  3.0 1.6 collective-permute-start
  4.7 3.2 %collective-permute-start.1 = (bf16[784,256]{1,0:T(8,128)(2,1)S(1)}, bf16[784,256]{1,0:T(8,128)(2,1)S(1)}, u32[]{:S(2)}, u32[]{:S(2)}) collective-permute-start(bf16[784,256]{1,0:T(8,128)(2,1)S(1)} %get-tuple-element.211), channel_id=1, source_target_pairs={{0,4},{1,0},{2,6},{3,2},{4,5},{5,1},{6,7},{7,3},{8,12},{9,8},{10,1... | collective-permute-start | bytes 1204232 | tf_op jit(solution)/shard_map/ppermute | solution.py:1035
  7.9 1.5 collective-permute-start.2
  15.6 1.6 concatenate.19.a0
  17.1 1.4 collective-permute-done.4.a1
  18.5 1.5 collective-permute-start.5
  20.0 10.8 %collective-permute-done.5.a2 = bf16[528,128]{1,0:T(8,128)(2,1)S(1)} collective-permute-done((bf16[528,128]{1,0:T(8,128)(2,1)S(1)}, bf16[528,128]{1,0:T(8,128)(2,1)S(1)}, u32[]{:S(2)}, u32[]{:S(2)}) %collective-permute-start.5) | collective-permute-done | bytes 135200 | tf_op jit(solution)/shard_map/ppermute | solution.py:1035
  31.5 1.7 collective-permute-start.12
  33.2 7.6 %collective-permute-done.12.b2 = bf16[1152,128]{1,0:T(8,128)(2,1)S(1)} collective-permute-done((bf16[1152,128]{1,0:T(8,128)(2,1)S(1)}, bf16[1152,128]{1,0:T(8,128)(2,1)S(1)}, u32[]{:S(2)}, u32[]{:S(2)}) %collective-permute-start.12) | collective-permute-done | bytes 294944 | tf_op jit(solution)/shard_map/ppermute | solution.py:1035
  41.4 1.8 collective-permute-start.19
  43.2 1.4 collective-permute-done.6.a3
  44.5 1.4 reduce_in.1
  47.1 3.6 %collective-permute-start.10 = (f32[2,256]{1,0:T(2,128)S(1)}, f32[2,256]{1,0:T(2,128)S(1)}, u32[]{:S(2)}, u32[]{:S(2)}) collective-permute-start(f32[2,256]{1,0:T(2,128)S(1)} %add.48.sums_refs_0_), channel_id=1, source_target_pairs={{0,24},{1,25},{2,26},{3,27},{4,28},{5,29},{6,30},{7,31},{8,16},{9,... | collective-permute-start | bytes 6152 | tf_op jit(solution)/shard_map/ppermute | solution.py:1035
  52.5 1.8 collective-permute-done.8.sums_refs_1_
  55.2 3.0 %conv_mid.1 = (bf16[3,976,256]{2,1,0:T(8,128)(2,1)S(1)}, f32[896,512]{1,0:T(8,128)S(1)}, f32[2,512]{1,0:T(2,128)S(1)}) custom-call(s32[4,8]{1,0:T(4,128)S(1)} %copy-done, f32[896,256]{1,0:T(8,128)S(1)} %get-tuple-element.111.pre_ref, f32[2,256]{1,0:T(2,128)S(1)} %add.48.sums_refs_0_, f32[2,256]{1,0:T(2,128)S(1)} %collective-permute-done.8.sums_refs_1_, ...), custom_call_target="tpu_custom_call" | custom-call | flops 1056964608 | bytes 5445760 | tf_op jit(solution)/shard_map/conv_mid/pallas_call | solution.py:148
  59.5 2.0 collective-permute-start.15
  61.5 2.4 collective-permute-start.17
  64.7 2.4 collective-permute-start.30
  68.2 2.1 collective-permute-start.32
  70.4 2.1 pool.1
  74.8 2.6 %collective-permute-done.22.gathered_refs_1_ = f32[16,128]{1,0:T(8,128)S(1)} collective-permute-done((f32[16,128]{1,0:T(8,128)S(1)}, f32[16,128]{1,0:T(8,128)S(1)}, u32[]{:S(2)}, u32[]{:S(2)}) %collective-permute-start.22) | collective-permute-done | bytes 8224 | tf_op jit(solution)/shard_map/ppermute | solution.py:1035
  77.9 4.1 %collective-permute-done.23.gathered_refs_2_ = f32[16,128]{1,0:T(8,128)S(1)} collective-permute-done((f32[16,128]{1,0:T(8,128)S(1)}, f32[16,128]{1,0:T(8,128)S(1)}, u32[]{:S(2)}, u32[]{:S(2)}) %collective-permute-start.23) | collective-permute-done | bytes 8224 | tf_op jit(solution)/shard_map/ppermute | solution.py:1035
  81.9 1.5 collective-permute-start.24
  83.4 3.9 %collective-permute-done.24.gathered_refs_3_ = f32[16,128]{1,0:T(8,128)S(1)} collective-permute-done((f32[16,128]{1,0:T(8,128)S(1)}, f32[16,128]{1,0:T(8,128)S(1)}, u32[]{:S(2)}, u32[]{:S(2)}) %collective-permute-start.24) | collective-permute-done | bytes 8224 | tf_op jit(solution)/shard_map/ppermute | solution.py:1035
  87.4 2.6 %attend.1 = (f32[2,4,128]{2,1,0:T(4,128)S(1)}, f32[4,512]{1,0:T(4,128)S(1)}, bf16[784,256]{1,0:T(8,128)(2,1)S(1)}, f32[4,784,256]{2,1,0:T(8,128)S(1)}, f32[8,256]{1,0:T(8,128)S(1)}) custom-call(s32[4,8]{1,0:T(4,128)S(1)} %copy-done, f32[16,128]{1,0:T(8,128)S(1)} %constant_dynamic-update-slice_fusion.gathered_refs_0_, ...), custom_call_target="tpu_custom_call" | custom-call | flops 411041792 | bytes 6196352 | tf_op jit(solution)/shard_map/attend/pallas_call | solution.py:148
  91.2 3.6 %collective-permute-done.26.sums_refs_1_ = f32[8,256]{1,0:T(8,128)S(1)} collective-permute-done((f32[8,256]{1,0:T(8,128)S(1)}, f32[8,256]{1,0:T(8,128)S(1)}, u32[]{:S(2)}, u32[]{:S(2)}) %collective-permute-start.26) | collective-permute-done | bytes 8224 | tf_op jit(solution)/shard_map/ppermute | solution.py:1035
  94.9 4.5 %collective-permute-done.27.sums_refs_2_ = f32[8,256]{1,0:T(8,128)S(1)} collective-permute-done((f32[8,256]{1,0:T(8,128)S(1)}, f32[8,256]{1,0:T(8,128)S(1)}, u32[]{:S(2)}, u32[]{:S(2)}) %collective-permute-start.27) | collective-permute-done | bytes 8224 | tf_op jit(solution)/shard_map/ppermute | solution.py:1035
  99.4 1.5 collective-permute-start.28
  100.9 4.0 %collective-permute-done.28.sums_refs_3_ = f32[8,256]{1,0:T(8,128)S(1)} collective-permute-done((f32[8,256]{1,0:T(8,128)S(1)}, f32[8,256]{1,0:T(8,128)S(1)}, u32[]{:S(2)}, u32[]{:S(2)}) %collective-permute-start.28) | collective-permute-done | bytes 8224 | tf_op jit(solution)/shard_map/ppermute | solution.py:1035
  104.9 4.2 %finish.1 = (bf16[784,256]{1,0:T(8,128)(2,1)S(1)}, bf16[784,256]{1,0:T(8,128)(2,1)S(1)}, bf16[784,256]{1,0:T(8,128)(2,1)S(1)}, bf16[784,256]{1,0:T(8,128)(2,1)S(...) custom-call(s32[4,8]{1,0:T(4,128)S(1)} %copy-done, f32[4,784,256]{2,1,0:T(8,128)S(1)} %get-tuple-element.128.out_ref, ...), custom_call_target="tpu_custom_call" | custom-call | bytes 11288704 | tf_op jit(solution)/shard_map/finish/pallas_call | solution.py:148
  110.3 2.0 collective-permute-start.39
  112.3 2.3 collective-permute-start.40
  114.8 2.9 %collective-permute-done.40.back_refs_3_.out_back_refs_3_ = f32[8,256]{1,0:T(8,128)S(1)} collective-permute-done((f32[8,256]{1,0:T(8,128)S(1)}, f32[8,256]{1,0:T(8,128)S(1)}, u32[]{:S(2)}, u32[]{:S(2)}) %collective-permute-start.40) | collective-permute-done | bytes 8224 | tf_op jit(solution)/shard_map/ppermute | solution.py:1035
  117.8 4.6 %back_out.1 = (bf16[4,784,256]{2,1,0:T(8,128)(2,1)S(1)}, f32[896,256]{1,0:T(8,128)S(1)}, f32[4,512]{1,0:T(4,128)S(1)}, f32[12,128]{1,0:T(8,128)S(1)}) custom-call(s32[4,8]{1,0:T(4,128)S(1)} %copy-done, f32[4,784,256]{2,1,0:T(8,128)S(1)} %get-tuple-element.140.grad_ref.summed_ref, f32[4,784,256]{2,1,0:T(8,128)S(1)} %get-tuple-element.128.out_ref, ...), custom_call_target="tpu_custom_call" | custom-call | flops 411041792 | bytes 11556992 | tf_op jit(solution)/shard_map/back_out/pallas_call | solution.py:148
  123.8 1.9 collective-permute-start.46
  126.7 1.5 collective-permute-start.48
  128.1 1.9 collective-permute-start.43
  130.1 1.5 collective-permute-start.44
  131.5 1.6 weight_out_term.1
  133.1 2.4 collective-permute-done.44.back_refs_3_
  135.5 5.6 %back_mid.1 = (bf16[976,512]{1,0:T(8,128)(2,1)S(1)}, f32[896,256]{1,0:T(8,128)S(1)}, f32[4,128]{1,0:T(4,128)S(1)}, f32[8,512]{1,0:T(8,128)S(1)}, f32[2,256]{1,0:T(2,128)S(1)}) custom-call(s32[4,8]{1,0:T(4,128)S(1)} %copy-done, f32[16,128]{1,0:T(8,128)S(1)} %pad_maximum_fusion.1.back_refs_0_, f32[16,128]{1,0:T(8,128)S(1)} %collective-permute-done.42.back_refs_1_, ...), custom_call_target="tpu_custom_call" | custom-call | flops 1056964608 | bytes 7105664 | tf_op jit(solution)/shard_map/back_mid/pallas_call | solution.py:148
  142.3 2.3 weight_mid_term.1
  145.3 2.1 collective-permute-start.51
  147.3 2.3 collective-permute-start.52
  149.7 3.0 %collective-permute-done.52.back_refs_3_ = f32[2,256]{1,0:T(2,128)S(1)} collective-permute-done((f32[2,256]{1,0:T(2,128)S(1)}, f32[2,256]{1,0:T(2,128)S(1)}, u32[]{:S(2)}, u32[]{:S(2)}) %collective-permute-start.52) | collective-permute-done | bytes 2080 | tf_op jit(solution)/shard_map/ppermute | solution.py:1035
  152.7 1.6 back_in.1
  155.1 1.7 collective-permute-start.61
  157.4 13.5 %collective-permute-done.54.arrived_refs_2_ = bf16[528,128]{1,0:T(8,128)(2,1)S(1)} collective-permute-done((bf16[528,128]{1,0:T(8,128)(2,1)S(1)}, bf16[528,128]{1,0:T(8,128)(2,1)S(1)}, u32[]{:S(2)}, u32[]{:S(2)}) %collective-permute-start.54) | collective-permute-done | bytes 135200 | tf_op jit(solution)/shard_map/ppermute | solution.py:1035
  172.3 8.4 %collective-permute-done.63.arrived_ref = bf16[1216,128]{1,0:T(8,128)(2,1)S(1)} collective-permute-done((bf16[1216,128]{1,0:T(8,128)(2,1)S(1)}, bf16[1216,128]{1,0:T(8,128)(2,1)S(1)}, u32[]{:S(2)}, u32[]{:S(2)}) %collective-permute-start.63) | collective-permute-done | bytes 311328 | tf_op jit(solution)/shard_map/ppermute | solution.py:1035
  181.5 2.9 %collective-permute-start.65 = (bf16[304,128]{1,0:T(8,128)(2,1)S(1)}, bf16[304,128]{1,0:T(8,128)(2,1)S(1)}, u32[]{:S(2)}, u32[]{:S(2)}) collective-permute-start(bf16[304,128]{1,0:T(8,128)(2,1)S(1)} %get-tuple-element.191), channel_id=1, source_target_pairs={{0,16},{1,17},{2,18},{3,19},{4,20},{5,21},{6,22},{7,23},{8,24},{9,... | collective-permute-start | bytes 233480 | tf_op jit(solution)/shard_map/ppermute | solution.py:1035
  185.1 1.9 collective-permute-start.34
  188.3 1.5 collective-permute-start.66
  189.8 4.7 %collective-permute-done.66.arrived_refs_2_ = bf16[304,128]{1,0:T(8,128)(2,1)S(1)} collective-permute-done((bf16[304,128]{1,0:T(8,128)(2,1)S(1)}, bf16[304,128]{1,0:T(8,128)(2,1)S(1)}, u32[]{:S(2)}, u32[]{:S(2)}) %collective-permute-start.66) | collective-permute-done | bytes 77856 | tf_op jit(solution)/shard_map/ppermute | solution.py:1035
  194.6 4.4 %collective-permute-done.67.piece_refs_1_ = bf16[304,128]{1,0:T(8,128)(2,1)S(1)} collective-permute-done((bf16[304,128]{1,0:T(8,128)(2,1)S(1)}, bf16[304,128]{1,0:T(8,128)(2,1)S(1)}, u32[]{:S(2)}, u32[]{:S(2)}) %collective-permute-start.67) | collective-permute-done | bytes 77856 | tf_op jit(solution)/shard_map/ppermute | solution.py:1035
  200.3 5.1 %collective-permute-done.68.piece_refs_2_ = bf16[304,128]{1,0:T(8,128)(2,1)S(1)} collective-permute-done((bf16[304,128]{1,0:T(8,128)(2,1)S(1)}, bf16[304,128]{1,0:T(8,128)(2,1)S(1)}, u32[]{:S(2)}, u32[]{:S(2)}) %collective-permute-start.68) | collective-permute-done | bytes 77856 | tf_op jit(solution)/shard_map/ppermute | solution.py:1035
  205.4 1.9 collective-permute-start.69
  207.3 4.3 %collective-permute-done.69.piece_refs_3_ = bf16[304,128]{1,0:T(8,128)(2,1)S(1)} collective-permute-done((bf16[304,128]{1,0:T(8,128)(2,1)S(1)}, bf16[304,128]{1,0:T(8,128)(2,1)S(1)}, u32[]{:S(2)}, u32[]{:S(2)}) %collective-permute-start.69) | collective-permute-done | bytes 77856 | tf_op jit(solution)/shard_map/ppermute | solution.py:1035
  212.2 2.3 collective-permute-start.70
  215.9 1.4 collective-permute-start.55
  218.6 1.9 collective-permute-start.58
  220.5 1.7 unpack.1
  225.8 2.3 collective-permute-done.56
  228.1 8.8 %collective-permute-done.58 = bf16[784,256]{1,0:T(8,128)(2,1)} collective-permute-done((bf16[784,256]{1,0:T(8,128)(2,1)S(1)}, bf16[784,256]{1,0:T(8,128)(2,1)}, u32[]{:S(2)}, u32[]{:S(2)}) %collective-permute-start.58) | collective-permute-done | bytes 401440 | tf_op jit(solution)/shard_map/ppermute | solution.py:1035
  (175 shorter events, 43.8 us)
Async XLA Ops:
  3.0 27.8 %collective-permute-start = (bf16[784,256]{1,0:T(8,128)(2,1)}, bf16[784,256]{1,0:T(8,128)(2,1)S(1)}, u32[]{:S(2)}, u32[]{:S(2)}) collective-permute-start(bf16[784,256]{1,0:T(8,128)(2,1)} %get-tuple-element.212), channel_id=1, source_target_pairs={{0,0},{1,4},{2,2},{3,6},{4,1},{5,5},{6,3},{7,7},{8,8},{9,12},{10,1... | collective-permute-start | bytes 1204232 | tf_op jit(solution)/shard_map/ppermute | solution.py:1035
  4.7 26.2 %collective-permute-start.1 = (bf16[784,256]{1,0:T(8,128)(2,1)S(1)}, bf16[784,256]{1,0:T(8,128)(2,1)S(1)}, u32[]{:S(2)}, u32[]{:S(2)}) collective-permute-start(bf16[784,256]{1,0:T(8,128)(2,1)S(1)} %get-tuple-element.211), channel_id=1, source_target_pairs={{0,4},{1,0},{2,6},{3,2},{4,5},{5,1},{6,7},{7,3},{8,12},{9,8},{10,1... | collective-permute-start | bytes 1204232 | tf_op jit(solution)/shard_map/ppermute | solution.py:1035
  7.9 22.9 %collective-permute-start.2 = (bf16[784,256]{1,0:T(8,128)(2,1)S(1)}, bf16[784,256]{1,0:T(8,128)(2,1)S(1)}, u32[]{:S(2)}, u32[]{:S(2)}) collective-permute-start(bf16[784,256]{1,0:T(8,128)(2,1)S(1)} %get-tuple-element.213), channel_id=1, source_target_pairs={{0,2},{1,6},{2,0},{3,4},{4,3},{5,7},{6,1},{7,5},{8,10},{9,14},{10,... | collective-permute-start | bytes 1204232 | tf_op jit(solution)/shard_map/ppermute | solution.py:1035
  9.4 21.4 %collective-permute-start.3 = (bf16[784,256]{1,0:T(8,128)(2,1)S(1)}, bf16[784,256]{1,0:T(8,128)(2,1)S(1)}, u32[]{:S(2)}, u32[]{:S(2)}) collective-permute-start(bf16[784,256]{1,0:T(8,128)(2,1)S(1)} %get-tuple-element.210), channel_id=1, source_target_pairs={{0,6},{1,2},{2,4},{3,0},{4,7},{5,3},{6,5},{7,1},{8,14},{9,10},{10,... | collective-permute-start | bytes 1204232 | tf_op jit(solution)/shard_map/ppermute | solution.py:1035
  17.1 1.4 collective-permute-start.4
  18.5 12.3 %collective-permute-start.5 = (bf16[528,128]{1,0:T(8,128)(2,1)S(1)}, bf16[528,128]{1,0:T(8,128)(2,1)S(1)}, u32[]{:S(2)}, u32[]{:S(2)}) collective-permute-start(bf16[528,128]{1,0:T(8,128)(2,1)S(1)} %concatenate.19.a0), channel_id=1, source_target_pairs={{0,2},{1,3},{2,0},{3,1},{4,6},{5,7},{6,4},{7,5},{8,10},{9,11},{10,... | collective-permute-start | bytes 405512 | tf_op jit(solution)/shard_map/ppermute | solution.py:1035
  30.9 2.4 collective-permute-start.11
  31.5 9.3 %collective-permute-start.12 = (bf16[1152,128]{1,0:T(8,128)(2,1)S(1)}, bf16[1152,128]{1,0:T(8,128)(2,1)S(1)}, u32[]{:S(2)}, u32[]{:S(2)}) collective-permute-start(bf16[1152,128]{1,0:T(8,128)(2,1)S(1)} %bitcast.65), channel_id=1, source_target_pairs={{0,2},{1,3},{2,0},{3,1},{4,6},{5,7},{6,4},{7,5},{8,10},{9,11},{10,... | collective-permute-start | bytes 884744 | tf_op jit(solution)/shard_map/ppermute | solution.py:1035
  40.8 10.7 %collective-permute-start.13 = (bf16[1152,128]{1,0:T(8,128)(2,1)S(1)}, bf16[1152,128]{1,0:T(8,128)(2,1)S(1)}, u32[]{:S(2)}, u32[]{:S(2)}) collective-permute-start(bf16[1152,128]{1,0:T(8,128)(2,1)S(1)} %collective-permute-done.12.b2), channel_id=1, source_target_pairs={{0,1},{1,0},{2,3},{3,2},{4,5},{5,4},{6,7},{7,6},{8,9},{9,8},{10,11... | collective-permute-start | bytes 884744 | tf_op jit(solution)/shard_map/ppermute | solution.py:1035
  40.8 9.9 %collective-permute-start.18 = (bf16[704,128]{1,0:T(8,128)(2,1)S(1)}, bf16[704,128]{1,0:T(8,128)(2,1)S(1)}, u32[]{:S(2)}, u32[]{:S(2)}) collective-permute-start(bf16[704,128]{1,0:T(8,128)(2,1)S(1)} %pad_maximum_fusion.b0), channel_id=1, source_target_pairs={{0,1},{1,0},{2,3},{3,2},{4,5},{5,4},{6,7},{7,6},{8,9},{9,8},{10,11... | collective-permute-start | bytes 540680 | tf_op jit(solution)/shard_map/ppermute | solution.py:1035
  41.4 10.1 %collective-permute-start.19 = (bf16[704,128]{1,0:T(8,128)(2,1)S(1)}, bf16[704,128]{1,0:T(8,128)(2,1)S(1)}, u32[]{:S(2)}, u32[]{:S(2)}) collective-permute-start(bf16[704,128]{1,0:T(8,128)(2,1)S(1)} %pad_maximum_fusion.b0), channel_id=1, source_target_pairs={{0,2},{1,3},{2,0},{3,1},{4,6},{5,7},{6,4},{7,5},{8,10},{9,11},{10,... | collective-permute-start | bytes 540680 | tf_op jit(solution)/shard_map/ppermute | solution.py:1035
  43.2 1.4 collective-permute-start.6
  47.1 5.4 %collective-permute-start.10 = (f32[2,256]{1,0:T(2,128)S(1)}, f32[2,256]{1,0:T(2,128)S(1)}, u32[]{:S(2)}, u32[]{:S(2)}) collective-permute-start(f32[2,256]{1,0:T(2,128)S(1)} %add.48.sums_refs_0_), channel_id=1, source_target_pairs={{0,24},{1,25},{2,26},{3,27},{4,28},{5,29},{6,30},{7,31},{8,16},{9,... | collective-permute-start | bytes 6152 | tf_op jit(solution)/shard_map/ppermute | solution.py:1035
  50.7 3.6 %collective-permute-start.8 = (f32[2,256]{1,0:T(2,128)S(1)}, f32[2,256]{1,0:T(2,128)S(1)}, u32[]{:S(2)}, u32[]{:S(2)}) collective-permute-start(f32[2,256]{1,0:T(2,128)S(1)} %add.48.sums_refs_0_), channel_id=1, source_target_pairs={{0,8},{1,9},{2,10},{3,11},{4,12},{5,13},{6,14},{7,15},{8,0},{9,1},... | collective-permute-start | bytes 6152 | tf_op jit(solution)/shard_map/ppermute | solution.py:1035
  50.7 4.5 %collective-permute-start.9 = (f32[2,256]{1,0:T(2,128)S(1)}, f32[2,256]{1,0:T(2,128)S(1)}, u32[]{:S(2)}, u32[]{:S(2)}) collective-permute-start(f32[2,256]{1,0:T(2,128)S(1)} %add.48.sums_refs_0_), channel_id=1, source_target_pairs={{0,16},{1,17},{2,18},{3,19},{4,20},{5,21},{6,22},{7,23},{8,24},{9,... | collective-permute-start | bytes 6152 | tf_op jit(solution)/shard_map/ppermute | solution.py:1035
  51.5 13.2 %collective-permute-start.20 = (bf16[704,128]{1,0:T(8,128)(2,1)S(1)}, bf16[704,128]{1,0:T(8,128)(2,1)S(1)}, u32[]{:S(2)}, u32[]{:S(2)}) collective-permute-start(bf16[704,128]{1,0:T(8,128)(2,1)S(1)} %collective-permute-done.19.b2), channel_id=1, source_target_pairs={{0,1},{1,0},{2,3},{3,2},{4,5},{5,4},{6,7},{7,6},{8,9},{9,8},{10,11... | collective-permute-start | bytes 540680 | tf_op jit(solution)/shard_map/ppermute | solution.py:1035
  59.5 8.4 %collective-permute-start.15 = (f32[2,512]{1,0:T(2,128)S(1)}, f32[2,512]{1,0:T(2,128)S(1)}, u32[]{:S(2)}, u32[]{:S(2)}) collective-permute-start(f32[2,512]{1,0:T(2,128)S(1)} %add.49.sums_refs_0_.mid_sums_refs_0_), channel_id=1, source_target_pairs={{0,8},{1,9},{2,10},{3,11},{4,12},{5,13},{6,14},{7,15},{8,0},{9,1},... | collective-permute-start | bytes 12296 | tf_op jit(solution)/shard_map/ppermute | solution.py:1035
  61.5 6.7 %collective-permute-start.16 = (f32[2,512]{1,0:T(2,128)S(1)}, f32[2,512]{1,0:T(2,128)S(1)}, u32[]{:S(2)}, u32[]{:S(2)}) collective-permute-start(f32[2,512]{1,0:T(2,128)S(1)} %add.49.sums_refs_0_.mid_sums_refs_0_), channel_id=1, source_target_pairs={{0,16},{1,17},{2,18},{3,19},{4,20},{5,21},{6,22},{7,23},{8,24},{9,... | collective-permute-start | bytes 12296 | tf_op jit(solution)/shard_map/ppermute | solution.py:1035
  61.5 8.9 %collective-permute-start.17 = (f32[2,512]{1,0:T(2,128)S(1)}, f32[2,512]{1,0:T(2,128)S(1)}, u32[]{:S(2)}, u32[]{:S(2)}) collective-permute-start(f32[2,512]{1,0:T(2,128)S(1)} %add.49.sums_refs_0_.mid_sums_refs_0_), channel_id=1, source_target_pairs={{0,24},{1,25},{2,26},{3,27},{4,28},{5,29},{6,30},{7,31},{8,16},{9,... | collective-permute-start | bytes 12296 | tf_op jit(solution)/shard_map/ppermute | solution.py:1035
  64.0 40.8 %collective-permute-start.29 = (bf16[784,256]{1,0:T(8,128)(2,1)S(1)}, bf16[784,256]{1,0:T(8,128)(2,1)S(1)}, u32[]{:S(2)}, u32[]{:S(2)}) collective-permute-start(bf16[784,256]{1,0:T(8,128)(2,1)S(1)} %get-tuple-element.209), channel_id=1, source_target_pairs={{0,0},{1,4},{2,2},{3,6},{4,1},{5,5},{6,3},{7,7},{8,8},{9,12},{10,1... | collective-permute-start | bytes 1204232 | tf_op jit(solution)/shard_map/ppermute | solution.py:1035
  64.7 40.1 %collective-permute-start.30 = (bf16[784,256]{1,0:T(8,128)(2,1)S(1)}, bf16[784,256]{1,0:T(8,128)(2,1)S(1)}, u32[]{:S(2)}, u32[]{:S(2)}) collective-permute-start(bf16[784,256]{1,0:T(8,128)(2,1)S(1)} %get-tuple-element.208), channel_id=1, source_target_pairs={{0,4},{1,0},{2,6},{3,2},{4,5},{5,1},{6,7},{7,3},{8,12},{9,8},{10,1... | collective-permute-start | bytes 1204232 | tf_op jit(solution)/shard_map/ppermute | solution.py:1035
  67.9 37.0 %collective-permute-start.31 = (bf16[784,256]{1,0:T(8,128)(2,1)S(1)}, bf16[784,256]{1,0:T(8,128)(2,1)S(1)}, u32[]{:S(2)}, u32[]{:S(2)}) collective-permute-start(bf16[784,256]{1,0:T(8,128)(2,1)S(1)} %get-tuple-element.207), channel_id=1, source_target_pairs={{0,2},{1,6},{2,0},{3,4},{4,3},{5,7},{6,1},{7,5},{8,10},{9,14},{10,... | collective-permute-start | bytes 1204232 | tf_op jit(solution)/shard_map/ppermute | solution.py:1035
  68.2 36.6 %collective-permute-start.32 = (bf16[784,256]{1,0:T(8,128)(2,1)S(1)}, bf16[784,256]{1,0:T(8,128)(2,1)S(1)}, u32[]{:S(2)}, u32[]{:S(2)}) collective-permute-start(bf16[784,256]{1,0:T(8,128)(2,1)S(1)} %get-tuple-element.206), channel_id=1, source_target_pairs={{0,6},{1,2},{2,4},{3,0},{4,7},{5,3},{6,5},{7,1},{8,14},{9,10},{10,... | collective-permute-start | bytes 1204232 | tf_op jit(solution)/shard_map/ppermute | solution.py:1035
  73.7 3.7 %collective-permute-start.22 = (f32[16,128]{1,0:T(8,128)S(1)}, f32[16,128]{1,0:T(8,128)S(1)}, u32[]{:S(2)}, u32[]{:S(2)}) collective-permute-start(f32[16,128]{1,0:T(8,128)S(1)} %constant_dynamic-update-slice_fusion.gathered_refs_0_), channel_id=1, source_target_pairs={{0,8},{1,9},{2,10},{3,11},{4,12},{5,13},{6,14},{7,15},{8,0},{9,1},... | collective-permute-start | bytes 24584 | tf_op jit(solution)/shard_map/ppermute | solution.py:1035
  77.4 4.5 %collective-permute-start.23 = (f32[16,128]{1,0:T(8,128)S(1)}, f32[16,128]{1,0:T(8,128)S(1)}, u32[]{:S(2)}, u32[]{:S(2)}) collective-permute-start(f32[16,128]{1,0:T(8,128)S(1)} %constant_dynamic-update-slice_fusion.gathered_refs_0_), channel_id=1, source_target_pairs={{0,16},{1,17},{2,18},{3,19},{4,20},{5,21},{6,22},{7,23},{8,24},{9,... | collective-permute-start | bytes 24584 | tf_op jit(solution)/shard_map/ppermute | solution.py:1035
  81.9 5.4 %collective-permute-start.24 = (f32[16,128]{1,0:T(8,128)S(1)}, f32[16,128]{1,0:T(8,128)S(1)}, u32[]{:S(2)}, u32[]{:S(2)}) collective-permute-start(f32[16,128]{1,0:T(8,128)S(1)} %constant_dynamic-update-slice_fusion.gathered_refs_0_), channel_id=1, source_target_pairs={{0,24},{1,25},{2,26},{3,27},{4,28},{5,29},{6,30},{7,31},{8,16},{9,... | collective-permute-start | bytes 24584 | tf_op jit(solution)/shard_map/ppermute | solution.py:1035
  91.2 3.7 %collective-permute-start.26 = (f32[8,256]{1,0:T(8,128)S(1)}, f32[8,256]{1,0:T(8,128)S(1)}, u32[]{:S(2)}, u32[]{:S(2)}) collective-permute-start(f32[8,256]{1,0:T(8,128)S(1)} %add.50.sums_refs_0_), channel_id=1, source_target_pairs={{0,8},{1,9},{2,10},{3,11},{4,12},{5,13},{6,14},{7,15},{8,0},{9,1},... | collective-permute-start | bytes 24584 | tf_op jit(solution)/shard_map/ppermute | solution.py:1035
  94.8 4.5 %collective-permute-start.27 = (f32[8,256]{1,0:T(8,128)S(1)}, f32[8,256]{1,0:T(8,128)S(1)}, u32[]{:S(2)}, u32[]{:S(2)}) collective-permute-start(f32[8,256]{1,0:T(8,128)S(1)} %add.50.sums_refs_0_), channel_id=1, source_target_pairs={{0,16},{1,17},{2,18},{3,19},{4,20},{5,21},{6,22},{7,23},{8,24},{9,... | collective-permute-start | bytes 24584 | tf_op jit(solution)/shard_map/ppermute | solution.py:1035
  99.4 5.4 %collective-permute-start.28 = (f32[8,256]{1,0:T(8,128)S(1)}, f32[8,256]{1,0:T(8,128)S(1)}, u32[]{:S(2)}, u32[]{:S(2)}) collective-permute-start(f32[8,256]{1,0:T(8,128)S(1)} %add.50.sums_refs_0_), channel_id=1, source_target_pairs={{0,24},{1,25},{2,26},{3,27},{4,28},{5,29},{6,30},{7,31},{8,16},{9,... | collective-permute-start | bytes 24584 | tf_op jit(solution)/shard_map/ppermute | solution.py:1035
  110.3 4.4 %collective-permute-start.38 = (f32[8,256]{1,0:T(8,128)S(1)}, f32[8,256]{1,0:T(8,128)S(1)}, u32[]{:S(2)}, u32[]{:S(2)}) collective-permute-start(f32[8,256]{1,0:T(8,128)S(1)} %add.51.back_refs_0_.out_back_refs_0_), channel_id=1, source_target_pairs={{0,8},{1,9},{2,10},{3,11},{4,12},{5,13},{6,14},{7,15},{8,0},{9,1},... | collective-permute-start | bytes 24584 | tf_op jit(solution)/shard_map/ppermute | solution.py:1035
  110.3 4.6 %collective-permute-start.39 = (f32[8,256]{1,0:T(8,128)S(1)}, f32[8,256]{1,0:T(8,128)S(1)}, u32[]{:S(2)}, u32[]{:S(2)}) collective-permute-start(f32[8,256]{1,0:T(8,128)S(1)} %add.51.back_refs_0_.out_back_refs_0_), channel_id=1, source_target_pairs={{0,16},{1,17},{2,18},{3,19},{4,20},{5,21},{6,22},{7,23},{8,24},{9,... | collective-permute-start | bytes 24584 | tf_op jit(solution)/shard_map/ppermute | solution.py:1035
  112.3 5.4 %collective-permute-start.40 = (f32[8,256]{1,0:T(8,128)S(1)}, f32[8,256]{1,0:T(8,128)S(1)}, u32[]{:S(2)}, u32[]{:S(2)}) collective-permute-start(f32[8,256]{1,0:T(8,128)S(1)} %add.51.back_refs_0_.out_back_refs_0_), channel_id=1, source_target_pairs={{0,24},{1,25},{2,26},{3,27},{4,28},{5,29},{6,30},{7,31},{8,16},{9,... | collective-permute-start | bytes 24584 | tf_op jit(solution)/shard_map/ppermute | solution.py:1035
  122.4 1.3 collective-permute-start.45
  123.6 6.5 %collective-permute-start.42 = (f32[16,128]{1,0:T(8,128)S(1)}, f32[16,128]{1,0:T(8,128)S(1)}, u32[]{:S(2)}, u32[]{:S(2)}) collective-permute-start(f32[16,128]{1,0:T(8,128)S(1)} %pad_maximum_fusion.1.back_refs_0_), channel_id=1, source_target_pairs={{0,8},{1,9},{2,10},{3,11},{4,12},{5,13},{6,14},{7,15},{8,0},{9,1},... | collective-permute-start | bytes 24584 | tf_op jit(solution)/shard_map/ppermute | solution.py:1035
  123.8 11.7 %collective-permute-start.46 = (f32[16,512]{1,0:T(8,128)S(1)}, f32[16,512]{1,0:T(8,128)S(1)}, u32[]{:S(2)}, u32[]{:S(2)}) collective-permute-start(f32[16,512]{1,0:T(8,128)S(1)} %constant_dynamic-update-slice_fusion.2.incline_refs_0_), channel_id=1, source_target_pairs={{0,8},{1,9},{2,10},{3,11},{4,12},{5,13},{6,14},{7,15},{8,0},{9,1},... | collective-permute-start | bytes 98312 | tf_op jit(solution)/shard_map/ppermute | solution.py:1035
  125.7 9.8 %collective-permute-start.47 = (f32[16,512]{1,0:T(8,128)S(1)}, f32[16,512]{1,0:T(8,128)S(1)}, u32[]{:S(2)}, u32[]{:S(2)}) collective-permute-start(f32[16,512]{1,0:T(8,128)S(1)} %constant_dynamic-update-slice_fusion.2.incline_refs_0_), channel_id=1, source_target_pairs={{0,16},{1,17},{2,18},{3,19},{4,20},{5,21},{6,22},{7,23},{8,24},{9,... | collective-permute-start | bytes 98312 | tf_op jit(solution)/shard_map/ppermute | solution.py:1035
  126.7 8.9 %collective-permute-start.48 = (f32[16,512]{1,0:T(8,128)S(1)}, f32[16,512]{1,0:T(8,128)S(1)}, u32[]{:S(2)}, u32[]{:S(2)}) collective-permute-start(f32[16,512]{1,0:T(8,128)S(1)} %constant_dynamic-update-slice_fusion.2.incline_refs_0_), channel_id=1, source_target_pairs={{0,24},{1,25},{2,26},{3,27},{4,28},{5,29},{6,30},{7,31},{8,16},{9,... | collective-permute-start | bytes 98312 | tf_op jit(solution)/shard_map/ppermute | solution.py:1035
  128.1 5.0 %collective-permute-start.43 = (f32[16,128]{1,0:T(8,128)S(1)}, f32[16,128]{1,0:T(8,128)S(1)}, u32[]{:S(2)}, u32[]{:S(2)}) collective-permute-start(f32[16,128]{1,0:T(8,128)S(1)} %pad_maximum_fusion.1.back_refs_0_), channel_id=1, source_target_pairs={{0,16},{1,17},{2,18},{3,19},{4,20},{5,21},{6,22},{7,23},{8,24},{9,... | collective-permute-start | bytes 24584 | tf_op jit(solution)/shard_map/ppermute | solution.py:1035
  130.1 5.4 %collective-permute-start.44 = (f32[16,128]{1,0:T(8,128)S(1)}, f32[16,128]{1,0:T(8,128)S(1)}, u32[]{:S(2)}, u32[]{:S(2)}) collective-permute-start(f32[16,128]{1,0:T(8,128)S(1)} %pad_maximum_fusion.1.back_refs_0_), channel_id=1, source_target_pairs={{0,24},{1,25},{2,26},{3,27},{4,28},{5,29},{6,30},{7,31},{8,16},{9,... | collective-permute-start | bytes 24584 | tf_op jit(solution)/shard_map/ppermute | solution.py:1035
  144.7 9.7 %collective-permute-start.60 = (bf16[2,1216,128]{2,1,0:T(8,128)(2,1)S(1)}, bf16[2,1216,128]{2,1,0:T(8,128)(2,1)S(1)}, u32[]{:S(2)}, u32[]{:S(2)}) collective-permute-start(bf16[2,1216,128]{2,1,0:T(8,128)(2,1)S(1)} %get-tuple-element.182), channel_id=1, source_target_pairs={{0,1},{1,0},{2,3},{3,2},{4,5},{5,4},{6,7},{7,6},{8,9},{9,8},{10,11... | collective-permute-start | bytes 1867784 | tf_op jit(solution)/shard_map/ppermute | solution.py:1035
  144.9 10.1 %collective-permute-start.59 = (bf16[2,656,128]{2,1,0:T(8,128)(2,1)S(1)}, bf16[2,656,128]{2,1,0:T(8,128)(2,1)S(1)}, u32[]{:S(2)}, u32[]{:S(2)}) collective-permute-start(bf16[2,656,128]{2,1,0:T(8,128)(2,1)S(1)} %get-tuple-element.180), channel_id=1, source_target_pairs={{0,1},{1,0},{2,3},{3,2},{4,5},{5,4},{6,7},{7,6},{8,9},{9,8},{10,11... | collective-permute-start | bytes 1007624 | tf_op jit(solution)/shard_map/ppermute | solution.py:1035
  145.2 4.4 %collective-permute-start.50 = (f32[2,256]{1,0:T(2,128)S(1)}, f32[2,256]{1,0:T(2,128)S(1)}, u32[]{:S(2)}, u32[]{:S(2)}) collective-permute-start(f32[2,256]{1,0:T(2,128)S(1)} %add.53.back_refs_0_), channel_id=1, source_target_pairs={{0,8},{1,9},{2,10},{3,11},{4,12},{5,13},{6,14},{7,15},{8,0},{9,1},... | collective-permute-start | bytes 6152 | tf_op jit(solution)/shard_map/ppermute | solution.py:1035
  145.3 4.5 %collective-permute-start.51 = (f32[2,256]{1,0:T(2,128)S(1)}, f32[2,256]{1,0:T(2,128)S(1)}, u32[]{:S(2)}, u32[]{:S(2)}) collective-permute-start(f32[2,256]{1,0:T(2,128)S(1)} %add.53.back_refs_0_), channel_id=1, source_target_pairs={{0,16},{1,17},{2,18},{3,19},{4,20},{5,21},{6,22},{7,23},{8,24},{9,... | collective-permute-start | bytes 6152 | tf_op jit(solution)/shard_map/ppermute | solution.py:1035
  147.3 5.4 %collective-permute-start.52 = (f32[2,256]{1,0:T(2,128)S(1)}, f32[2,256]{1,0:T(2,128)S(1)}, u32[]{:S(2)}, u32[]{:S(2)}) collective-permute-start(f32[2,256]{1,0:T(2,128)S(1)} %add.53.back_refs_0_), channel_id=1, source_target_pairs={{0,24},{1,25},{2,26},{3,27},{4,28},{5,29},{6,30},{7,31},{8,16},{9,... | collective-permute-start | bytes 6152 | tf_op jit(solution)/shard_map/ppermute | solution.py:1035
  154.3 2.5 %collective-permute-start.53 = (bf16[2,528,128]{2,1,0:T(8,128)(2,1)S(1)}, bf16[2,528,128]{2,1,0:T(8,128)(2,1)S(1)}, u32[]{:S(2)}, u32[]{:S(2)}) collective-permute-start(bf16[2,528,128]{2,1,0:T(8,128)(2,1)S(1)} %get-tuple-element.172), channel_id=1, source_target_pairs={{0,1},{1,0},{2,3},{3,2},{4,5},{5,4},{6,7},{7,6},{8,9},{9,8},{10,11... | collective-permute-start | bytes 811016 | tf_op jit(solution)/shard_map/ppermute | solution.py:1035
  154.6 16.3 %collective-permute-start.62 = (bf16[1216,128]{1,0:T(8,128)(2,1)S(1)}, bf16[1216,128]{1,0:T(8,128)(2,1)S(1)}, u32[]{:S(2)}, u32[]{:S(2)}) collective-permute-start(bf16[1216,128]{1,0:T(8,128)(2,1)S(1)} %get-tuple-element.186), channel_id=1, source_target_pairs={{0,2},{1,3},{2,0},{3,1},{4,6},{5,7},{6,4},{7,5},{8,10},{9,11},{10,... | collective-permute-start | bytes 933896 | tf_op jit(solution)/shard_map/ppermute | solution.py:1035
  155.1 15.7 %collective-permute-start.61 = (bf16[656,128]{1,0:T(8,128)(2,1)S(1)}, bf16[656,128]{1,0:T(8,128)(2,1)S(1)}, u32[]{:S(2)}, u32[]{:S(2)}) collective-permute-start(bf16[656,128]{1,0:T(8,128)(2,1)S(1)} %get-tuple-element.185), channel_id=1, source_target_pairs={{0,2},{1,3},{2,0},{3,1},{4,6},{5,7},{6,4},{7,5},{8,10},{9,11},{10,... | collective-permute-start | bytes 503816 | tf_op jit(solution)/shard_map/ppermute | solution.py:1035
  156.9 14.0 %collective-permute-start.54 = (bf16[528,128]{1,0:T(8,128)(2,1)S(1)}, bf16[528,128]{1,0:T(8,128)(2,1)S(1)}, u32[]{:S(2)}, u32[]{:S(2)}) collective-permute-start(bf16[528,128]{1,0:T(8,128)(2,1)S(1)} %get-tuple-element.173), channel_id=1, source_target_pairs={{0,2},{1,3},{2,0},{3,1},{4,6},{5,7},{6,4},{7,5},{8,10},{9,11},{10,... | collective-permute-start | bytes 405512 | tf_op jit(solution)/shard_map/ppermute | solution.py:1035
  171.7 9.0 %collective-permute-start.63 = (bf16[1216,128]{1,0:T(8,128)(2,1)S(1)}, bf16[1216,128]{1,0:T(8,128)(2,1)S(1)}, u32[]{:S(2)}, u32[]{:S(2)}) collective-permute-start(bf16[1216,128]{1,0:T(8,128)(2,1)S(1)} %get-tuple-element.188), channel_id=1, source_target_pairs={{0,4},{1,5},{2,6},{3,7},{4,0},{5,1},{6,2},{7,3},{8,12},{9,13},{10,... | collective-permute-start | bytes 933896 | tf_op jit(solution)/shard_map/ppermute | solution.py:1035
  181.4 6.1 %collective-permute-start.64 = (bf16[304,128]{1,0:T(8,128)(2,1)S(1)}, bf16[304,128]{1,0:T(8,128)(2,1)S(1)}, u32[]{:S(2)}, u32[]{:S(2)}) collective-permute-start(bf16[304,128]{1,0:T(8,128)(2,1)S(1)} %get-tuple-element.190), channel_id=1, source_target_pairs={{0,8},{1,9},{2,10},{3,11},{4,12},{5,13},{6,14},{7,15},{8,0},{9,1},... | collective-permute-start | bytes 233480 | tf_op jit(solution)/shard_map/ppermute | solution.py:1035
  181.5 6.8 %collective-permute-start.65 = (bf16[304,128]{1,0:T(8,128)(2,1)S(1)}, bf16[304,128]{1,0:T(8,128)(2,1)S(1)}, u32[]{:S(2)}, u32[]{:S(2)}) collective-permute-start(bf16[304,128]{1,0:T(8,128)(2,1)S(1)} %get-tuple-element.191), channel_id=1, source_target_pairs={{0,16},{1,17},{2,18},{3,19},{4,20},{5,21},{6,22},{7,23},{8,24},{9,... | collective-permute-start | bytes 233480 | tf_op jit(solution)/shard_map/ppermute | solution.py:1035
  184.4 30.1 %collective-permute-start.33 = (bf16[784,256]{1,0:T(8,128)(2,1)S(1)}, bf16[784,256]{1,0:T(8,128)(2,1)S(1)}, u32[]{:S(2)}, u32[]{:S(2)}) collective-permute-start(bf16[784,256]{1,0:T(8,128)(2,1)S(1)} %get-tuple-element.132), channel_id=1, source_target_pairs={{0,0},{1,4},{2,2},{3,6},{4,1},{5,5},{6,3},{7,7},{8,8},{9,12},{10,1... | collective-permute-start | bytes 1204232 | tf_op jit(solution)/shard_map/ppermute | solution.py:1035
  185.1 29.4 %collective-permute-start.34 = (bf16[784,256]{1,0:T(8,128)(2,1)S(1)}, bf16[784,256]{1,0:T(8,128)(2,1)S(1)}, u32[]{:S(2)}, u32[]{:S(2)}) collective-permute-start(bf16[784,256]{1,0:T(8,128)(2,1)S(1)} %get-tuple-element.133), channel_id=1, source_target_pairs={{0,1},{1,5},{2,3},{3,7},{4,0},{5,4},{6,2},{7,6},{8,9},{9,13},{10,1... | collective-permute-start | bytes 1204232 | tf_op jit(solution)/shard_map/ppermute | solution.py:1035
  187.0 27.5 %collective-permute-start.35 = (bf16[784,256]{1,0:T(8,128)(2,1)S(1)}, bf16[784,256]{1,0:T(8,128)(2,1)S(1)}, u32[]{:S(2)}, u32[]{:S(2)}) collective-permute-start(bf16[784,256]{1,0:T(8,128)(2,1)S(1)} %get-tuple-element.134), channel_id=1, source_target_pairs={{0,2},{1,6},{2,0},{3,4},{4,3},{5,7},{6,1},{7,5},{8,10},{9,14},{10,... | collective-permute-start | bytes 1204232 | tf_op jit(solution)/shard_map/ppermute | solution.py:1035
  187.5 27.0 %collective-permute-start.36 = (bf16[784,256]{1,0:T(8,128)(2,1)S(1)}, bf16[784,256]{1,0:T(8,128)(2,1)S(1)}, u32[]{:S(2)}, u32[]{:S(2)}) collective-permute-start(bf16[784,256]{1,0:T(8,128)(2,1)S(1)} %get-tuple-element.135), channel_id=1, source_target_pairs={{0,3},{1,7},{2,1},{3,5},{4,2},{5,6},{6,0},{7,4},{8,11},{9,15},{10,... | collective-permute-start | bytes 1204232 | tf_op jit(solution)/shard_map/ppermute | solution.py:1035
  188.3 6.2 %collective-permute-start.66 = (bf16[304,128]{1,0:T(8,128)(2,1)S(1)}, bf16[304,128]{1,0:T(8,128)(2,1)S(1)}, u32[]{:S(2)}, u32[]{:S(2)}) collective-permute-start(bf16[304,128]{1,0:T(8,128)(2,1)S(1)} %get-tuple-element.192), channel_id=1, source_target_pairs={{0,24},{1,25},{2,26},{3,27},{4,28},{5,29},{6,30},{7,31},{8,16},{9,... | collective-permute-start | bytes 233480 | tf_op jit(solution)/shard_map/ppermute | solution.py:1035
  194.5 4.5 %collective-permute-start.67 = (bf16[304,128]{1,0:T(8,128)(2,1)S(1)}, bf16[304,128]{1,0:T(8,128)(2,1)S(1)}, u32[]{:S(2)}, u32[]{:S(2)}) collective-permute-start(bf16[304,128]{1,0:T(8,128)(2,1)S(1)} %add_depth.1.piece_refs_0_), channel_id=1, source_target_pairs={{0,8},{1,9},{2,10},{3,11},{4,12},{5,13},{6,14},{7,15},{8,0},{9,1},... | collective-permute-start | bytes 233480 | tf_op jit(solution)/shard_map/ppermute | solution.py:1035
  199.0 6.4 %collective-permute-start.68 = (bf16[304,128]{1,0:T(8,128)(2,1)S(1)}, bf16[304,128]{1,0:T(8,128)(2,1)S(1)}, u32[]{:S(2)}, u32[]{:S(2)}) collective-permute-start(bf16[304,128]{1,0:T(8,128)(2,1)S(1)} %add_depth.1.piece_refs_0_), channel_id=1, source_target_pairs={{0,16},{1,17},{2,18},{3,19},{4,20},{5,21},{6,22},{7,23},{8,24},{9,... | collective-permute-start | bytes 233480 | tf_op jit(solution)/shard_map/ppermute | solution.py:1035
  205.4 6.2 %collective-permute-start.69 = (bf16[304,128]{1,0:T(8,128)(2,1)S(1)}, bf16[304,128]{1,0:T(8,128)(2,1)S(1)}, u32[]{:S(2)}, u32[]{:S(2)}) collective-permute-start(bf16[304,128]{1,0:T(8,128)(2,1)S(1)} %add_depth.1.piece_refs_0_), channel_id=1, source_target_pairs={{0,24},{1,25},{2,26},{3,27},{4,28},{5,29},{6,30},{7,31},{8,16},{9,... | collective-permute-start | bytes 233480 | tf_op jit(solution)/shard_map/ppermute | solution.py:1035
  212.2 8.3 %collective-permute-start.70 = (bf16[1216,128]{1,0:T(8,128)(2,1)S(1)}, bf16[1216,128]{1,0:T(8,128)(2,1)S(1)}, u32[]{:S(2)}, u32[]{:S(2)}) collective-permute-start(bf16[1216,128]{1,0:T(8,128)(2,1)S(1)} %join_depth.1.half_refs_0_), channel_id=1, source_target_pairs={{0,4},{1,5},{2,6},{3,7},{4,0},{5,1},{6,2},{7,3},{8,12},{9,13},{10,... | collective-permute-start | bytes 933896 | tf_op jit(solution)/shard_map/ppermute | solution.py:1035
  215.9 9.9 %collective-permute-start.55 = (bf16[784,256]{1,0:T(8,128)(2,1)S(1)}, bf16[784,256]{1,0:T(8,128)(2,1)}, u32[]{:S(2)}, u32[]{:S(2)}) collective-permute-start(bf16[784,256]{1,0:T(8,128)(2,1)S(1)} %get-tuple-element.176), channel_id=1, source_target_pairs={{0,0},{1,4},{2,2},{3,6},{4,1},{5,5},{6,3},{7,7},{8,8},{9,12},{10,1... | collective-permute-start | bytes 1204232 | tf_op jit(solution)/shard_map/ppermute | solution.py:1035
  217.3 10.8 %collective-permute-start.56 = (bf16[784,256]{1,0:T(8,128)(2,1)S(1)}, bf16[784,256]{1,0:T(8,128)(2,1)}, u32[]{:S(2)}, u32[]{:S(2)}) collective-permute-start(bf16[784,256]{1,0:T(8,128)(2,1)S(1)} %get-tuple-element.177), channel_id=1, source_target_pairs={{0,1},{1,5},{2,3},{3,7},{4,0},{5,4},{6,2},{7,6},{8,9},{9,13},{10,1... | collective-permute-start | bytes 1204232 | tf_op jit(solution)/shard_map/ppermute | solution.py:1035
  218.0 10.1 %collective-permute-start.57 = (bf16[784,256]{1,0:T(8,128)(2,1)S(1)}, bf16[784,256]{1,0:T(8,128)(2,1)}, u32[]{:S(2)}, u32[]{:S(2)}) collective-permute-start(bf16[784,256]{1,0:T(8,128)(2,1)S(1)} %get-tuple-element.178), channel_id=1, source_target_pairs={{0,2},{1,6},{2,0},{3,4},{4,3},{5,7},{6,1},{7,5},{8,10},{9,14},{10,... | collective-permute-start | bytes 1204232 | tf_op jit(solution)/shard_map/ppermute | solution.py:1035
  218.6 18.3 %collective-permute-start.58 = (bf16[784,256]{1,0:T(8,128)(2,1)S(1)}, bf16[784,256]{1,0:T(8,128)(2,1)}, u32[]{:S(2)}, u32[]{:S(2)}) collective-permute-start(bf16[784,256]{1,0:T(8,128)(2,1)S(1)} %get-tuple-element.179), channel_id=1, source_target_pairs={{0,3},{1,7},{2,1},{3,5},{4,2},{5,6},{6,0},{7,4},{8,11},{9,15},{10,... | collective-permute-start | bytes 1204232 | tf_op jit(solution)/shard_map/ppermute | solution.py:1035
  (25 other events, 288.3 us)

commit v3 on v2

--- a/solution.py
+++ b/solution.py
@@ -16,6 +16,7 @@
 UNROLL = 2
 VMEM_LIMIT = 24 * 2**20
 SLOTS = (0, 1, 2, 3)
+GATHERED = 40
 ORDER = (0, 2, 1, 3)
 EPSILON = 1e-05
 HIGHEST = lax.Precision.HIGHEST
@@ -161,26 +162,12 @@
     return jax.ShapeDtypeStruct(dims, kind)
 
 
+def slot_refs(even_ref, odd_ref, across_ref):
+    return even_ref.at[0], odd_ref.at[0], across_ref.at[0], across_ref.at[1]
+
+
 def reduce_in(
-    counts_ref,
-    x0,
-    x1,
-    x2,
-    x3,
-    a0,
-    a1,
-    a2,
-    a3,
-    pre_ref,
-    msg_ref,
-    w_ref,
-    in_affine_ref,
-    mid_affine_ref,
-    bias_ref,
-    out_affine_ref,
-    wall_ref,
-    flat_ref,
-    small_ref,
+    counts_ref, x0, x1, x2, x3, a0, a1, a2, a3, pre_ref, msg_ref, w_ref, wall_ref, flat_ref
 ):
     place = Place(counts_ref)
     images = wall_ref.shape[0] // place.groups
@@ -191,21 +178,56 @@
         here = (spot >= slot * images) & (spot < slot * images + number)
         real = jnp.where(here, 1, real)
     wall_ref[...] = real.astype(F32)
-    chan, batch = place.chan, place.batch
     own = w_ref.shape[1] // len(SLOTS)
-    half = w_ref.shape[2] // 2
-    weights = 2 * w_ref.shape[0] * own
+    lanes = w_ref.shape[2]
     for s, piece in enumerate((a0, a1, a2, a3)):
-        here = pl.ds(pl.multiple_of((chan ^ s) * own, own), own)
-        for block in range(2 * w_ref.shape[0]):
-            lane = slice((block % 2) * half, (block % 2 + 1) * half)
-            w_ref[block // 2, here, lane] = piece[block * own : (block + 1) * own, :]
-        small = piece[weights:, :].astype(F32)
-        small_ref[chan ^ s] = small
+        here = pl.ds(pl.multiple_of((place.chan ^ s) * own, own), own)
+        for block in range(w_ref.shape[0]):
+            w_ref[block, here, :] = piece[:, block * lanes : (block + 1) * lanes]
+    parts = [dot_nt(x[...], w_ref[place.batch ^ s]) for s, x in enumerate((x0, x1, x2, x3))]
+    flat_ref[...] = functools.reduce(jnp.add, parts)
+    spread_map_rows(flat_ref, pre_ref)
+    first = jnp.zeros((1, pre_ref.shape[1]), F32)
+    second = jnp.zeros((1, pre_ref.shape[1]), F32)
+    for image in range(pre_ref.shape[0] // PADDED):
+        real = place.real(image)
+        value = pre_ref[image * PADDED : (image + 1) * PADDED, :]
+        first = first + real * total_of(value)
+        second = second + real * total_of(value * value)
+    msg_ref[...] = jnp.concatenate([first, second], axis=0)
+
+
+def place_mid(
+    counts_ref,
+    b0,
+    b1,
+    b2,
+    b3,
+    w_ref,
+    w_back_ref,
+    squeeze_ref,
+    in_affine_ref,
+    mid_affine_ref,
+    bias_ref,
+    out_affine_ref,
+    small_ref,
+):
+    place = Place(counts_ref)
+    width, lanes = w_ref.shape[1], b0.shape[1]
+    own = width // len(SLOTS)
+    for s, piece in enumerate((b0, b1, b2, b3)):
+        at = pl.multiple_of((place.chan ^ s) * own, own)
+        for tap in range(9):
+            for r in range(2):
+                block = piece[(2 * tap + r) * own : (2 * tap + r + 1) * own, :]
+                w_ref[r, pl.ds(at, own), tap * lanes : (tap + 1) * lanes] = block
+                w_back_ref[r, pl.ds(tap * width + at, own), :] = block
+        squeeze_ref[pl.ds(at, own), :] = piece[18 * own : 19 * own, :]
+        small = piece[19 * own : 19 * own + 16, :].astype(F32)
+        small_ref[place.chan ^ s] = small
         for t in range(2):
-            out_affine_ref[t, chan ^ s, :, :half] = small[4 + 2 * t : 5 + 2 * t, :]
-            out_affine_ref[t, chan ^ s, :, half:] = small[5 + 2 * t : 6 + 2 * t, :]
-    width = own * len(SLOTS)
+            out_affine_ref[t, place.chan ^ s, :, :lanes] = small[4 + 2 * t : 5 + 2 * t, :]
+            out_affine_ref[t, place.chan ^ s, :, lanes:] = small[5 + 2 * t : 6 + 2 * t, :]
     for k in range(len(SLOTS)):
         here = slice(k * own, (k + 1) * own)
         there = slice(width + k * own, width + (k + 1) * own)
@@ -216,42 +238,18 @@
             mid_affine_ref[t : t + 1, there] = small_ref[k, 1 + t : 2 + t, own:]
         bias_ref[0:1, here] = small_ref[k, 3:4, :own]
         bias_ref[0:1, there] = small_ref[k, 3:4, own:]
-    parts = [dot_nt(x[...], w_ref[batch ^ s]) for s, x in enumerate((x0, x1, x2, x3))]
-    flat_ref[...] = functools.reduce(jnp.add, parts)
-    spread_map_rows(flat_ref, pre_ref)
-    first = jnp.zeros((1, pre_ref.shape[1]), F32)
-    second = jnp.zeros((1, pre_ref.shape[1]), F32)
-    for image in range(pre_ref.shape[0] // PADDED):
-        real = place.real(image)
-        value = pre_ref[image * PADDED : (image + 1) * PADDED, :]
-        first = first + real * total_of(value)
-        second = second + real * total_of(value * value)
-    msg_ref[...] = jnp.concatenate([first, second], axis=0)
-
-
-def place_mid(counts_ref, b0, b1, b2, b3, w_ref, w_back_ref):
+
+
+def place_rest(counts_ref, b0, b1, b2, b3, excite_ref, w_out_ref):
     place = Place(counts_ref)
-    width, lanes = w_ref.shape[1], b0.shape[1]
+    width, lanes = w_out_ref.shape[1], b0.shape[1]
     own = width // len(SLOTS)
     for s, piece in enumerate((b0, b1, b2, b3)):
-        at = pl.multiple_of((place.chan ^ s) * own, own)
-        for tap in range(9):
-            for r in range(2):
-                block = piece[(2 * tap + r) * own : (2 * tap + r + 1) * own, :]
-                w_ref[r, pl.ds(at, own), tap * lanes : (tap + 1) * lanes] = block
-                w_back_ref[r, pl.ds(tap * width + at, own), :] = block
-
-
-def place_rest(counts_ref, b0, b1, b2, b3, excite_ref, squeeze_ref, w_out_ref):
-    place = Place(counts_ref)
-    width, lanes = squeeze_ref.shape
-    own = width // len(SLOTS)
-    for s, piece in enumerate((b0, b1, b2, b3)):
-        at = pl.multiple_of((place.chan ^ s) * own, own)
+        row = 19 * own + 16
         for r in range(2):
-            excite_ref[pl.ds(r * width + at, own), :] = piece[r * own : (r + 1) * own, :]
-        squeeze_ref[pl.ds(at, own), :] = piece[2 * own : 3 * own, :]
-        row = 3 * own
+            at = pl.multiple_of(r * width + (place.chan ^ s) * own, own)
+            excite_ref[pl.ds(at, own), :] = piece[row : row + own, :]
+            row += own
         w_out_ref[place.chan ^ s, :, :lanes] = piece[row : row + width, :]
         w_out_ref[place.chan ^ s, :, lanes:] = piece[row + width : row + 2 * width, :]
 
@@ -334,7 +332,6 @@
     squeeze_ref,
     pooled_ref,
     msg_ref,
-    incline_ref,
 ):
     place = Place(counts_ref)
     images = mid_ref.shape[0] // PADDED
@@ -363,8 +360,11 @@
         pooled_ref[image : image + 1, :] = (active[:, :width] + active[:, width:]) / PIXELS
         inclines[0].append(total_of(rise))
         inclines[1].append(total_of(lean))
-    incline_ref[...] = jnp.concatenate(inclines[0] + inclines[1], axis=0)
+    inclined = jnp.concatenate(inclines[0] + inclines[1], axis=0)
     msg_ref[...] = jnp.zeros_like(msg_ref)
+    for q in range(2 * width // lanes):
+        row = 8 + q * 2 * images
+        msg_ref[row : row + 2 * images, :] = inclined[:, q * lanes : (q + 1) * lanes]
     msg_ref[0:images, :] = dot_nn(pooled_ref[...], squeeze_ref[...].astype(F32), HIGHEST)
     real = [place.real(image) * pooled_ref[image : image + 1, :] for image in range(images)]
     real = functools.reduce(jnp.add, real)
@@ -402,7 +402,7 @@
     place = Place(counts_ref)
     images = mid_ref.shape[0] // PADDED
     width = mid_ref.shape[1] // 2
-    rows = slot_rows(gathered_refs, 8, 0, images)
+    rows = slot_rows(gathered_refs, GATHERED, 0, images)
     center, scale = gate_norm(place, rows, wall_ref[...])
     normed = (rows[0:images] - center) * scale
     gate_pre = normed * gate_affine_ref[0:1, :] + gate_affine_ref[1:2, :]
@@ -445,22 +445,17 @@
     out_ref,
     sums_refs,
     affine_ref,
-    x0,
-    x1,
-    x2,
-    x3,
-    c0,
-    c1,
-    c2,
-    c3,
-    r0,
-    r1,
-    r2,
-    r3,
+    x_refs,
+    cot_even_ref,
+    cot_odd_ref,
+    cot_across_ref,
+    even_ref,
+    odd_ref,
     grad_ref,
     msg_ref,
 ):
     place = Place(counts_ref)
+    cot_refs = slot_refs(cot_even_ref, cot_odd_ref, cot_across_ref)
     blocks, rows, lanes = out_ref.shape
     sums = summed_over(sums_refs)
     center, scale = moments(sums[:blocks], sums[blocks:], place.total() * PIXELS)
@@ -469,11 +464,11 @@
         mu, r = center[k : k + 1], scale[k : k + 1]
         block = place.batch ^ k
         gain, shift = affine_ref[0, block], affine_ref[1, block]
-        x_ref, cot_ref, result_ref = (x0, x1, x2, x3)[k], (c0, c1, c2, c3)[k], (r0, r1, r2, r3)[k]
+        x_ref, cot_ref, summed_ref = x_refs[k], cot_refs[k], (even_ref, odd_ref)[k & 1].at[k >> 1]
 
         def chunk(
             step, carry, k=k, mu=mu, r=r, gain=gain, shift=shift,
-            x_ref=x_ref, cot_ref=cot_ref, result_ref=result_ref,
+            x_ref=x_ref, cot_ref=cot_ref, summed_ref=summed_ref,
         ):
             first, second = carry
             at = pl.multiple_of(step * CHUNK, CHUNK)
@@ -482,10 +477,9 @@
             real = (spot < limit).astype(F32)
             normed = (out_ref[k, here, :] - mu) * r
             summed = x_ref[here, :].astype(F32) + (normed * gain + shift)
-            share = logistic(summed) * real
-            result_ref[here, :] = (summed * share).astype(BF16)
-            upstream = cot_ref[here, :].astype(F32)
-            grad = upstream * share * (1.0 + summed * (1.0 - share))
+            summed_ref[here, :] = summed.astype(BF16)
+            share = logistic(summed)
+            grad = cot_ref[here, :].astype(F32) * real * (share * (1.0 + summed * (1.0 - share)))
             grad_ref[k, here, :] = grad
             return first + fold(grad), second + fold(grad * normed)
 
@@ -495,6 +489,30 @@
         )
         for t, row in enumerate((total_of(first), total_of(second))):
             msg_ref[t * blocks + k : t * blocks + k + 1, :] = row
+
+
+def finish_owned(counts_ref, even_ref, odd_ref, across_ref, cot_ref, result_ref, grad_ref):
+    chan, group = lax.axis_index("chan"), lax.axis_index("dp")
+    pieces = slot_refs(even_ref, odd_ref, across_ref)
+    rows = cot_ref.shape[1]
+    for s, piece in enumerate(pieces):
+        batch = chan ^ s
+        limit = counts_ref[batch, group] * PIXELS
+
+        def chunk(step, carry, piece=piece, batch=batch, limit=limit):
+            at = pl.multiple_of(step * CHUNK, CHUNK)
+            here = pl.ds(at, CHUNK)
+            spot = lax.broadcasted_iota(jnp.int32, (CHUNK, 1), 0) + at
+            real = (spot < limit).astype(F32)
+            summed = piece[here, :].astype(F32)
+            share = logistic(summed)
+            held = share * real
+            result_ref[batch, here, :] = (summed * held).astype(BF16)
+            grad = cot_ref[batch, here, :].astype(F32) * (held * (1.0 + summed * (1.0 - share)))
+            grad_ref[batch, here, :] = grad.astype(BF16)
+            return carry
+
+        lax.fori_loop(0, rows // CHUNK, chunk, 0, unroll=UNROLL)
 
 
 def back_out(
@@ -589,7 +607,6 @@
     counts_ref,
     back_refs,
     gathered_refs,
-    incline_refs,
     wall_ref,
     gate_affine_ref,
     squeeze_ref,
@@ -616,7 +633,7 @@
     pieces = 2 * width // lanes
     total = place.total() * PIXELS
     wall = wall_ref[...]
-    rows = slot_rows(gathered_refs, 8, 0, images)
+    rows = slot_rows(gathered_refs, GATHERED, 0, images)
     center, scale = gate_norm(place, rows, wall)
     gain = gate_affine_ref[0:1, :] * scale
     normed = (rows - center) * scale
@@ -630,11 +647,14 @@
     pooled_grad = jnp.concatenate([pooled_grad, pooled_grad], axis=1)
     slot = 0
     terms = jnp.zeros((2 * images, 2 * width), F32)
-    for ref in incline_refs:
-        inclines = ref[...]
-        for at in range(0, inclines.shape[0], 2 * images):
+    for ref in gathered_refs:
+        for at in range(8, ref.shape[0], GATHERED):
+            inclines = [
+                ref[at + q * 2 * images : at + (q + 1) * 2 * images, :] for q in range(pieces)
+            ]
             grad = pooled_grad[slot * images : (slot + 1) * images, :]
-            terms = terms + inclines[at : at + 2 * images] * jnp.concatenate([grad, grad], axis=0)
+            grad = jnp.concatenate([grad, grad], axis=0)
+            terms = terms + jnp.concatenate(inclines, axis=1) * grad
             slot += 1
     sums = functools.reduce(jnp.add, [ref[0 : 2 * pieces, :] for ref in back_refs])
     back = []
@@ -759,13 +779,9 @@
     counts_ref,
     taps_ref,
     low_ref,
-    pooled_ref,
-    gathered_refs,
-    squeezed_ref,
     keep_ref,
     send_ref,
     wide_ref,
-    narrow_ref,
 ):
     place = Place(counts_ref)
     half = taps_ref.shape[2] // 2
@@ -790,16 +806,6 @@
                 target[turn % 2, row : row + own, :] = wide_ref[
                     here, tap * half : (tap + 1) * half
                 ].astype(BF16)
-    images, lanes = pooled_ref.shape[0], squeezed_ref.shape[1]
-    mean = [
-        total_of(slot_rows(gathered_refs, 8, images + q, 1)) for q in range(width // lanes)
-    ]
-    mean = jnp.concatenate(mean, axis=1) / place.total()
-    narrow_ref[...] = dot_tn(pooled_ref[...] - mean, squeezed_ref[...], HIGHEST)
-    for turn, s in enumerate(ORDER):
-        target = keep_ref if turn < 2 else send_ref
-        here = pl.ds(pl.multiple_of((place.chan ^ s) * own, own), own)
-        target[turn % 2, 18 * own : 19 * own, :] = narrow_ref[here, :].astype(BF16)
 
 
 def back_in(
@@ -816,11 +822,15 @@
     x3,
     vector_ref,
     out_back_refs,
+    pooled_ref,
+    gathered_refs,
+    squeezed_ref,
     low_ref,
     keep_ref,
     send_ref,
     flat_ref,
     wide_ref,
+    narrow_ref,
     small_ref,
 ):
     place = Place(counts_ref)
@@ -855,6 +865,16 @@
                 target[turn % 2, pl.ds(at, own), :] = wide_ref[
                     here, part * lanes : (part + 1) * lanes
                 ].astype(BF16)
+    mean = [
+        total_of(slot_rows(gathered_refs, GATHERED, images + q, 1)) for q in range(width // lanes)
+    ]
+    mean = jnp.concatenate(mean, axis=1) / place.total()
+    narrow_ref[...] = dot_tn(pooled_ref[...] - mean, squeezed_ref[...], HIGHEST)
+    row = keep_ref.shape[1] - small_ref.shape[1] - own
+    for turn, s in enumerate(ORDER):
+        target = keep_ref if turn < 2 else send_ref
+        here = pl.ds(pl.multiple_of((chan ^ s) * own, own), own)
+        target[turn % 2, row : row + own, :] = narrow_ref[here, :].astype(BF16)
     small_ref[...] = jnp.zeros_like(small_ref)
     outs = summed_over(out_back_refs)
     for k in range(len(SLOTS)):
@@ -876,19 +896,11 @@
     sort_pieces(place, small_ref, keep_ref, send_ref, keep_ref.shape[1] - small_ref.shape[1])
 
 
-def grad_input(
-    counts_ref,
-    low_ref,
-    w_ref,
-    summed_ref,
-    g0,
-    g1,
-    g2,
-    g3,
-):
-    place = Place(counts_ref)
-    for s, target in enumerate((g0, g1, g2, g3)):
-        target[...] = (dot_nn(low_ref[...], w_ref[place.batch ^ s]) + summed_ref[s]).astype(BF16)
+def grad_owned(low_refs, w_ref, summed_ref, result_ref):
+    chan = lax.axis_index("chan")
+    for s, low_ref in enumerate(low_refs):
+        value = dot_nn(low_ref[...], w_ref[chan]) + summed_ref[chan ^ s].astype(F32)
+        result_ref[chan ^ s] = value.astype(BF16)
 
 
 def add_groups(terms_ref, sum_ref):
@@ -900,42 +912,57 @@
     return left_ref[...].astype(F32) + right_ref[...].astype(F32)
 
 
-def add_core(keep_ref, arrived_ref, kept_ref, send_ref):
-    value = added(keep_ref, arrived_ref).astype(BF16)
+def add_core(keep_refs, arrived_refs, kept_ref, send_ref):
+    at = 0
+    for keep_ref, arrived_ref in zip(keep_refs, arrived_refs):
+        value = added(keep_ref, arrived_ref).astype(BF16)
+        rows = keep_ref.shape[1]
+        kept_ref[at : at + rows, :] = value[0]
+        send_ref[at : at + rows, :] = value[1]
+        at += rows
+    if at < kept_ref.shape[0]:
+        for ref in (kept_ref, send_ref):
+            ref[at:, :] = jnp.zeros((kept_ref.shape[0] - at, ref.shape[1]), BF16)
+
+
+def split_rows(parity, whole_ref, kept_ref, send_ref):
+    rows = kept_ref.shape[-2]
+    mine = pl.ds(pl.multiple_of(parity * rows, 16), rows)
+    other = pl.ds(pl.multiple_of((1 - parity) * rows, 16), rows)
+    if whole_ref.ndim == 2:
+        kept_ref[...] = whole_ref[mine, :]
+        send_ref[...] = whole_ref[other, :].astype(BF16)
+    else:
+        kept_ref[...] = whole_ref[:, mine, :]
+        send_ref[...] = whole_ref[:, other, :].astype(BF16)
+
+
+def add_core_first(counts_ref, keep_ref, arrived_ref, kept_ref, send_ref, whole_ref):
+    whole_ref[...] = added(keep_ref, arrived_ref)
+    split_rows(Place(counts_ref).parity, whole_ref, kept_ref, send_ref)
+
+
+def add_parity_first(keep_ref, arrived_ref, kept_ref, send_ref):
+    value = added(keep_ref, arrived_ref)
     kept_ref[...] = value[0]
-    send_ref[...] = value[1]
-
-
-def add_chip(counts_ref, keep_refs, arrived_refs, kept_ref, send_ref, whole_ref):
+    send_ref[...] = value[1].astype(BF16)
+
+
+def add_chip(counts_ref, keep_ref, arrived_ref, kept_ref, send_ref, whole_ref):
+    whole_ref[...] = added(keep_ref, arrived_ref)
+    split_rows(Place(counts_ref).parity, whole_ref, kept_ref, send_ref)
+
+
+def add_last(counts_ref, keep_refs, arrived_refs, kept_ref, s1, s2, s3, whole_refs):
     place = Place(counts_ref)
     at = 0
-    for keep_ref, arrived_ref in zip(keep_refs, arrived_refs):
-        whole_ref[at : at + keep_ref.shape[0], :] = added(keep_ref, arrived_ref)
-        at += keep_ref.shape[0]
-    if at < whole_ref.shape[0]:
-        whole_ref[at:, :] = jnp.zeros((whole_ref.shape[0] - at, whole_ref.shape[1]), F32)
-    rows = kept_ref.shape[0]
-    own = place.parity
-    kept_ref[...] = whole_ref[pl.ds(pl.multiple_of(own * rows, 16), rows), :]
-    send_ref[...] = whole_ref[pl.ds(pl.multiple_of((1 - own) * rows, 16), rows), :].astype(BF16)
-
-
-def add_parity(
-    counts_ref,
-    keep_ref,
-    arrived_ref,
-    kept_ref,
-    s1,
-    s2,
-    s3,
-    whole_ref,
-):
-    place = Place(counts_ref)
-    whole_ref[...] = added(keep_ref, arrived_ref)
-    rows = kept_ref.shape[0]
-    for t, target in enumerate((kept_ref, s1, s2, s3)):
-        at = pl.multiple_of((place.depth ^ t) * rows, 16)
-        target[...] = whole_ref[pl.ds(at, rows), :].astype(target.dtype)
+    for keep_ref, arrived_ref, whole_ref in zip(keep_refs, arrived_refs, whole_refs):
+        whole_ref[...] = added(keep_ref, arrived_ref)
+        rows = keep_ref.shape[0] // len(SLOTS)
+        for t, target in enumerate((kept_ref, s1, s2, s3)):
+            here = pl.ds(pl.multiple_of((place.depth ^ t) * rows, 16), rows)
+            target[at : at + rows, :] = whole_ref[here, :].astype(target.dtype)
+        at += rows
 
 
 def add_depth(keep_ref, arrived_refs, sum_ref):
@@ -956,42 +983,75 @@
         whole_ref[pl.ds(pl.multiple_of((place.depth ^ t) * rows, 16), rows), :] = ref[...]
 
 
-def join_parity(
-    place,
-    half_refs,
-    whole_ref,
-):
-    rows = half_refs[0].shape[0]
+def join_halves(counts_ref, half_refs, first_ref, second_ref):
+    place = Place(counts_ref)
     for t, ref in enumerate(half_refs):
-        at = pl.multiple_of((place.parity ^ t) * rows, 16)
-        whole_ref[pl.ds(at, rows), :] = ref[...].astype(F32)
+        piece = ref.shape[0] // len(SLOTS)
+        row = 0
+        for target in (first_ref, second_ref):
+            rows = target.shape[0] // 2 // len(SLOTS)
+            for z in range(len(SLOTS)):
+                at = ((place.parity ^ t) * len(SLOTS) + z) * rows
+                source = ref[z * piece + row : z * piece + row + rows, :]
+                target[pl.ds(pl.multiple_of(at, 16), rows), :] = source.astype(F32)
+            row += rows
 
 
 def unpack(
+    joined,
     counts_ref,
-    half_refs,
+    term_refs,
     in_ref,
+    gain_in_ref,
+    shift_in_ref,
     mid_ref,
+    gain_mid_ref,
+    shift_mid_ref,
     squeeze_ref,
+    gain_gate_ref,
+    shift_gate_ref,
     excite_ref,
     bias_ref,
     out_ref,
-    small_ref,
-    whole_ref,
-):
-    join_parity(Place(counts_ref), half_refs, whole_ref)
+    gain_out_ref,
+    shift_out_ref,
+    first_ref,
+    second_ref,
+):
+    if joined:
+        first_ref[...] = term_refs[0][...].astype(F32)
+        second_ref[...] = term_refs[1][...].astype(F32)
+    else:
+        join_halves(counts_ref, term_refs, first_ref, second_ref)
     own, lanes = squeeze_ref.shape
     width = out_ref.shape[0]
-    out_ref[:, :lanes] = whole_ref[0:width, :]
-    out_ref[:, lanes:] = whole_ref[width : 2 * width, :]
+
+    def halves(target, row):
+        target[0:1, :] = second_ref[row : row + 1, :own]
+        target[1:2, :] = second_ref[row : row + 1, own:]
+
+    mid_ref[...] = first_ref[...]
+    out_ref[:, :lanes] = second_ref[0:width, :]
+    out_ref[:, lanes:] = second_ref[width : 2 * width, :]
     row = 2 * width
-    for target in (excite_ref, bias_ref, mid_ref, squeeze_ref):
-        target[...] = whole_ref[row : row + target.shape[0], :]
-        row += target.shape[0]
+    excite_ref[...] = second_ref[row : row + 2 * own, :]
+    row += 2 * own
+    halves(bias_ref, row)
+    row += 16
     for block in range(in_ref.shape[1] // lanes):
-        in_ref[:, block * lanes : (block + 1) * lanes] = whole_ref[row : row + own, :]
+        in_ref[:, block * lanes : (block + 1) * lanes] = second_ref[row : row + own, :]
         row += own
-    small_ref[...] = whole_ref[row : row + small_ref.shape[0], :]
+    squeeze_ref[...] = second_ref[row : row + own, :]
+    row += own
+    gain_in_ref[...] = second_ref[row : row + 1, :own]
+    shift_in_ref[...] = second_ref[row : row + 1, own:]
+    halves(gain_mid_ref, row + 1)
+    halves(shift_mid_ref, row + 2)
+    gain_gate_ref[...] = second_ref[row + 3 : row + 4, :]
+    shift_gate_ref[...] = second_ref[row + 4 : row + 5, :]
+    for t, target in enumerate((gain_out_ref, shift_out_ref)):
+        target[:, :lanes] = second_ref[row + 5 + 2 * t : row + 6 + 2 * t, :]
+        target[:, lanes:] = second_ref[row + 6 + 2 * t : row + 7 + 2 * t, :]
 
 
 def per_device(
@@ -1037,8 +1097,11 @@
     def home(tensor, s):
         return permute(tensor, lambda z, x, y, c: (z, c ^ (s & 1), y ^ (s >> 1), x))
 
-    def away(tensor, s):
-        return permute(tensor, lambda z, x, y, c: (z, c, y ^ (s >> 1), x ^ (s & 1)))
+    def away_plane(tensor, odd=0):
+        return permute(tensor, lambda z, x, y, c: (z, c, y, x ^ odd))
+
+    def cross(even, odd):
+        return even, odd, across(jnp.stack([even[1], odd[1]]))
 
     def core(tensor):
         return permute(tensor, lambda z, x, y, c: (z, x, y, c ^ 1))
@@ -1080,58 +1143,94 @@
 
         return run
 
-    def add_over_chan(keep, send):
-        rows = keep.shape[1]
-        keep, send = call(
-            add_core, [shape((rows, 2 * own), BF16)] * 2, [], 0, keep, core(send), smem=0
+    def padded(rows):
+        return -(-rows // (16 * groups)) * 16 * groups
+
+    def kernel(body, outs, *args, smem=1):
+        return call(body, outs, [], 0, *args, smem=smem)
+
+    def add_over_all(first, second, low, result):
+        first_rows, second_rows = first[0].shape[1], sum(k.shape[1] for k in second[0])
+        if groups != 8:
+            rows = padded(first_rows + second_rows)
+            keep, send = kernel(
+                add_core,
+                [shape((rows, 2 * own), BF16)] * 2,
+                (first[0],) + second[0],
+                (first[1],) + second[1],
+                smem=0,
+            )
+            terms = (keep.astype(F32) + across(send).astype(F32)).astype(BF16)
+            terms = lax.all_to_all(terms.reshape(groups, rows // groups, -1), "dp", 0, 0)
+            (terms,) = kernel(add_groups, [shape(terms.shape, BF16)], terms, smem=0)
+            terms = lax.all_to_all(terms, "dp", 0, 0).reshape(rows, -1)
+            terms = terms[:first_rows], terms[first_rows : first_rows + second_rows]
+            low = away_plane(low)
+            return terms, low, across(low)
+        second_rows = padded(second_rows)
+        halves = (first_rows // 2, second_rows // 2)
+        pieces = (first_rows // groups, second_rows // groups)
+
+        def rows(number, kind=F32):
+            return shape((number, 2 * own), kind)
+
+        keep, send = kernel(add_core, [rows(second_rows, BF16)] * 2, *second, smem=0)
+        arrived = after(across(send), result)
+        pair = (2, halves[0], 2 * own)
+        first_keep, send = call(
+            add_core_first,
+            [shape(pair), shape(pair, BF16)],
+            [pltpu.VMEM((2, first_rows, 2 * own), F32)],
+            0,
+            counts,
+            *first,
         )
-        return keep, across(send)
-
-    def add_over_dp(keep, arrived):
-        rows = sum(k.shape[0] for k in keep)
-        if groups != 8:
-            whole = -(-rows // (16 * groups)) * 16 * groups
-            terms = jnp.concatenate(keep).astype(F32) + jnp.concatenate(arrived).astype(F32)
-            terms = jnp.pad(terms.astype(BF16), ((0, whole - rows), (0, 0)))
-            terms = lax.all_to_all(terms.reshape(groups, whole // groups, -1), "dp", 0, 0)
-            (terms,) = call(add_groups, [shape(terms.shape, BF16)], [], 0, terms, smem=0)
-            terms = lax.all_to_all(terms, "dp", 0, 0).reshape(2, whole // 2, -1)
-            swap = group % 2 == 1
-            return (
-                jnp.where(swap, terms[1], terms[0]),
-                jnp.where(swap, terms[0], terms[1]),
-            )
-        piece = -(-rows // (16 * groups)) * 16
-        half = piece * depth
+        first_arrived = parity(send)
         keep, send = call(
             add_chip,
-            [shape((half, 2 * own)), shape((half, 2 * own), BF16)],
-            [pltpu.VMEM((2 * half, 2 * own), F32)],
+            [rows(halves[1]), rows(halves[1], BF16)],
+            [pltpu.VMEM((second_rows, 2 * own), F32)],
             0,
             counts,
             keep,
             arrived,
         )
+        arrived = parity(send)
+        first_keep, send = kernel(
+            add_parity_first,
+            [rows(halves[0]), rows(halves[0], BF16)],
+            first_keep,
+            first_arrived,
+            smem=0,
+        )
+        first_arrived = across(send)
+        arrived = after(arrived, first_arrived)
+        low = away_plane(after(low, arrived))
         keep, *send = call(
-            add_parity,
-            [shape((piece, 2 * own))] + [shape((piece, 2 * own), BF16)] * (depth - 1),
-            [pltpu.VMEM((half, 2 * own), F32)],
+            add_last,
+            [rows(sum(pieces))] + [rows(sum(pieces), BF16)] * (depth - 1),
+            [tuple(pltpu.VMEM((half, 2 * own), F32) for half in halves)],
             0,
             counts,
-            keep,
-            parity(send),
+            (first_keep, keep),
+            (first_arrived, arrived),
         )
         arrived = tuple(along(send[t - 1], t) for t in range(1, depth))
-        (mine,) = call(add_depth, [shape((piece, 2 * own), BF16)], [], 0, keep, arrived, smem=0)
-        pieces = (mine,) + tuple(along(mine, t) for t in range(1, depth))
-        (mine,) = call(join_depth, [shape((half, 2 * own), BF16)], [], 0, counts, pieces)
-        return mine, parity(mine)
-
-    def send_home(tensor):
-        pieces = [lax.dynamic_index_in_dim(tensor, chan ^ s, 0, keepdims=False) for s in SLOTS]
-        return tuple(home(piece, s) for s, piece in enumerate(pieces))
-
-    x = send_home(activations)
+        (mine,) = kernel(add_depth, [rows(sum(pieces), BF16)], keep, arrived, smem=0)
+        mine = (mine,) + tuple(along(mine, t) for t in range(1, depth))
+        low, low_other = after_all((low, across(low)), *mine)
+        (mine,) = kernel(join_depth, [rows(sum(halves), BF16)], counts, mine)
+        return (mine, parity(mine)), low, low_other
+
+    def slots_of(tensor, *which):
+        return [lax.dynamic_index_in_dim(tensor, chan ^ s, 0, keepdims=False) for s in which]
+
+    first = weight_in.T
+    other, near = across(first), core(first)
+    far = slots_of(activations, 2, 3)
+    x = slots_of(after(activations, near, far[0]), 0, 1) + far
+    x = tuple(home(piece, s) for s, piece in enumerate(x))
+
     small = jnp.concatenate(
         [
             jnp.concatenate([gain_in, shift_in])[None],
@@ -1147,64 +1246,55 @@
     def lane_blocks(tensor):
         return [tensor[:, at : at + 2 * own] for at in range(0, tensor.shape[1], 2 * own)]
 
-    first = jnp.concatenate(lane_blocks(weight_in.T) + [small])
-    second = weight_mid.transpose(0, 1, 3, 4, 2).reshape(-1, 2 * own)
-    third = jnp.concatenate(
-        [weight_excite.transpose(1, 2, 0).reshape(-1, inter), weight_squeeze]
+    weights = jnp.concatenate(
+        [weight_mid.transpose(0, 1, 3, 4, 2).reshape(-1, 2 * own), weight_squeeze, small]
+        + [weight_excite.transpose(1, 2, 0).reshape(-1, inter)]
         + lane_blocks(weight_out)
     )
-
-    def gather_slots(tensor, *others):
-        near, other = core(tensor), across(tensor)
-        other = after(other, near, *others)
-        return tensor, near, other, core(other)
-
-    first = gather_slots(first, x[0], x[1])
-    second = gather_slots(after(second, x[2], x[3], first[2]))
-    third = gather_slots(after(third, second[2]))
+    other = after(other, weights)
+    first = (first, near, other, core(other))
+    near = core(weights)
+    cot = slots_of(after(cotangent, x[0], x[1]), *SLOTS)
+    even, odd = jnp.stack([cot[0], cot[2]]), jnp.stack([cot[1], cot[3]])
+    other = across(after(weights, x[2], x[3], first[3]))
+    even = home(after(even, x[2], x[3]), 0)
     gate_affine = jnp.stack([gain_gate, shift_gate]).astype(F32)
 
     product = 2 * rows * lanes * parts * width
-    pre_in, msg, w_in, in_affine, mid_affine, bias, out_affine, wall = call(
+    pre_in, msg, w_in, wall = call(
         reduce_in,
         [
             shape((wide_rows, width)),
             shape((2, width)),
             shape((parts, width, lanes), BF16),
+            shape((groups * images, inter)),
+        ],
+        [pltpu.VMEM((rows, width), F32)],
+        product,
+        counts,
+        *x,
+        *first,
+    )
+    in_sums = exchange(2, 0)(after(msg, near, odd))
+    other = after(other, *in_sums)
+    odd = home(after(odd, *in_sums), 1)
+    weights = (weights, near, other, core(other))
+    w_mid, w_mid_back, squeeze, in_affine, mid_affine, bias, out_affine = call(
+        place_mid,
+        [
+            shape((2, width, 9 * inter), BF16),
+            shape((2, 9 * width, inter), BF16),
+            shape((width, inter), BF16),
             shape((2, width)),
             shape((2, 2 * width)),
             shape((1, 2 * width)),
             shape((2, parts, 1, lanes)),
-            shape((groups * images, inter)),
         ],
-        [pltpu.VMEM((rows, width), F32), pltpu.VMEM((parts, 16, 2 * own), F32)],
-        product,
-        counts,
-        *x,
-        *first,
-    )
-    in_sums = exchange(2, 0)(msg)
-    w_mid, w_mid_back = call(
-        place_mid,
-        [shape((2, width, 9 * inter), BF16), shape((2, 9 * width, inter), BF16)],
-        [],
+        [pltpu.VMEM((parts, 16, 2 * own), F32)],
         0,
         counts,
-        *second,
-    )
-    excite, squeeze, w_out = call(
-        place_rest,
-        [
-            shape((2 * width, inter), BF16),
-            shape((width, inter), BF16),
-            shape((parts, width, lanes), BF16),
-        ],
-        [],
-        0,
-        counts,
-        *third,
-    )
-    cot = send_home(after(cotangent, third[2]))
+        *weights,
+    )
     conv = 2 * wide_rows * 9 * width * width
     taps, mid, msg = call(
         conv_mid,
@@ -1222,9 +1312,22 @@
         w_mid,
     )
     mid_sums = exchange(2, 0)(msg)
-    pooled, msg, inclines = call(
+    even, odd = after_all((even, odd), *mid_sums)
+    cot = cross(even, odd)
+    excite, w_out = call(
+        place_rest,
+        [
+            shape((2 * width, inter), BF16),
+            shape((parts, width, lanes), BF16),
+        ],
+        [],
+        0,
+        counts,
+        *weights,
+    )
+    pooled, msg = call(
         pool,
-        [shape((images, width)), shape((8, inter)), shape((2 * images, 2 * width))],
+        [shape((images, width)), shape((GATHERED, inter))],
         [],
         0,
         counts,
@@ -1233,8 +1336,7 @@
         mid_affine,
         squeeze,
     )
-    gathered = exchange(None, 8)(msg)
-    inclines = exchange(None, 2 * images)(inclines)
+    gathered = exchange(None, GATHERED)(msg)
     gate, attention, weighted, out, msg = call(
         attend,
         [
@@ -1258,9 +1360,9 @@
         w_out,
     )
     out_sums = exchange(2 * parts, 0)(msg)
-    *result, grad, msg = call(
+    *summed, grad, msg = call(
         finish,
-        [shape((rows, lanes), BF16)] * parts
+        [shape((2, rows, lanes), BF16)] * 2
         + [shape((parts, rows, lanes)), shape((2 * parts, lanes))],
         [],
         0,
@@ -1268,19 +1370,12 @@
         out,
         out_sums,
         out_affine,
-        *x,
+        x,
         *cot,
     )
     out_back = exchange(2 * parts, 0)(msg)
 
-    def settle(pieces, *others):
-        pieces = after_all([away(piece, s) for s, piece in enumerate(pieces)], *others)
-        settled = jnp.zeros((batches, rows, lanes), BF16)
-        for s, piece in enumerate(pieces):
-            settled = lax.dynamic_update_index_in_dim(settled, piece, chan ^ s, 0)
-        return settled
-
-    result = settle(result)
+    summed = [away_plane(pair, odd) for odd, pair in enumerate(summed)]
 
     sums_rows = 2 * 2 * width // inter
     low_out, grad_weighted, grad_logits, msg = call(
@@ -1320,8 +1415,9 @@
         gate,
         grad_logits,
     )
-    mid_back = after_all(mid_back, keep)
-    out_keep, out_arrived = add_over_chan(keep, send)
+    out_keep, out_arrived = keep, core(send)
+    mid_back = after_all(mid_back, keep, *summed)
+    summed = cross(*after_all(summed, mid_back[0]))
     low_mid, grad_hidden, grad_squeeze, vectors, msg = call(
         back_mid,
         [
@@ -1336,7 +1432,6 @@
         counts,
         mid_back,
         gathered,
-        inclines,
         wall,
         gate_affine,
         squeeze,
@@ -1351,27 +1446,14 @@
         w_mid_back,
     )
     in_back = exchange(2, 0)(msg)
-    keep, send = call(
-        weight_mid_term,
-        [shape((2, 19 * own, 2 * own), BF16)] * 2,
-        [pltpu.VMEM((width, 9 * inter), F32), pltpu.VMEM((width, inter), F32)],
-        conv,
-        counts,
-        after(taps, in_back[0]),
-        low_mid,
-        pooled,
-        gathered,
-        grad_squeeze,
-    )
-    in_back = after_all(in_back, keep)
-    mid_keep, mid_arrived = add_over_chan(keep, send)
     in_rows = parts * lanes // (2 * own) * own
-    low_in, keep, send = call(
+    low_in, in_keep, in_send = call(
         functools.partial(back_in, 1.0 / groups),
-        [shape((rows, width), BF16)] + [shape((2, in_rows + 16, 2 * own), BF16)] * 2,
+        [shape((rows, width), BF16)] + [shape((2, in_rows + own + 16, 2 * own), BF16)] * 2,
         [
             pltpu.VMEM((rows, width), F32),
             pltpu.VMEM((width, lanes), F32),
+            pltpu.VMEM((width, inter), F32),
             pltpu.VMEM((parts, 16, 2 * own), F32),
         ],
         product,
@@ -1384,48 +1466,91 @@
         *x,
         vectors,
         out_back,
-    )
-    in_keep, in_arrived = add_over_chan(keep, send)
-    low_in = after(low_in, in_arrived)
-    grad_x = call(
-        grad_input, [shape((rows, lanes), BF16)] * parts, [], product, counts, low_in, w_in, grad
-    )
-    halves = add_over_dp((out_keep, mid_keep, in_keep), (out_arrived, mid_arrived, in_arrived))
-    g_in, g_mid, g_squeeze, g_excite, g_bias, g_out, sums = call(
-        unpack,
+        pooled,
+        gathered,
+        grad_squeeze,
+    )
+    keep, send = call(
+        weight_mid_term,
+        [shape((2, 18 * own, 2 * own), BF16)] * 2,
+        [pltpu.VMEM((width, 9 * inter), F32)],
+        conv,
+        counts,
+        after(taps, low_in),
+        low_mid,
+    )
+    owned = shape((batches, rows, lanes), BF16)
+    result, grad_summed = call(finish_owned, [owned, owned], [], 0, counts, *summed, cotangent)
+    send = after(send, summed[2])
+    terms, low_in, low_other = add_over_all(
+        (keep, core(send)),
+        ((out_keep, in_keep), (out_arrived, core(in_send))),
+        low_in,
+        result,
+    )
+    lows = (low_in, core(low_in), low_other, core(low_other))
+    (grad_x,) = call(grad_owned, [owned], [], product, lows, w_in, grad_summed, smem=0)
+    terms = after_all(terms, grad_x)
+    (
+        g_in,
+        g_gain_in,
+        g_shift_in,
+        g_mid,
+        g_gain_mid,
+        g_shift_mid,
+        g_squeeze,
+        g_gain_gate,
+        g_shift_gate,
+        g_excite,
+        g_bias,
+        g_out,
+        g_gain_out,
+        g_shift_out,
+    ) = call(
+        functools.partial(unpack, groups != 8),
         [
             shape((own, parts * lanes)),
+            shape((1, own)),
+            shape((1, own)),
             shape((18 * own, inter)),
+            shape((2, own)),
+            shape((2, own)),
             shape((own, inter)),
+            shape((1, inter)),
+            shape((1, inter)),
             shape((2 * own, inter)),
-            shape((16, 2 * own)),
+            shape((2, own)),
             shape((width, lanes)),
-            shape((16, 2 * own)),
+            shape((1, lanes)),
+            shape((1, lanes)),
         ],
-        [pltpu.VMEM((2 * halves[0].shape[0], 2 * own), F32)],
+        [
+            pltpu.VMEM((18 * own, 2 * own), F32),
+            pltpu.VMEM((terms[0].shape[0] * 2 - 18 * own, 2 * own), F32)
+            if groups == 8
+            else pltpu.VMEM(terms[1].shape, F32),
+        ],
         0,
         counts,
-        halves,
-    )
-    grad_x = settle(grad_x, g_in)
-    outs = lanes // (2 * own)
+        terms,
+    )
     return (
         result,
         grad_x,
         g_in.T,
-        sums[0, :own],
-        sums[0, own:],
+        g_gain_in.reshape(-1),
+        g_shift_in.reshape(-1),
         g_mid.reshape(3, 3, 2, own, inter).transpose(0, 1, 4, 2, 3),
-        sums[1].reshape(2, own),
-        sums[2].reshape(2, own),
+        g_gain_mid,
+        g_shift_mid,
         g_squeeze,
-        sums[3],
-        sums[4],
+        g_gain_gate.reshape(-1),
+        g_shift_gate.reshape(-1),
         g_excite.reshape(2, own, inter).transpose(2, 0, 1),
-        g_bias[0].reshape(2, own),
+        g_bias,
         g_out,
-        sums[5 : 5 + outs].reshape(-1),
-        sums[5 + outs : 5 + 2 * outs].reshape(-1),
+        g_gain_out.reshape(-1),
+        g_shift_out.reshape(-1),
     )
 
 

time: 245 us -> 190 us (0.78)
  waiting for transfers between devices: 114 us -> 56.7 us
  Pallas kernels: 35.8 us -> 42.4 us
  local copies, waits for them, and re-layouts: 17.5 us -> 13.8 us
    ppermute x71 -> x62, waiting for transfers between devices: 114 us -> 56.7 us  [permute(): return lax.ppermute(tensor, ('dp', 'chan'), pairs)]
    pallas_call x21 -> x22, Pallas kernels: 35.8 us -> 42.4 us  [call(): pl.pallas_call(body, out_shape=outs, in_specs=specs, out_specs=[pl.BlockS...]
    concatenate x1, local copies, waits for them, and re-layouts: 1.55 us -> 6.48 us  [per_device(): jnp.concatenate([weight_mid.transpose(0, 1, 3, 4, 2).reshape(-1, 2 * own)...]
    dynamic_update_slice x7 -> x0, local copies, waits for them, and re-layouts: 4.35 us -> none  [settle(): settled = lax.dynamic_update_index_in_dim(settled, piece, chan ^ s, 0)]
    ppermute x71 -> x62, starting transfers between devices: 72.8 us -> 74.4 us  [permute(): return lax.ppermute(tensor, ('dp', 'chan'), pairs)]
  transfers between devices with their start and end apart: 71 -> 62, of which waited for: 34 -> 34; matrix products, arithmetic and copies ran while one was open for 4% -> 7% of each run, Pallas kernels for 7% -> 19%
where the time goes in v3:
time: 190 us; the launch traced here: 189 us
  starting transfers between devices  74.4 us (39%)
  waiting for transfers between devices  56.7 us (30%)
  Pallas kernels  42.4 us (22%)
  local copies, waits for them, and re-layouts  13.8 us (7%)
    ppermute x62, starting transfers between devices, permute(): return lax.ppermute(tensor, ('dp', 'chan'), pairs)  74.4 us
    ppermute x62, waiting for transfers between devices, permute(): return lax.ppermute(tensor, ('dp', 'chan'), pairs)  56.7 us
    pallas_call x22, Pallas kernels, call(): pl.pallas_call(body, out_shape=outs, in_specs=specs, out_specs=[pl.BlockS...  42.4 us
    concatenate x1, local copies, waits for them, and re-layouts, per_device(): jnp.concatenate([weight_mid.transpose(0, 1, 3, 4, 2).reshape(-1, 2 * own)...  6.48 us
  transfers between devices with their start and end apart: 62, of which 34 were waited for; matrix products, arithmetic and copies ran while one was open for 7% of the time, Pallas kernels for 19%

profile of v3, /device:TPU:0, one launch (start us, length us, event | category | flops | bytes accessed | tf_op | source)
XLA Modules:
  0.0 189.5 jit_solution(6162094882492668398)
XLA Ops:
  0.7 3.0 %collective-permute-start.5 = (bf16[64,1024]{1,0:T(8,128)(2,1)}, bf16[64,1024]{1,0:T(8,128)(2,1)S(1)}, u32[]{:S(2)}, u32[]{:S(2)}) collective-permute-start(bf16[64,1024]{1,0:T(8,128)(2,1)} %bitcast.34), channel_id=1, source_target_pairs={{0,2},{1,3},{2,0},{3,1},{4,6},{5,7},{6,4},{7,5},{8,10},{9,11},{10,... | collective-permute-start | bytes 393224 | tf_op jit(solution)/shard_map/ppermute | solution.py:1095
  3.7 2.2 %dynamic-slice_bitcast_fusion = (bf16[784,256]{1,0:T(8,128)(2,1)}, bf16[784,256]{1,0:T(8,128)(2,1)}) fusion(bf16[4,784,256]{2,1,0:T(8,128)(2,1)} %param.17, s32[]{:T(128)S(6)} %select_n.20, s32[]{:T(128)S(6)} %select_n.17), kind=kLoop, calls=%fused_computation.4 | loop fusion | bytes 1605640 | tf_op jit(solution)/shard_map/jit(dynamic_index_in_dim)/squeeze | solution.py:1226
  5.9 1.4 collective-permute-start.4
  7.3 1.5 collective-permute-start.3
  10.1 4.9 %collective-permute-start.1 = (bf16[784,256]{1,0:T(8,128)(2,1)}, bf16[784,256]{1,0:T(8,128)(2,1)}, u32[]{:S(2)}, u32[]{:S(2)}) collective-permute-start(bf16[784,256]{1,0:T(8,128)(2,1)} %get-tuple-element.217), channel_id=1, source_target_pairs={{0,0},{1,4},{2,2},{3,6},{4,1},{5,5},{6,3},{7,7},{8,8},{9,12},{10,1... | collective-permute-start | bytes 1204232 | tf_op jit(solution)/shard_map/ppermute | solution.py:1095
  18.6 6.5 %concatenate.13.b0 = bf16[1872,128]{1,0:T(8,128)(2,1)S(1)} concatenate(bf16[1152,128]{1,0:T(8,128)(2,1)} %bitcast.37, bf16[64,128]{1,0:T(8,128)(2,1)} %param.25, bf16[1,128]{1,0:T(2,128)(2,1)} %maximum_bitcast_fusion, bf16[1,128]{1,0:T(2,128)(2,1)} %reshape.78, bf16[1,128]{1,0:T(2,128)(2,1)} %reshape.79, bf16[1,128]{1,0:T(2,128)(2,1)} %reshape.80, bf16[2,128]{1,0:T(2,128)(2,1)} %bitcast.39, ...), dimensions={0} | concatenate | bytes 958464 | tf_op jit(solution)/shard_map/concatenate | solution.py:1249
  25.2 1.3 collective-permute-done.6.a3
  28.1 1.8 reduce_in.1
  30.2 1.1 collective-permute-done.8
  31.3 3.6 %collective-permute-start.11 = (f32[2,256]{1,0:T(2,128)S(1)}, f32[2,256]{1,0:T(2,128)S(1)}, u32[]{:S(2)}, u32[]{:S(2)}) collective-permute-start(f32[2,256]{1,0:T(2,128)S(1)} %add.39.sums_refs_0_), channel_id=1, source_target_pairs={{0,24},{1,25},{2,26},{3,27},{4,28},{5,29},{6,30},{7,31},{8,16},{9,... | collective-permute-start | bytes 6152 | tf_op jit(solution)/shard_map/ppermute | solution.py:1095
  36.7 2.7 %collective-permute-done.10.sums_refs_2_ = f32[2,256]{1,0:T(2,128)S(1)} collective-permute-done((f32[2,256]{1,0:T(2,128)S(1)}, f32[2,256]{1,0:T(2,128)S(1)}, u32[]{:S(2)}, u32[]{:S(2)}) %collective-permute-start.10) | collective-permute-done | bytes 2080 | tf_op jit(solution)/shard_map/ppermute | solution.py:1095
  39.4 1.6 collective-permute-start.27
  41.0 1.8 collective-permute-done.13.b3
  43.7 3.0 %conv_mid.1 = (bf16[3,976,256]{2,1,0:T(8,128)(2,1)S(1)}, f32[896,512]{1,0:T(8,128)S(1)}, f32[2,512]{1,0:T(2,128)S(1)}) custom-call(s32[4,8]{1,0:T(4,128)S(1)} %copy-done.1, f32[896,256]{1,0:T(8,128)S(1)} %get-tuple-element.115.pre_ref, f32[2,256]{1,0:T(2,128)S(1)} %add.39.sums_refs_0_, f32[2,256]{1,0:T(2,128)S(1)} %collective-permute-done.9.sums_refs_1_, ...), custom_call_target="tpu_custom_call" | custom-call | flops 1056964608 | bytes 5445760 | tf_op jit(solution)/shard_map/conv_mid/pallas_call | solution.py:149
  46.9 1.0 collective-permute-done.14
  48.0 2.7 %collective-permute-start.17 = (f32[2,512]{1,0:T(2,128)S(1)}, f32[2,512]{1,0:T(2,128)S(1)}, u32[]{:S(2)}, u32[]{:S(2)}) collective-permute-start(f32[2,512]{1,0:T(2,128)S(1)} %add.40.sums_refs_0_.mid_sums_refs_0_), channel_id=1, source_target_pairs={{0,24},{1,25},{2,26},{3,27},{4,28},{5,29},{6,30},{7,31},{8,16},{9,... | collective-permute-start | bytes 12296 | tf_op jit(solution)/shard_map/ppermute | solution.py:1095
  50.7 1.7 collective-permute-start.15
  52.4 4.6 %collective-permute-done.27.cot_odd_ref = bf16[2,784,256]{2,1,0:T(8,128)(2,1)S(1)} collective-permute-done((bf16[2,784,256]{2,1,0:T(8,128)(2,1)S(1)}, bf16[2,784,256]{2,1,0:T(8,128)(2,1)S(1)}, u32[]{:S(2)}, u32[]{:S(2)}) %collective-permute-start.27) | collective-permute-done | bytes 802848 | tf_op jit(solution)/shard_map/ppermute | solution.py:1095
  57.1 1.6 collective-permute-start.28
  58.8 2.1 %pool.1 = (f32[4,256]{1,0:T(4,128)S(1)}, f32[40,128]{1,0:T(8,128)S(1)}) custom-call(s32[4,8]{1,0:T(4,128)S(1)} %copy-done.1, f32[896,512]{1,0:T(8,128)S(1)} %get-tuple-element.123.mid_ref, f32[2,512]{1,0:T(2,128)S(1)} %add.40.sums_refs_0_.mid_sums_refs_0_, f32[2,512]{1,0:T(2,128)S(1)} %collective-permute-done.15.sums_refs_1_.mid_sums_refs_1_, ...), custom_call_target="tpu_custom_call" | custom-call | bytes 1945728 | tf_op jit(solution)/shard_map/pool/pallas_call | solution.py:149
  62.4 3.6 %collective-permute-start.21 = (f32[80,128]{1,0:T(8,128)S(1)}, f32[80,128]{1,0:T(8,128)S(1)}, u32[]{:S(2)}, u32[]{:S(2)}) collective-permute-start(f32[80,128]{1,0:T(8,128)S(1)} %constant_dynamic-update-slice_fusion.gathered_refs_0_), channel_id=1, source_target_pairs={{0,24},{1,25},{2,26},{3,27},{4,28},{5,29},{6,30},{7,31},{8,16},{9,... | collective-permute-start | bytes 122888 | tf_op jit(solution)/shard_map/ppermute | solution.py:1095
  68.3 2.6 %collective-permute-done.20.gathered_refs_2_ = f32[80,128]{1,0:T(8,128)S(1)} collective-permute-done((f32[80,128]{1,0:T(8,128)S(1)}, f32[80,128]{1,0:T(8,128)S(1)}, u32[]{:S(2)}, u32[]{:S(2)}) %collective-permute-start.20) | collective-permute-done | bytes 40992 | tf_op jit(solution)/shard_map/ppermute | solution.py:1095
  70.9 2.6 %attend.1 = (f32[2,4,128]{2,1,0:T(4,128)S(1)}, f32[4,512]{1,0:T(4,128)S(1)}, bf16[784,256]{1,0:T(8,128)(2,1)S(1)}, f32[4,784,256]{2,1,0:T(8,128)S(1)}, f32[8,256]{1,0:T(8,128)S(1)}) custom-call(s32[4,8]{1,0:T(4,128)S(1)} %copy-done.1, f32[80,128]{1,0:T(8,128)S(1)} %constant_dynamic-update-slice_fusion.gathered_refs_0_, ...), custom_call_target="tpu_custom_call" | custom-call | flops 411041792 | bytes 6327424 | tf_op jit(solution)/shard_map/attend/pallas_call | solution.py:149
  73.5 1.2 collective-permute-done.22
  74.7 2.0 %collective-permute-start.25 = (f32[8,256]{1,0:T(8,128)S(1)}, f32[8,256]{1,0:T(8,128)S(1)}, u32[]{:S(2)}, u32[]{:S(2)}) collective-permute-start(f32[8,256]{1,0:T(8,128)S(1)} %add.41.sums_refs_0_), channel_id=1, source_target_pairs={{0,24},{1,25},{2,26},{3,27},{4,28},{5,29},{6,30},{7,31},{8,16},{9,... | collective-permute-start | bytes 24584 | tf_op jit(solution)/shard_map/ppermute | solution.py:1095
  76.9 2.2 %collective-permute-start.23 = (f32[8,256]{1,0:T(8,128)S(1)}, f32[8,256]{1,0:T(8,128)S(1)}, u32[]{:S(2)}, u32[]{:S(2)}) collective-permute-start(f32[8,256]{1,0:T(8,128)S(1)} %add.41.sums_refs_0_), channel_id=1, source_target_pairs={{0,8},{1,9},{2,10},{3,11},{4,12},{5,13},{6,14},{7,15},{8,0},{9,1},... | collective-permute-start | bytes 24584 | tf_op jit(solution)/shard_map/ppermute | solution.py:1095
  79.1 1.2 collective-permute-done.25.sums_refs_3_
  81.3 4.5 %finish.1 = (bf16[2,784,256]{2,1,0:T(8,128)(2,1)S(1)}, bf16[2,784,256]{2,1,0:T(8,128)(2,1)S(1)}, f32[4,784,256]{2,1,0:T(8,128)S(1)}, f32[8,256]{1,0:T(8,128)S(1)}) custom-call(s32[4,8]{1,0:T(4,128)S(1)} %copy-done.1, f32[4,784,256]{2,1,0:T(8,128)S(1)} %get-tuple-element.132.out_ref, f32[8,256]{1,0:T(8,128)S(1)} %add.41.sums_refs_0_, ...), custom_call_target="tpu_custom_call" | custom-call | bytes 12091520 | tf_op jit(solution)/shard_map/finish/pallas_call | solution.py:149
  86.7 3.4 %collective-permute-start.30 = (bf16[2,784,256]{2,1,0:T(8,128)(2,1)S(1)}, bf16[2,784,256]{2,1,0:T(8,128)(2,1)S(1)}, u32[]{:S(2)}, u32[]{:S(2)}) collective-permute-start(bf16[2,784,256]{2,1,0:T(8,128)(2,1)S(1)} %get-tuple-element.140), channel_id=1, source_target_pairs={{0,1},{1,5},{2,3},{3,7},{4,0},{5,4},{6,2},{7,6},{8,9},{9,13},{10,1... | collective-permute-start | bytes 2408456 | tf_op jit(solution)/shard_map/ppermute | solution.py:1095
  90.2 1.9 collective-permute-done.31
  92.1 2.2 %collective-permute-start.34 = (f32[8,256]{1,0:T(8,128)S(1)}, f32[8,256]{1,0:T(8,128)S(1)}, u32[]{:S(2)}, u32[]{:S(2)}) collective-permute-start(f32[8,256]{1,0:T(8,128)S(1)} %add.42.back_refs_0_.out_back_refs_0_), channel_id=1, source_target_pairs={{0,24},{1,25},{2,26},{3,27},{4,28},{5,29},{6,30},{7,31},{8,16},{9,... | collective-permute-start | bytes 24584 | tf_op jit(solution)/shard_map/ppermute | solution.py:1095
  95.2 1.3 collective-permute-start.32
  96.5 1.1 collective-permute-done.34.back_refs_3_.out_back_refs_3_
  97.5 1.4 collective-permute-done.33.back_refs_2_.out_back_refs_2_
  98.9 4.6 %back_out.1 = (bf16[4,784,256]{2,1,0:T(8,128)(2,1)S(1)}, f32[896,256]{1,0:T(8,128)S(1)}, f32[4,512]{1,0:T(4,128)S(1)}, f32[12,128]{1,0:T(8,128)S(1)}) custom-call(s32[4,8]{1,0:T(4,128)S(1)} %copy-done.1, f32[4,784,256]{2,1,0:T(8,128)S(1)} %get-tuple-element.141.grad_ref, f32[4,784,256]{2,1,0:T(8,128)S(1)} %get-tuple-element.132.out_ref, ...), custom_call_target="tpu_custom_call" | custom-call | flops 411041792 | bytes 11556992 | tf_op jit(solution)/shard_map/back_out/pallas_call | solution.py:149
  103.6 1.1 collective-permute-done.35
  104.8 1.8 collective-permute-start.38
  107.5 1.7 collective-permute-start.36
  109.2 1.6 weight_out_term.1
  111.9 5.2 %back_mid.1 = (bf16[976,512]{1,0:T(8,128)(2,1)S(1)}, f32[896,256]{1,0:T(8,128)S(1)}, f32[4,128]{1,0:T(4,128)S(1)}, f32[8,512]{1,0:T(8,128)S(1)}, f32[2,256]{1,0:T(2,128)S(1)}) custom-call(s32[4,8]{1,0:T(4,128)S(1)} %copy-done.1, f32[16,128]{1,0:T(8,128)S(1)} %pad_maximum_fusion.4.back_refs_0_, f32[16,128]{1,0:T(8,128)S(1)} %collective-permute-done.36.back_refs_1_, ...), custom_call_target="tpu_custom_call" | custom-call | flops 1056964608 | bytes 7105664 | tf_op jit(solution)/shard_map/back_mid/pallas_call | solution.py:149
  117.2 1.1 collective-permute-done.40
  118.4 2.1 %collective-permute-start.43 = (f32[2,256]{1,0:T(2,128)S(1)}, f32[2,256]{1,0:T(2,128)S(1)}, u32[]{:S(2)}, u32[]{:S(2)}) collective-permute-start(f32[2,256]{1,0:T(2,128)S(1)} %add.44.back_refs_0_), channel_id=1, source_target_pairs={{0,24},{1,25},{2,26},{3,27},{4,28},{5,29},{6,30},{7,31},{8,16},{9,... | collective-permute-start | bytes 6152 | tf_op jit(solution)/shard_map/ppermute | solution.py:1095
  121.5 1.3 collective-permute-start.41
  123.8 1.2 collective-permute-done.42.back_refs_2_
  125.1 2.2 %back_in.1 = (bf16[784,256]{1,0:T(8,128)(2,1)S(1)}, bf16[2,592,128]{2,1,0:T(8,128)(2,1)S(1)}, bf16[2,592,128]{2,1,0:T(8,128)(2,1)S(1)}) custom-call(s32[4,8]{1,0:T(4,128)S(1)} %copy-done.1, f32[896,256]{1,0:T(8,128)S(1)} %get-tuple-element.160.grad_ref, f32[896,256]{1,0:T(8,128)S(1)} %get-tuple-element.115.pre_ref, f32[2,256]{1,0:T(2,128)S(1)} %add.39.sums_refs_0_, ...), custom_call_target="tpu_custom_call" | custom-call | flops 411041792 | bytes 4685952 | tf_op jit(solution)/shard_map/back_in/pallas_call | solution.py:149
  127.3 2.2 %weight_mid_term.1 = (bf16[2,1152,128]{2,1,0:T(8,128)(2,1)S(1)}, bf16[2,1152,128]{2,1,0:T(8,128)(2,1)S(1)}) custom-call(s32[4,8]{1,0:T(4,128)S(1)} %copy-done.1, bf16[3,976,256]{2,1,0:T(8,128)(2,1)S(1)} %get-tuple-element.174.taps_ref, bf16[976,512]{1,0:T(8,128)(2,1)S(1)} %get-tuple-element.175.low_ref), custom_call_target="tpu_custom_call" | custom-call | flops 1056964608 | bytes 3678336 | tf_op jit(solution)/shard_map/weight_mid_term/pallas_call | solution.py:149
  130.7 2.0 %collective-permute-done.44.arrived_refs_0_ = bf16[2,656,128]{2,1,0:T(8,128)(2,1)S(1)} collective-permute-done((bf16[2,656,128]{2,1,0:T(8,128)(2,1)S(1)}, bf16[2,656,128]{2,1,0:T(8,128)(2,1)S(1)}, u32[]{:S(2)}, u32[]{:S(2)}) %collective-permute-start.44) | collective-permute-done | bytes 335904 | tf_op jit(solution)/shard_map/ppermute | solution.py:1095
  135.5 4.3 %finish_owned.1 = (bf16[4,784,256]{2,1,0:T(8,128)(2,1)}, bf16[4,784,256]{2,1,0:T(8,128)(2,1)S(1)}) custom-call(s32[4,8]{1,0:T(4,128)S(1)} %copy-done.1, bf16[2,784,256]{2,1,0:T(8,128)(2,1)S(1)} %collective-permute-done.29.even_ref, bf16[2,784,256]{2,1,0:T(8,128)(2,1)S(1)} %collective-permute-done.30.odd_ref, ...), custom_call_target="tpu_custom_call" | custom-call | bytes 7225472 | tf_op jit(solution)/shard_map/finish_owned/pallas_call | solution.py:149
  139.8 3.3 %collective-permute-done.46.arrived_ref = bf16[1280,128]{1,0:T(8,128)(2,1)S(1)} collective-permute-done((bf16[1280,128]{1,0:T(8,128)(2,1)S(1)}, bf16[1280,128]{1,0:T(8,128)(2,1)S(1)}, u32[]{:S(2)}, u32[]{:S(2)}) %collective-permute-start.46) | collective-permute-done | bytes 327712 | tf_op jit(solution)/shard_map/ppermute | solution.py:1095
  145.2 4.0 %collective-permute-done.47.arrived_refs_1_ = bf16[640,128]{1,0:T(8,128)(2,1)S(1)} collective-permute-done((bf16[640,128]{1,0:T(8,128)(2,1)S(1)}, bf16[640,128]{1,0:T(8,128)(2,1)S(1)}, u32[]{:S(2)}, u32[]{:S(2)}) %collective-permute-start.47) | collective-permute-done | bytes 163872 | tf_op jit(solution)/shard_map/ppermute | solution.py:1095
  151.8 1.5 collective-permute-start.53
  153.3 1.1 collective-permute-start.54
  154.4 1.9 collective-permute-start.55
  156.3 3.1 %collective-permute-done.54.arrived_refs_1_ = bf16[304,128]{1,0:T(8,128)(2,1)S(1)} collective-permute-done((bf16[304,128]{1,0:T(8,128)(2,1)S(1)}, bf16[304,128]{1,0:T(8,128)(2,1)S(1)}, u32[]{:S(2)}, u32[]{:S(2)}) %collective-permute-start.54) | collective-permute-done | bytes 77856 | tf_op jit(solution)/shard_map/ppermute | solution.py:1095
  159.4 1.3 collective-permute-done.55.arrived_refs_2_
  160.8 1.9 %collective-permute-start.58 = (bf16[304,128]{1,0:T(8,128)(2,1)S(1)}, bf16[304,128]{1,0:T(8,128)(2,1)S(1)}, u32[]{:S(2)}, u32[]{:S(2)}) collective-permute-start(bf16[304,128]{1,0:T(8,128)(2,1)S(1)} %add_depth.1.piece_refs_0_), channel_id=1, source_target_pairs={{0,24},{1,25},{2,26},{3,27},{4,28},{5,29},{6,30},{7,31},{8,16},{9,... | collective-permute-start | bytes 233480 | tf_op jit(solution)/shard_map/ppermute | solution.py:1095
  163.2 2.0 %collective-permute-start.56 = (bf16[304,128]{1,0:T(8,128)(2,1)S(1)}, bf16[304,128]{1,0:T(8,128)(2,1)S(1)}, u32[]{:S(2)}, u32[]{:S(2)}) collective-permute-start(bf16[304,128]{1,0:T(8,128)(2,1)S(1)} %add_depth.1.piece_refs_0_), channel_id=1, source_target_pairs={{0,8},{1,9},{2,10},{3,11},{4,12},{5,13},{6,14},{7,15},{8,0},{9,1},... | collective-permute-start | bytes 233480 | tf_op jit(solution)/shard_map/ppermute | solution.py:1095
  165.2 2.4 %collective-permute-done.58.piece_refs_3_ = bf16[304,128]{1,0:T(8,128)(2,1)S(1)} collective-permute-done((bf16[304,128]{1,0:T(8,128)(2,1)S(1)}, bf16[304,128]{1,0:T(8,128)(2,1)S(1)}, u32[]{:S(2)}, u32[]{:S(2)}) %collective-permute-start.58) | collective-permute-done | bytes 77856 | tf_op jit(solution)/shard_map/ppermute | solution.py:1095
  167.6 3.7 %collective-permute-done.57.piece_refs_2_ = bf16[304,128]{1,0:T(8,128)(2,1)S(1)} collective-permute-done((bf16[304,128]{1,0:T(8,128)(2,1)S(1)}, bf16[304,128]{1,0:T(8,128)(2,1)S(1)}, u32[]{:S(2)}, u32[]{:S(2)}) %collective-permute-start.57) | collective-permute-done | bytes 77856 | tf_op jit(solution)/shard_map/ppermute | solution.py:1095
  171.3 5.9 %collective-permute-start.59 = (bf16[784,256]{1,0:T(8,128)(2,1)S(1)}, bf16[784,256]{1,0:T(8,128)(2,1)S(1)}, u32[]{:S(2)}, u32[]{:S(2)}) collective-permute-start(bf16[784,256]{1,0:T(8,128)(2,1)S(1)} %collective-permute-done.51.low_refs_0_), channel_id=1, source_target_pairs={{0,1},{1,0},{2,3},{3,2},{4,5},{5,4},{6,7},{7,6},{8,9},{9,8},{10,11... | collective-permute-start | bytes 1204232 | tf_op jit(solution)/shard_map/ppermute | solution.py:1095
  177.8 2.0 %collective-permute-start.61 = (bf16[1216,128]{1,0:T(8,128)(2,1)S(1)}, bf16[1216,128]{1,0:T(8,128)(2,1)S(1)}, u32[]{:S(2)}, u32[]{:S(2)}) collective-permute-start(bf16[1216,128]{1,0:T(8,128)(2,1)S(1)} %join_depth.1.term_refs_0_), channel_id=1, source_target_pairs={{0,4},{1,5},{2,6},{3,7},{4,0},{5,1},{6,2},{7,3},{8,12},{9,13},{10,... | collective-permute-start | bytes 933896 | tf_op jit(solution)/shard_map/ppermute | solution.py:1095
  179.9 1.9 grad_owned.1
  181.7 5.9 %collective-permute-done.61.term_refs_1_ = bf16[1216,128]{1,0:T(8,128)(2,1)S(1)} collective-permute-done((bf16[1216,128]{1,0:T(8,128)(2,1)S(1)}, bf16[1216,128]{1,0:T(8,128)(2,1)S(1)}, u32[]{:S(2)}, u32[]{:S(2)}) %collective-permute-start.61) | collective-permute-done | bytes 311328 | tf_op jit(solution)/shard_map/ppermute | solution.py:1095
  187.6 1.7 unpack.1
  (140 shorter events, 30.8 us)
Async XLA Ops:
  0.7 24.4 %collective-permute-start.5 = (bf16[64,1024]{1,0:T(8,128)(2,1)}, bf16[64,1024]{1,0:T(8,128)(2,1)S(1)}, u32[]{:S(2)}, u32[]{:S(2)}) collective-permute-start(bf16[64,1024]{1,0:T(8,128)(2,1)} %bitcast.34), channel_id=1, source_target_pairs={{0,2},{1,3},{2,0},{3,1},{4,6},{5,7},{6,4},{7,5},{8,10},{9,11},{10,... | collective-permute-start | bytes 393224 | tf_op jit(solution)/shard_map/ppermute | solution.py:1095
  3.7 5.2 %collective-permute-start = (bf16[64,1024]{1,0:T(8,128)(2,1)}, bf16[64,1024]{1,0:T(8,128)(2,1)S(1)}, u32[]{:S(2)}, u32[]{:S(2)}) collective-permute-start(bf16[64,1024]{1,0:T(8,128)(2,1)} %bitcast.35), channel_id=1, source_target_pairs={{0,1},{1,0},{2,3},{3,2},{4,5},{5,4},{6,7},{7,6},{8,9},{9,8},{10,11... | collective-permute-start | bytes 393224 | tf_op jit(solution)/shard_map/ppermute | solution.py:1095
  5.9 21.2 %copy-start.1 = (s32[4,8]{1,0:T(4,128)S(1)}, s32[4,8]{1,0:T(4,128)}, u32[]{:S(2)}) copy-start(s32[4,8]{1,0:T(4,128)} %counts_ref.35) | copy-start | bytes 388
  5.9 21.2 %copy-start.2 = (bf16[1024,64]{0,1:T(8,128)(2,1)S(1)}, bf16[1024,64]{0,1:T(8,128)(2,1)}, u32[]{:S(2)}) copy-start(bf16[1024,64]{0,1:T(8,128)(2,1)} %param.19) | copy-start | bytes 393220
  5.9 20.7 %collective-permute-start.4 = (bf16[784,256]{1,0:T(8,128)(2,1)}, bf16[784,256]{1,0:T(8,128)(2,1)S(1)}, u32[]{:S(2)}, u32[]{:S(2)}) collective-permute-start(bf16[784,256]{1,0:T(8,128)(2,1)} %get-tuple-element.214), channel_id=1, source_target_pairs={{0,6},{1,2},{2,4},{3,0},{4,7},{5,3},{6,5},{7,1},{8,14},{9,10},{10,... | collective-permute-start | bytes 1204232 | tf_op jit(solution)/shard_map/ppermute | solution.py:1095
  7.3 19.3 %collective-permute-start.3 = (bf16[784,256]{1,0:T(8,128)(2,1)}, bf16[784,256]{1,0:T(8,128)(2,1)S(1)}, u32[]{:S(2)}, u32[]{:S(2)}) collective-permute-start(bf16[784,256]{1,0:T(8,128)(2,1)} %get-tuple-element.215), channel_id=1, source_target_pairs={{0,2},{1,6},{2,0},{3,4},{4,3},{5,7},{6,1},{7,5},{8,10},{9,14},{10,... | collective-permute-start | bytes 1204232 | tf_op jit(solution)/shard_map/ppermute | solution.py:1095
  9.8 17.3 %collective-permute-start.2 = (bf16[784,256]{1,0:T(8,128)(2,1)}, bf16[784,256]{1,0:T(8,128)(2,1)S(1)}, u32[]{:S(2)}, u32[]{:S(2)}) collective-permute-start(bf16[784,256]{1,0:T(8,128)(2,1)} %get-tuple-element.216), channel_id=1, source_target_pairs={{0,4},{1,0},{2,6},{3,2},{4,5},{5,1},{6,7},{7,3},{8,12},{9,8},{10,1... | collective-permute-start | bytes 1204232 | tf_op jit(solution)/shard_map/ppermute | solution.py:1095
  10.1 17.1 %collective-permute-start.1 = (bf16[784,256]{1,0:T(8,128)(2,1)}, bf16[784,256]{1,0:T(8,128)(2,1)}, u32[]{:S(2)}, u32[]{:S(2)}) collective-permute-start(bf16[784,256]{1,0:T(8,128)(2,1)} %get-tuple-element.217), channel_id=1, source_target_pairs={{0,0},{1,4},{2,2},{3,6},{4,1},{5,5},{6,3},{7,7},{8,8},{9,12},{10,1... | collective-permute-start | bytes 1204232 | tf_op jit(solution)/shard_map/ppermute | solution.py:1095
  25.1 1.4 collective-permute-start.6
  26.5 3.6 %collective-permute-start.7 = (bf16[1872,128]{1,0:T(8,128)(2,1)S(1)}, bf16[1872,128]{1,0:T(8,128)(2,1)S(1)}, u32[]{:S(2)}, u32[]{:S(2)}) collective-permute-start(bf16[1872,128]{1,0:T(8,128)(2,1)S(1)} %concatenate.13.b0), channel_id=1, source_target_pairs={{0,1},{1,0},{2,3},{3,2},{4,5},{5,4},{6,7},{7,6},{8,9},{9,8},{10,11... | collective-permute-start | bytes 1437704 | tf_op jit(solution)/shard_map/ppermute | solution.py:1095
  26.7 14.3 %collective-permute-start.12 = (bf16[1872,128]{1,0:T(8,128)(2,1)S(1)}, bf16[1872,128]{1,0:T(8,128)(2,1)S(1)}, u32[]{:S(2)}, u32[]{:S(2)}) collective-permute-start(bf16[1872,128]{1,0:T(8,128)(2,1)S(1)} %concatenate.13.b0), channel_id=1, source_target_pairs={{0,2},{1,3},{2,0},{3,1},{4,6},{5,7},{6,4},{7,5},{8,10},{9,11},{10,... | collective-permute-start | bytes 1437704 | tf_op jit(solution)/shard_map/ppermute | solution.py:1095
  30.1 1.2 collective-permute-start.8
  31.3 5.4 %collective-permute-start.11 = (f32[2,256]{1,0:T(2,128)S(1)}, f32[2,256]{1,0:T(2,128)S(1)}, u32[]{:S(2)}, u32[]{:S(2)}) collective-permute-start(f32[2,256]{1,0:T(2,128)S(1)} %add.39.sums_refs_0_), channel_id=1, source_target_pairs={{0,24},{1,25},{2,26},{3,27},{4,28},{5,29},{6,30},{7,31},{8,16},{9,... | collective-permute-start | bytes 6152 | tf_op jit(solution)/shard_map/ppermute | solution.py:1095
  34.9 4.5 %collective-permute-start.10 = (f32[2,256]{1,0:T(2,128)S(1)}, f32[2,256]{1,0:T(2,128)S(1)}, u32[]{:S(2)}, u32[]{:S(2)}) collective-permute-start(f32[2,256]{1,0:T(2,128)S(1)} %add.39.sums_refs_0_), channel_id=1, source_target_pairs={{0,16},{1,17},{2,18},{3,19},{4,20},{5,21},{6,22},{7,23},{8,24},{9,... | collective-permute-start | bytes 6152 | tf_op jit(solution)/shard_map/ppermute | solution.py:1095
  34.9 4.5 %collective-permute-start.9 = (f32[2,256]{1,0:T(2,128)S(1)}, f32[2,256]{1,0:T(2,128)S(1)}, u32[]{:S(2)}, u32[]{:S(2)}) collective-permute-start(f32[2,256]{1,0:T(2,128)S(1)} %add.39.sums_refs_0_), channel_id=1, source_target_pairs={{0,8},{1,9},{2,10},{3,11},{4,12},{5,13},{6,14},{7,15},{8,0},{9,1},... | collective-permute-start | bytes 6152 | tf_op jit(solution)/shard_map/ppermute | solution.py:1095
  35.8 16.6 %collective-permute-start.26 = (bf16[2,784,256]{2,1,0:T(8,128)(2,1)S(1)}, bf16[2,784,256]{2,1,0:T(8,128)(2,1)S(1)}, u32[]{:S(2)}, u32[]{:S(2)}) collective-permute-start(bf16[2,784,256]{2,1,0:T(8,128)(2,1)S(1)} %pad_maximum_fusion.1), channel_id=1, source_target_pairs={{0,0},{1,4},{2,2},{3,6},{4,1},{5,5},{6,3},{7,7},{8,8},{9,12},{10,1... | collective-permute-start | bytes 2408456 | tf_op jit(solution)/shard_map/ppermute | solution.py:1095
  39.4 17.5 %collective-permute-start.27 = (bf16[2,784,256]{2,1,0:T(8,128)(2,1)S(1)}, bf16[2,784,256]{2,1,0:T(8,128)(2,1)S(1)}, u32[]{:S(2)}, u32[]{:S(2)}) collective-permute-start(bf16[2,784,256]{2,1,0:T(8,128)(2,1)S(1)} %pad_maximum_fusion), channel_id=1, source_target_pairs={{0,4},{1,0},{2,6},{3,2},{4,5},{5,1},{6,7},{7,3},{8,12},{9,8},{10,1... | collective-permute-start | bytes 2408456 | tf_op jit(solution)/shard_map/ppermute | solution.py:1095
  41.0 1.8 collective-permute-start.13
  46.8 1.2 collective-permute-start.14
  48.0 9.0 %collective-permute-start.17 = (f32[2,512]{1,0:T(2,128)S(1)}, f32[2,512]{1,0:T(2,128)S(1)}, u32[]{:S(2)}, u32[]{:S(2)}) collective-permute-start(f32[2,512]{1,0:T(2,128)S(1)} %add.40.sums_refs_0_.mid_sums_refs_0_), channel_id=1, source_target_pairs={{0,24},{1,25},{2,26},{3,27},{4,28},{5,29},{6,30},{7,31},{8,16},{9,... | collective-permute-start | bytes 12296 | tf_op jit(solution)/shard_map/ppermute | solution.py:1095
  50.7 6.3 %collective-permute-start.16 = (f32[2,512]{1,0:T(2,128)S(1)}, f32[2,512]{1,0:T(2,128)S(1)}, u32[]{:S(2)}, u32[]{:S(2)}) collective-permute-start(f32[2,512]{1,0:T(2,128)S(1)} %add.40.sums_refs_0_.mid_sums_refs_0_), channel_id=1, source_target_pairs={{0,16},{1,17},{2,18},{3,19},{4,20},{5,21},{6,22},{7,23},{8,24},{9,... | collective-permute-start | bytes 12296 | tf_op jit(solution)/shard_map/ppermute | solution.py:1095
  50.7 6.3 %collective-permute-start.15 = (f32[2,512]{1,0:T(2,128)S(1)}, f32[2,512]{1,0:T(2,128)S(1)}, u32[]{:S(2)}, u32[]{:S(2)}) collective-permute-start(f32[2,512]{1,0:T(2,128)S(1)} %add.40.sums_refs_0_.mid_sums_refs_0_), channel_id=1, source_target_pairs={{0,8},{1,9},{2,10},{3,11},{4,12},{5,13},{6,14},{7,15},{8,0},{9,1},... | collective-permute-start | bytes 12296 | tf_op jit(solution)/shard_map/ppermute | solution.py:1095
  57.1 24.1 %collective-permute-start.28 = (bf16[2,784,256]{2,1,0:T(8,128)(2,1)S(1)}, bf16[2,784,256]{2,1,0:T(8,128)(2,1)S(1)}, u32[]{:S(2)}, u32[]{:S(2)}) collective-permute-start(bf16[2,784,256]{2,1,0:T(8,128)(2,1)S(1)} %pad_maximum_fusion.2), channel_id=1, source_target_pairs={{0,2},{1,3},{2,0},{3,1},{4,6},{5,7},{6,4},{7,5},{8,10},{9,11},{10,... | collective-permute-start | bytes 2408456 | tf_op jit(solution)/shard_map/ppermute | solution.py:1095
  60.9 1.5 collective-permute-start.18
  62.4 5.9 %collective-permute-start.21 = (f32[80,128]{1,0:T(8,128)S(1)}, f32[80,128]{1,0:T(8,128)S(1)}, u32[]{:S(2)}, u32[]{:S(2)}) collective-permute-start(f32[80,128]{1,0:T(8,128)S(1)} %constant_dynamic-update-slice_fusion.gathered_refs_0_), channel_id=1, source_target_pairs={{0,24},{1,25},{2,26},{3,27},{4,28},{5,29},{6,30},{7,31},{8,16},{9,... | collective-permute-start | bytes 122888 | tf_op jit(solution)/shard_map/ppermute | solution.py:1095
  66.0 4.9 %collective-permute-start.20 = (f32[80,128]{1,0:T(8,128)S(1)}, f32[80,128]{1,0:T(8,128)S(1)}, u32[]{:S(2)}, u32[]{:S(2)}) collective-permute-start(f32[80,128]{1,0:T(8,128)S(1)} %constant_dynamic-update-slice_fusion.gathered_refs_0_), channel_id=1, source_target_pairs={{0,16},{1,17},{2,18},{3,19},{4,20},{5,21},{6,22},{7,23},{8,24},{9,... | collective-permute-start | bytes 122888 | tf_op jit(solution)/shard_map/ppermute | solution.py:1095
  66.0 4.9 %collective-permute-start.19 = (f32[80,128]{1,0:T(8,128)S(1)}, f32[80,128]{1,0:T(8,128)S(1)}, u32[]{:S(2)}, u32[]{:S(2)}) collective-permute-start(f32[80,128]{1,0:T(8,128)S(1)} %constant_dynamic-update-slice_fusion.gathered_refs_0_), channel_id=1, source_target_pairs={{0,8},{1,9},{2,10},{3,11},{4,12},{5,13},{6,14},{7,15},{8,0},{9,1},... | collective-permute-start | bytes 122888 | tf_op jit(solution)/shard_map/ppermute | solution.py:1095
  73.5 1.2 collective-permute-start.22
  74.7 5.6 %collective-permute-start.25 = (f32[8,256]{1,0:T(8,128)S(1)}, f32[8,256]{1,0:T(8,128)S(1)}, u32[]{:S(2)}, u32[]{:S(2)}) collective-permute-start(f32[8,256]{1,0:T(8,128)S(1)} %add.41.sums_refs_0_), channel_id=1, source_target_pairs={{0,24},{1,25},{2,26},{3,27},{4,28},{5,29},{6,30},{7,31},{8,16},{9,... | collective-permute-start | bytes 24584 | tf_op jit(solution)/shard_map/ppermute | solution.py:1095
  76.7 4.6 %collective-permute-start.24 = (f32[8,256]{1,0:T(8,128)S(1)}, f32[8,256]{1,0:T(8,128)S(1)}, u32[]{:S(2)}, u32[]{:S(2)}) collective-permute-start(f32[8,256]{1,0:T(8,128)S(1)} %add.41.sums_refs_0_), channel_id=1, source_target_pairs={{0,16},{1,17},{2,18},{3,19},{4,20},{5,21},{6,22},{7,23},{8,24},{9,... | collective-permute-start | bytes 24584 | tf_op jit(solution)/shard_map/ppermute | solution.py:1095
  76.9 4.4 %collective-permute-start.23 = (f32[8,256]{1,0:T(8,128)S(1)}, f32[8,256]{1,0:T(8,128)S(1)}, u32[]{:S(2)}, u32[]{:S(2)}) collective-permute-start(f32[8,256]{1,0:T(8,128)S(1)} %add.41.sums_refs_0_), channel_id=1, source_target_pairs={{0,8},{1,9},{2,10},{3,11},{4,12},{5,13},{6,14},{7,15},{8,0},{9,1},... | collective-permute-start | bytes 24584 | tf_op jit(solution)/shard_map/ppermute | solution.py:1095
  85.8 25.4 %collective-permute-start.29 = (bf16[2,784,256]{2,1,0:T(8,128)(2,1)S(1)}, bf16[2,784,256]{2,1,0:T(8,128)(2,1)S(1)}, u32[]{:S(2)}, u32[]{:S(2)}) collective-permute-start(bf16[2,784,256]{2,1,0:T(8,128)(2,1)S(1)} %get-tuple-element.139), channel_id=1, source_target_pairs={{0,0},{1,4},{2,2},{3,6},{4,1},{5,5},{6,3},{7,7},{8,8},{9,12},{10,1... | collective-permute-start | bytes 2408456 | tf_op jit(solution)/shard_map/ppermute | solution.py:1095
  86.7 24.5 %collective-permute-start.30 = (bf16[2,784,256]{2,1,0:T(8,128)(2,1)S(1)}, bf16[2,784,256]{2,1,0:T(8,128)(2,1)S(1)}, u32[]{:S(2)}, u32[]{:S(2)}) collective-permute-start(bf16[2,784,256]{2,1,0:T(8,128)(2,1)S(1)} %get-tuple-element.140), channel_id=1, source_target_pairs={{0,1},{1,5},{2,3},{3,7},{4,0},{5,4},{6,2},{7,6},{8,9},{9,13},{10,1... | collective-permute-start | bytes 2408456 | tf_op jit(solution)/shard_map/ppermute | solution.py:1095
  90.1 1.9 %collective-permute-start.31 = (f32[8,256]{1,0:T(8,128)S(1)}, f32[8,256]{1,0:T(8,128)S(1)}, u32[]{:S(2)}, u32[]{:S(2)}) collective-permute-start(f32[8,256]{1,0:T(8,128)S(1)} %get-tuple-element.142), channel_id=1, source_target_pairs={{0,1},{1,0},{2,3},{3,2},{4,5},{5,4},{6,7},{7,6},{8,9},{9,8},{10,11... | collective-permute-start | bytes 24584 | tf_op jit(solution)/shard_map/ppermute | solution.py:1095
  92.1 5.5 %collective-permute-start.34 = (f32[8,256]{1,0:T(8,128)S(1)}, f32[8,256]{1,0:T(8,128)S(1)}, u32[]{:S(2)}, u32[]{:S(2)}) collective-permute-start(f32[8,256]{1,0:T(8,128)S(1)} %add.42.back_refs_0_.out_back_refs_0_), channel_id=1, source_target_pairs={{0,24},{1,25},{2,26},{3,27},{4,28},{5,29},{6,30},{7,31},{8,16},{9,... | collective-permute-start | bytes 24584 | tf_op jit(solution)/shard_map/ppermute | solution.py:1095
  94.3 4.6 %collective-permute-start.33 = (f32[8,256]{1,0:T(8,128)S(1)}, f32[8,256]{1,0:T(8,128)S(1)}, u32[]{:S(2)}, u32[]{:S(2)}) collective-permute-start(f32[8,256]{1,0:T(8,128)S(1)} %add.42.back_refs_0_.out_back_refs_0_), channel_id=1, source_target_pairs={{0,16},{1,17},{2,18},{3,19},{4,20},{5,21},{6,22},{7,23},{8,24},{9,... | collective-permute-start | bytes 24584 | tf_op jit(solution)/shard_map/ppermute | solution.py:1095
  95.2 3.7 %collective-permute-start.32 = (f32[8,256]{1,0:T(8,128)S(1)}, f32[8,256]{1,0:T(8,128)S(1)}, u32[]{:S(2)}, u32[]{:S(2)}) collective-permute-start(f32[8,256]{1,0:T(8,128)S(1)} %add.42.back_refs_0_.out_back_refs_0_), channel_id=1, source_target_pairs={{0,8},{1,9},{2,10},{3,11},{4,12},{5,13},{6,14},{7,15},{8,0},{9,1},... | collective-permute-start | bytes 24584 | tf_op jit(solution)/shard_map/ppermute | solution.py:1095
  103.5 1.2 collective-permute-start.35
  104.8 6.0 %collective-permute-start.38 = (f32[16,128]{1,0:T(8,128)S(1)}, f32[16,128]{1,0:T(8,128)S(1)}, u32[]{:S(2)}, u32[]{:S(2)}) collective-permute-start(f32[16,128]{1,0:T(8,128)S(1)} %pad_maximum_fusion.4.back_refs_0_), channel_id=1, source_target_pairs={{0,24},{1,25},{2,26},{3,27},{4,28},{5,29},{6,30},{7,31},{8,16},{9,... | collective-permute-start | bytes 24584 | tf_op jit(solution)/shard_map/ppermute | solution.py:1095
  106.6 4.6 %collective-permute-start.37 = (f32[16,128]{1,0:T(8,128)S(1)}, f32[16,128]{1,0:T(8,128)S(1)}, u32[]{:S(2)}, u32[]{:S(2)}) collective-permute-start(f32[16,128]{1,0:T(8,128)S(1)} %pad_maximum_fusion.4.back_refs_0_), channel_id=1, source_target_pairs={{0,16},{1,17},{2,18},{3,19},{4,20},{5,21},{6,22},{7,23},{8,24},{9,... | collective-permute-start | bytes 24584 | tf_op jit(solution)/shard_map/ppermute | solution.py:1095
  107.5 3.7 %collective-permute-start.36 = (f32[16,128]{1,0:T(8,128)S(1)}, f32[16,128]{1,0:T(8,128)S(1)}, u32[]{:S(2)}, u32[]{:S(2)}) collective-permute-start(f32[16,128]{1,0:T(8,128)S(1)} %pad_maximum_fusion.4.back_refs_0_), channel_id=1, source_target_pairs={{0,8},{1,9},{2,10},{3,11},{4,12},{5,13},{6,14},{7,15},{8,0},{9,1},... | collective-permute-start | bytes 24584 | tf_op jit(solution)/shard_map/ppermute | solution.py:1095
  111.4 18.8 %collective-permute-start.39 = (bf16[2,784,256]{2,1,0:T(8,128)(2,1)S(1)}, bf16[2,784,256]{2,1,0:T(8,128)(2,1)S(1)}, u32[]{:S(2)}, u32[]{:S(2)}) collective-permute-start(bf16[2,784,256]{2,1,0:T(8,128)(2,1)S(1)} %pad_maximum_fusion.3), channel_id=1, source_target_pairs={{0,2},{1,3},{2,0},{3,1},{4,6},{5,7},{6,4},{7,5},{8,10},{9,11},{10,... | collective-permute-start | bytes 2408456 | tf_op jit(solution)/shard_map/ppermute | solution.py:1095
  117.2 1.2 collective-permute-start.40
  118.4 5.4 %collective-permute-start.43 = (f32[2,256]{1,0:T(2,128)S(1)}, f32[2,256]{1,0:T(2,128)S(1)}, u32[]{:S(2)}, u32[]{:S(2)}) collective-permute-start(f32[2,256]{1,0:T(2,128)S(1)} %add.44.back_refs_0_), channel_id=1, source_target_pairs={{0,24},{1,25},{2,26},{3,27},{4,28},{5,29},{6,30},{7,31},{8,16},{9,... | collective-permute-start | bytes 6152 | tf_op jit(solution)/shard_map/ppermute | solution.py:1095
  120.5 4.5 %collective-permute-start.42 = (f32[2,256]{1,0:T(2,128)S(1)}, f32[2,256]{1,0:T(2,128)S(1)}, u32[]{:S(2)}, u32[]{:S(2)}) collective-permute-start(f32[2,256]{1,0:T(2,128)S(1)} %add.44.back_refs_0_), channel_id=1, source_target_pairs={{0,16},{1,17},{2,18},{3,19},{4,20},{5,21},{6,22},{7,23},{8,24},{9,... | collective-permute-start | bytes 6152 | tf_op jit(solution)/shard_map/ppermute | solution.py:1095
  121.5 3.6 %collective-permute-start.41 = (f32[2,256]{1,0:T(2,128)S(1)}, f32[2,256]{1,0:T(2,128)S(1)}, u32[]{:S(2)}, u32[]{:S(2)}) collective-permute-start(f32[2,256]{1,0:T(2,128)S(1)} %add.44.back_refs_0_), channel_id=1, source_target_pairs={{0,8},{1,9},{2,10},{3,11},{4,12},{5,13},{6,14},{7,15},{8,0},{9,1},... | collective-permute-start | bytes 6152 | tf_op jit(solution)/shard_map/ppermute | solution.py:1095
  130.2 4.1 %collective-permute-start.48 = (bf16[2,1152,128]{2,1,0:T(8,128)(2,1)S(1)}, bf16[2,1152,128]{2,1,0:T(8,128)(2,1)S(1)}, u32[]{:S(2)}, u32[]{:S(2)}) collective-permute-start(bf16[2,1152,128]{2,1,0:T(8,128)(2,1)S(1)} %get-tuple-element.178), channel_id=1, source_target_pairs={{0,1},{1,0},{2,3},{3,2},{4,5},{5,4},{6,7},{7,6},{8,9},{9,8},{10,11... | collective-permute-start | bytes 1769480 | tf_op jit(solution)/shard_map/ppermute | solution.py:1095
  130.2 2.5 %collective-permute-start.44 = (bf16[2,656,128]{2,1,0:T(8,128)(2,1)S(1)}, bf16[2,656,128]{2,1,0:T(8,128)(2,1)S(1)}, u32[]{:S(2)}, u32[]{:S(2)}) collective-permute-start(bf16[2,656,128]{2,1,0:T(8,128)(2,1)S(1)} %get-tuple-element.167), channel_id=1, source_target_pairs={{0,1},{1,0},{2,3},{3,2},{4,5},{5,4},{6,7},{7,6},{8,9},{9,8},{10,11... | collective-permute-start | bytes 1007624 | tf_op jit(solution)/shard_map/ppermute | solution.py:1095
  130.7 2.4 %collective-permute-start.45 = (bf16[2,592,128]{2,1,0:T(8,128)(2,1)S(1)}, bf16[2,592,128]{2,1,0:T(8,128)(2,1)S(1)}, u32[]{:S(2)}, u32[]{:S(2)}) collective-permute-start(bf16[2,592,128]{2,1,0:T(8,128)(2,1)S(1)} %get-tuple-element.168), channel_id=1, source_target_pairs={{0,1},{1,0},{2,3},{3,2},{4,5},{5,4},{6,7},{7,6},{8,9},{9,8},{10,11... | collective-permute-start | bytes 909320 | tf_op jit(solution)/shard_map/ppermute | solution.py:1095
  133.3 9.8 %collective-permute-start.46 = (bf16[1280,128]{1,0:T(8,128)(2,1)S(1)}, bf16[1280,128]{1,0:T(8,128)(2,1)S(1)}, u32[]{:S(2)}, u32[]{:S(2)}) collective-permute-start(bf16[1280,128]{1,0:T(8,128)(2,1)S(1)} %get-tuple-element.170), channel_id=1, source_target_pairs={{0,2},{1,3},{2,0},{3,1},{4,6},{5,7},{6,4},{7,5},{8,10},{9,11},{10,... | collective-permute-start | bytes 983048 | tf_op jit(solution)/shard_map/ppermute | solution.py:1095
  135.2 9.0 %collective-permute-start.49 = (bf16[2,576,128]{2,1,0:T(8,128)(2,1)S(1)}, bf16[2,576,128]{2,1,0:T(8,128)(2,1)S(1)}, u32[]{:S(2)}, u32[]{:S(2)}) collective-permute-start(bf16[2,576,128]{2,1,0:T(8,128)(2,1)S(1)} %get-tuple-element.180), channel_id=1, source_target_pairs={{0,4},{1,5},{2,6},{3,7},{4,0},{5,1},{6,2},{7,3},{8,12},{9,13},{10,... | collective-permute-start | bytes 884744 | tf_op jit(solution)/shard_map/ppermute | solution.py:1095
  143.8 5.5 %collective-permute-start.47 = (bf16[640,128]{1,0:T(8,128)(2,1)S(1)}, bf16[640,128]{1,0:T(8,128)(2,1)S(1)}, u32[]{:S(2)}, u32[]{:S(2)}) collective-permute-start(bf16[640,128]{1,0:T(8,128)(2,1)S(1)} %get-tuple-element.172), channel_id=1, source_target_pairs={{0,4},{1,5},{2,6},{3,7},{4,0},{5,1},{6,2},{7,3},{8,12},{9,13},{10,... | collective-permute-start | bytes 491528 | tf_op jit(solution)/shard_map/ppermute | solution.py:1095
  144.2 5.2 %collective-permute-start.50 = (bf16[576,128]{1,0:T(8,128)(2,1)S(1)}, bf16[576,128]{1,0:T(8,128)(2,1)S(1)}, u32[]{:S(2)}, u32[]{:S(2)}) collective-permute-start(bf16[576,128]{1,0:T(8,128)(2,1)S(1)} %get-tuple-element.181), channel_id=1, source_target_pairs={{0,2},{1,3},{2,0},{3,1},{4,6},{5,7},{6,4},{7,5},{8,10},{9,11},{10,... | collective-permute-start | bytes 442376 | tf_op jit(solution)/shard_map/ppermute | solution.py:1095
  149.4 0.7 collective-permute-start.51
  150.1 21.2 %collective-permute-start.52 = (bf16[784,256]{1,0:T(8,128)(2,1)S(1)}, bf16[784,256]{1,0:T(8,128)(2,1)S(1)}, u32[]{:S(2)}, u32[]{:S(2)}) collective-permute-start(bf16[784,256]{1,0:T(8,128)(2,1)S(1)} %collective-permute-done.51.low_refs_0_), channel_id=1, source_target_pairs={{0,2},{1,3},{2,0},{3,1},{4,6},{5,7},{6,4},{7,5},{8,10},{9,11},{10,... | collective-permute-start | bytes 1204232 | tf_op jit(solution)/shard_map/ppermute | solution.py:1095
  151.8 4.5 %collective-permute-start.53 = (bf16[304,128]{1,0:T(8,128)(2,1)S(1)}, bf16[304,128]{1,0:T(8,128)(2,1)S(1)}, u32[]{:S(2)}, u32[]{:S(2)}) collective-permute-start(bf16[304,128]{1,0:T(8,128)(2,1)S(1)} %get-tuple-element.187), channel_id=1, source_target_pairs={{0,8},{1,9},{2,10},{3,11},{4,12},{5,13},{6,14},{7,15},{8,0},{9,1},... | collective-permute-start | bytes 233480 | tf_op jit(solution)/shard_map/ppermute | solution.py:1095
  153.3 6.1 %collective-permute-start.54 = (bf16[304,128]{1,0:T(8,128)(2,1)S(1)}, bf16[304,128]{1,0:T(8,128)(2,1)S(1)}, u32[]{:S(2)}, u32[]{:S(2)}) collective-permute-start(bf16[304,128]{1,0:T(8,128)(2,1)S(1)} %get-tuple-element.188), channel_id=1, source_target_pairs={{0,16},{1,17},{2,18},{3,19},{4,20},{5,21},{6,22},{7,23},{8,24},{9,... | collective-permute-start | bytes 233480 | tf_op jit(solution)/shard_map/ppermute | solution.py:1095
  154.4 6.3 %collective-permute-start.55 = (bf16[304,128]{1,0:T(8,128)(2,1)S(1)}, bf16[304,128]{1,0:T(8,128)(2,1)S(1)}, u32[]{:S(2)}, u32[]{:S(2)}) collective-permute-start(bf16[304,128]{1,0:T(8,128)(2,1)S(1)} %get-tuple-element.189), channel_id=1, source_target_pairs={{0,24},{1,25},{2,26},{3,27},{4,28},{5,29},{6,30},{7,31},{8,16},{9,... | collective-permute-start | bytes 233480 | tf_op jit(solution)/shard_map/ppermute | solution.py:1095
  160.8 6.8 %collective-permute-start.58 = (bf16[304,128]{1,0:T(8,128)(2,1)S(1)}, bf16[304,128]{1,0:T(8,128)(2,1)S(1)}, u32[]{:S(2)}, u32[]{:S(2)}) collective-permute-start(bf16[304,128]{1,0:T(8,128)(2,1)S(1)} %add_depth.1.piece_refs_0_), channel_id=1, source_target_pairs={{0,24},{1,25},{2,26},{3,27},{4,28},{5,29},{6,30},{7,31},{8,16},{9,... | collective-permute-start | bytes 233480 | tf_op jit(solution)/shard_map/ppermute | solution.py:1095
  162.7 8.6 %collective-permute-start.57 = (bf16[304,128]{1,0:T(8,128)(2,1)S(1)}, bf16[304,128]{1,0:T(8,128)(2,1)S(1)}, u32[]{:S(2)}, u32[]{:S(2)}) collective-permute-start(bf16[304,128]{1,0:T(8,128)(2,1)S(1)} %add_depth.1.piece_refs_0_), channel_id=1, source_target_pairs={{0,16},{1,17},{2,18},{3,19},{4,20},{5,21},{6,22},{7,23},{8,24},{9,... | collective-permute-start | bytes 233480 | tf_op jit(solution)/shard_map/ppermute | solution.py:1095
  163.2 8.0 %collective-permute-start.56 = (bf16[304,128]{1,0:T(8,128)(2,1)S(1)}, bf16[304,128]{1,0:T(8,128)(2,1)S(1)}, u32[]{:S(2)}, u32[]{:S(2)}) collective-permute-start(bf16[304,128]{1,0:T(8,128)(2,1)S(1)} %add_depth.1.piece_refs_0_), channel_id=1, source_target_pairs={{0,8},{1,9},{2,10},{3,11},{4,12},{5,13},{6,14},{7,15},{8,0},{9,1},... | collective-permute-start | bytes 233480 | tf_op jit(solution)/shard_map/ppermute | solution.py:1095
  171.3 8.6 %collective-permute-start.59 = (bf16[784,256]{1,0:T(8,128)(2,1)S(1)}, bf16[784,256]{1,0:T(8,128)(2,1)S(1)}, u32[]{:S(2)}, u32[]{:S(2)}) collective-permute-start(bf16[784,256]{1,0:T(8,128)(2,1)S(1)} %collective-permute-done.51.low_refs_0_), channel_id=1, source_target_pairs={{0,1},{1,0},{2,3},{3,2},{4,5},{5,4},{6,7},{7,6},{8,9},{9,8},{10,11... | collective-permute-start | bytes 1204232 | tf_op jit(solution)/shard_map/ppermute | solution.py:1095
  177.1 2.7 %collective-permute-start.60 = (bf16[784,256]{1,0:T(8,128)(2,1)S(1)}, bf16[784,256]{1,0:T(8,128)(2,1)S(1)}, u32[]{:S(2)}, u32[]{:S(2)}) collective-permute-start(bf16[784,256]{1,0:T(8,128)(2,1)S(1)} %collective-permute-done.52.low_refs_2_), channel_id=1, source_target_pairs={{0,1},{1,0},{2,3},{3,2},{4,5},{5,4},{6,7},{7,6},{8,9},{9,8},{10,11... | collective-permute-start | bytes 1204232 | tf_op jit(solution)/shard_map/ppermute | solution.py:1095
  177.8 9.8 %collective-permute-start.61 = (bf16[1216,128]{1,0:T(8,128)(2,1)S(1)}, bf16[1216,128]{1,0:T(8,128)(2,1)S(1)}, u32[]{:S(2)}, u32[]{:S(2)}) collective-permute-start(bf16[1216,128]{1,0:T(8,128)(2,1)S(1)} %join_depth.1.term_refs_0_), channel_id=1, source_target_pairs={{0,4},{1,5},{2,6},{3,7},{4,0},{5,1},{6,2},{7,3},{8,12},{9,13},{10,... | collective-permute-start | bytes 933896 | tf_op jit(solution)/shard_map/ppermute | solution.py:1095
  (12 other events, 120.1 us)

commit v4 on v3

--- a/solution.py
+++ b/solution.py
@@ -13,7 +13,7 @@
 PADDED = SIDE * WIDE
 STRIDE = PADDED + WIDE
 CHUNK = 16
-UNROLL = 2
+UNROLL = 7
 VMEM_LIMIT = 24 * 2**20
 SLOTS = (0, 1, 2, 3)
 GATHERED = 40
@@ -30,6 +30,21 @@
     )
 
 
+def parts_of(value):
+    high = value.astype(BF16)
+    rest = value - high.astype(F32)
+    middle = rest.astype(BF16)
+    return jnp.concatenate([high, middle, (rest - middle.astype(F32)).astype(BF16)], axis=0)
+
+
+def exact_dot(dot, left, right):
+    rows = -(-left.shape[0] // 16) * 16
+    if rows > left.shape[0]:
+        left = jnp.concatenate([left, jnp.zeros((rows - left.shape[0], left.shape[1]), F32)], axis=0)
+    value = dot(parts_of(left), right)
+    return value[:rows] + value[rows : 2 * rows] + value[2 * rows :]
+
+
 def dot_nt(left, right, precision=None):
     return lax.dot_general(
         left, right, (((1,), (1,)), ((), ())), preferred_element_type=F32, precision=precision
@@ -52,7 +67,7 @@
 
 def slope(value):
     share = logistic(value)
-    return share * (1.0 + value * (1.0 - share))
+    return share + value * (share * (1.0 - share))
 
 
 def moments(first, second, total):
@@ -164,6 +179,44 @@
 
 def slot_refs(even_ref, odd_ref, across_ref):
     return even_ref.at[0], odd_ref.at[0], across_ref.at[0], across_ref.at[1]
+
+
+def pack(
+    mid_ref,
+    squeeze_ref,
+    gain_in_ref,
+    shift_in_ref,
+    gain_mid_ref,
+    shift_mid_ref,
+    bias_ref,
+    gain_out_ref,
+    shift_out_ref,
+    excite_ref,
+    out_ref,
+    target_ref,
+    small_ref,
+):
+    lanes = target_ref.shape[1]
+    own = lanes // 2
+    small_ref[...] = jnp.zeros_like(small_ref)
+    small_ref[0:1, :own] = gain_in_ref[...].astype(F32)
+    small_ref[0:1, own:] = shift_in_ref[...].astype(F32)
+    for row, ref in enumerate((gain_mid_ref, shift_mid_ref, bias_ref)):
+        value = ref[...].astype(F32)
+        small_ref[row + 1 : row + 2, :own] = value[0:1]
+        small_ref[row + 1 : row + 2, own:] = value[1:2]
+    for t, ref in enumerate((gain_out_ref, shift_out_ref)):
+        value = ref[...].astype(F32)
+        small_ref[4 + 2 * t : 5 + 2 * t, :] = value[:, :lanes]
+        small_ref[5 + 2 * t : 6 + 2 * t, :] = value[:, lanes:]
+    row = 0
+    for ref in (mid_ref, squeeze_ref, small_ref, excite_ref):
+        target_ref[row : row + ref.shape[0], :] = ref[...].astype(BF16)
+        row += ref.shape[0]
+    for block in range(out_ref.shape[1] // lanes):
+        rows = out_ref.shape[0]
+        target_ref[row : row + rows, :] = out_ref[:, block * lanes : (block + 1) * lanes]
+        row += rows
 
 
 def reduce_in(
@@ -270,7 +323,7 @@
     sums = summed_over(sums_refs)
     center, scale = moments(sums[0:1], sums[1:2], total)
     gain = affine_ref[0:1, :] * scale
-    shift = affine_ref[1:2, :]
+    shift = affine_ref[1:2, :] - center * gain
     clear_gaps(taps_ref, images)
     keep = columns_real(WIDE)
     for image in range(images):
@@ -278,7 +331,7 @@
         def normalize(step, carry, image=image):
             rows = pl.multiple_of(step * WIDE, WIDE)
             value = pre_ref[pl.ds(image * PADDED + rows, WIDE), :]
-            value = silu((value - center) * gain + shift) * keep
+            value = silu(value * gain + shift) * keep
             store_taps(taps_ref, image * STRIDE + WIDE + rows, value)
             return carry
 
@@ -321,7 +374,8 @@
 ):
     sums = summed_over(sums_refs)
     center, scale = moments(sums[0:1], sums[1:2], place.total() * PIXELS)
-    return center, scale, affine_ref[0:1, :], affine_ref[1:2, :]
+    gain = affine_ref[0:1, :] * scale
+    return center, scale, gain, affine_ref[1:2, :] - center * gain
 
 
 def pool(
@@ -345,12 +399,12 @@
         def gather(step, carry, image=image):
             active, rise, lean = carry
             at = pl.multiple_of(image * PADDED + step * CHUNK, CHUNK)
-            normed = (mid_ref[pl.ds(at, CHUNK), :] - center) * scale
-            value = normed * gain + shift
-            share = logistic(value)
-            active = active + fold(value * share * keep)
-            inclined = share * (1.0 + value * (1.0 - share)) * keep
-            return active, rise + fold(inclined), lean + fold(inclined * normed)
+            before = mid_ref[pl.ds(at, CHUNK), :]
+            value = before * gain + shift
+            share = logistic(value) * keep
+            active = active + fold(value * share)
+            inclined = share + value * (share * (1.0 - share))
+            return active, rise + fold(inclined), lean + fold(inclined * before)
 
         nothing = jnp.zeros((8, 2 * width), F32)
         active, rise, lean = lax.fori_loop(
@@ -358,14 +412,15 @@
         )
         active = total_of(active)
         pooled_ref[image : image + 1, :] = (active[:, :width] + active[:, width:]) / PIXELS
-        inclines[0].append(total_of(rise))
-        inclines[1].append(total_of(lean))
+        rise = total_of(rise)
+        inclines[0].append(rise)
+        inclines[1].append(scale * (total_of(lean) - center * rise))
     inclined = jnp.concatenate(inclines[0] + inclines[1], axis=0)
     msg_ref[...] = jnp.zeros_like(msg_ref)
     for q in range(2 * width // lanes):
         row = 8 + q * 2 * images
         msg_ref[row : row + 2 * images, :] = inclined[:, q * lanes : (q + 1) * lanes]
-    msg_ref[0:images, :] = dot_nn(pooled_ref[...], squeeze_ref[...].astype(F32), HIGHEST)
+    msg_ref[0:images, :] = exact_dot(dot_nn, pooled_ref[...], squeeze_ref[...])[:images]
     real = [place.real(image) * pooled_ref[image : image + 1, :] for image in range(images)]
     real = functools.reduce(jnp.add, real)
     for q in range(width // lanes):
@@ -410,7 +465,7 @@
     gate_ref[0] = gate
     gate_ref[1] = slope(gate_pre)
     logits = (
-        dot_nt(gate, excite_ref[...].astype(F32), HIGHEST) + bias_ref[...]
+        exact_dot(dot_nt, gate, excite_ref[...])[:images] + bias_ref[...]
     )
     lean = 0.5 * jnp.tanh(0.5 * (logits[:, :width] - logits[:, width:]))
     attention_ref[:, :width] = 0.5 + lean
@@ -421,8 +476,7 @@
 
         def weigh(step, carry, image=image, share=share):
             at = pl.multiple_of(image * PADDED + step * CHUNK, CHUNK)
-            normed = (mid_ref[pl.ds(at, CHUNK), :] - center) * scale
-            value = share * silu(normed * gain + shift)
+            value = share * silu(mid_ref[pl.ds(at, CHUNK), :] * gain + shift)
             wide_ref[pl.ds(at, CHUNK), :] = value[:, :width] + value[:, width:]
             return carry
 
@@ -463,31 +517,34 @@
     for k in range(blocks):
         mu, r = center[k : k + 1], scale[k : k + 1]
         block = place.batch ^ k
-        gain, shift = affine_ref[0, block], affine_ref[1, block]
-        x_ref, cot_ref, summed_ref = x_refs[k], cot_refs[k], (even_ref, odd_ref)[k & 1].at[k >> 1]
+        gain = affine_ref[0, block] * r
+        shift = affine_ref[1, block] - mu * gain
+        x_ref, upstream_ref = x_refs[k], cot_refs[k]
+        summed_ref = (even_ref, odd_ref)[k & 1].at[k >> 1]
 
         def chunk(
-            step, carry, k=k, mu=mu, r=r, gain=gain, shift=shift,
-            x_ref=x_ref, cot_ref=cot_ref, summed_ref=summed_ref,
+            step, carry, k=k, gain=gain, shift=shift,
+            x_ref=x_ref, upstream_ref=upstream_ref, summed_ref=summed_ref,
         ):
             first, second = carry
             at = pl.multiple_of(step * CHUNK, CHUNK)
             here = pl.ds(at, CHUNK)
             spot = lax.broadcasted_iota(jnp.int32, (CHUNK, 1), 0) + at
             real = (spot < limit).astype(F32)
-            normed = (out_ref[k, here, :] - mu) * r
-            summed = x_ref[here, :].astype(F32) + (normed * gain + shift)
+            before = out_ref[k, here, :]
+            summed = x_ref[here, :].astype(F32) + (before * gain + shift)
             summed_ref[here, :] = summed.astype(BF16)
             share = logistic(summed)
-            grad = cot_ref[here, :].astype(F32) * real * (share * (1.0 + summed * (1.0 - share)))
+            grad = upstream_ref[here, :].astype(F32) * real * (share * (1.0 + summed * (1.0 - share)))
             grad_ref[k, here, :] = grad
-            return first + fold(grad), second + fold(grad * normed)
+            return first + fold(grad), second + fold(grad * before)
 
         nothing = jnp.zeros((8, lanes), F32)
         first, second = lax.fori_loop(
             0, rows // CHUNK, chunk, (nothing, nothing), unroll=UNROLL
         )
-        for t, row in enumerate((total_of(first), total_of(second))):
+        first = total_of(first)
+        for t, row in enumerate((first, r * (total_of(second) - mu * first))):
             msg_ref[t * blocks + k : t * blocks + k + 1, :] = row
 
 
@@ -547,15 +604,15 @@
     for k in range(blocks):
         mu, r = center[k : k + 1], scale[k : k + 1]
         gain = affine_ref[0, place.batch ^ k] * r
-        first, second = back[k : k + 1], back[blocks + k : blocks + k + 1]
-
-        def chunk(step, carry, k=k, mu=mu, r=r, gain=gain, first=first, second=second):
+        second = gain * r * back[blocks + k : blocks + k + 1]
+        first = gain * back[k : k + 1] - mu * second
+
+        def chunk(step, carry, k=k, gain=gain, first=first, second=second):
             at = pl.multiple_of(step * CHUNK, CHUNK)
             here = pl.ds(at, CHUNK)
             spot = lax.broadcasted_iota(jnp.int32, (CHUNK, 1), 0) + at
             real = (spot < limit).astype(F32)
-            normed = (out_ref[k, here, :] - mu) * r
-            value = gain * (grad_ref[k, here, :] - real * (first + normed * second))
+            value = gain * grad_ref[k, here, :] - real * (first + out_ref[k, here, :] * second)
             low_ref[k, here, :] = value.astype(BF16)
             return carry
 
@@ -570,15 +627,15 @@
         def gather(step, carry, image=image):
             attended, rise, lean = carry
             at = pl.multiple_of(image * PADDED + step * CHUNK, CHUNK)
-            normed = (mid_ref[pl.ds(at, CHUNK), :] - center) * scale
-            value = normed * gain + shift
+            before = mid_ref[pl.ds(at, CHUNK), :]
+            value = before * gain + shift
             share = logistic(value)
             grad = gw_ref[pl.ds(at, CHUNK), :]
             grad = jnp.concatenate([grad, grad], axis=1)
             active = grad * share
             attended = attended + fold(active * value)
             inclined = active * (1.0 + value * (1.0 - share))
-            return attended, rise + fold(inclined), lean + fold(inclined * normed)
+            return attended, rise + fold(inclined), lean + fold(inclined * before)
 
         nothing = jnp.zeros((8, 2 * width), F32)
         parts = lax.fori_loop(
@@ -586,15 +643,16 @@
         )
         share = attention_ref[image : image + 1, :]
         attended.append(total_of(parts[0]))
-        rises.append(share * total_of(parts[1]))
-        leans.append(share * total_of(parts[2]))
+        rise = total_of(parts[1])
+        rises.append(share * rise)
+        leans.append(share * (scale * (total_of(parts[2]) - center * rise)))
     grad = jnp.concatenate(attended, axis=0)
     attention = attention_ref[...]
     inner = attention * grad
     inner = inner[:, :width] + inner[:, width:]
     logits = attention * (grad - jnp.concatenate([inner, inner], axis=1))
     logits_ref[...] = logits
-    gate = dot_nn(logits, excite_ref[...].astype(F32), HIGHEST) * gate_ref[1]
+    gate = exact_dot(dot_nn, logits, excite_ref[...])[:images] * gate_ref[1]
     pack = msg_ref.shape[1]
     pieces = 2 * width // pack
     for t, row in enumerate((functools.reduce(jnp.add, rises), functools.reduce(jnp.add, leans))):
@@ -643,7 +701,7 @@
     vector_ref[0:1, lanes : 2 * lanes] = first
     squeezed = gain * (grads - wall * (first + normed * second) / place.total())
     gate_ref[...] = squeezed[0:images]
-    pooled_grad = dot_nt(squeezed, squeeze_ref[...].astype(F32), HIGHEST) / PIXELS
+    pooled_grad = exact_dot(dot_nt, squeezed, squeeze_ref[...]) / PIXELS
     pooled_grad = jnp.concatenate([pooled_grad, pooled_grad], axis=1)
     slot = 0
     terms = jnp.zeros((2 * images, 2 * width), F32)
@@ -666,25 +724,25 @@
     vector_ref[1:2, :] = back[1]
     vector_ref[2:3, :] = back[0]
     own = pooled_grad[0:images]
-    first, second = back[0] / total, back[1] / total
     center, scale, gain, shift = mid_norm(place, mid_sums_refs, mid_affine_ref)
-    gained = gain * scale
+    second = gain * scale * back[1] / total
+    first = gain * back[0] / total - center * second
     clear_gaps(taps_ref, images)
     keep = columns_real(WIDE)
     for image in range(images):
-        share = attention_ref[image : image + 1, :]
-        offset = own[image : image + 1, :]
+        share = gain * attention_ref[image : image + 1, :]
+        offset = gain * own[image : image + 1, :]
         real = place.real(image)
         lead, lag = real * first, real * second
 
         def chunk(step, carry, image=image, share=share, offset=offset, lead=lead, lag=lag):
             rows = pl.multiple_of(step * WIDE, WIDE)
             here = pl.ds(image * PADDED + rows, WIDE)
-            normed = (mid_ref[here, :] - center) * scale
+            before = mid_ref[here, :]
             grad = gw_ref[here, :]
             grad = jnp.concatenate([grad, grad], axis=1)
-            grad = (share * grad + offset) * slope(normed * gain + shift)
-            value = gained * (grad - (lead + normed * lag)) * keep
+            grad = (share * grad + offset) * slope(before * gain + shift)
+            value = (grad - (lead + before * lag)) * keep
             store_taps(taps_ref, image * STRIDE + WIDE + rows, value)
             return carry
 
@@ -692,7 +750,8 @@
     low_ref[...] = taps_ref[1]
     sums = summed_over(sums_refs)
     center, scale = moments(sums[0:1], sums[1:2], total)
-    gain, shift = affine_ref[0:1, :], affine_ref[1:2, :]
+    gain = affine_ref[0:1, :] * scale
+    shift = affine_ref[1:2, :] - center * gain
     half = width // 2
     keep = columns_real(PADDED)
     firsts = [jnp.zeros((1, half), F32) for _ in range(2)]
@@ -714,15 +773,15 @@
                 axis=1,
             )
             lane = slice(r * half, (r + 1) * half)
-            normed = (pre_ref[here, lane] - center[:, lane]) * scale[:, lane]
-            value = dot_nn(left, w_ref[r]) * slope(normed * gain[:, lane] + shift[:, lane])
+            before = pre_ref[here, lane]
+            value = dot_nn(left, w_ref[r]) * slope(before * gain[:, lane] + shift[:, lane])
             value = value * (keep * real)
             grad_ref[here, lane] = value
             firsts[r] = firsts[r] + total_of(value)
-            seconds[r] = seconds[r] + total_of(value * normed)
-    sums = jnp.concatenate(
-        [jnp.concatenate(firsts, axis=1), jnp.concatenate(seconds, axis=1)], axis=0
-    )
+            seconds[r] = seconds[r] + total_of(value * before)
+    first = jnp.concatenate(firsts, axis=1)
+    second = scale * (jnp.concatenate(seconds, axis=1) - center * first)
+    sums = jnp.concatenate([first, second], axis=0)
     msg_ref[...] = sums
 
 
@@ -842,15 +901,16 @@
     sums = summed_over(sums_refs)
     center, scale = moments(sums[0:1], sums[1:2], total)
     back = summed_over(back_refs)
-    first, second = back[0:1] / total, back[1:2] / total
     gain = affine_ref[0:1, :] * scale
+    second = gain * scale * back[1:2] / total
+    first = gain * back[0:1] / total - center * second
     for image in range(images):
         real = place.real(image)
         lead, lag = real * first, real * second
         for line in range(SIDE):
             at = image * PADDED + line * WIDE
-            normed = (pre_ref[at : at + WIDE, :] - center) * scale
-            value = gain * (grad_ref[at : at + WIDE, :] - (lead + normed * lag))
+            before = pre_ref[at : at + WIDE, :]
+            value = gain * grad_ref[at : at + WIDE, :] - (lead + before * lag)
             at = image * PIXELS + line * SIDE
             flat_ref[at : at + SIDE, :] = value[:SIDE]
     low_ref[...] = flat_ref[...].astype(BF16)
@@ -1165,7 +1225,6 @@
             (terms,) = kernel(add_groups, [shape(terms.shape, BF16)], terms, smem=0)
             terms = lax.all_to_all(terms, "dp", 0, 0).reshape(rows, -1)
             terms = terms[:first_rows], terms[first_rows : first_rows + second_rows]
-            low = away_plane(low)
             return terms, low, across(low)
         second_rows = padded(second_rows)
         halves = (first_rows // 2, second_rows // 2)
@@ -1205,7 +1264,6 @@
         )
         first_arrived = across(send)
         arrived = after(arrived, first_arrived)
-        low = away_plane(after(low, arrived))
         keep, *send = call(
             add_last,
             [rows(sum(pieces))] + [rows(sum(pieces), BF16)] * (depth - 1),
@@ -1215,41 +1273,40 @@
             (first_keep, keep),
             (first_arrived, arrived),
         )
+        low_other = across(after(low, keep))
         arrived = tuple(along(send[t - 1], t) for t in range(1, depth))
         (mine,) = kernel(add_depth, [rows(sum(pieces), BF16)], keep, arrived, smem=0)
         mine = (mine,) + tuple(along(mine, t) for t in range(1, depth))
-        low, low_other = after_all((low, across(low)), *mine)
+        low, low_other = after_all((low, low_other), *mine)
         (mine,) = kernel(join_depth, [rows(sum(halves), BF16)], counts, mine)
         return (mine, parity(mine)), low, low_other
 
     def slots_of(tensor, *which):
         return [lax.dynamic_index_in_dim(tensor, chan ^ s, 0, keepdims=False) for s in which]
 
-    first = weight_in.T
+    far = slots_of(activations, 2, 3)
+    first = after(weight_in.T, *far)
     other, near = across(first), core(first)
-    far = slots_of(activations, 2, 3)
-    x = slots_of(after(activations, near, far[0]), 0, 1) + far
+    x = slots_of(after(activations, near), 0, 1) + far
     x = tuple(home(piece, s) for s, piece in enumerate(x))
 
-    small = jnp.concatenate(
-        [
-            jnp.concatenate([gain_in, shift_in])[None],
-            gain_mid.reshape(1, 2 * own),
-            shift_mid.reshape(1, 2 * own),
-            shift_excite.reshape(1, 2 * own),
-            gain_out.reshape(-1, 2 * own),
-            shift_out.reshape(-1, 2 * own),
-            jnp.zeros((8, 2 * own), BF16),
-        ]
-    )
-
-    def lane_blocks(tensor):
-        return [tensor[:, at : at + 2 * own] for at in range(0, tensor.shape[1], 2 * own)]
-
-    weights = jnp.concatenate(
-        [weight_mid.transpose(0, 1, 3, 4, 2).reshape(-1, 2 * own), weight_squeeze, small]
-        + [weight_excite.transpose(1, 2, 0).reshape(-1, inter)]
-        + lane_blocks(weight_out)
+    (weights,) = call(
+        pack,
+        [shape((19 * own + 16 + inter + 2 * width, 2 * own), BF16)],
+        [pltpu.VMEM((16, 2 * own), F32)],
+        0,
+        weight_mid.transpose(0, 1, 3, 4, 2).reshape(-1, 2 * own),
+        weight_squeeze,
+        gain_in.reshape(1, -1),
+        shift_in.reshape(1, -1),
+        gain_mid,
+        shift_mid,
+        shift_excite,
+        gain_out.reshape(1, -1),
+        shift_out.reshape(1, -1),
+        weight_excite.transpose(1, 2, 0).reshape(-1, inter),
+        weight_out,
+        smem=0,
     )
     other = after(other, weights)
     first = (first, near, other, core(other))
@@ -1312,8 +1369,6 @@
         w_mid,
     )
     mid_sums = exchange(2, 0)(msg)
-    even, odd = after_all((even, odd), *mid_sums)
-    cot = cross(even, odd)
     excite, w_out = call(
         place_rest,
         [
@@ -1336,6 +1391,7 @@
         mid_affine,
         squeeze,
     )
+    cot = cross(*after_all((even, odd), msg))
     gathered = exchange(None, GATHERED)(msg)
     gate, attention, weighted, out, msg = call(
         attend,
@@ -1445,7 +1501,7 @@
         in_affine,
         w_mid_back,
     )
-    in_back = exchange(2, 0)(msg)
+    in_back = exchange(2, 0)(after(msg, out_arrived))
     in_rows = parts * lanes // (2 * own) * own
     low_in, in_keep, in_send = call(
         functools.partial(back_in, 1.0 / groups),
@@ -1482,6 +1538,7 @@
     owned = shape((batches, rows, lanes), BF16)
     result, grad_summed = call(finish_owned, [owned, owned], [], 0, counts, *summed, cotangent)
     send = after(send, summed[2])
+    low_in = away_plane(low_in)
     terms, low_in, low_other = add_over_all(
         (keep, core(send)),
         ((out_keep, in_keep), (out_arrived, core(in_send))),

time: 190 us -> 178 us (0.937)
  local copies, waits for them, and re-layouts: 13.8 us -> 2.87 us
  waiting for transfers between devices: 56.7 us -> 66.3 us
  Pallas kernels: 42.4 us -> 36.9 us
  starting transfers between devices: 74.4 us -> 69.6 us
    ppermute x62, waiting for transfers between devices: 56.7 us -> 66.3 us  [permute(): return lax.ppermute(tensor, ('dp', 'chan'), pairs)]
    concatenate x1 -> x0, local copies, waits for them, and re-layouts: 6.48 us -> none  [per_device(): jnp.concatenate([weight_mid.transpose(0, 1, 3, 4, 2).reshape(-1, 2 * own)...]
    pallas_call x22 -> x23, Pallas kernels: 42.4 us -> 36.9 us  [call(): pl.pallas_call(body, out_shape=outs, in_specs=specs, out_specs=[pl.BlockS...]
    ppermute x62, starting transfers between devices: 74.4 us -> 69.6 us  [permute(): return lax.ppermute(tensor, ('dp', 'chan'), pairs)]
  transfers between devices with their start and end apart: 62 -> 62, of which waited for: 34 -> 39; matrix products, arithmetic and copies ran while one was open for 7% -> 1% of each run, Pallas kernels for 19% -> 18%
where the time goes in v4:
time: 178 us; the launch traced here: 177 us
  starting transfers between devices  69.6 us (39%)
  waiting for transfers between devices  66.3 us (37%)
  Pallas kernels  36.9 us (21%)
  local copies, waits for them, and re-layouts  2.87 us (2%)
    ppermute x62, starting transfers between devices, permute(): return lax.ppermute(tensor, ('dp', 'chan'), pairs)  69.6 us
    ppermute x62, waiting for transfers between devices, permute(): return lax.ppermute(tensor, ('dp', 'chan'), pairs)  66.3 us
    pallas_call x23, Pallas kernels, call(): pl.pallas_call(body, out_shape=outs, in_specs=specs, out_specs=[pl.BlockS...  36.9 us
  transfers between devices with their start and end apart: 62, of which 39 were waited for; matrix products, arithmetic and copies ran while one was open for 1% of the time, Pallas kernels for 18%

profile of v4, /device:TPU:0, one launch (start us, length us, event | category | flops | bytes accessed | tf_op | source)
XLA Modules:
  0.0 177.5 jit_solution(13677504098291226655)
XLA Ops:
  0.8 1.4 dynamic-slice_bitcast_fusion.2
  2.7 2.6 %collective-permute-start.5 = (bf16[64,1024]{1,0:T(8,128)(2,1)S(1)}, bf16[64,1024]{1,0:T(8,128)(2,1)S(1)}, u32[]{:S(2)}, u32[]{:S(2)}) collective-permute-start(bf16[64,1024]{1,0:T(8,128)(2,1)S(1)} %bitcast.34), channel_id=1, source_target_pairs={{0,2},{1,3},{2,0},{3,1},{4,6},{5,7},{6,4},{7,5},{8,10},{9,11},{10,... | collective-permute-start | bytes 393224 | tf_op jit(solution)/shard_map/ppermute | solution.py:1155
  5.3 1.4 collective-permute-start.4
  6.7 1.5 collective-permute-start.3
  8.3 1.2 dynamic-slice_bitcast_fusion
  10.8 7.5 %collective-permute-done.5.a2 = bf16[64,1024]{1,0:T(8,128)(2,1)S(1)} collective-permute-done((bf16[64,1024]{1,0:T(8,128)(2,1)S(1)}, bf16[64,1024]{1,0:T(8,128)(2,1)S(1)}, u32[]{:S(2)}, u32[]{:S(2)}) %collective-permute-start.5) | collective-permute-done | bytes 131104 | tf_op jit(solution)/shard_map/ppermute | solution.py:1155
  18.3 1.3 collective-permute-done.6.a3
  19.8 6.6 %collective-permute-done.4.x3.x_refs_3_ = bf16[784,256]{1,0:T(8,128)(2,1)S(1)} collective-permute-done((bf16[784,256]{1,0:T(8,128)(2,1)S(1)}, bf16[784,256]{1,0:T(8,128)(2,1)S(1)}, u32[]{:S(2)}, u32[]{:S(2)}) %collective-permute-start.4) | collective-permute-done | bytes 401440 | tf_op jit(solution)/shard_map/ppermute | solution.py:1155
  26.6 1.8 collective-permute-start.12
  28.4 1.3 reduce_in.1
  30.0 1.1 collective-permute-done.8
  31.2 3.6 %collective-permute-start.11 = (f32[2,256]{1,0:T(2,128)S(1)}, f32[2,256]{1,0:T(2,128)S(1)}, u32[]{:S(2)}, u32[]{:S(2)}) collective-permute-start(f32[2,256]{1,0:T(2,128)S(1)} %add.39.sums_refs_0_), channel_id=1, source_target_pairs={{0,24},{1,25},{2,26},{3,27},{4,28},{5,29},{6,30},{7,31},{8,16},{9,... | collective-permute-start | bytes 6152 | tf_op jit(solution)/shard_map/ppermute | solution.py:1155
  36.5 2.7 %collective-permute-done.10.sums_refs_2_ = f32[2,256]{1,0:T(2,128)S(1)} collective-permute-done((f32[2,256]{1,0:T(2,128)S(1)}, f32[2,256]{1,0:T(2,128)S(1)}, u32[]{:S(2)}, u32[]{:S(2)}) %collective-permute-start.10) | collective-permute-done | bytes 2080 | tf_op jit(solution)/shard_map/ppermute | solution.py:1155
  40.0 2.3 %collective-permute-done.13.b3 = bf16[1872,128]{1,0:T(8,128)(2,1)S(1)} collective-permute-done((bf16[1872,128]{1,0:T(8,128)(2,1)S(1)}, bf16[1872,128]{1,0:T(8,128)(2,1)S(1)}, u32[]{:S(2)}, u32[]{:S(2)}) %collective-permute-start.13) | collective-permute-done | bytes 479264 | tf_op jit(solution)/shard_map/ppermute | solution.py:1155
  43.1 2.8 %conv_mid.1 = (bf16[3,976,256]{2,1,0:T(8,128)(2,1)S(1)}, f32[896,512]{1,0:T(8,128)S(1)}, f32[2,512]{1,0:T(2,128)S(1)}) custom-call(s32[4,8]{1,0:T(4,128)S(1)} %copy-done.1, f32[896,256]{1,0:T(8,128)S(1)} %get-tuple-element.118.pre_ref, f32[2,256]{1,0:T(2,128)S(1)} %add.39.sums_refs_0_, f32[2,256]{1,0:T(2,128)S(1)} %collective-permute-done.9.sums_refs_1_, ...), custom_call_target="tpu_custom_call" | custom-call | flops 1056964608 | bytes 5445760 | tf_op jit(solution)/shard_map/conv_mid/pallas_call | solution.py:164
  47.2 2.3 %collective-permute-start.17 = (f32[2,512]{1,0:T(2,128)S(1)}, f32[2,512]{1,0:T(2,128)S(1)}, u32[]{:S(2)}, u32[]{:S(2)}) collective-permute-start(f32[2,512]{1,0:T(2,128)S(1)} %add.40.sums_refs_0_.mid_sums_refs_0_), channel_id=1, source_target_pairs={{0,24},{1,25},{2,26},{3,27},{4,28},{5,29},{6,30},{7,31},{8,16},{9,... | collective-permute-start | bytes 12296 | tf_op jit(solution)/shard_map/ppermute | solution.py:1155
  49.4 2.1 %collective-permute-start.15 = (f32[2,512]{1,0:T(2,128)S(1)}, f32[2,512]{1,0:T(2,128)S(1)}, u32[]{:S(2)}, u32[]{:S(2)}) collective-permute-start(f32[2,512]{1,0:T(2,128)S(1)} %add.40.sums_refs_0_.mid_sums_refs_0_), channel_id=1, source_target_pairs={{0,8},{1,9},{2,10},{3,11},{4,12},{5,13},{6,14},{7,15},{8,0},{9,1},... | collective-permute-start | bytes 12296 | tf_op jit(solution)/shard_map/ppermute | solution.py:1155
  52.6 1.4 collective-permute-done.16.sums_refs_2_.mid_sums_refs_2_
  53.9 1.8 %pool.1 = (f32[4,256]{1,0:T(4,128)S(1)}, f32[40,128]{1,0:T(8,128)S(1)}) custom-call(s32[4,8]{1,0:T(4,128)S(1)} %copy-done.1, f32[896,512]{1,0:T(8,128)S(1)} %get-tuple-element.126.mid_ref, f32[2,512]{1,0:T(2,128)S(1)} %add.40.sums_refs_0_.mid_sums_refs_0_, f32[2,512]{1,0:T(2,128)S(1)} %collective-permute-done.15.sums_refs_1_.mid_sums_refs_1_, ...), custom_call_target="tpu_custom_call" | custom-call | bytes 1945728 | tf_op jit(solution)/shard_map/pool/pallas_call | solution.py:164
  58.4 3.5 %collective-permute-start.21 = (f32[80,128]{1,0:T(8,128)S(1)}, f32[80,128]{1,0:T(8,128)S(1)}, u32[]{:S(2)}, u32[]{:S(2)}) collective-permute-start(f32[80,128]{1,0:T(8,128)S(1)} %constant_dynamic-update-slice_fusion.gathered_refs_0_), channel_id=1, source_target_pairs={{0,24},{1,25},{2,26},{3,27},{4,28},{5,29},{6,30},{7,31},{8,16},{9,... | collective-permute-start | bytes 122888 | tf_op jit(solution)/shard_map/ppermute | solution.py:1155
  64.2 2.6 %collective-permute-done.20.gathered_refs_2_ = f32[80,128]{1,0:T(8,128)S(1)} collective-permute-done((f32[80,128]{1,0:T(8,128)S(1)}, f32[80,128]{1,0:T(8,128)S(1)}, u32[]{:S(2)}, u32[]{:S(2)}) %collective-permute-start.20) | collective-permute-done | bytes 40992 | tf_op jit(solution)/shard_map/ppermute | solution.py:1155
  66.8 2.1 %attend.1 = (f32[2,4,128]{2,1,0:T(4,128)S(1)}, f32[4,512]{1,0:T(4,128)S(1)}, bf16[784,256]{1,0:T(8,128)(2,1)S(1)}, f32[4,784,256]{2,1,0:T(8,128)S(1)}, f32[8,256]{1,0:T(8,128)S(1)}) custom-call(s32[4,8]{1,0:T(4,128)S(1)} %copy-done.1, f32[80,128]{1,0:T(8,128)S(1)} %constant_dynamic-update-slice_fusion.gathered_refs_0_, ...), custom_call_target="tpu_custom_call" | custom-call | flops 411041792 | bytes 6327424 | tf_op jit(solution)/shard_map/attend/pallas_call | solution.py:164
  69.0 1.2 collective-permute-done.22
  70.2 2.0 %collective-permute-start.25 = (f32[8,256]{1,0:T(8,128)S(1)}, f32[8,256]{1,0:T(8,128)S(1)}, u32[]{:S(2)}, u32[]{:S(2)}) collective-permute-start(f32[8,256]{1,0:T(8,128)S(1)} %add.41.sums_refs_0_), channel_id=1, source_target_pairs={{0,24},{1,25},{2,26},{3,27},{4,28},{5,29},{6,30},{7,31},{8,16},{9,... | collective-permute-start | bytes 24584 | tf_op jit(solution)/shard_map/ppermute | solution.py:1155
  72.3 2.3 %collective-permute-start.23 = (f32[8,256]{1,0:T(8,128)S(1)}, f32[8,256]{1,0:T(8,128)S(1)}, u32[]{:S(2)}, u32[]{:S(2)}) collective-permute-start(f32[8,256]{1,0:T(8,128)S(1)} %add.41.sums_refs_0_), channel_id=1, source_target_pairs={{0,8},{1,9},{2,10},{3,11},{4,12},{5,13},{6,14},{7,15},{8,0},{9,1},... | collective-permute-start | bytes 24584 | tf_op jit(solution)/shard_map/ppermute | solution.py:1155
  74.5 1.1 collective-permute-done.25.sums_refs_3_
  75.7 1.2 collective-permute-done.24.sums_refs_2_
  76.8 3.1 %finish.1 = (bf16[2,784,256]{2,1,0:T(8,128)(2,1)S(1)}, bf16[2,784,256]{2,1,0:T(8,128)(2,1)S(1)}, f32[4,784,256]{2,1,0:T(8,128)S(1)}, f32[8,256]{1,0:T(8,128)S(1)}) custom-call(s32[4,8]{1,0:T(4,128)S(1)} %copy-done.1, f32[4,784,256]{2,1,0:T(8,128)S(1)} %get-tuple-element.135.out_ref, f32[8,256]{1,0:T(8,128)S(1)} %add.41.sums_refs_0_, ...), custom_call_target="tpu_custom_call" | custom-call | bytes 12091520 | tf_op jit(solution)/shard_map/finish/pallas_call | solution.py:164
  80.8 3.1 %collective-permute-start.30 = (bf16[2,784,256]{2,1,0:T(8,128)(2,1)S(1)}, bf16[2,784,256]{2,1,0:T(8,128)(2,1)S(1)}, u32[]{:S(2)}, u32[]{:S(2)}) collective-permute-start(bf16[2,784,256]{2,1,0:T(8,128)(2,1)S(1)} %get-tuple-element.143), channel_id=1, source_target_pairs={{0,1},{1,5},{2,3},{3,7},{4,0},{5,4},{6,2},{7,6},{8,9},{9,13},{10,1... | collective-permute-start | bytes 2408456 | tf_op jit(solution)/shard_map/ppermute | solution.py:1155
  84.0 1.9 %collective-permute-done.31 = f32[8,256]{1,0:T(8,128)S(1)} collective-permute-done((f32[8,256]{1,0:T(8,128)S(1)}, f32[8,256]{1,0:T(8,128)S(1)}, u32[]{:S(2)}, u32[]{:S(2)}) %collective-permute-start.31) | collective-permute-done | bytes 8224 | tf_op jit(solution)/shard_map/ppermute | solution.py:1155
  85.8 2.2 %collective-permute-start.34 = (f32[8,256]{1,0:T(8,128)S(1)}, f32[8,256]{1,0:T(8,128)S(1)}, u32[]{:S(2)}, u32[]{:S(2)}) collective-permute-start(f32[8,256]{1,0:T(8,128)S(1)} %add.42.back_refs_0_.out_back_refs_0_), channel_id=1, source_target_pairs={{0,24},{1,25},{2,26},{3,27},{4,28},{5,29},{6,30},{7,31},{8,16},{9,... | collective-permute-start | bytes 24584 | tf_op jit(solution)/shard_map/ppermute | solution.py:1155
  88.9 1.3 collective-permute-start.32
  91.3 1.3 collective-permute-done.33.back_refs_2_.out_back_refs_2_
  92.7 3.5 %back_out.1 = (bf16[4,784,256]{2,1,0:T(8,128)(2,1)S(1)}, f32[896,256]{1,0:T(8,128)S(1)}, f32[4,512]{1,0:T(4,128)S(1)}, f32[12,128]{1,0:T(8,128)S(1)}) custom-call(s32[4,8]{1,0:T(4,128)S(1)} %copy-done.1, f32[4,784,256]{2,1,0:T(8,128)S(1)} %get-tuple-element.144.grad_ref, f32[4,784,256]{2,1,0:T(8,128)S(1)} %get-tuple-element.135.out_ref, ...), custom_call_target="tpu_custom_call" | custom-call | flops 411041792 | bytes 11556992 | tf_op jit(solution)/shard_map/back_out/pallas_call | solution.py:164
  96.3 1.1 collective-permute-done.35
  97.5 1.8 %collective-permute-start.38 = (f32[16,128]{1,0:T(8,128)S(1)}, f32[16,128]{1,0:T(8,128)S(1)}, u32[]{:S(2)}, u32[]{:S(2)}) collective-permute-start(f32[16,128]{1,0:T(8,128)S(1)} %pad_maximum_fusion.4.back_refs_0_), channel_id=1, source_target_pairs={{0,24},{1,25},{2,26},{3,27},{4,28},{5,29},{6,30},{7,31},{8,16},{9,... | collective-permute-start | bytes 24584 | tf_op jit(solution)/shard_map/ppermute | solution.py:1155
  100.2 1.7 collective-permute-start.36
  101.9 1.6 weight_out_term.1
  104.1 1.6 collective-permute-start.39
  105.7 4.9 %back_mid.1 = (bf16[976,512]{1,0:T(8,128)(2,1)S(1)}, f32[896,256]{1,0:T(8,128)S(1)}, f32[4,128]{1,0:T(4,128)S(1)}, f32[8,512]{1,0:T(8,128)S(1)}, f32[2,256]{1,0:T(2,128)S(1)}) custom-call(s32[4,8]{1,0:T(4,128)S(1)} %copy-done.1, f32[16,128]{1,0:T(8,128)S(1)} %pad_maximum_fusion.4.back_refs_0_, f32[16,128]{1,0:T(8,128)S(1)} %collective-permute-done.36.back_refs_1_, ...), custom_call_target="tpu_custom_call" | custom-call | flops 1056964608 | bytes 7105664 | tf_op jit(solution)/shard_map/back_mid/pallas_call | solution.py:164
  112.0 2.1 %collective-permute-start.44 = (f32[2,256]{1,0:T(2,128)S(1)}, f32[2,256]{1,0:T(2,128)S(1)}, u32[]{:S(2)}, u32[]{:S(2)}) collective-permute-start(f32[2,256]{1,0:T(2,128)S(1)} %add.44.back_refs_0_), channel_id=1, source_target_pairs={{0,24},{1,25},{2,26},{3,27},{4,28},{5,29},{6,30},{7,31},{8,16},{9,... | collective-permute-start | bytes 6152 | tf_op jit(solution)/shard_map/ppermute | solution.py:1155
  115.1 1.3 collective-permute-start.42
  117.4 1.2 collective-permute-done.43.back_refs_2_
  118.7 1.7 back_in.1
  120.4 2.3 %weight_mid_term.1 = (bf16[2,1152,128]{2,1,0:T(8,128)(2,1)S(1)}, bf16[2,1152,128]{2,1,0:T(8,128)(2,1)S(1)}) custom-call(s32[4,8]{1,0:T(4,128)S(1)} %copy-done.1, bf16[3,976,256]{2,1,0:T(8,128)(2,1)S(1)} %get-tuple-element.172.taps_ref, bf16[976,512]{1,0:T(8,128)(2,1)S(1)} %get-tuple-element.173.low_ref), custom_call_target="tpu_custom_call" | custom-call | flops 1056964608 | bytes 3678336 | tf_op jit(solution)/shard_map/weight_mid_term/pallas_call | solution.py:164
  123.4 1.9 %collective-permute-done.48.arrived_refs_1_ = bf16[2,592,128]{2,1,0:T(8,128)(2,1)S(1)} collective-permute-done((bf16[2,592,128]{2,1,0:T(8,128)(2,1)S(1)}, bf16[2,592,128]{2,1,0:T(8,128)(2,1)S(1)}, u32[]{:S(2)}, u32[]{:S(2)}) %collective-permute-start.48) | collective-permute-done | bytes 303136 | tf_op jit(solution)/shard_map/ppermute | solution.py:1155
  125.5 1.6 collective-permute-start.49
  129.9 3.6 %finish_owned.1 = (bf16[4,784,256]{2,1,0:T(8,128)(2,1)}, bf16[4,784,256]{2,1,0:T(8,128)(2,1)S(1)}) custom-call(s32[4,8]{1,0:T(4,128)S(1)} %copy-done.1, bf16[2,784,256]{2,1,0:T(8,128)(2,1)S(1)} %collective-permute-done.29.even_ref, bf16[2,784,256]{2,1,0:T(8,128)(2,1)S(1)} %collective-permute-done.30.odd_ref, ...), custom_call_target="tpu_custom_call" | custom-call | bytes 7225472 | tf_op jit(solution)/shard_map/finish_owned/pallas_call | solution.py:164
  133.4 1.9 %collective-permute-done.49.arrived_ref = bf16[1280,128]{1,0:T(8,128)(2,1)S(1)} collective-permute-done((bf16[1280,128]{1,0:T(8,128)(2,1)S(1)}, bf16[1280,128]{1,0:T(8,128)(2,1)S(1)}, u32[]{:S(2)}, u32[]{:S(2)}) %collective-permute-start.49) | collective-permute-done | bytes 327712 | tf_op jit(solution)/shard_map/ppermute | solution.py:1155
  136.0 1.6 collective-permute-start.51
  138.7 5.9 %collective-permute-done.51.arrived_refs_1_ = bf16[640,128]{1,0:T(8,128)(2,1)S(1)} collective-permute-done((bf16[640,128]{1,0:T(8,128)(2,1)S(1)}, bf16[640,128]{1,0:T(8,128)(2,1)S(1)}, u32[]{:S(2)}, u32[]{:S(2)}) %collective-permute-start.51) | collective-permute-done | bytes 163872 | tf_op jit(solution)/shard_map/ppermute | solution.py:1155
  145.9 1.4 collective-permute-start.53
  147.3 1.1 collective-permute-start.54
  148.4 1.8 %collective-permute-start.55 = (bf16[304,128]{1,0:T(8,128)(2,1)S(1)}, bf16[304,128]{1,0:T(8,128)(2,1)S(1)}, u32[]{:S(2)}, u32[]{:S(2)}) collective-permute-start(bf16[304,128]{1,0:T(8,128)(2,1)S(1)} %get-tuple-element.193), channel_id=1, source_target_pairs={{0,24},{1,25},{2,26},{3,27},{4,28},{5,29},{6,30},{7,31},{8,16},{9,... | collective-permute-start | bytes 233480 | tf_op jit(solution)/shard_map/ppermute | solution.py:1155
  150.4 4.6 %collective-permute-done.54.arrived_refs_1_ = bf16[304,128]{1,0:T(8,128)(2,1)S(1)} collective-permute-done((bf16[304,128]{1,0:T(8,128)(2,1)S(1)}, bf16[304,128]{1,0:T(8,128)(2,1)S(1)}, u32[]{:S(2)}, u32[]{:S(2)}) %collective-permute-start.54) | collective-permute-done | bytes 77856 | tf_op jit(solution)/shard_map/ppermute | solution.py:1155
  155.0 1.8 %collective-permute-start.58 = (bf16[304,128]{1,0:T(8,128)(2,1)S(1)}, bf16[304,128]{1,0:T(8,128)(2,1)S(1)}, u32[]{:S(2)}, u32[]{:S(2)}) collective-permute-start(bf16[304,128]{1,0:T(8,128)(2,1)S(1)} %add_depth.1.piece_refs_0_), channel_id=1, source_target_pairs={{0,24},{1,25},{2,26},{3,27},{4,28},{5,29},{6,30},{7,31},{8,16},{9,... | collective-permute-start | bytes 233480 | tf_op jit(solution)/shard_map/ppermute | solution.py:1155
  156.8 1.1 collective-permute-start.57
  157.9 1.5 collective-permute-start.56
  159.4 1.8 %collective-permute-done.58.piece_refs_3_ = bf16[304,128]{1,0:T(8,128)(2,1)S(1)} collective-permute-done((bf16[304,128]{1,0:T(8,128)(2,1)S(1)}, bf16[304,128]{1,0:T(8,128)(2,1)S(1)}, u32[]{:S(2)}, u32[]{:S(2)}) %collective-permute-start.58) | collective-permute-done | bytes 77856 | tf_op jit(solution)/shard_map/ppermute | solution.py:1155
  161.3 1.8 collective-permute-done.57.piece_refs_2_
  164.2 3.7 %collective-permute-start.61 = (bf16[1216,128]{1,0:T(8,128)(2,1)S(1)}, bf16[1216,128]{1,0:T(8,128)(2,1)S(1)}, u32[]{:S(2)}, u32[]{:S(2)}) collective-permute-start(bf16[1216,128]{1,0:T(8,128)(2,1)S(1)} %join_depth.1.term_refs_0_), channel_id=1, source_target_pairs={{0,4},{1,5},{2,6},{3,7},{4,0},{5,1},{6,2},{7,3},{8,12},{9,13},{10,... | collective-permute-start | bytes 933896 | tf_op jit(solution)/shard_map/ppermute | solution.py:1155
  168.0 1.8 %grad_owned.1 = bf16[4,784,256]{2,1,0:T(8,128)(2,1)} custom-call(bf16[784,256]{1,0:T(8,128)(2,1)S(1)} %collective-permute-done.45.low_refs_0_, bf16[784,256]{1,0:T(8,128)(2,1)S(1)} %collective-permute-done.59.low_refs_1_, bf16[784,256]{1,0:T(8,128)(2,1)S(1)} %collective-permute-done.52.low_refs_2_, bf16[784,256]{1,0:T(8,128)(2,1)S(1)} %collective-permute-done.60.low_refs_3_, ...), custom_call_target="tpu_custom_call" | custom-call | flops 411041792 | bytes 5341184 | tf_op jit(solution)/shard_map/grad_owned/pallas_call | solution.py:164
  169.8 5.8 %collective-permute-done.61.term_refs_1_ = bf16[1216,128]{1,0:T(8,128)(2,1)S(1)} collective-permute-done((bf16[1216,128]{1,0:T(8,128)(2,1)S(1)}, bf16[1216,128]{1,0:T(8,128)(2,1)S(1)}, u32[]{:S(2)}, u32[]{:S(2)}) %collective-permute-start.61) | collective-permute-done | bytes 311328 | tf_op jit(solution)/shard_map/ppermute | solution.py:1155
  175.6 1.7 unpack.1
  (140 shorter events, 29.3 us)
Async XLA Ops:
  2.2 26.2 %copy-start.1 = (s32[4,8]{1,0:T(4,128)S(1)}, s32[4,8]{1,0:T(4,128)}, u32[]{:S(2)}) copy-start(s32[4,8]{1,0:T(4,128)} %counts_ref.35) | copy-start | bytes 388
  2.2 6.1 %collective-permute-start = (bf16[64,1024]{1,0:T(8,128)(2,1)S(1)}, bf16[64,1024]{1,0:T(8,128)(2,1)S(1)}, u32[]{:S(2)}, u32[]{:S(2)}) collective-permute-start(bf16[64,1024]{1,0:T(8,128)(2,1)S(1)} %bitcast.33), channel_id=1, source_target_pairs={{0,1},{1,0},{2,3},{3,2},{4,5},{5,4},{6,7},{7,6},{8,9},{9,8},{10,11... | collective-permute-start | bytes 393224 | tf_op jit(solution)/shard_map/ppermute | solution.py:1155
  2.7 15.5 %collective-permute-start.5 = (bf16[64,1024]{1,0:T(8,128)(2,1)S(1)}, bf16[64,1024]{1,0:T(8,128)(2,1)S(1)}, u32[]{:S(2)}, u32[]{:S(2)}) collective-permute-start(bf16[64,1024]{1,0:T(8,128)(2,1)S(1)} %bitcast.34), channel_id=1, source_target_pairs={{0,2},{1,3},{2,0},{3,1},{4,6},{5,7},{6,4},{7,5},{8,10},{9,11},{10,... | collective-permute-start | bytes 393224 | tf_op jit(solution)/shard_map/ppermute | solution.py:1155
  5.3 21.0 %collective-permute-start.4 = (bf16[784,256]{1,0:T(8,128)(2,1)S(1)}, bf16[784,256]{1,0:T(8,128)(2,1)S(1)}, u32[]{:S(2)}, u32[]{:S(2)}) collective-permute-start(bf16[784,256]{1,0:T(8,128)(2,1)S(1)} %get-tuple-element.220), channel_id=1, source_target_pairs={{0,6},{1,2},{2,4},{3,0},{4,7},{5,3},{6,5},{7,1},{8,14},{9,10},{10,... | collective-permute-start | bytes 1204232 | tf_op jit(solution)/shard_map/ppermute | solution.py:1155
  6.7 19.9 %collective-permute-start.3 = (bf16[784,256]{1,0:T(8,128)(2,1)S(1)}, bf16[784,256]{1,0:T(8,128)(2,1)S(1)}, u32[]{:S(2)}, u32[]{:S(2)}) collective-permute-start(bf16[784,256]{1,0:T(8,128)(2,1)S(1)} %get-tuple-element.221), channel_id=1, source_target_pairs={{0,2},{1,6},{2,0},{3,4},{4,3},{5,7},{6,1},{7,5},{8,10},{9,14},{10,... | collective-permute-start | bytes 1204232 | tf_op jit(solution)/shard_map/ppermute | solution.py:1155
  9.4 20.3 %copy-start = (bf16[4,784,256]{2,1,0:T(8,128)(2,1)S(1)}, bf16[4,784,256]{2,1,0:T(8,128)(2,1)}, u32[]{:S(2)}) copy-start(bf16[4,784,256]{2,1,0:T(8,128)(2,1)} %cot_ref.1) | copy-start | bytes 4816900
  9.4 18.9 %collective-permute-start.2 = (bf16[784,256]{1,0:T(8,128)(2,1)S(1)}, bf16[784,256]{1,0:T(8,128)(2,1)S(1)}, u32[]{:S(2)}, u32[]{:S(2)}) collective-permute-start(bf16[784,256]{1,0:T(8,128)(2,1)S(1)} %get-tuple-element.218), channel_id=1, source_target_pairs={{0,4},{1,0},{2,6},{3,2},{4,5},{5,1},{6,7},{7,3},{8,12},{9,8},{10,1... | collective-permute-start | bytes 1204232 | tf_op jit(solution)/shard_map/ppermute | solution.py:1155
  9.7 18.6 %collective-permute-start.1 = (bf16[784,256]{1,0:T(8,128)(2,1)S(1)}, bf16[784,256]{1,0:T(8,128)(2,1)S(1)}, u32[]{:S(2)}, u32[]{:S(2)}) collective-permute-start(bf16[784,256]{1,0:T(8,128)(2,1)S(1)} %get-tuple-element.219), channel_id=1, source_target_pairs={{0,0},{1,4},{2,2},{3,6},{4,1},{5,5},{6,3},{7,7},{8,8},{9,12},{10,1... | collective-permute-start | bytes 1204232 | tf_op jit(solution)/shard_map/ppermute | solution.py:1155
  18.3 1.3 collective-permute-start.6
  19.6 10.3 %collective-permute-start.7 = (bf16[1872,128]{1,0:T(8,128)(2,1)S(1)}, bf16[1872,128]{1,0:T(8,128)(2,1)S(1)}, u32[]{:S(2)}, u32[]{:S(2)}) collective-permute-start(bf16[1872,128]{1,0:T(8,128)(2,1)S(1)} %pack.1.b0), channel_id=1, source_target_pairs={{0,1},{1,0},{2,3},{3,2},{4,5},{5,4},{6,7},{7,6},{8,9},{9,8},{10,11... | collective-permute-start | bytes 1437704 | tf_op jit(solution)/shard_map/ppermute | solution.py:1155
  26.6 13.4 %collective-permute-start.12 = (bf16[1872,128]{1,0:T(8,128)(2,1)S(1)}, bf16[1872,128]{1,0:T(8,128)(2,1)S(1)}, u32[]{:S(2)}, u32[]{:S(2)}) collective-permute-start(bf16[1872,128]{1,0:T(8,128)(2,1)S(1)} %pack.1.b0), channel_id=1, source_target_pairs={{0,2},{1,3},{2,0},{3,1},{4,6},{5,7},{6,4},{7,5},{8,10},{9,11},{10,... | collective-permute-start | bytes 1437704 | tf_op jit(solution)/shard_map/ppermute | solution.py:1155
  29.9 1.2 collective-permute-start.8
  31.2 5.4 %collective-permute-start.11 = (f32[2,256]{1,0:T(2,128)S(1)}, f32[2,256]{1,0:T(2,128)S(1)}, u32[]{:S(2)}, u32[]{:S(2)}) collective-permute-start(f32[2,256]{1,0:T(2,128)S(1)} %add.39.sums_refs_0_), channel_id=1, source_target_pairs={{0,24},{1,25},{2,26},{3,27},{4,28},{5,29},{6,30},{7,31},{8,16},{9,... | collective-permute-start | bytes 6152 | tf_op jit(solution)/shard_map/ppermute | solution.py:1155
  34.8 4.5 %collective-permute-start.10 = (f32[2,256]{1,0:T(2,128)S(1)}, f32[2,256]{1,0:T(2,128)S(1)}, u32[]{:S(2)}, u32[]{:S(2)}) collective-permute-start(f32[2,256]{1,0:T(2,128)S(1)} %add.39.sums_refs_0_), channel_id=1, source_target_pairs={{0,16},{1,17},{2,18},{3,19},{4,20},{5,21},{6,22},{7,23},{8,24},{9,... | collective-permute-start | bytes 6152 | tf_op jit(solution)/shard_map/ppermute | solution.py:1155
  34.8 4.5 %collective-permute-start.9 = (f32[2,256]{1,0:T(2,128)S(1)}, f32[2,256]{1,0:T(2,128)S(1)}, u32[]{:S(2)}, u32[]{:S(2)}) collective-permute-start(f32[2,256]{1,0:T(2,128)S(1)} %add.39.sums_refs_0_), channel_id=1, source_target_pairs={{0,8},{1,9},{2,10},{3,11},{4,12},{5,13},{6,14},{7,15},{8,0},{9,1},... | collective-permute-start | bytes 6152 | tf_op jit(solution)/shard_map/ppermute | solution.py:1155
  35.6 20.1 %collective-permute-start.26 = (bf16[2,784,256]{2,1,0:T(8,128)(2,1)S(1)}, bf16[2,784,256]{2,1,0:T(8,128)(2,1)S(1)}, u32[]{:S(2)}, u32[]{:S(2)}) collective-permute-start(bf16[2,784,256]{2,1,0:T(8,128)(2,1)S(1)} %pad_maximum_fusion.1), channel_id=1, source_target_pairs={{0,0},{1,4},{2,2},{3,6},{4,1},{5,5},{6,3},{7,7},{8,8},{9,12},{10,1... | collective-permute-start | bytes 2408456 | tf_op jit(solution)/shard_map/ppermute | solution.py:1155
  39.2 16.7 %collective-permute-start.27 = (bf16[2,784,256]{2,1,0:T(8,128)(2,1)S(1)}, bf16[2,784,256]{2,1,0:T(8,128)(2,1)S(1)}, u32[]{:S(2)}, u32[]{:S(2)}) collective-permute-start(bf16[2,784,256]{2,1,0:T(8,128)(2,1)S(1)} %pad_maximum_fusion), channel_id=1, source_target_pairs={{0,4},{1,0},{2,6},{3,2},{4,5},{5,1},{6,7},{7,3},{8,12},{9,8},{10,1... | collective-permute-start | bytes 2408456 | tf_op jit(solution)/shard_map/ppermute | solution.py:1155
  40.0 2.3 %collective-permute-start.13 = (bf16[1872,128]{1,0:T(8,128)(2,1)S(1)}, bf16[1872,128]{1,0:T(8,128)(2,1)S(1)}, u32[]{:S(2)}, u32[]{:S(2)}) collective-permute-start(bf16[1872,128]{1,0:T(8,128)(2,1)S(1)} %collective-permute-done.12.b2), channel_id=1, source_target_pairs={{0,1},{1,0},{2,3},{3,2},{4,5},{5,4},{6,7},{7,6},{8,9},{9,8},{10,11... | collective-permute-start | bytes 1437704 | tf_op jit(solution)/shard_map/ppermute | solution.py:1155
  45.9 1.2 collective-permute-start.14
  47.2 5.4 %collective-permute-start.17 = (f32[2,512]{1,0:T(2,128)S(1)}, f32[2,512]{1,0:T(2,128)S(1)}, u32[]{:S(2)}, u32[]{:S(2)}) collective-permute-start(f32[2,512]{1,0:T(2,128)S(1)} %add.40.sums_refs_0_.mid_sums_refs_0_), channel_id=1, source_target_pairs={{0,24},{1,25},{2,26},{3,27},{4,28},{5,29},{6,30},{7,31},{8,16},{9,... | collective-permute-start | bytes 12296 | tf_op jit(solution)/shard_map/ppermute | solution.py:1155
  49.4 4.5 %collective-permute-start.16 = (f32[2,512]{1,0:T(2,128)S(1)}, f32[2,512]{1,0:T(2,128)S(1)}, u32[]{:S(2)}, u32[]{:S(2)}) collective-permute-start(f32[2,512]{1,0:T(2,128)S(1)} %add.40.sums_refs_0_.mid_sums_refs_0_), channel_id=1, source_target_pairs={{0,16},{1,17},{2,18},{3,19},{4,20},{5,21},{6,22},{7,23},{8,24},{9,... | collective-permute-start | bytes 12296 | tf_op jit(solution)/shard_map/ppermute | solution.py:1155
  49.4 4.5 %collective-permute-start.15 = (f32[2,512]{1,0:T(2,128)S(1)}, f32[2,512]{1,0:T(2,128)S(1)}, u32[]{:S(2)}, u32[]{:S(2)}) collective-permute-start(f32[2,512]{1,0:T(2,128)S(1)} %add.40.sums_refs_0_.mid_sums_refs_0_), channel_id=1, source_target_pairs={{0,8},{1,9},{2,10},{3,11},{4,12},{5,13},{6,14},{7,15},{8,0},{9,1},... | collective-permute-start | bytes 12296 | tf_op jit(solution)/shard_map/ppermute | solution.py:1155
  56.1 20.8 %collective-permute-start.28 = (bf16[2,784,256]{2,1,0:T(8,128)(2,1)S(1)}, bf16[2,784,256]{2,1,0:T(8,128)(2,1)S(1)}, u32[]{:S(2)}, u32[]{:S(2)}) collective-permute-start(bf16[2,784,256]{2,1,0:T(8,128)(2,1)S(1)} %pad_maximum_fusion.2), channel_id=1, source_target_pairs={{0,2},{1,3},{2,0},{3,1},{4,6},{5,7},{6,4},{7,5},{8,10},{9,11},{10,... | collective-permute-start | bytes 2408456 | tf_op jit(solution)/shard_map/ppermute | solution.py:1155
  56.7 1.7 collective-permute-start.18
  58.4 5.8 %collective-permute-start.21 = (f32[80,128]{1,0:T(8,128)S(1)}, f32[80,128]{1,0:T(8,128)S(1)}, u32[]{:S(2)}, u32[]{:S(2)}) collective-permute-start(f32[80,128]{1,0:T(8,128)S(1)} %constant_dynamic-update-slice_fusion.gathered_refs_0_), channel_id=1, source_target_pairs={{0,24},{1,25},{2,26},{3,27},{4,28},{5,29},{6,30},{7,31},{8,16},{9,... | collective-permute-start | bytes 122888 | tf_op jit(solution)/shard_map/ppermute | solution.py:1155
  61.9 4.9 %collective-permute-start.20 = (f32[80,128]{1,0:T(8,128)S(1)}, f32[80,128]{1,0:T(8,128)S(1)}, u32[]{:S(2)}, u32[]{:S(2)}) collective-permute-start(f32[80,128]{1,0:T(8,128)S(1)} %constant_dynamic-update-slice_fusion.gathered_refs_0_), channel_id=1, source_target_pairs={{0,16},{1,17},{2,18},{3,19},{4,20},{5,21},{6,22},{7,23},{8,24},{9,... | collective-permute-start | bytes 122888 | tf_op jit(solution)/shard_map/ppermute | solution.py:1155
  61.9 4.9 %collective-permute-start.19 = (f32[80,128]{1,0:T(8,128)S(1)}, f32[80,128]{1,0:T(8,128)S(1)}, u32[]{:S(2)}, u32[]{:S(2)}) collective-permute-start(f32[80,128]{1,0:T(8,128)S(1)} %constant_dynamic-update-slice_fusion.gathered_refs_0_), channel_id=1, source_target_pairs={{0,8},{1,9},{2,10},{3,11},{4,12},{5,13},{6,14},{7,15},{8,0},{9,1},... | collective-permute-start | bytes 122888 | tf_op jit(solution)/shard_map/ppermute | solution.py:1155
  68.9 1.2 collective-permute-start.22
  70.2 5.5 %collective-permute-start.25 = (f32[8,256]{1,0:T(8,128)S(1)}, f32[8,256]{1,0:T(8,128)S(1)}, u32[]{:S(2)}, u32[]{:S(2)}) collective-permute-start(f32[8,256]{1,0:T(8,128)S(1)} %add.41.sums_refs_0_), channel_id=1, source_target_pairs={{0,24},{1,25},{2,26},{3,27},{4,28},{5,29},{6,30},{7,31},{8,16},{9,... | collective-permute-start | bytes 24584 | tf_op jit(solution)/shard_map/ppermute | solution.py:1155
  72.2 4.6 %collective-permute-start.24 = (f32[8,256]{1,0:T(8,128)S(1)}, f32[8,256]{1,0:T(8,128)S(1)}, u32[]{:S(2)}, u32[]{:S(2)}) collective-permute-start(f32[8,256]{1,0:T(8,128)S(1)} %add.41.sums_refs_0_), channel_id=1, source_target_pairs={{0,16},{1,17},{2,18},{3,19},{4,20},{5,21},{6,22},{7,23},{8,24},{9,... | collective-permute-start | bytes 24584 | tf_op jit(solution)/shard_map/ppermute | solution.py:1155
  72.3 4.5 %collective-permute-start.23 = (f32[8,256]{1,0:T(8,128)S(1)}, f32[8,256]{1,0:T(8,128)S(1)}, u32[]{:S(2)}, u32[]{:S(2)}) collective-permute-start(f32[8,256]{1,0:T(8,128)S(1)} %add.41.sums_refs_0_), channel_id=1, source_target_pairs={{0,8},{1,9},{2,10},{3,11},{4,12},{5,13},{6,14},{7,15},{8,0},{9,1},... | collective-permute-start | bytes 24584 | tf_op jit(solution)/shard_map/ppermute | solution.py:1155
  79.9 24.0 %collective-permute-start.29 = (bf16[2,784,256]{2,1,0:T(8,128)(2,1)S(1)}, bf16[2,784,256]{2,1,0:T(8,128)(2,1)S(1)}, u32[]{:S(2)}, u32[]{:S(2)}) collective-permute-start(bf16[2,784,256]{2,1,0:T(8,128)(2,1)S(1)} %get-tuple-element.142), channel_id=1, source_target_pairs={{0,0},{1,4},{2,2},{3,6},{4,1},{5,5},{6,3},{7,7},{8,8},{9,12},{10,1... | collective-permute-start | bytes 2408456 | tf_op jit(solution)/shard_map/ppermute | solution.py:1155
  80.8 23.1 %collective-permute-start.30 = (bf16[2,784,256]{2,1,0:T(8,128)(2,1)S(1)}, bf16[2,784,256]{2,1,0:T(8,128)(2,1)S(1)}, u32[]{:S(2)}, u32[]{:S(2)}) collective-permute-start(bf16[2,784,256]{2,1,0:T(8,128)(2,1)S(1)} %get-tuple-element.143), channel_id=1, source_target_pairs={{0,1},{1,5},{2,3},{3,7},{4,0},{5,4},{6,2},{7,6},{8,9},{9,13},{10,1... | collective-permute-start | bytes 2408456 | tf_op jit(solution)/shard_map/ppermute | solution.py:1155
  83.9 1.9 %collective-permute-start.31 = (f32[8,256]{1,0:T(8,128)S(1)}, f32[8,256]{1,0:T(8,128)S(1)}, u32[]{:S(2)}, u32[]{:S(2)}) collective-permute-start(f32[8,256]{1,0:T(8,128)S(1)} %get-tuple-element.145), channel_id=1, source_target_pairs={{0,1},{1,0},{2,3},{3,2},{4,5},{5,4},{6,7},{7,6},{8,9},{9,8},{10,11... | collective-permute-start | bytes 24584 | tf_op jit(solution)/shard_map/ppermute | solution.py:1155
  85.8 5.5 %collective-permute-start.34 = (f32[8,256]{1,0:T(8,128)S(1)}, f32[8,256]{1,0:T(8,128)S(1)}, u32[]{:S(2)}, u32[]{:S(2)}) collective-permute-start(f32[8,256]{1,0:T(8,128)S(1)} %add.42.back_refs_0_.out_back_refs_0_), channel_id=1, source_target_pairs={{0,24},{1,25},{2,26},{3,27},{4,28},{5,29},{6,30},{7,31},{8,16},{9,... | collective-permute-start | bytes 24584 | tf_op jit(solution)/shard_map/ppermute | solution.py:1155
  88.0 4.6 %collective-permute-start.33 = (f32[8,256]{1,0:T(8,128)S(1)}, f32[8,256]{1,0:T(8,128)S(1)}, u32[]{:S(2)}, u32[]{:S(2)}) collective-permute-start(f32[8,256]{1,0:T(8,128)S(1)} %add.42.back_refs_0_.out_back_refs_0_), channel_id=1, source_target_pairs={{0,16},{1,17},{2,18},{3,19},{4,20},{5,21},{6,22},{7,23},{8,24},{9,... | collective-permute-start | bytes 24584 | tf_op jit(solution)/shard_map/ppermute | solution.py:1155
  88.9 3.7 %collective-permute-start.32 = (f32[8,256]{1,0:T(8,128)S(1)}, f32[8,256]{1,0:T(8,128)S(1)}, u32[]{:S(2)}, u32[]{:S(2)}) collective-permute-start(f32[8,256]{1,0:T(8,128)S(1)} %add.42.back_refs_0_.out_back_refs_0_), channel_id=1, source_target_pairs={{0,8},{1,9},{2,10},{3,11},{4,12},{5,13},{6,14},{7,15},{8,0},{9,1},... | collective-permute-start | bytes 24584 | tf_op jit(solution)/shard_map/ppermute | solution.py:1155
  96.2 1.2 collective-permute-start.35
  97.5 6.0 %collective-permute-start.38 = (f32[16,128]{1,0:T(8,128)S(1)}, f32[16,128]{1,0:T(8,128)S(1)}, u32[]{:S(2)}, u32[]{:S(2)}) collective-permute-start(f32[16,128]{1,0:T(8,128)S(1)} %pad_maximum_fusion.4.back_refs_0_), channel_id=1, source_target_pairs={{0,24},{1,25},{2,26},{3,27},{4,28},{5,29},{6,30},{7,31},{8,16},{9,... | collective-permute-start | bytes 24584 | tf_op jit(solution)/shard_map/ppermute | solution.py:1155
  99.3 4.6 %collective-permute-start.37 = (f32[16,128]{1,0:T(8,128)S(1)}, f32[16,128]{1,0:T(8,128)S(1)}, u32[]{:S(2)}, u32[]{:S(2)}) collective-permute-start(f32[16,128]{1,0:T(8,128)S(1)} %pad_maximum_fusion.4.back_refs_0_), channel_id=1, source_target_pairs={{0,16},{1,17},{2,18},{3,19},{4,20},{5,21},{6,22},{7,23},{8,24},{9,... | collective-permute-start | bytes 24584 | tf_op jit(solution)/shard_map/ppermute | solution.py:1155
  100.2 3.7 %collective-permute-start.36 = (f32[16,128]{1,0:T(8,128)S(1)}, f32[16,128]{1,0:T(8,128)S(1)}, u32[]{:S(2)}, u32[]{:S(2)}) collective-permute-start(f32[16,128]{1,0:T(8,128)S(1)} %pad_maximum_fusion.4.back_refs_0_), channel_id=1, source_target_pairs={{0,8},{1,9},{2,10},{3,11},{4,12},{5,13},{6,14},{7,15},{8,0},{9,1},... | collective-permute-start | bytes 24584 | tf_op jit(solution)/shard_map/ppermute | solution.py:1155
  104.1 18.8 %collective-permute-start.39 = (bf16[2,784,256]{2,1,0:T(8,128)(2,1)S(1)}, bf16[2,784,256]{2,1,0:T(8,128)(2,1)S(1)}, u32[]{:S(2)}, u32[]{:S(2)}) collective-permute-start(bf16[2,784,256]{2,1,0:T(8,128)(2,1)S(1)} %pad_maximum_fusion.3), channel_id=1, source_target_pairs={{0,2},{1,3},{2,0},{3,1},{4,6},{5,7},{6,4},{7,5},{8,10},{9,11},{10,... | collective-permute-start | bytes 2408456 | tf_op jit(solution)/shard_map/ppermute | solution.py:1155
  105.7 4.9 %collective-permute-start.40 = (bf16[2,656,128]{2,1,0:T(8,128)(2,1)S(1)}, bf16[2,656,128]{2,1,0:T(8,128)(2,1)S(1)}, u32[]{:S(2)}, u32[]{:S(2)}) collective-permute-start(bf16[2,656,128]{2,1,0:T(8,128)(2,1)S(1)} %get-tuple-element.165), channel_id=1, source_target_pairs={{0,1},{1,0},{2,3},{3,2},{4,5},{5,4},{6,7},{7,6},{8,9},{9,8},{10,11... | collective-permute-start | bytes 1007624 | tf_op jit(solution)/shard_map/ppermute | solution.py:1155
  110.6 1.4 collective-permute-start.41
  112.0 5.4 %collective-permute-start.44 = (f32[2,256]{1,0:T(2,128)S(1)}, f32[2,256]{1,0:T(2,128)S(1)}, u32[]{:S(2)}, u32[]{:S(2)}) collective-permute-start(f32[2,256]{1,0:T(2,128)S(1)} %add.44.back_refs_0_), channel_id=1, source_target_pairs={{0,24},{1,25},{2,26},{3,27},{4,28},{5,29},{6,30},{7,31},{8,16},{9,... | collective-permute-start | bytes 6152 | tf_op jit(solution)/shard_map/ppermute | solution.py:1155
  114.1 4.5 %collective-permute-start.43 = (f32[2,256]{1,0:T(2,128)S(1)}, f32[2,256]{1,0:T(2,128)S(1)}, u32[]{:S(2)}, u32[]{:S(2)}) collective-permute-start(f32[2,256]{1,0:T(2,128)S(1)} %add.44.back_refs_0_), channel_id=1, source_target_pairs={{0,16},{1,17},{2,18},{3,19},{4,20},{5,21},{6,22},{7,23},{8,24},{9,... | collective-permute-start | bytes 6152 | tf_op jit(solution)/shard_map/ppermute | solution.py:1155
  115.1 3.6 %collective-permute-start.42 = (f32[2,256]{1,0:T(2,128)S(1)}, f32[2,256]{1,0:T(2,128)S(1)}, u32[]{:S(2)}, u32[]{:S(2)}) collective-permute-start(f32[2,256]{1,0:T(2,128)S(1)} %add.44.back_refs_0_), channel_id=1, source_target_pairs={{0,8},{1,9},{2,10},{3,11},{4,12},{5,13},{6,14},{7,15},{8,0},{9,1},... | collective-permute-start | bytes 6152 | tf_op jit(solution)/shard_map/ppermute | solution.py:1155
  122.9 4.2 %collective-permute-start.46 = (bf16[2,1152,128]{2,1,0:T(8,128)(2,1)S(1)}, bf16[2,1152,128]{2,1,0:T(8,128)(2,1)S(1)}, u32[]{:S(2)}, u32[]{:S(2)}) collective-permute-start(bf16[2,1152,128]{2,1,0:T(8,128)(2,1)S(1)} %get-tuple-element.176), channel_id=1, source_target_pairs={{0,1},{1,0},{2,3},{3,2},{4,5},{5,4},{6,7},{7,6},{8,9},{9,8},{10,11... | collective-permute-start | bytes 1769480 | tf_op jit(solution)/shard_map/ppermute | solution.py:1155
  122.9 2.4 %collective-permute-start.48 = (bf16[2,592,128]{2,1,0:T(8,128)(2,1)S(1)}, bf16[2,592,128]{2,1,0:T(8,128)(2,1)S(1)}, u32[]{:S(2)}, u32[]{:S(2)}) collective-permute-start(bf16[2,592,128]{2,1,0:T(8,128)(2,1)S(1)} %get-tuple-element.181), channel_id=1, source_target_pairs={{0,1},{1,0},{2,3},{3,2},{4,5},{5,4},{6,7},{7,6},{8,9},{9,8},{10,11... | collective-permute-start | bytes 909320 | tf_op jit(solution)/shard_map/ppermute | solution.py:1155
  125.5 9.8 %collective-permute-start.49 = (bf16[1280,128]{1,0:T(8,128)(2,1)S(1)}, bf16[1280,128]{1,0:T(8,128)(2,1)S(1)}, u32[]{:S(2)}, u32[]{:S(2)}) collective-permute-start(bf16[1280,128]{1,0:T(8,128)(2,1)S(1)} %get-tuple-element.183), channel_id=1, source_target_pairs={{0,2},{1,3},{2,0},{3,1},{4,6},{5,7},{6,4},{7,5},{8,10},{9,11},{10,... | collective-permute-start | bytes 983048 | tf_op jit(solution)/shard_map/ppermute | solution.py:1155
  128.0 9.7 %collective-permute-start.47 = (bf16[2,576,128]{2,1,0:T(8,128)(2,1)S(1)}, bf16[2,576,128]{2,1,0:T(8,128)(2,1)S(1)}, u32[]{:S(2)}, u32[]{:S(2)}) collective-permute-start(bf16[2,576,128]{2,1,0:T(8,128)(2,1)S(1)} %get-tuple-element.178), channel_id=1, source_target_pairs={{0,4},{1,5},{2,6},{3,7},{4,0},{5,1},{6,2},{7,3},{8,12},{9,13},{10,... | collective-permute-start | bytes 884744 | tf_op jit(solution)/shard_map/ppermute | solution.py:1155
  129.0 16.3 %collective-permute-start.45 = (bf16[784,256]{1,0:T(8,128)(2,1)S(1)}, bf16[784,256]{1,0:T(8,128)(2,1)S(1)}, u32[]{:S(2)}, u32[]{:S(2)}) collective-permute-start(bf16[784,256]{1,0:T(8,128)(2,1)S(1)} %get-tuple-element.170), channel_id=1, source_target_pairs={{0,0},{1,4},{2,2},{3,6},{4,1},{5,5},{6,3},{7,7},{8,8},{9,12},{10,1... | collective-permute-start | bytes 1204232 | tf_op jit(solution)/shard_map/ppermute | solution.py:1155
  136.0 8.6 %collective-permute-start.51 = (bf16[640,128]{1,0:T(8,128)(2,1)S(1)}, bf16[640,128]{1,0:T(8,128)(2,1)S(1)}, u32[]{:S(2)}, u32[]{:S(2)}) collective-permute-start(bf16[640,128]{1,0:T(8,128)(2,1)S(1)} %get-tuple-element.187), channel_id=1, source_target_pairs={{0,4},{1,5},{2,6},{3,7},{4,0},{5,1},{6,2},{7,3},{8,12},{9,13},{10,... | collective-permute-start | bytes 491528 | tf_op jit(solution)/shard_map/ppermute | solution.py:1155
  137.7 6.9 %collective-permute-start.50 = (bf16[576,128]{1,0:T(8,128)(2,1)S(1)}, bf16[576,128]{1,0:T(8,128)(2,1)S(1)}, u32[]{:S(2)}, u32[]{:S(2)}) collective-permute-start(bf16[576,128]{1,0:T(8,128)(2,1)S(1)} %get-tuple-element.186), channel_id=1, source_target_pairs={{0,2},{1,3},{2,0},{3,1},{4,6},{5,7},{6,4},{7,5},{8,10},{9,11},{10,... | collective-permute-start | bytes 442376 | tf_op jit(solution)/shard_map/ppermute | solution.py:1155
  145.3 17.8 %collective-permute-start.52 = (bf16[784,256]{1,0:T(8,128)(2,1)S(1)}, bf16[784,256]{1,0:T(8,128)(2,1)S(1)}, u32[]{:S(2)}, u32[]{:S(2)}) collective-permute-start(bf16[784,256]{1,0:T(8,128)(2,1)S(1)} %collective-permute-done.45.low_refs_0_), channel_id=1, source_target_pairs={{0,2},{1,3},{2,0},{3,1},{4,6},{5,7},{6,4},{7,5},{8,10},{9,11},{10,... | collective-permute-start | bytes 1204232 | tf_op jit(solution)/shard_map/ppermute | solution.py:1155
  145.9 4.5 %collective-permute-start.53 = (bf16[304,128]{1,0:T(8,128)(2,1)S(1)}, bf16[304,128]{1,0:T(8,128)(2,1)S(1)}, u32[]{:S(2)}, u32[]{:S(2)}) collective-permute-start(bf16[304,128]{1,0:T(8,128)(2,1)S(1)} %get-tuple-element.191), channel_id=1, source_target_pairs={{0,8},{1,9},{2,10},{3,11},{4,12},{5,13},{6,14},{7,15},{8,0},{9,1},... | collective-permute-start | bytes 233480 | tf_op jit(solution)/shard_map/ppermute | solution.py:1155
  147.3 7.6 %collective-permute-start.54 = (bf16[304,128]{1,0:T(8,128)(2,1)S(1)}, bf16[304,128]{1,0:T(8,128)(2,1)S(1)}, u32[]{:S(2)}, u32[]{:S(2)}) collective-permute-start(bf16[304,128]{1,0:T(8,128)(2,1)S(1)} %get-tuple-element.192), channel_id=1, source_target_pairs={{0,16},{1,17},{2,18},{3,19},{4,20},{5,21},{6,22},{7,23},{8,24},{9,... | collective-permute-start | bytes 233480 | tf_op jit(solution)/shard_map/ppermute | solution.py:1155
  148.4 6.5 %collective-permute-start.55 = (bf16[304,128]{1,0:T(8,128)(2,1)S(1)}, bf16[304,128]{1,0:T(8,128)(2,1)S(1)}, u32[]{:S(2)}, u32[]{:S(2)}) collective-permute-start(bf16[304,128]{1,0:T(8,128)(2,1)S(1)} %get-tuple-element.193), channel_id=1, source_target_pairs={{0,24},{1,25},{2,26},{3,27},{4,28},{5,29},{6,30},{7,31},{8,16},{9,... | collective-permute-start | bytes 233480 | tf_op jit(solution)/shard_map/ppermute | solution.py:1155
  155.0 6.3 %collective-permute-start.58 = (bf16[304,128]{1,0:T(8,128)(2,1)S(1)}, bf16[304,128]{1,0:T(8,128)(2,1)S(1)}, u32[]{:S(2)}, u32[]{:S(2)}) collective-permute-start(bf16[304,128]{1,0:T(8,128)(2,1)S(1)} %add_depth.1.piece_refs_0_), channel_id=1, source_target_pairs={{0,24},{1,25},{2,26},{3,27},{4,28},{5,29},{6,30},{7,31},{8,16},{9,... | collective-permute-start | bytes 233480 | tf_op jit(solution)/shard_map/ppermute | solution.py:1155
  156.8 6.3 %collective-permute-start.57 = (bf16[304,128]{1,0:T(8,128)(2,1)S(1)}, bf16[304,128]{1,0:T(8,128)(2,1)S(1)}, u32[]{:S(2)}, u32[]{:S(2)}) collective-permute-start(bf16[304,128]{1,0:T(8,128)(2,1)S(1)} %add_depth.1.piece_refs_0_), channel_id=1, source_target_pairs={{0,16},{1,17},{2,18},{3,19},{4,20},{5,21},{6,22},{7,23},{8,24},{9,... | collective-permute-start | bytes 233480 | tf_op jit(solution)/shard_map/ppermute | solution.py:1155
  157.9 5.2 %collective-permute-start.56 = (bf16[304,128]{1,0:T(8,128)(2,1)S(1)}, bf16[304,128]{1,0:T(8,128)(2,1)S(1)}, u32[]{:S(2)}, u32[]{:S(2)}) collective-permute-start(bf16[304,128]{1,0:T(8,128)(2,1)S(1)} %add_depth.1.piece_refs_0_), channel_id=1, source_target_pairs={{0,8},{1,9},{2,10},{3,11},{4,12},{5,13},{6,14},{7,15},{8,0},{9,1},... | collective-permute-start | bytes 233480 | tf_op jit(solution)/shard_map/ppermute | solution.py:1155
  163.1 4.9 %collective-permute-start.59 = (bf16[784,256]{1,0:T(8,128)(2,1)S(1)}, bf16[784,256]{1,0:T(8,128)(2,1)S(1)}, u32[]{:S(2)}, u32[]{:S(2)}) collective-permute-start(bf16[784,256]{1,0:T(8,128)(2,1)S(1)} %collective-permute-done.45.low_refs_0_), channel_id=1, source_target_pairs={{0,1},{1,0},{2,3},{3,2},{4,5},{5,4},{6,7},{7,6},{8,9},{9,8},{10,11... | collective-permute-start | bytes 1204232 | tf_op jit(solution)/shard_map/ppermute | solution.py:1155
  163.1 4.9 %collective-permute-start.60 = (bf16[784,256]{1,0:T(8,128)(2,1)S(1)}, bf16[784,256]{1,0:T(8,128)(2,1)S(1)}, u32[]{:S(2)}, u32[]{:S(2)}) collective-permute-start(bf16[784,256]{1,0:T(8,128)(2,1)S(1)} %collective-permute-done.52.low_refs_2_), channel_id=1, source_target_pairs={{0,1},{1,0},{2,3},{3,2},{4,5},{5,4},{6,7},{7,6},{8,9},{9,8},{10,11... | collective-permute-start | bytes 1204232 | tf_op jit(solution)/shard_map/ppermute | solution.py:1155
  164.2 11.3 %collective-permute-start.61 = (bf16[1216,128]{1,0:T(8,128)(2,1)S(1)}, bf16[1216,128]{1,0:T(8,128)(2,1)S(1)}, u32[]{:S(2)}, u32[]{:S(2)}) collective-permute-start(bf16[1216,128]{1,0:T(8,128)(2,1)S(1)} %join_depth.1.term_refs_0_), channel_id=1, source_target_pairs={{0,4},{1,5},{2,6},{3,7},{4,0},{5,1},{6,2},{7,3},{8,12},{9,13},{10,... | collective-permute-start | bytes 933896 | tf_op jit(solution)/shard_map/ppermute | solution.py:1155
  (14 other events, 123.9 us)

commit v5 on v4

--- a/solution.py
+++ b/solution.py
@@ -13,7 +13,7 @@
 PADDED = SIDE * WIDE
 STRIDE = PADDED + WIDE
 CHUNK = 16
-UNROLL = 7
+UNROLL = 49
 VMEM_LIMIT = 24 * 2**20
 SLOTS = (0, 1, 2, 3)
 GATHERED = 40
@@ -55,6 +55,25 @@
     return lax.dot_general(
         left, right, (((0,), (0,)), ((), ())), preferred_element_type=F32, precision=precision
     )
+
+
+def row_sums(matrix):
+    return dot_nn(jnp.ones((16, matrix.shape[0]), BF16), matrix)[0:1]
+
+
+def outer(column, row, row_exact=False):
+    exact, rounded = (row, column) if row_exact else (column, row)
+    high = exact.astype(BF16).astype(F32)
+    middle = (exact - high).astype(BF16).astype(F32)
+    empty = jnp.zeros((13, exact.shape[1]), F32)
+    exact = jnp.concatenate([high, middle, exact - high - middle, empty], axis=0).astype(BF16)
+    rounded = jnp.broadcast_to(rounded, (16, rounded.shape[1])).astype(BF16)
+    return dot_tn(rounded, exact) if row_exact else dot_tn(exact, rounded)
+
+
+def expected(gain, shift):
+    reach = 3.0**0.5 * gain
+    return (4.0 * silu(shift) + silu(shift + reach) + silu(shift - reach)) / 6.0
 
 
 def logistic(value):
@@ -247,7 +266,11 @@
         value = pre_ref[image * PADDED : (image + 1) * PADDED, :]
         first = first + real * total_of(value)
         second = second + real * total_of(value * value)
-    msg_ref[...] = jnp.concatenate([first, second], axis=0)
+    rows = x0.shape[0]
+    spot = lax.broadcasted_iota(jnp.int32, (16, rows), 1)
+    real = (spot < place.images(place.depth, place.core) * PIXELS).astype(BF16)
+    columns = [dot_nn(real, x[...])[0:1] for x in (x0, x1, x2, x3)]
+    msg_ref[...] = jnp.concatenate([first, second] + columns, axis=0)
 
 
 def place_mid(
@@ -335,7 +358,7 @@
             store_taps(taps_ref, image * STRIDE + WIDE + rows, value)
             return carry
 
-        lax.fori_loop(0, SIDE, normalize, 0, unroll=UNROLL)
+        lax.fori_loop(0, SIDE, normalize, 0, unroll=SIDE)
     half = pre_ref.shape[1] // 2
     width = pre_ref.shape[1]
     keep = columns_real(PADDED)
@@ -408,7 +431,7 @@
 
         nothing = jnp.zeros((8, 2 * width), F32)
         active, rise, lean = lax.fori_loop(
-            0, PADDED // CHUNK, gather, (nothing, nothing, nothing), unroll=UNROLL
+            0, SIDE, gather, (nothing, nothing, nothing), unroll=SIDE
         )
         active = total_of(active)
         pooled_ref[image : image + 1, :] = (active[:, :width] + active[:, width:]) / PIXELS
@@ -480,7 +503,7 @@
             wide_ref[pl.ds(at, CHUNK), :] = value[:, :width] + value[:, width:]
             return carry
 
-        lax.fori_loop(0, PADDED // CHUNK, weigh, 0, unroll=UNROLL)
+        lax.fori_loop(0, SIDE, weigh, 0, unroll=SIDE)
     pack_map_rows(wide_ref, flat_ref)
     weighted_ref[...] = flat_ref[...].astype(BF16)
     spot = lax.broadcasted_iota(jnp.int32, (flat_ref.shape[0], 1), 0)
@@ -503,8 +526,8 @@
     cot_even_ref,
     cot_odd_ref,
     cot_across_ref,
-    even_ref,
-    odd_ref,
+    near_ref,
+    far_ref,
     grad_ref,
     msg_ref,
 ):
@@ -520,7 +543,7 @@
         gain = affine_ref[0, block] * r
         shift = affine_ref[1, block] - mu * gain
         x_ref, upstream_ref = x_refs[k], cot_refs[k]
-        summed_ref = (even_ref, odd_ref)[k & 1].at[k >> 1]
+        summed_ref = (near_ref, far_ref)[k >> 1].at[k & 1]
 
         def chunk(
             step, carry, k=k, gain=gain, shift=shift,
@@ -548,9 +571,9 @@
             msg_ref[t * blocks + k : t * blocks + k + 1, :] = row
 
 
-def finish_owned(counts_ref, even_ref, odd_ref, across_ref, cot_ref, result_ref, grad_ref):
+def finish_owned(counts_ref, summed_ref, swapped_ref, cot_ref, result_ref, grad_ref):
     chan, group = lax.axis_index("chan"), lax.axis_index("dp")
-    pieces = slot_refs(even_ref, odd_ref, across_ref)
+    pieces = summed_ref.at[0], swapped_ref.at[0], summed_ref.at[2], swapped_ref.at[1]
     rows = cot_ref.shape[1]
     for s, piece in enumerate(pieces):
         batch = chan ^ s
@@ -639,7 +662,7 @@
 
         nothing = jnp.zeros((8, 2 * width), F32)
         parts = lax.fori_loop(
-            0, PADDED // CHUNK, gather, (nothing, nothing, nothing), unroll=UNROLL
+            0, SIDE, gather, (nothing, nothing, nothing), unroll=SIDE
         )
         share = attention_ref[image : image + 1, :]
         attended.append(total_of(parts[0]))
@@ -746,7 +769,7 @@
             store_taps(taps_ref, image * STRIDE + WIDE + rows, value)
             return carry
 
-        lax.fori_loop(0, SIDE, chunk, 0, unroll=UNROLL)
+        lax.fori_loop(0, SIDE, chunk, 0, unroll=SIDE)
     low_ref[...] = taps_ref[1]
     sums = summed_over(sums_refs)
     center, scale = moments(sums[0:1], sums[1:2], total)
@@ -804,6 +827,7 @@
     low_ref,
     gate_ref,
     logits_ref,
+    affine_ref,
     keep_ref,
     send_ref,
     wide_ref,
@@ -813,10 +837,13 @@
     width = weighted_ref.shape[1]
     lanes = keep_ref.shape[2]
     own = width // len(SLOTS)
+    center = expected(affine_ref[0:1, :], affine_ref[1:2, :])
+    center = 0.5 * (center[:, :width] + center[:, width:])
     for turn, s in enumerate(ORDER):
         target = keep_ref if turn < 2 else send_ref
         held = place.batch ^ place.chan ^ s
-        term = dot_tn(weighted_ref[...], low_ref[held]).astype(BF16)
+        term = dot_tn(weighted_ref[...], low_ref[held])
+        term = (term - outer(center, row_sums(low_ref[held]), True)).astype(BF16)
         target[turn % 2, 0:width, :] = term[:, :lanes]
         target[turn % 2, width : 2 * width, :] = term[:, lanes:]
     wide_ref[...] = dot_tn(logits_ref[...], gate_ref[0], HIGHEST)
@@ -838,11 +865,13 @@
     counts_ref,
     taps_ref,
     low_ref,
+    affine_ref,
     keep_ref,
     send_ref,
     wide_ref,
 ):
     place = Place(counts_ref)
+    center = expected(affine_ref[0:1, :], affine_ref[1:2, :])
     half = taps_ref.shape[2] // 2
     width = low_ref.shape[1] // 2
     own = width // len(SLOTS)
@@ -856,7 +885,9 @@
             ],
             axis=1,
         )
-        wide_ref[...] = dot_tn(low_ref[WIDE : WIDE + rows, r * width : (r + 1) * width], right)
+        low = low_ref[WIDE : WIDE + rows, r * width : (r + 1) * width]
+        offset = jnp.concatenate([center[:, r * half : (r + 1) * half]] * 9, axis=1)
+        wide_ref[...] = dot_tn(low, right) - outer(row_sums(low), offset)
         for turn, s in enumerate(ORDER):
             target = keep_ref if turn < 2 else send_ref
             here = pl.ds(pl.multiple_of((place.chan ^ s) * own, own), own)
@@ -915,8 +946,9 @@
             flat_ref[at : at + SIDE, :] = value[:SIDE]
     low_ref[...] = flat_ref[...].astype(BF16)
     lanes = keep_ref.shape[2]
+    low_sums = row_sums(low_ref[...])
     for k, x in enumerate((x0, x1, x2, x3)):
-        wide_ref[...] = dot_tn(low_ref[...], x[...])
+        wide_ref[...] = dot_tn(low_ref[...], x[...]) - outer(low_sums, sums[2 + k : 3 + k] / total)
         for turn, s in enumerate(ORDER):
             target = keep_ref if turn < 2 else send_ref
             here = pl.ds(pl.multiple_of((chan ^ s) * own, own), own)
@@ -985,43 +1017,39 @@
             ref[at:, :] = jnp.zeros((kept_ref.shape[0] - at, ref.shape[1]), BF16)
 
 
-def split_rows(parity, whole_ref, kept_ref, send_ref):
+def split_rows(parity, keep_ref, arrived_ref, kept_ref, send_ref):
     rows = kept_ref.shape[-2]
-    mine = pl.ds(pl.multiple_of(parity * rows, 16), rows)
-    other = pl.ds(pl.multiple_of((1 - parity) * rows, 16), rows)
-    if whole_ref.ndim == 2:
-        kept_ref[...] = whole_ref[mine, :]
-        send_ref[...] = whole_ref[other, :].astype(BF16)
-    else:
-        kept_ref[...] = whole_ref[:, mine, :]
-        send_ref[...] = whole_ref[:, other, :].astype(BF16)
-
-
-def add_core_first(counts_ref, keep_ref, arrived_ref, kept_ref, send_ref, whole_ref):
-    whole_ref[...] = added(keep_ref, arrived_ref)
-    split_rows(Place(counts_ref).parity, whole_ref, kept_ref, send_ref)
+    for own, target in ((parity, kept_ref), (1 - parity, send_ref)):
+        here = pl.ds(pl.multiple_of(own * rows, 16), rows)
+        if target.ndim == 2:
+            value = added(keep_ref.at[here, :], arrived_ref.at[here, :])
+        else:
+            value = added(keep_ref.at[:, here, :], arrived_ref.at[:, here, :])
+        target[...] = value.astype(target.dtype)
+
+
+def add_core_first(counts_ref, keep_ref, arrived_ref, kept_ref, send_ref):
+    split_rows(Place(counts_ref).parity, keep_ref, arrived_ref, kept_ref, send_ref)
 
 
 def add_parity_first(keep_ref, arrived_ref, kept_ref, send_ref):
-    value = added(keep_ref, arrived_ref)
-    kept_ref[...] = value[0]
-    send_ref[...] = value[1].astype(BF16)
-
-
-def add_chip(counts_ref, keep_ref, arrived_ref, kept_ref, send_ref, whole_ref):
-    whole_ref[...] = added(keep_ref, arrived_ref)
-    split_rows(Place(counts_ref).parity, whole_ref, kept_ref, send_ref)
-
-
-def add_last(counts_ref, keep_refs, arrived_refs, kept_ref, s1, s2, s3, whole_refs):
+    kept_ref[...] = added(keep_ref.at[0], arrived_ref.at[0])
+    send_ref[...] = added(keep_ref.at[1], arrived_ref.at[1]).astype(BF16)
+
+
+def add_chip(counts_ref, keep_ref, arrived_ref, kept_ref, send_ref):
+    split_rows(Place(counts_ref).parity, keep_ref, arrived_ref, kept_ref, send_ref)
+
+
+def add_last(counts_ref, keep_refs, arrived_refs, kept_ref, s1, s2, s3):
     place = Place(counts_ref)
     at = 0
-    for keep_ref, arrived_ref, whole_ref in zip(keep_refs, arrived_refs, whole_refs):
-        whole_ref[...] = added(keep_ref, arrived_ref)
+    for keep_ref, arrived_ref in zip(keep_refs, arrived_refs):
         rows = keep_ref.shape[0] // len(SLOTS)
         for t, target in enumerate((kept_ref, s1, s2, s3)):
             here = pl.ds(pl.multiple_of((place.depth ^ t) * rows, 16), rows)
-            target[at : at + rows, :] = whole_ref[here, :].astype(target.dtype)
+            value = added(keep_ref.at[here, :], arrived_ref.at[here, :])
+            target[at : at + rows, :] = value.astype(target.dtype)
         at += rows
 
 
@@ -1041,20 +1069,6 @@
     rows = piece_refs[0].shape[0]
     for t, ref in enumerate(piece_refs):
         whole_ref[pl.ds(pl.multiple_of((place.depth ^ t) * rows, 16), rows), :] = ref[...]
-
-
-def join_halves(counts_ref, half_refs, first_ref, second_ref):
-    place = Place(counts_ref)
-    for t, ref in enumerate(half_refs):
-        piece = ref.shape[0] // len(SLOTS)
-        row = 0
-        for target in (first_ref, second_ref):
-            rows = target.shape[0] // 2 // len(SLOTS)
-            for z in range(len(SLOTS)):
-                at = ((place.parity ^ t) * len(SLOTS) + z) * rows
-                source = ref[z * piece + row : z * piece + row + rows, :]
-                target[pl.ds(pl.multiple_of(at, 16), rows), :] = source.astype(F32)
-            row += rows
 
 
 def unpack(
@@ -1075,34 +1089,46 @@
     out_ref,
     gain_out_ref,
     shift_out_ref,
-    first_ref,
     second_ref,
 ):
-    if joined:
-        first_ref[...] = term_refs[0][...].astype(F32)
-        second_ref[...] = term_refs[1][...].astype(F32)
-    else:
-        join_halves(counts_ref, term_refs, first_ref, second_ref)
     own, lanes = squeeze_ref.shape
     width = out_ref.shape[0]
+    places = [(out_ref, 0, 0, width), (out_ref, 0, 1, width), (excite_ref, 0, 0, 2 * own)]
+    places += [(second_ref, 0, 0, 16)]
+    places += [(in_ref, 0, block, own) for block in range(in_ref.shape[1] // lanes)]
+    places += [(squeeze_ref, 0, 0, own), (second_ref, 16, 0, 16)]
+
+    def write(value, row):
+        start = 0
+        for target, at, block, rows in places:
+            first, last = max(row, start), min(row + value.shape[0], start + rows)
+            if first < last:
+                there = slice(at + first - start, at + last - start)
+                target[there, block * lanes : (block + 1) * lanes] = value[first - row : last - row]
+            start += rows
+
+    if joined:
+        mid_ref[...] = term_refs[0][...].astype(F32)
+        write(term_refs[1][...].astype(F32), 0)
+    else:
+        even = Place(counts_ref).parity == 0
+        piece = term_refs[0].shape[0] // len(SLOTS)
+        rows = mid_ref.shape[0] // 2 // len(SLOTS)
+        for half in range(2):
+            mine, other = term_refs[half], term_refs[1 - half]
+            for z in range(len(SLOTS)):
+                here = slice(z * piece, (z + 1) * piece)
+                value = jnp.where(even, mine[here, :].astype(F32), other[here, :].astype(F32))
+                at = (half * len(SLOTS) + z) * rows
+                mid_ref[at : at + rows, :] = value[:rows]
+                write(value[rows:], (half * len(SLOTS) + z) * (piece - rows))
 
     def halves(target, row):
         target[0:1, :] = second_ref[row : row + 1, :own]
         target[1:2, :] = second_ref[row : row + 1, own:]
 
-    mid_ref[...] = first_ref[...]
-    out_ref[:, :lanes] = second_ref[0:width, :]
-    out_ref[:, lanes:] = second_ref[width : 2 * width, :]
-    row = 2 * width
-    excite_ref[...] = second_ref[row : row + 2 * own, :]
-    row += 2 * own
-    halves(bias_ref, row)
-    row += 16
-    for block in range(in_ref.shape[1] // lanes):
-        in_ref[:, block * lanes : (block + 1) * lanes] = second_ref[row : row + own, :]
-        row += own
-    squeeze_ref[...] = second_ref[row : row + own, :]
-    row += own
+    halves(bias_ref, 0)
+    row = 16
     gain_in_ref[...] = second_ref[row : row + 1, :own]
     shift_in_ref[...] = second_ref[row : row + 1, own:]
     halves(gain_mid_ref, row + 1)
@@ -1157,8 +1183,8 @@
     def home(tensor, s):
         return permute(tensor, lambda z, x, y, c: (z, c ^ (s & 1), y ^ (s >> 1), x))
 
-    def away_plane(tensor, odd=0):
-        return permute(tensor, lambda z, x, y, c: (z, c, y, x ^ odd))
+    def away_plane(tensor):
+        return permute(tensor, lambda z, x, y, c: (z, c, y, x))
 
     def cross(even, odd):
         return even, odd, across(jnp.stack([even[1], odd[1]]))
@@ -1209,7 +1235,7 @@
     def kernel(body, outs, *args, smem=1):
         return call(body, outs, [], 0, *args, smem=smem)
 
-    def add_over_all(first, second, low, result):
+    def add_over_all(first, second, low, summed, finish_own):
         first_rows, second_rows = first[0].shape[1], sum(k.shape[1] for k in second[0])
         if groups != 8:
             rows = padded(first_rows + second_rows)
@@ -1225,7 +1251,7 @@
             (terms,) = kernel(add_groups, [shape(terms.shape, BF16)], terms, smem=0)
             terms = lax.all_to_all(terms, "dp", 0, 0).reshape(rows, -1)
             terms = terms[:first_rows], terms[first_rows : first_rows + second_rows]
-            return terms, low, across(low)
+            return (terms, low, across(low)) + tuple(finish_own(summed))
         second_rows = padded(second_rows)
         halves = (first_rows // 2, second_rows // 2)
         pieces = (first_rows // groups, second_rows // groups)
@@ -1233,22 +1259,23 @@
         def rows(number, kind=F32):
             return shape((number, 2 * own), kind)
 
-        keep, send = kernel(add_core, [rows(second_rows, BF16)] * 2, *second, smem=0)
-        arrived = after(across(send), result)
+        keep, second_send = kernel(add_core, [rows(second_rows, BF16)] * 2, *second, smem=0)
+        arrived = across(second_send)
         pair = (2, halves[0], 2 * own)
         first_keep, send = call(
             add_core_first,
             [shape(pair), shape(pair, BF16)],
-            [pltpu.VMEM((2, first_rows, 2 * own), F32)],
+            [],
             0,
             counts,
             *first,
         )
         first_arrived = parity(send)
+        arrived = after(arrived, summed, low)
         keep, send = call(
             add_chip,
             [rows(halves[1]), rows(halves[1], BF16)],
-            [pltpu.VMEM((second_rows, 2 * own), F32)],
+            [],
             0,
             counts,
             keep,
@@ -1267,19 +1294,21 @@
         keep, *send = call(
             add_last,
             [rows(sum(pieces))] + [rows(sum(pieces), BF16)] * (depth - 1),
-            [tuple(pltpu.VMEM((half, 2 * own), F32) for half in halves)],
+            [],
             0,
             counts,
             (first_keep, keep),
             (first_arrived, arrived),
         )
         low_other = across(after(low, keep))
+        result, grad_summed = finish_own(after(summed, keep))
         arrived = tuple(along(send[t - 1], t) for t in range(1, depth))
+        arrived = after_all(arrived, result)
         (mine,) = kernel(add_depth, [rows(sum(pieces), BF16)], keep, arrived, smem=0)
         mine = (mine,) + tuple(along(mine, t) for t in range(1, depth))
         low, low_other = after_all((low, low_other), *mine)
         (mine,) = kernel(join_depth, [rows(sum(halves), BF16)], counts, mine)
-        return (mine, parity(mine)), low, low_other
+        return (mine, parity(mine)), low, low_other, result, grad_summed
 
     def slots_of(tensor, *which):
         return [lax.dynamic_index_in_dim(tensor, chan ^ s, 0, keepdims=False) for s in which]
@@ -1322,7 +1351,7 @@
         reduce_in,
         [
             shape((wide_rows, width)),
-            shape((2, width)),
+            shape((2 + parts, lanes)),
             shape((parts, width, lanes), BF16),
             shape((groups * images, inter)),
         ],
@@ -1332,7 +1361,7 @@
         *x,
         *first,
     )
-    in_sums = exchange(2, 0)(after(msg, near, odd))
+    in_sums = exchange(2 + parts, 0)(after(msg, near, odd))
     other = after(other, *in_sums)
     odd = home(after(odd, *in_sums), 1)
     weights = (weights, near, other, core(other))
@@ -1431,7 +1460,8 @@
     )
     out_back = exchange(2 * parts, 0)(msg)
 
-    summed = [away_plane(pair, odd) for odd, pair in enumerate(summed)]
+    near, far = summed
+    far = across(far)
 
     sums_rows = 2 * 2 * width // inter
     low_out, grad_weighted, grad_logits, msg = call(
@@ -1470,10 +1500,11 @@
         low_out,
         gate,
         grad_logits,
-    )
-    out_keep, out_arrived = keep, core(send)
-    mid_back = after_all(mid_back, keep, *summed)
-    summed = cross(*after_all(summed, mid_back[0]))
+        mid_affine,
+    )
+    mid_back = after_all(mid_back, keep, far)
+    summed = away_plane(after(jnp.concatenate([near, far]), mid_back[0]))
+    out_keep, out_arrived = keep, core(after(send, mid_back[0]))
     low_mid, grad_hidden, grad_squeeze, vectors, msg = call(
         back_mid,
         [
@@ -1502,6 +1533,17 @@
         w_mid_back,
     )
     in_back = exchange(2, 0)(after(msg, out_arrived))
+    keep, send = call(
+        weight_mid_term,
+        [shape((2, 18 * own, 2 * own), BF16)] * 2,
+        [pltpu.VMEM((width, 9 * inter), F32)],
+        conv,
+        counts,
+        after(taps, in_back[0]),
+        low_mid,
+        in_affine,
+    )
+    in_back = after_all(in_back, keep)
     in_rows = parts * lanes // (2 * own) * own
     low_in, in_keep, in_send = call(
         functools.partial(back_in, 1.0 / groups),
@@ -1526,24 +1568,20 @@
         gathered,
         grad_squeeze,
     )
-    keep, send = call(
-        weight_mid_term,
-        [shape((2, 18 * own, 2 * own), BF16)] * 2,
-        [pltpu.VMEM((width, 9 * inter), F32)],
-        conv,
-        counts,
-        after(taps, low_in),
-        low_mid,
-    )
     owned = shape((batches, rows, lanes), BF16)
-    result, grad_summed = call(finish_owned, [owned, owned], [], 0, counts, *summed, cotangent)
-    send = after(send, summed[2])
+
+    def finish_own(summed):
+        swapped = core(jnp.stack([summed[1], summed[3]]))
+        return call(finish_owned, [owned, owned], [], 0, counts, summed, swapped, cotangent)
+
+    send = after(send, low_in)
     low_in = away_plane(low_in)
-    terms, low_in, low_other = add_over_all(
+    terms, low_in, low_other, result, grad_summed = add_over_all(
         (keep, core(send)),
         ((out_keep, in_keep), (out_arrived, core(in_send))),
         low_in,
-        result,
+        summed,
+        finish_own,
     )
     lows = (low_in, core(low_in), low_other, core(low_other))
     (grad_x,) = call(grad_owned, [owned], [], product, lows, w_in, grad_summed, smem=0)
@@ -1581,12 +1619,7 @@
             shape((1, lanes)),
             shape((1, lanes)),
         ],
-        [
-            pltpu.VMEM((18 * own, 2 * own), F32),
-            pltpu.VMEM((terms[0].shape[0] * 2 - 18 * own, 2 * own), F32)
-            if groups == 8
-            else pltpu.VMEM(terms[1].shape, F32),
-        ],
+        [pltpu.VMEM((32, 2 * own), F32)],
         0,
         counts,
         terms,

time: 178 us -> 173 us (0.972)
  starting transfers between devices: 69.6 us -> 63.8 us
  waiting for transfers between devices: 66.3 us -> 68.6 us
    ppermute x62, starting transfers between devices: 69.6 us -> 63.8 us  [permute(): return lax.ppermute(tensor, ('dp', 'chan'), pairs)]
    ppermute x62, waiting for transfers between devices: 66.3 us -> 68.6 us  [permute(): return lax.ppermute(tensor, ('dp', 'chan'), pairs)]
  transfers between devices with their start and end apart: 62 -> 62, of which waited for: 39 -> 31; matrix products, arithmetic and copies ran while one was open for 1% -> 1% of each run, Pallas kernels for 18% -> 18%
where the time goes in v5:
time: 173 us; the launch traced here: 172 us
  waiting for transfers between devices  68.6 us (40%)
  starting transfers between devices  63.8 us (37%)
  Pallas kernels  35.2 us (20%)
  local copies, waits for them, and re-layouts  2.87 us (2%)
    ppermute x62, waiting for transfers between devices, permute(): return lax.ppermute(tensor, ('dp', 'chan'), pairs)  68.6 us
    ppermute x62, starting transfers between devices, permute(): return lax.ppermute(tensor, ('dp', 'chan'), pairs)  63.8 us
    pallas_call x23, Pallas kernels, call(): pl.pallas_call(body, out_shape=outs, in_specs=specs, out_specs=[pl.BlockS...  35.2 us
  transfers between devices with their start and end apart: 62, of which 31 were waited for; matrix products, arithmetic and copies ran while one was open for 1% of the time, Pallas kernels for 18%

profile of v5, /device:TPU:0, one launch (start us, length us, event | category | flops | bytes accessed | tf_op | source)
XLA Modules:
  0.0 172.4 jit_solution(2701487485438059031)
XLA Ops:
  0.8 1.4 dynamic-slice_bitcast_fusion.2
  2.7 2.6 %collective-permute-start.5 = (bf16[64,1024]{1,0:T(8,128)(2,1)S(1)}, bf16[64,1024]{1,0:T(8,128)(2,1)S(1)}, u32[]{:S(2)}, u32[]{:S(2)}) collective-permute-start(bf16[64,1024]{1,0:T(8,128)(2,1)S(1)} %bitcast.34), channel_id=1, source_target_pairs={{0,2},{1,3},{2,0},{3,1},{4,6},{5,7},{6,4},{7,5},{8,10},{9,11},{10,... | collective-permute-start | bytes 393224 | tf_op jit(solution)/shard_map/ppermute | solution.py:1181
  5.3 1.4 collective-permute-start.4
  6.7 1.5 collective-permute-start.3
  8.3 1.2 dynamic-slice_bitcast_fusion
  10.8 7.5 %collective-permute-done.5.a2 = bf16[64,1024]{1,0:T(8,128)(2,1)S(1)} collective-permute-done((bf16[64,1024]{1,0:T(8,128)(2,1)S(1)}, bf16[64,1024]{1,0:T(8,128)(2,1)S(1)}, u32[]{:S(2)}, u32[]{:S(2)}) %collective-permute-start.5) | collective-permute-done | bytes 131104 | tf_op jit(solution)/shard_map/ppermute | solution.py:1181
  18.3 1.3 collective-permute-done.6.a3
  19.8 6.6 %collective-permute-done.4.x3.x_refs_3_ = bf16[784,256]{1,0:T(8,128)(2,1)S(1)} collective-permute-done((bf16[784,256]{1,0:T(8,128)(2,1)S(1)}, bf16[784,256]{1,0:T(8,128)(2,1)S(1)}, u32[]{:S(2)}, u32[]{:S(2)}) %collective-permute-start.4) | collective-permute-done | bytes 401440 | tf_op jit(solution)/shard_map/ppermute | solution.py:1181
  26.6 1.8 %collective-permute-start.12 = (bf16[1872,128]{1,0:T(8,128)(2,1)S(1)}, bf16[1872,128]{1,0:T(8,128)(2,1)S(1)}, u32[]{:S(2)}, u32[]{:S(2)}) collective-permute-start(bf16[1872,128]{1,0:T(8,128)(2,1)S(1)} %pack.1.b0), channel_id=1, source_target_pairs={{0,2},{1,3},{2,0},{3,1},{4,6},{5,7},{6,4},{7,5},{8,10},{9,11},{10,... | collective-permute-start | bytes 1437704 | tf_op jit(solution)/shard_map/ppermute | solution.py:1181
  28.4 1.6 reduce_in.1
  30.3 1.2 collective-permute-done.8
  31.4 3.6 %collective-permute-start.11 = (f32[6,256]{1,0:T(8,128)S(1)}, f32[6,256]{1,0:T(8,128)S(1)}, u32[]{:S(2)}, u32[]{:S(2)}) collective-permute-start(f32[6,256]{1,0:T(8,128)S(1)} %add.39.sums_refs_0_), channel_id=1, source_target_pairs={{0,24},{1,25},{2,26},{3,27},{4,28},{5,29},{6,30},{7,31},{8,16},{9,... | collective-permute-start | bytes 18440 | tf_op jit(solution)/shard_map/ppermute | solution.py:1181
  36.9 2.7 %collective-permute-done.10.sums_refs_2_ = f32[6,256]{1,0:T(8,128)S(1)} collective-permute-done((f32[6,256]{1,0:T(8,128)S(1)}, f32[6,256]{1,0:T(8,128)S(1)}, u32[]{:S(2)}, u32[]{:S(2)}) %collective-permute-start.10) | collective-permute-done | bytes 6176 | tf_op jit(solution)/shard_map/ppermute | solution.py:1181
  40.3 2.3 %collective-permute-done.13.b3 = bf16[1872,128]{1,0:T(8,128)(2,1)S(1)} collective-permute-done((bf16[1872,128]{1,0:T(8,128)(2,1)S(1)}, bf16[1872,128]{1,0:T(8,128)(2,1)S(1)}, u32[]{:S(2)}, u32[]{:S(2)}) %collective-permute-start.13) | collective-permute-done | bytes 479264 | tf_op jit(solution)/shard_map/ppermute | solution.py:1181
  43.5 2.3 %conv_mid.1 = (bf16[3,976,256]{2,1,0:T(8,128)(2,1)S(1)}, f32[896,512]{1,0:T(8,128)S(1)}, f32[2,512]{1,0:T(2,128)S(1)}) custom-call(s32[4,8]{1,0:T(4,128)S(1)} %copy-done.1, f32[896,256]{1,0:T(8,128)S(1)} %get-tuple-element.126.pre_ref, f32[6,256]{1,0:T(8,128)S(1)} %add.39.sums_refs_0_, f32[6,256]{1,0:T(8,128)S(1)} %collective-permute-done.9.sums_refs_1_, ...), custom_call_target="tpu_custom_call" | custom-call | flops 1056964608 | bytes 5462144 | tf_op jit(solution)/shard_map/conv_mid/pallas_call | solution.py:183
  47.0 2.4 %collective-permute-start.17 = (f32[2,512]{1,0:T(2,128)S(1)}, f32[2,512]{1,0:T(2,128)S(1)}, u32[]{:S(2)}, u32[]{:S(2)}) collective-permute-start(f32[2,512]{1,0:T(2,128)S(1)} %add.40.sums_refs_0_.mid_sums_refs_0_), channel_id=1, source_target_pairs={{0,24},{1,25},{2,26},{3,27},{4,28},{5,29},{6,30},{7,31},{8,16},{9,... | collective-permute-start | bytes 12296 | tf_op jit(solution)/shard_map/ppermute | solution.py:1181
  49.4 2.0 %collective-permute-start.15 = (f32[2,512]{1,0:T(2,128)S(1)}, f32[2,512]{1,0:T(2,128)S(1)}, u32[]{:S(2)}, u32[]{:S(2)}) collective-permute-start(f32[2,512]{1,0:T(2,128)S(1)} %add.40.sums_refs_0_.mid_sums_refs_0_), channel_id=1, source_target_pairs={{0,8},{1,9},{2,10},{3,11},{4,12},{5,13},{6,14},{7,15},{8,0},{9,1},... | collective-permute-start | bytes 12296 | tf_op jit(solution)/shard_map/ppermute | solution.py:1181
  52.4 1.5 collective-permute-done.16.sums_refs_2_.mid_sums_refs_2_
  53.9 1.7 %pool.1 = (f32[4,256]{1,0:T(4,128)S(1)}, f32[40,128]{1,0:T(8,128)S(1)}) custom-call(s32[4,8]{1,0:T(4,128)S(1)} %copy-done.1, f32[896,512]{1,0:T(8,128)S(1)} %get-tuple-element.134.mid_ref, f32[2,512]{1,0:T(2,128)S(1)} %add.40.sums_refs_0_.mid_sums_refs_0_, f32[2,512]{1,0:T(2,128)S(1)} %collective-permute-done.15.sums_refs_1_.mid_sums_refs_1_, ...), custom_call_target="tpu_custom_call" | custom-call | bytes 1945728 | tf_op jit(solution)/shard_map/pool/pallas_call | solution.py:183
  58.7 3.5 %collective-permute-start.21 = (f32[80,128]{1,0:T(8,128)S(1)}, f32[80,128]{1,0:T(8,128)S(1)}, u32[]{:S(2)}, u32[]{:S(2)}) collective-permute-start(f32[80,128]{1,0:T(8,128)S(1)} %constant_dynamic-update-slice_fusion.gathered_refs_0_), channel_id=1, source_target_pairs={{0,24},{1,25},{2,26},{3,27},{4,28},{5,29},{6,30},{7,31},{8,16},{9,... | collective-permute-start | bytes 122888 | tf_op jit(solution)/shard_map/ppermute | solution.py:1181
  64.5 2.6 %collective-permute-done.20.gathered_refs_2_ = f32[80,128]{1,0:T(8,128)S(1)} collective-permute-done((f32[80,128]{1,0:T(8,128)S(1)}, f32[80,128]{1,0:T(8,128)S(1)}, u32[]{:S(2)}, u32[]{:S(2)}) %collective-permute-start.20) | collective-permute-done | bytes 40992 | tf_op jit(solution)/shard_map/ppermute | solution.py:1181
  67.1 2.0 %attend.1 = (f32[2,4,128]{2,1,0:T(4,128)S(1)}, f32[4,512]{1,0:T(4,128)S(1)}, bf16[784,256]{1,0:T(8,128)(2,1)S(1)}, f32[4,784,256]{2,1,0:T(8,128)S(1)}, f32[8,256]{1,0:T(8,128)S(1)}) custom-call(s32[4,8]{1,0:T(4,128)S(1)} %copy-done.1, f32[80,128]{1,0:T(8,128)S(1)} %constant_dynamic-update-slice_fusion.gathered_refs_0_, ...), custom_call_target="tpu_custom_call" | custom-call | flops 411041792 | bytes 6327424 | tf_op jit(solution)/shard_map/attend/pallas_call | solution.py:183
  69.1 1.2 collective-permute-done.22
  70.3 2.0 %collective-permute-start.25 = (f32[8,256]{1,0:T(8,128)S(1)}, f32[8,256]{1,0:T(8,128)S(1)}, u32[]{:S(2)}, u32[]{:S(2)}) collective-permute-start(f32[8,256]{1,0:T(8,128)S(1)} %add.41.sums_refs_0_), channel_id=1, source_target_pairs={{0,24},{1,25},{2,26},{3,27},{4,28},{5,29},{6,30},{7,31},{8,16},{9,... | collective-permute-start | bytes 24584 | tf_op jit(solution)/shard_map/ppermute | solution.py:1181
  72.4 2.3 %collective-permute-start.23 = (f32[8,256]{1,0:T(8,128)S(1)}, f32[8,256]{1,0:T(8,128)S(1)}, u32[]{:S(2)}, u32[]{:S(2)}) collective-permute-start(f32[8,256]{1,0:T(8,128)S(1)} %add.41.sums_refs_0_), channel_id=1, source_target_pairs={{0,8},{1,9},{2,10},{3,11},{4,12},{5,13},{6,14},{7,15},{8,0},{9,1},... | collective-permute-start | bytes 24584 | tf_op jit(solution)/shard_map/ppermute | solution.py:1181
  74.7 1.1 collective-permute-done.25.sums_refs_3_
  75.8 1.2 collective-permute-done.24.sums_refs_2_
  77.0 2.6 %finish.1 = (bf16[2,784,256]{2,1,0:T(8,128)(2,1)S(1)}, bf16[2,784,256]{2,1,0:T(8,128)(2,1)S(1)}, f32[4,784,256]{2,1,0:T(8,128)S(1)}, f32[8,256]{1,0:T(8,128)S(1)}) custom-call(s32[4,8]{1,0:T(4,128)S(1)} %copy-done.1, f32[4,784,256]{2,1,0:T(8,128)S(1)} %get-tuple-element.143.out_ref, f32[8,256]{1,0:T(8,128)S(1)} %add.41.sums_refs_0_, ...), custom_call_target="tpu_custom_call" | custom-call | bytes 12091520 | tf_op jit(solution)/shard_map/finish/pallas_call | solution.py:183
  79.6 1.6 collective-permute-start.29
  81.2 1.2 collective-permute-done.30
  82.4 2.6 %collective-permute-start.33 = (f32[8,256]{1,0:T(8,128)S(1)}, f32[8,256]{1,0:T(8,128)S(1)}, u32[]{:S(2)}, u32[]{:S(2)}) collective-permute-start(f32[8,256]{1,0:T(8,128)S(1)} %add.42.back_refs_0_.out_back_refs_0_), channel_id=1, source_target_pairs={{0,24},{1,25},{2,26},{3,27},{4,28},{5,29},{6,30},{7,31},{8,16},{9,... | collective-permute-start | bytes 24584 | tf_op jit(solution)/shard_map/ppermute | solution.py:1181
  85.2 1.5 collective-permute-start.31
  86.8 1.1 collective-permute-done.33.back_refs_3_.out_back_refs_3_
  87.9 1.7 collective-permute-done.32.back_refs_2_.out_back_refs_2_
  89.6 2.8 %back_out.1 = (bf16[4,784,256]{2,1,0:T(8,128)(2,1)S(1)}, f32[896,256]{1,0:T(8,128)S(1)}, f32[4,512]{1,0:T(4,128)S(1)}, f32[12,128]{1,0:T(8,128)S(1)}) custom-call(s32[4,8]{1,0:T(4,128)S(1)} %copy-done.1, f32[4,784,256]{2,1,0:T(8,128)S(1)} %get-tuple-element.152.grad_ref, f32[4,784,256]{2,1,0:T(8,128)S(1)} %get-tuple-element.143.out_ref, ...), custom_call_target="tpu_custom_call" | custom-call | flops 411041792 | bytes 11556992 | tf_op jit(solution)/shard_map/back_out/pallas_call | solution.py:183
  92.4 1.1 collective-permute-done.34
  93.6 1.5 collective-permute-start.37
  96.0 2.1 %collective-permute-start.35 = (f32[16,128]{1,0:T(8,128)S(1)}, f32[16,128]{1,0:T(8,128)S(1)}, u32[]{:S(2)}, u32[]{:S(2)}) collective-permute-start(f32[16,128]{1,0:T(8,128)S(1)} %pad_maximum_fusion.5.back_refs_0_), channel_id=1, source_target_pairs={{0,8},{1,9},{2,10},{3,11},{4,12},{5,13},{6,14},{7,15},{8,0},{9,1},... | collective-permute-start | bytes 24584 | tf_op jit(solution)/shard_map/ppermute | solution.py:1181
  98.1 2.1 %weight_out_term.1 = (bf16[2,656,128]{2,1,0:T(8,128)(2,1)S(1)}, bf16[2,656,128]{2,1,0:T(8,128)(2,1)S(1)}) custom-call(s32[4,8]{1,0:T(4,128)S(1)} %copy-done.1, bf16[784,256]{1,0:T(8,128)(2,1)S(1)} %get-tuple-element.158.weighted_ref, bf16[4,784,256]{2,1,0:T(8,128)(2,1)S(1)} %get-tuple-element.159.low_ref, f32[2,4,128]{2,1,0:T(4,128)S(1)} %get-tuple-element.155.gate_ref, ...), custom_call_target="tpu_custom_call" | custom-call | flops 411041792 | bytes 2695296 | tf_op jit(solution)/shard_map/weight_out_term/pallas_call | solution.py:183
  101.3 2.7 %collective-permute-start.39 = (bf16[2,656,128]{2,1,0:T(8,128)(2,1)S(1)}, bf16[2,656,128]{2,1,0:T(8,128)(2,1)S(1)}, u32[]{:S(2)}, u32[]{:S(2)}) collective-permute-start(bf16[2,656,128]{2,1,0:T(8,128)(2,1)S(1)} %get-tuple-element.172), channel_id=1, source_target_pairs={{0,1},{1,0},{2,3},{3,2},{4,5},{5,4},{6,7},{7,6},{8,9},{9,8},{10,11... | collective-permute-start | bytes 1007624 | tf_op jit(solution)/shard_map/ppermute | solution.py:1181
  104.0 3.6 %back_mid.1 = (bf16[976,512]{1,0:T(8,128)(2,1)S(1)}, f32[896,256]{1,0:T(8,128)S(1)}, f32[4,128]{1,0:T(4,128)S(1)}, f32[8,512]{1,0:T(8,128)S(1)}, f32[2,256]{1,0:T(2,128)S(1)}) custom-call(s32[4,8]{1,0:T(4,128)S(1)} %copy-done.1, f32[16,128]{1,0:T(8,128)S(1)} %pad_maximum_fusion.5.back_refs_0_, f32[16,128]{1,0:T(8,128)S(1)} %collective-permute-done.35.back_refs_1_, ...), custom_call_target="tpu_custom_call" | custom-call | flops 1056964608 | bytes 7122048 | tf_op jit(solution)/shard_map/back_mid/pallas_call | solution.py:183
  107.7 1.1 collective-permute-done.40
  108.8 2.0 %collective-permute-start.43 = (f32[2,256]{1,0:T(2,128)S(1)}, f32[2,256]{1,0:T(2,128)S(1)}, u32[]{:S(2)}, u32[]{:S(2)}) collective-permute-start(f32[2,256]{1,0:T(2,128)S(1)} %add.44.back_refs_0_), channel_id=1, source_target_pairs={{0,24},{1,25},{2,26},{3,27},{4,28},{5,29},{6,30},{7,31},{8,16},{9,... | collective-permute-start | bytes 6152 | tf_op jit(solution)/shard_map/ppermute | solution.py:1181
  111.8 1.4 collective-permute-start.41
  113.2 3.0 %weight_mid_term.1 = (bf16[2,1152,128]{2,1,0:T(8,128)(2,1)S(1)}, bf16[2,1152,128]{2,1,0:T(8,128)(2,1)S(1)}) custom-call(s32[4,8]{1,0:T(4,128)S(1)} %copy-done.1, bf16[3,976,256]{2,1,0:T(8,128)(2,1)S(1)} %get-tuple-element.174.taps_ref, bf16[976,512]{1,0:T(8,128)(2,1)S(1)} %get-tuple-element.175.low_ref, f32[2,256]{1,0:T(2,128)S(1)} %get-tuple-element.132.affine_ref), custom_call_target="tpu_custom_call" | custom-call | flops 1056964608 | bytes 3680384 | tf_op jit(solution)/shard_map/weight_mid_term/pallas_call | solution.py:183
  116.3 2.0 %back_in.1 = (bf16[784,256]{1,0:T(8,128)(2,1)S(1)}, bf16[2,592,128]{2,1,0:T(8,128)(2,1)S(1)}, bf16[2,592,128]{2,1,0:T(8,128)(2,1)S(1)}) custom-call(s32[4,8]{1,0:T(4,128)S(1)} %copy-done.1, f32[896,256]{1,0:T(8,128)S(1)} %get-tuple-element.178.grad_ref, f32[896,256]{1,0:T(8,128)S(1)} %get-tuple-element.126.pre_ref, f32[6,256]{1,0:T(8,128)S(1)} %add.39.sums_refs_0_, ...), custom_call_target="tpu_custom_call" | custom-call | flops 411041792 | bytes 4702336 | tf_op jit(solution)/shard_map/back_in/pallas_call | solution.py:183
  119.5 1.2 collective-permute-done.46.arrived_refs_1_
  122.2 1.8 %collective-permute-start.45 = (bf16[2,576,128]{2,1,0:T(8,128)(2,1)S(1)}, bf16[2,576,128]{2,1,0:T(8,128)(2,1)S(1)}, u32[]{:S(2)}, u32[]{:S(2)}) collective-permute-start(bf16[2,576,128]{2,1,0:T(8,128)(2,1)S(1)} %get-tuple-element.189), channel_id=1, source_target_pairs={{0,4},{1,5},{2,6},{3,7},{4,0},{5,1},{6,2},{7,3},{8,12},{9,13},{10,... | collective-permute-start | bytes 884744 | tf_op jit(solution)/shard_map/ppermute | solution.py:1181
  124.0 6.8 %collective-permute-done.47.arrived_ref = bf16[1280,128]{1,0:T(8,128)(2,1)S(1)} collective-permute-done((bf16[1280,128]{1,0:T(8,128)(2,1)S(1)}, bf16[1280,128]{1,0:T(8,128)(2,1)S(1)}, u32[]{:S(2)}, u32[]{:S(2)}) %collective-permute-start.47) | collective-permute-done | bytes 327712 | tf_op jit(solution)/shard_map/ppermute | solution.py:1181
  131.6 3.3 %collective-permute-done.45.arrived_ref = bf16[2,576,128]{2,1,0:T(8,128)(2,1)S(1)} collective-permute-done((bf16[2,576,128]{2,1,0:T(8,128)(2,1)S(1)}, bf16[2,576,128]{2,1,0:T(8,128)(2,1)S(1)}, u32[]{:S(2)}, u32[]{:S(2)}) %collective-permute-start.45) | collective-permute-done | bytes 294944 | tf_op jit(solution)/shard_map/ppermute | solution.py:1181
  135.3 4.9 %collective-permute-done.49.arrived_refs_0_ = bf16[576,128]{1,0:T(8,128)(2,1)S(1)} collective-permute-done((bf16[576,128]{1,0:T(8,128)(2,1)S(1)}, bf16[576,128]{1,0:T(8,128)(2,1)S(1)}, u32[]{:S(2)}, u32[]{:S(2)}) %collective-permute-start.49) | collective-permute-done | bytes 147488 | tf_op jit(solution)/shard_map/ppermute | solution.py:1181
  142.2 1.8 %collective-permute-start.54 = (bf16[304,128]{1,0:T(8,128)(2,1)S(1)}, bf16[304,128]{1,0:T(8,128)(2,1)S(1)}, u32[]{:S(2)}, u32[]{:S(2)}) collective-permute-start(bf16[304,128]{1,0:T(8,128)(2,1)S(1)} %get-tuple-element.205), channel_id=1, source_target_pairs={{0,16},{1,17},{2,18},{3,19},{4,20},{5,21},{6,22},{7,23},{8,24},{9,... | collective-permute-start | bytes 233480 | tf_op jit(solution)/shard_map/ppermute | solution.py:1181
  143.9 1.8 %collective-permute-start.55 = (bf16[304,128]{1,0:T(8,128)(2,1)S(1)}, bf16[304,128]{1,0:T(8,128)(2,1)S(1)}, u32[]{:S(2)}, u32[]{:S(2)}) collective-permute-start(bf16[304,128]{1,0:T(8,128)(2,1)S(1)} %get-tuple-element.206), channel_id=1, source_target_pairs={{0,24},{1,25},{2,26},{3,27},{4,28},{5,29},{6,30},{7,31},{8,16},{9,... | collective-permute-start | bytes 233480 | tf_op jit(solution)/shard_map/ppermute | solution.py:1181
  145.7 3.5 %finish_owned.1 = (bf16[4,784,256]{2,1,0:T(8,128)(2,1)}, bf16[4,784,256]{2,1,0:T(8,128)(2,1)S(1)}) custom-call(s32[4,8]{1,0:T(4,128)S(1)} %copy-done.1, bf16[4,784,256]{2,1,0:T(8,128)(2,1)S(1)} %collective-permute-done.38.summed_ref, bf16[2,784,256]{2,1,0:T(8,128)(2,1)S(1)} %collective-permute-done.51.swapped_ref, bf16[4,784,256]{2,1,0:T(8,128)(2,1)S(1)} %copy-done), custom_call_target="tpu_custom_call" | custom-call | bytes 7225472 | tf_op jit(solution)/shard_map/finish_owned/pallas_call | solution.py:183
  149.2 2.1 %collective-permute-done.54.arrived_refs_1_ = bf16[304,128]{1,0:T(8,128)(2,1)S(1)} collective-permute-done((bf16[304,128]{1,0:T(8,128)(2,1)S(1)}, bf16[304,128]{1,0:T(8,128)(2,1)S(1)}, u32[]{:S(2)}, u32[]{:S(2)}) %collective-permute-start.54) | collective-permute-done | bytes 77856 | tf_op jit(solution)/shard_map/ppermute | solution.py:1181
  151.4 1.9 %collective-permute-start.58 = (bf16[304,128]{1,0:T(8,128)(2,1)S(1)}, bf16[304,128]{1,0:T(8,128)(2,1)S(1)}, u32[]{:S(2)}, u32[]{:S(2)}) collective-permute-start(bf16[304,128]{1,0:T(8,128)(2,1)S(1)} %add_depth.1.piece_refs_0_), channel_id=1, source_target_pairs={{0,24},{1,25},{2,26},{3,27},{4,28},{5,29},{6,30},{7,31},{8,16},{9,... | collective-permute-start | bytes 233480 | tf_op jit(solution)/shard_map/ppermute | solution.py:1181
  153.3 1.0 collective-permute-start.57
  154.3 1.5 collective-permute-start.56
  155.8 2.4 %collective-permute-done.58.piece_refs_3_ = bf16[304,128]{1,0:T(8,128)(2,1)S(1)} collective-permute-done((bf16[304,128]{1,0:T(8,128)(2,1)S(1)}, bf16[304,128]{1,0:T(8,128)(2,1)S(1)}, u32[]{:S(2)}, u32[]{:S(2)}) %collective-permute-start.58) | collective-permute-done | bytes 77856 | tf_op jit(solution)/shard_map/ppermute | solution.py:1181
  158.2 1.9 %collective-permute-done.57.piece_refs_2_ = bf16[304,128]{1,0:T(8,128)(2,1)S(1)} collective-permute-done((bf16[304,128]{1,0:T(8,128)(2,1)S(1)}, bf16[304,128]{1,0:T(8,128)(2,1)S(1)}, u32[]{:S(2)}, u32[]{:S(2)}) %collective-permute-start.57) | collective-permute-done | bytes 77856 | tf_op jit(solution)/shard_map/ppermute | solution.py:1181
  161.2 1.3 collective-permute-start.61
  162.5 1.8 %grad_owned.1 = bf16[4,784,256]{2,1,0:T(8,128)(2,1)} custom-call(bf16[784,256]{1,0:T(8,128)(2,1)S(1)} %collective-permute-done.48.low_refs_0_, bf16[784,256]{1,0:T(8,128)(2,1)S(1)} %collective-permute-done.59.low_refs_1_, bf16[784,256]{1,0:T(8,128)(2,1)S(1)} %collective-permute-done.52.low_refs_2_, bf16[784,256]{1,0:T(8,128)(2,1)S(1)} %collective-permute-done.60.low_refs_3_, ...), custom_call_target="tpu_custom_call" | custom-call | flops 411041792 | bytes 5341184 | tf_op jit(solution)/shard_map/grad_owned/pallas_call | solution.py:183
  164.4 6.2 %collective-permute-done.61.term_refs_1_ = bf16[1216,128]{1,0:T(8,128)(2,1)S(1)} collective-permute-done((bf16[1216,128]{1,0:T(8,128)(2,1)S(1)}, bf16[1216,128]{1,0:T(8,128)(2,1)S(1)}, u32[]{:S(2)}, u32[]{:S(2)}) %collective-permute-start.61) | collective-permute-done | bytes 311328 | tf_op jit(solution)/shard_map/ppermute | solution.py:1181
  170.5 1.7 unpack.1
  (140 shorter events, 24.0 us)
Async XLA Ops:
  2.2 26.2 %copy-start.1 = (s32[4,8]{1,0:T(4,128)S(1)}, s32[4,8]{1,0:T(4,128)}, u32[]{:S(2)}) copy-start(s32[4,8]{1,0:T(4,128)} %counts_ref.35) | copy-start | bytes 388
  2.2 6.1 %collective-permute-start = (bf16[64,1024]{1,0:T(8,128)(2,1)S(1)}, bf16[64,1024]{1,0:T(8,128)(2,1)S(1)}, u32[]{:S(2)}, u32[]{:S(2)}) collective-permute-start(bf16[64,1024]{1,0:T(8,128)(2,1)S(1)} %bitcast.33), channel_id=1, source_target_pairs={{0,1},{1,0},{2,3},{3,2},{4,5},{5,4},{6,7},{7,6},{8,9},{9,8},{10,11... | collective-permute-start | bytes 393224 | tf_op jit(solution)/shard_map/ppermute | solution.py:1181
  2.7 15.5 %collective-permute-start.5 = (bf16[64,1024]{1,0:T(8,128)(2,1)S(1)}, bf16[64,1024]{1,0:T(8,128)(2,1)S(1)}, u32[]{:S(2)}, u32[]{:S(2)}) collective-permute-start(bf16[64,1024]{1,0:T(8,128)(2,1)S(1)} %bitcast.34), channel_id=1, source_target_pairs={{0,2},{1,3},{2,0},{3,1},{4,6},{5,7},{6,4},{7,5},{8,10},{9,11},{10,... | collective-permute-start | bytes 393224 | tf_op jit(solution)/shard_map/ppermute | solution.py:1181
  5.3 21.0 %collective-permute-start.4 = (bf16[784,256]{1,0:T(8,128)(2,1)S(1)}, bf16[784,256]{1,0:T(8,128)(2,1)S(1)}, u32[]{:S(2)}, u32[]{:S(2)}) collective-permute-start(bf16[784,256]{1,0:T(8,128)(2,1)S(1)} %get-tuple-element.238), channel_id=1, source_target_pairs={{0,6},{1,2},{2,4},{3,0},{4,7},{5,3},{6,5},{7,1},{8,14},{9,10},{10,... | collective-permute-start | bytes 1204232 | tf_op jit(solution)/shard_map/ppermute | solution.py:1181
  6.7 19.9 %collective-permute-start.3 = (bf16[784,256]{1,0:T(8,128)(2,1)S(1)}, bf16[784,256]{1,0:T(8,128)(2,1)S(1)}, u32[]{:S(2)}, u32[]{:S(2)}) collective-permute-start(bf16[784,256]{1,0:T(8,128)(2,1)S(1)} %get-tuple-element.239), channel_id=1, source_target_pairs={{0,2},{1,6},{2,0},{3,4},{4,3},{5,7},{6,1},{7,5},{8,10},{9,14},{10,... | collective-permute-start | bytes 1204232 | tf_op jit(solution)/shard_map/ppermute | solution.py:1181
  9.4 20.5 %copy-start = (bf16[4,784,256]{2,1,0:T(8,128)(2,1)S(1)}, bf16[4,784,256]{2,1,0:T(8,128)(2,1)}, u32[]{:S(2)}) copy-start(bf16[4,784,256]{2,1,0:T(8,128)(2,1)} %cot_ref.1) | copy-start | bytes 4816900
  9.4 18.9 %collective-permute-start.2 = (bf16[784,256]{1,0:T(8,128)(2,1)S(1)}, bf16[784,256]{1,0:T(8,128)(2,1)S(1)}, u32[]{:S(2)}, u32[]{:S(2)}) collective-permute-start(bf16[784,256]{1,0:T(8,128)(2,1)S(1)} %get-tuple-element.236), channel_id=1, source_target_pairs={{0,4},{1,0},{2,6},{3,2},{4,5},{5,1},{6,7},{7,3},{8,12},{9,8},{10,1... | collective-permute-start | bytes 1204232 | tf_op jit(solution)/shard_map/ppermute | solution.py:1181
  9.7 18.6 %collective-permute-start.1 = (bf16[784,256]{1,0:T(8,128)(2,1)S(1)}, bf16[784,256]{1,0:T(8,128)(2,1)S(1)}, u32[]{:S(2)}, u32[]{:S(2)}) collective-permute-start(bf16[784,256]{1,0:T(8,128)(2,1)S(1)} %get-tuple-element.237), channel_id=1, source_target_pairs={{0,0},{1,4},{2,2},{3,6},{4,1},{5,5},{6,3},{7,7},{8,8},{9,12},{10,1... | collective-permute-start | bytes 1204232 | tf_op jit(solution)/shard_map/ppermute | solution.py:1181
  18.3 1.3 collective-permute-start.6
  19.6 10.6 %collective-permute-start.7 = (bf16[1872,128]{1,0:T(8,128)(2,1)S(1)}, bf16[1872,128]{1,0:T(8,128)(2,1)S(1)}, u32[]{:S(2)}, u32[]{:S(2)}) collective-permute-start(bf16[1872,128]{1,0:T(8,128)(2,1)S(1)} %pack.1.b0), channel_id=1, source_target_pairs={{0,1},{1,0},{2,3},{3,2},{4,5},{5,4},{6,7},{7,6},{8,9},{9,8},{10,11... | collective-permute-start | bytes 1437704 | tf_op jit(solution)/shard_map/ppermute | solution.py:1181
  26.6 13.7 %collective-permute-start.12 = (bf16[1872,128]{1,0:T(8,128)(2,1)S(1)}, bf16[1872,128]{1,0:T(8,128)(2,1)S(1)}, u32[]{:S(2)}, u32[]{:S(2)}) collective-permute-start(bf16[1872,128]{1,0:T(8,128)(2,1)S(1)} %pack.1.b0), channel_id=1, source_target_pairs={{0,2},{1,3},{2,0},{3,1},{4,6},{5,7},{6,4},{7,5},{8,10},{9,11},{10,... | collective-permute-start | bytes 1437704 | tf_op jit(solution)/shard_map/ppermute | solution.py:1181
  30.2 1.2 collective-permute-start.8
  31.4 5.4 %collective-permute-start.11 = (f32[6,256]{1,0:T(8,128)S(1)}, f32[6,256]{1,0:T(8,128)S(1)}, u32[]{:S(2)}, u32[]{:S(2)}) collective-permute-start(f32[6,256]{1,0:T(8,128)S(1)} %add.39.sums_refs_0_), channel_id=1, source_target_pairs={{0,24},{1,25},{2,26},{3,27},{4,28},{5,29},{6,30},{7,31},{8,16},{9,... | collective-permute-start | bytes 18440 | tf_op jit(solution)/shard_map/ppermute | solution.py:1181
  35.0 4.5 %collective-permute-start.10 = (f32[6,256]{1,0:T(8,128)S(1)}, f32[6,256]{1,0:T(8,128)S(1)}, u32[]{:S(2)}, u32[]{:S(2)}) collective-permute-start(f32[6,256]{1,0:T(8,128)S(1)} %add.39.sums_refs_0_), channel_id=1, source_target_pairs={{0,16},{1,17},{2,18},{3,19},{4,20},{5,21},{6,22},{7,23},{8,24},{9,... | collective-permute-start | bytes 18440 | tf_op jit(solution)/shard_map/ppermute | solution.py:1181
  35.0 4.5 %collective-permute-start.9 = (f32[6,256]{1,0:T(8,128)S(1)}, f32[6,256]{1,0:T(8,128)S(1)}, u32[]{:S(2)}, u32[]{:S(2)}) collective-permute-start(f32[6,256]{1,0:T(8,128)S(1)} %add.39.sums_refs_0_), channel_id=1, source_target_pairs={{0,8},{1,9},{2,10},{3,11},{4,12},{5,13},{6,14},{7,15},{8,0},{9,1},... | collective-permute-start | bytes 18440 | tf_op jit(solution)/shard_map/ppermute | solution.py:1181
  35.9 19.8 %collective-permute-start.26 = (bf16[2,784,256]{2,1,0:T(8,128)(2,1)S(1)}, bf16[2,784,256]{2,1,0:T(8,128)(2,1)S(1)}, u32[]{:S(2)}, u32[]{:S(2)}) collective-permute-start(bf16[2,784,256]{2,1,0:T(8,128)(2,1)S(1)} %pad_maximum_fusion.2), channel_id=1, source_target_pairs={{0,0},{1,4},{2,2},{3,6},{4,1},{5,5},{6,3},{7,7},{8,8},{9,12},{10,1... | collective-permute-start | bytes 2408456 | tf_op jit(solution)/shard_map/ppermute | solution.py:1181
  39.6 16.6 %collective-permute-start.27 = (bf16[2,784,256]{2,1,0:T(8,128)(2,1)S(1)}, bf16[2,784,256]{2,1,0:T(8,128)(2,1)S(1)}, u32[]{:S(2)}, u32[]{:S(2)}) collective-permute-start(bf16[2,784,256]{2,1,0:T(8,128)(2,1)S(1)} %pad_maximum_fusion.1), channel_id=1, source_target_pairs={{0,4},{1,0},{2,6},{3,2},{4,5},{5,1},{6,7},{7,3},{8,12},{9,8},{10,1... | collective-permute-start | bytes 2408456 | tf_op jit(solution)/shard_map/ppermute | solution.py:1181
  40.3 2.3 %collective-permute-start.13 = (bf16[1872,128]{1,0:T(8,128)(2,1)S(1)}, bf16[1872,128]{1,0:T(8,128)(2,1)S(1)}, u32[]{:S(2)}, u32[]{:S(2)}) collective-permute-start(bf16[1872,128]{1,0:T(8,128)(2,1)S(1)} %collective-permute-done.12.b2), channel_id=1, source_target_pairs={{0,1},{1,0},{2,3},{3,2},{4,5},{5,4},{6,7},{7,6},{8,9},{9,8},{10,11... | collective-permute-start | bytes 1437704 | tf_op jit(solution)/shard_map/ppermute | solution.py:1181
  45.8 1.2 collective-permute-start.14
  47.0 5.4 %collective-permute-start.17 = (f32[2,512]{1,0:T(2,128)S(1)}, f32[2,512]{1,0:T(2,128)S(1)}, u32[]{:S(2)}, u32[]{:S(2)}) collective-permute-start(f32[2,512]{1,0:T(2,128)S(1)} %add.40.sums_refs_0_.mid_sums_refs_0_), channel_id=1, source_target_pairs={{0,24},{1,25},{2,26},{3,27},{4,28},{5,29},{6,30},{7,31},{8,16},{9,... | collective-permute-start | bytes 12296 | tf_op jit(solution)/shard_map/ppermute | solution.py:1181
  49.4 4.5 %collective-permute-start.16 = (f32[2,512]{1,0:T(2,128)S(1)}, f32[2,512]{1,0:T(2,128)S(1)}, u32[]{:S(2)}, u32[]{:S(2)}) collective-permute-start(f32[2,512]{1,0:T(2,128)S(1)} %add.40.sums_refs_0_.mid_sums_refs_0_), channel_id=1, source_target_pairs={{0,16},{1,17},{2,18},{3,19},{4,20},{5,21},{6,22},{7,23},{8,24},{9,... | collective-permute-start | bytes 12296 | tf_op jit(solution)/shard_map/ppermute | solution.py:1181
  49.4 4.5 %collective-permute-start.15 = (f32[2,512]{1,0:T(2,128)S(1)}, f32[2,512]{1,0:T(2,128)S(1)}, u32[]{:S(2)}, u32[]{:S(2)}) collective-permute-start(f32[2,512]{1,0:T(2,128)S(1)} %add.40.sums_refs_0_.mid_sums_refs_0_), channel_id=1, source_target_pairs={{0,8},{1,9},{2,10},{3,11},{4,12},{5,13},{6,14},{7,15},{8,0},{9,1},... | collective-permute-start | bytes 12296 | tf_op jit(solution)/shard_map/ppermute | solution.py:1181
  56.3 20.6 %collective-permute-start.28 = (bf16[2,784,256]{2,1,0:T(8,128)(2,1)S(1)}, bf16[2,784,256]{2,1,0:T(8,128)(2,1)S(1)}, u32[]{:S(2)}, u32[]{:S(2)}) collective-permute-start(bf16[2,784,256]{2,1,0:T(8,128)(2,1)S(1)} %pad_maximum_fusion.3), channel_id=1, source_target_pairs={{0,2},{1,3},{2,0},{3,1},{4,6},{5,7},{6,4},{7,5},{8,10},{9,11},{10,... | collective-permute-start | bytes 2408456 | tf_op jit(solution)/shard_map/ppermute | solution.py:1181
  56.9 1.7 %collective-permute-start.18 = (f32[40,128]{1,0:T(8,128)S(1)}, f32[40,128]{1,0:T(8,128)S(1)}, u32[]{:S(2)}, u32[]{:S(2)}) collective-permute-start(f32[40,128]{1,0:T(8,128)S(1)} %get-tuple-element.138), channel_id=1, source_target_pairs={{0,1},{1,0},{2,3},{3,2},{4,5},{5,4},{6,7},{7,6},{8,9},{9,8},{10,11... | collective-permute-start | bytes 61448 | tf_op jit(solution)/shard_map/ppermute | solution.py:1181
  58.7 5.8 %collective-permute-start.21 = (f32[80,128]{1,0:T(8,128)S(1)}, f32[80,128]{1,0:T(8,128)S(1)}, u32[]{:S(2)}, u32[]{:S(2)}) collective-permute-start(f32[80,128]{1,0:T(8,128)S(1)} %constant_dynamic-update-slice_fusion.gathered_refs_0_), channel_id=1, source_target_pairs={{0,24},{1,25},{2,26},{3,27},{4,28},{5,29},{6,30},{7,31},{8,16},{9,... | collective-permute-start | bytes 122888 | tf_op jit(solution)/shard_map/ppermute | solution.py:1181
  62.2 4.9 %collective-permute-start.20 = (f32[80,128]{1,0:T(8,128)S(1)}, f32[80,128]{1,0:T(8,128)S(1)}, u32[]{:S(2)}, u32[]{:S(2)}) collective-permute-start(f32[80,128]{1,0:T(8,128)S(1)} %constant_dynamic-update-slice_fusion.gathered_refs_0_), channel_id=1, source_target_pairs={{0,16},{1,17},{2,18},{3,19},{4,20},{5,21},{6,22},{7,23},{8,24},{9,... | collective-permute-start | bytes 122888 | tf_op jit(solution)/shard_map/ppermute | solution.py:1181
  62.2 4.9 %collective-permute-start.19 = (f32[80,128]{1,0:T(8,128)S(1)}, f32[80,128]{1,0:T(8,128)S(1)}, u32[]{:S(2)}, u32[]{:S(2)}) collective-permute-start(f32[80,128]{1,0:T(8,128)S(1)} %constant_dynamic-update-slice_fusion.gathered_refs_0_), channel_id=1, source_target_pairs={{0,8},{1,9},{2,10},{3,11},{4,12},{5,13},{6,14},{7,15},{8,0},{9,1},... | collective-permute-start | bytes 122888 | tf_op jit(solution)/shard_map/ppermute | solution.py:1181
  69.1 1.2 collective-permute-start.22
  70.3 5.5 %collective-permute-start.25 = (f32[8,256]{1,0:T(8,128)S(1)}, f32[8,256]{1,0:T(8,128)S(1)}, u32[]{:S(2)}, u32[]{:S(2)}) collective-permute-start(f32[8,256]{1,0:T(8,128)S(1)} %add.41.sums_refs_0_), channel_id=1, source_target_pairs={{0,24},{1,25},{2,26},{3,27},{4,28},{5,29},{6,30},{7,31},{8,16},{9,... | collective-permute-start | bytes 24584 | tf_op jit(solution)/shard_map/ppermute | solution.py:1181
  72.3 4.6 %collective-permute-start.24 = (f32[8,256]{1,0:T(8,128)S(1)}, f32[8,256]{1,0:T(8,128)S(1)}, u32[]{:S(2)}, u32[]{:S(2)}) collective-permute-start(f32[8,256]{1,0:T(8,128)S(1)} %add.41.sums_refs_0_), channel_id=1, source_target_pairs={{0,16},{1,17},{2,18},{3,19},{4,20},{5,21},{6,22},{7,23},{8,24},{9,... | collective-permute-start | bytes 24584 | tf_op jit(solution)/shard_map/ppermute | solution.py:1181
  72.4 4.5 %collective-permute-start.23 = (f32[8,256]{1,0:T(8,128)S(1)}, f32[8,256]{1,0:T(8,128)S(1)}, u32[]{:S(2)}, u32[]{:S(2)}) collective-permute-start(f32[8,256]{1,0:T(8,128)S(1)} %add.41.sums_refs_0_), channel_id=1, source_target_pairs={{0,8},{1,9},{2,10},{3,11},{4,12},{5,13},{6,14},{7,15},{8,0},{9,1},... | collective-permute-start | bytes 24584 | tf_op jit(solution)/shard_map/ppermute | solution.py:1181
  79.6 20.5 %collective-permute-start.29 = (bf16[2,784,256]{2,1,0:T(8,128)(2,1)S(1)}, bf16[2,784,256]{2,1,0:T(8,128)(2,1)S(1)}, u32[]{:S(2)}, u32[]{:S(2)}) collective-permute-start(bf16[2,784,256]{2,1,0:T(8,128)(2,1)S(1)} %get-tuple-element.151), channel_id=1, source_target_pairs={{0,2},{1,3},{2,0},{3,1},{4,6},{5,7},{6,4},{7,5},{8,10},{9,11},{10,... | collective-permute-start | bytes 2408456 | tf_op jit(solution)/shard_map/ppermute | solution.py:1181
  81.2 1.2 collective-permute-start.30
  82.4 5.5 %collective-permute-start.33 = (f32[8,256]{1,0:T(8,128)S(1)}, f32[8,256]{1,0:T(8,128)S(1)}, u32[]{:S(2)}, u32[]{:S(2)}) collective-permute-start(f32[8,256]{1,0:T(8,128)S(1)} %add.42.back_refs_0_.out_back_refs_0_), channel_id=1, source_target_pairs={{0,24},{1,25},{2,26},{3,27},{4,28},{5,29},{6,30},{7,31},{8,16},{9,... | collective-permute-start | bytes 24584 | tf_op jit(solution)/shard_map/ppermute | solution.py:1181
  85.0 4.5 %collective-permute-start.32 = (f32[8,256]{1,0:T(8,128)S(1)}, f32[8,256]{1,0:T(8,128)S(1)}, u32[]{:S(2)}, u32[]{:S(2)}) collective-permute-start(f32[8,256]{1,0:T(8,128)S(1)} %add.42.back_refs_0_.out_back_refs_0_), channel_id=1, source_target_pairs={{0,16},{1,17},{2,18},{3,19},{4,20},{5,21},{6,22},{7,23},{8,24},{9,... | collective-permute-start | bytes 24584 | tf_op jit(solution)/shard_map/ppermute | solution.py:1181
  85.2 4.4 %collective-permute-start.31 = (f32[8,256]{1,0:T(8,128)S(1)}, f32[8,256]{1,0:T(8,128)S(1)}, u32[]{:S(2)}, u32[]{:S(2)}) collective-permute-start(f32[8,256]{1,0:T(8,128)S(1)} %add.42.back_refs_0_.out_back_refs_0_), channel_id=1, source_target_pairs={{0,8},{1,9},{2,10},{3,11},{4,12},{5,13},{6,14},{7,15},{8,0},{9,1},... | collective-permute-start | bytes 24584 | tf_op jit(solution)/shard_map/ppermute | solution.py:1181
  92.3 1.2 collective-permute-start.34
  93.6 6.5 %collective-permute-start.37 = (f32[16,128]{1,0:T(8,128)S(1)}, f32[16,128]{1,0:T(8,128)S(1)}, u32[]{:S(2)}, u32[]{:S(2)}) collective-permute-start(f32[16,128]{1,0:T(8,128)S(1)} %pad_maximum_fusion.5.back_refs_0_), channel_id=1, source_target_pairs={{0,24},{1,25},{2,26},{3,27},{4,28},{5,29},{6,30},{7,31},{8,16},{9,... | collective-permute-start | bytes 24584 | tf_op jit(solution)/shard_map/ppermute | solution.py:1181
  95.1 5.0 %collective-permute-start.36 = (f32[16,128]{1,0:T(8,128)S(1)}, f32[16,128]{1,0:T(8,128)S(1)}, u32[]{:S(2)}, u32[]{:S(2)}) collective-permute-start(f32[16,128]{1,0:T(8,128)S(1)} %pad_maximum_fusion.5.back_refs_0_), channel_id=1, source_target_pairs={{0,16},{1,17},{2,18},{3,19},{4,20},{5,21},{6,22},{7,23},{8,24},{9,... | collective-permute-start | bytes 24584 | tf_op jit(solution)/shard_map/ppermute | solution.py:1181
  96.0 4.2 %collective-permute-start.35 = (f32[16,128]{1,0:T(8,128)S(1)}, f32[16,128]{1,0:T(8,128)S(1)}, u32[]{:S(2)}, u32[]{:S(2)}) collective-permute-start(f32[16,128]{1,0:T(8,128)S(1)} %pad_maximum_fusion.5.back_refs_0_), channel_id=1, source_target_pairs={{0,8},{1,9},{2,10},{3,11},{4,12},{5,13},{6,14},{7,15},{8,0},{9,1},... | collective-permute-start | bytes 24584 | tf_op jit(solution)/shard_map/ppermute | solution.py:1181
  100.3 30.5 %collective-permute-start.38 = (bf16[4,784,256]{2,1,0:T(8,128)(2,1)S(1)}, bf16[4,784,256]{2,1,0:T(8,128)(2,1)S(1)}, u32[]{:S(2)}, u32[]{:S(2)}) collective-permute-start(bf16[4,784,256]{2,1,0:T(8,128)(2,1)S(1)} %pad_maximum_fusion), channel_id=1, source_target_pairs={{0,0},{1,4},{2,2},{3,6},{4,1},{5,5},{6,3},{7,7},{8,8},{9,12},{10,1... | collective-permute-start | bytes 4816904 | tf_op jit(solution)/shard_map/ppermute | solution.py:1181
  101.3 6.3 %collective-permute-start.39 = (bf16[2,656,128]{2,1,0:T(8,128)(2,1)S(1)}, bf16[2,656,128]{2,1,0:T(8,128)(2,1)S(1)}, u32[]{:S(2)}, u32[]{:S(2)}) collective-permute-start(bf16[2,656,128]{2,1,0:T(8,128)(2,1)S(1)} %get-tuple-element.172), channel_id=1, source_target_pairs={{0,1},{1,0},{2,3},{3,2},{4,5},{5,4},{6,7},{7,6},{8,9},{9,8},{10,11... | collective-permute-start | bytes 1007624 | tf_op jit(solution)/shard_map/ppermute | solution.py:1181
  107.6 1.2 collective-permute-start.40
  108.8 7.4 %collective-permute-start.43 = (f32[2,256]{1,0:T(2,128)S(1)}, f32[2,256]{1,0:T(2,128)S(1)}, u32[]{:S(2)}, u32[]{:S(2)}) collective-permute-start(f32[2,256]{1,0:T(2,128)S(1)} %add.44.back_refs_0_), channel_id=1, source_target_pairs={{0,24},{1,25},{2,26},{3,27},{4,28},{5,29},{6,30},{7,31},{8,16},{9,... | collective-permute-start | bytes 6152 | tf_op jit(solution)/shard_map/ppermute | solution.py:1181
  110.8 5.4 %collective-permute-start.42 = (f32[2,256]{1,0:T(2,128)S(1)}, f32[2,256]{1,0:T(2,128)S(1)}, u32[]{:S(2)}, u32[]{:S(2)}) collective-permute-start(f32[2,256]{1,0:T(2,128)S(1)} %add.44.back_refs_0_), channel_id=1, source_target_pairs={{0,16},{1,17},{2,18},{3,19},{4,20},{5,21},{6,22},{7,23},{8,24},{9,... | collective-permute-start | bytes 6152 | tf_op jit(solution)/shard_map/ppermute | solution.py:1181
  111.8 4.4 %collective-permute-start.41 = (f32[2,256]{1,0:T(2,128)S(1)}, f32[2,256]{1,0:T(2,128)S(1)}, u32[]{:S(2)}, u32[]{:S(2)}) collective-permute-start(f32[2,256]{1,0:T(2,128)S(1)} %add.44.back_refs_0_), channel_id=1, source_target_pairs={{0,8},{1,9},{2,10},{3,11},{4,12},{5,13},{6,14},{7,15},{8,0},{9,1},... | collective-permute-start | bytes 6152 | tf_op jit(solution)/shard_map/ppermute | solution.py:1181
  118.3 3.2 %collective-permute-start.44 = (bf16[2,1152,128]{2,1,0:T(8,128)(2,1)S(1)}, bf16[2,1152,128]{2,1,0:T(8,128)(2,1)S(1)}, u32[]{:S(2)}, u32[]{:S(2)}) collective-permute-start(bf16[2,1152,128]{2,1,0:T(8,128)(2,1)S(1)} %get-tuple-element.187), channel_id=1, source_target_pairs={{0,1},{1,0},{2,3},{3,2},{4,5},{5,4},{6,7},{7,6},{8,9},{9,8},{10,11... | collective-permute-start | bytes 1769480 | tf_op jit(solution)/shard_map/ppermute | solution.py:1181
  118.4 2.4 %collective-permute-start.46 = (bf16[2,592,128]{2,1,0:T(8,128)(2,1)S(1)}, bf16[2,592,128]{2,1,0:T(8,128)(2,1)S(1)}, u32[]{:S(2)}, u32[]{:S(2)}) collective-permute-start(bf16[2,592,128]{2,1,0:T(8,128)(2,1)S(1)} %get-tuple-element.192), channel_id=1, source_target_pairs={{0,1},{1,0},{2,3},{3,2},{4,5},{5,4},{6,7},{7,6},{8,9},{9,8},{10,11... | collective-permute-start | bytes 909320 | tf_op jit(solution)/shard_map/ppermute | solution.py:1181
  118.9 5.1 %collective-permute-start.48 = (bf16[784,256]{1,0:T(8,128)(2,1)S(1)}, bf16[784,256]{1,0:T(8,128)(2,1)S(1)}, u32[]{:S(2)}, u32[]{:S(2)}) collective-permute-start(bf16[784,256]{1,0:T(8,128)(2,1)S(1)} %get-tuple-element.186), channel_id=1, source_target_pairs={{0,0},{1,4},{2,2},{3,6},{4,1},{5,5},{6,3},{7,7},{8,8},{9,12},{10,1... | collective-permute-start | bytes 1204232 | tf_op jit(solution)/shard_map/ppermute | solution.py:1181
  121.0 9.9 %collective-permute-start.47 = (bf16[1280,128]{1,0:T(8,128)(2,1)S(1)}, bf16[1280,128]{1,0:T(8,128)(2,1)S(1)}, u32[]{:S(2)}, u32[]{:S(2)}) collective-permute-start(bf16[1280,128]{1,0:T(8,128)(2,1)S(1)} %get-tuple-element.194), channel_id=1, source_target_pairs={{0,2},{1,3},{2,0},{3,1},{4,6},{5,7},{6,4},{7,5},{8,10},{9,11},{10,... | collective-permute-start | bytes 983048 | tf_op jit(solution)/shard_map/ppermute | solution.py:1181
  122.2 12.6 %collective-permute-start.45 = (bf16[2,576,128]{2,1,0:T(8,128)(2,1)S(1)}, bf16[2,576,128]{2,1,0:T(8,128)(2,1)S(1)}, u32[]{:S(2)}, u32[]{:S(2)}) collective-permute-start(bf16[2,576,128]{2,1,0:T(8,128)(2,1)S(1)} %get-tuple-element.189), channel_id=1, source_target_pairs={{0,4},{1,5},{2,6},{3,7},{4,0},{5,1},{6,2},{7,3},{8,12},{9,13},{10,... | collective-permute-start | bytes 884744 | tf_op jit(solution)/shard_map/ppermute | solution.py:1181
  131.5 8.7 %collective-permute-start.50 = (bf16[640,128]{1,0:T(8,128)(2,1)S(1)}, bf16[640,128]{1,0:T(8,128)(2,1)S(1)}, u32[]{:S(2)}, u32[]{:S(2)}) collective-permute-start(bf16[640,128]{1,0:T(8,128)(2,1)S(1)} %get-tuple-element.198), channel_id=1, source_target_pairs={{0,4},{1,5},{2,6},{3,7},{4,0},{5,1},{6,2},{7,3},{8,12},{9,13},{10,... | collective-permute-start | bytes 491528 | tf_op jit(solution)/shard_map/ppermute | solution.py:1181
  134.9 5.2 %collective-permute-start.49 = (bf16[576,128]{1,0:T(8,128)(2,1)S(1)}, bf16[576,128]{1,0:T(8,128)(2,1)S(1)}, u32[]{:S(2)}, u32[]{:S(2)}) collective-permute-start(bf16[576,128]{1,0:T(8,128)(2,1)S(1)} %get-tuple-element.197), channel_id=1, source_target_pairs={{0,2},{1,3},{2,0},{3,1},{4,6},{5,7},{6,4},{7,5},{8,10},{9,11},{10,... | collective-permute-start | bytes 442376 | tf_op jit(solution)/shard_map/ppermute | solution.py:1181
  140.9 4.8 %collective-permute-start.51 = (bf16[2,784,256]{2,1,0:T(8,128)(2,1)S(1)}, bf16[2,784,256]{2,1,0:T(8,128)(2,1)S(1)}, u32[]{:S(2)}, u32[]{:S(2)}) collective-permute-start(bf16[2,784,256]{2,1,0:T(8,128)(2,1)S(1)} %pad_maximum_fusion.4), channel_id=1, source_target_pairs={{0,1},{1,0},{2,3},{3,2},{4,5},{5,4},{6,7},{7,6},{8,9},{9,8},{10,11... | collective-permute-start | bytes 2408456 | tf_op jit(solution)/shard_map/ppermute | solution.py:1181
  141.0 14.8 %collective-permute-start.52 = (bf16[784,256]{1,0:T(8,128)(2,1)S(1)}, bf16[784,256]{1,0:T(8,128)(2,1)S(1)}, u32[]{:S(2)}, u32[]{:S(2)}) collective-permute-start(bf16[784,256]{1,0:T(8,128)(2,1)S(1)} %collective-permute-done.48.low_refs_0_), channel_id=1, source_target_pairs={{0,2},{1,3},{2,0},{3,1},{4,6},{5,7},{6,4},{7,5},{8,10},{9,11},{10,... | collective-permute-start | bytes 1204232 | tf_op jit(solution)/shard_map/ppermute | solution.py:1181
  141.3 7.9 %collective-permute-start.53 = (bf16[304,128]{1,0:T(8,128)(2,1)S(1)}, bf16[304,128]{1,0:T(8,128)(2,1)S(1)}, u32[]{:S(2)}, u32[]{:S(2)}) collective-permute-start(bf16[304,128]{1,0:T(8,128)(2,1)S(1)} %get-tuple-element.204), channel_id=1, source_target_pairs={{0,8},{1,9},{2,10},{3,11},{4,12},{5,13},{6,14},{7,15},{8,0},{9,1},... | collective-permute-start | bytes 233480 | tf_op jit(solution)/shard_map/ppermute | solution.py:1181
  142.2 9.1 %collective-permute-start.54 = (bf16[304,128]{1,0:T(8,128)(2,1)S(1)}, bf16[304,128]{1,0:T(8,128)(2,1)S(1)}, u32[]{:S(2)}, u32[]{:S(2)}) collective-permute-start(bf16[304,128]{1,0:T(8,128)(2,1)S(1)} %get-tuple-element.205), channel_id=1, source_target_pairs={{0,16},{1,17},{2,18},{3,19},{4,20},{5,21},{6,22},{7,23},{8,24},{9,... | collective-permute-start | bytes 233480 | tf_op jit(solution)/shard_map/ppermute | solution.py:1181
  143.9 7.4 %collective-permute-start.55 = (bf16[304,128]{1,0:T(8,128)(2,1)S(1)}, bf16[304,128]{1,0:T(8,128)(2,1)S(1)}, u32[]{:S(2)}, u32[]{:S(2)}) collective-permute-start(bf16[304,128]{1,0:T(8,128)(2,1)S(1)} %get-tuple-element.206), channel_id=1, source_target_pairs={{0,24},{1,25},{2,26},{3,27},{4,28},{5,29},{6,30},{7,31},{8,16},{9,... | collective-permute-start | bytes 233480 | tf_op jit(solution)/shard_map/ppermute | solution.py:1181
  151.4 6.8 %collective-permute-start.58 = (bf16[304,128]{1,0:T(8,128)(2,1)S(1)}, bf16[304,128]{1,0:T(8,128)(2,1)S(1)}, u32[]{:S(2)}, u32[]{:S(2)}) collective-permute-start(bf16[304,128]{1,0:T(8,128)(2,1)S(1)} %add_depth.1.piece_refs_0_), channel_id=1, source_target_pairs={{0,24},{1,25},{2,26},{3,27},{4,28},{5,29},{6,30},{7,31},{8,16},{9,... | collective-permute-start | bytes 233480 | tf_op jit(solution)/shard_map/ppermute | solution.py:1181
  153.3 6.8 %collective-permute-start.57 = (bf16[304,128]{1,0:T(8,128)(2,1)S(1)}, bf16[304,128]{1,0:T(8,128)(2,1)S(1)}, u32[]{:S(2)}, u32[]{:S(2)}) collective-permute-start(bf16[304,128]{1,0:T(8,128)(2,1)S(1)} %add_depth.1.piece_refs_0_), channel_id=1, source_target_pairs={{0,16},{1,17},{2,18},{3,19},{4,20},{5,21},{6,22},{7,23},{8,24},{9,... | collective-permute-start | bytes 233480 | tf_op jit(solution)/shard_map/ppermute | solution.py:1181
  154.3 5.7 %collective-permute-start.56 = (bf16[304,128]{1,0:T(8,128)(2,1)S(1)}, bf16[304,128]{1,0:T(8,128)(2,1)S(1)}, u32[]{:S(2)}, u32[]{:S(2)}) collective-permute-start(bf16[304,128]{1,0:T(8,128)(2,1)S(1)} %add_depth.1.piece_refs_0_), channel_id=1, source_target_pairs={{0,8},{1,9},{2,10},{3,11},{4,12},{5,13},{6,14},{7,15},{8,0},{9,1},... | collective-permute-start | bytes 233480 | tf_op jit(solution)/shard_map/ppermute | solution.py:1181
  160.1 2.4 %collective-permute-start.59 = (bf16[784,256]{1,0:T(8,128)(2,1)S(1)}, bf16[784,256]{1,0:T(8,128)(2,1)S(1)}, u32[]{:S(2)}, u32[]{:S(2)}) collective-permute-start(bf16[784,256]{1,0:T(8,128)(2,1)S(1)} %collective-permute-done.48.low_refs_0_), channel_id=1, source_target_pairs={{0,1},{1,0},{2,3},{3,2},{4,5},{5,4},{6,7},{7,6},{8,9},{9,8},{10,11... | collective-permute-start | bytes 1204232 | tf_op jit(solution)/shard_map/ppermute | solution.py:1181
  160.1 2.4 %collective-permute-start.60 = (bf16[784,256]{1,0:T(8,128)(2,1)S(1)}, bf16[784,256]{1,0:T(8,128)(2,1)S(1)}, u32[]{:S(2)}, u32[]{:S(2)}) collective-permute-start(bf16[784,256]{1,0:T(8,128)(2,1)S(1)} %collective-permute-done.52.low_refs_2_), channel_id=1, source_target_pairs={{0,1},{1,0},{2,3},{3,2},{4,5},{5,4},{6,7},{7,6},{8,9},{9,8},{10,11... | collective-permute-start | bytes 1204232 | tf_op jit(solution)/shard_map/ppermute | solution.py:1181
  161.2 9.3 %collective-permute-start.61 = (bf16[1216,128]{1,0:T(8,128)(2,1)S(1)}, bf16[1216,128]{1,0:T(8,128)(2,1)S(1)}, u32[]{:S(2)}, u32[]{:S(2)}) collective-permute-start(bf16[1216,128]{1,0:T(8,128)(2,1)S(1)} %join_depth.1.term_refs_0_), channel_id=1, source_target_pairs={{0,4},{1,5},{2,6},{3,7},{4,0},{5,1},{6,2},{7,3},{8,12},{9,13},{10,... | collective-permute-start | bytes 933896 | tf_op jit(solution)/shard_map/ppermute | solution.py:1181
  (14 other events, 123.9 us)

commit v6 on v5

--- a/solution.py
+++ b/solution.py
@@ -57,18 +57,27 @@
     )
 
 
-def row_sums(matrix):
-    return dot_nn(jnp.ones((16, matrix.shape[0]), BF16), matrix)[0:1]
-
-
-def outer(column, row, row_exact=False):
-    exact, rounded = (row, column) if row_exact else (column, row)
-    high = exact.astype(BF16).astype(F32)
-    middle = (exact - high).astype(BF16).astype(F32)
-    empty = jnp.zeros((13, exact.shape[1]), F32)
-    exact = jnp.concatenate([high, middle, exact - high - middle, empty], axis=0).astype(BF16)
-    rounded = jnp.broadcast_to(rounded, (16, rounded.shape[1])).astype(BF16)
-    return dot_tn(rounded, exact) if row_exact else dot_tn(exact, rounded)
+def sum_rows(matrix):
+    value = dot_nn(jnp.ones((16, matrix.shape[0]), BF16), matrix)[0:1]
+    high = value.astype(BF16).astype(F32)
+    middle = (value - high).astype(BF16).astype(F32)
+    empty = jnp.zeros((13, value.shape[1]), F32)
+    rows = jnp.concatenate([high, middle, value - high - middle, empty], axis=0)
+    return rows.astype(BF16)
+
+
+def same_rows(row):
+    return jnp.broadcast_to(row, (16, row.shape[1])).astype(BF16)
+
+
+def centred_dot(centred, center, other):
+    left = jnp.concatenate([centred, same_rows(-center)], axis=0)
+    return dot_tn(left, jnp.concatenate([other, sum_rows(other)], axis=0))
+
+
+def dot_centred(other, centred, center):
+    right = jnp.concatenate([centred, same_rows(-center)], axis=0)
+    return dot_tn(jnp.concatenate([other, sum_rows(other)], axis=0), right)
 
 
 def expected(gain, shift):
@@ -522,17 +531,18 @@
     out_ref,
     sums_refs,
     affine_ref,
+    weighted_ref,
     x_refs,
-    cot_even_ref,
+    cot_near_ref,
     cot_odd_ref,
     cot_across_ref,
-    near_ref,
-    far_ref,
+    shared_ref,
     grad_ref,
     msg_ref,
+    map_ref,
 ):
     place = Place(counts_ref)
-    cot_refs = slot_refs(cot_even_ref, cot_odd_ref, cot_across_ref)
+    cot_refs = slot_refs(cot_near_ref, cot_odd_ref, cot_across_ref)
     blocks, rows, lanes = out_ref.shape
     sums = summed_over(sums_refs)
     center, scale = moments(sums[:blocks], sums[blocks:], place.total() * PIXELS)
@@ -542,12 +552,12 @@
         block = place.batch ^ k
         gain = affine_ref[0, block] * r
         shift = affine_ref[1, block] - mu * gain
+        map_ref[block] = gain
+        map_ref[blocks + block] = shift
         x_ref, upstream_ref = x_refs[k], cot_refs[k]
-        summed_ref = (near_ref, far_ref)[k >> 1].at[k & 1]
 
         def chunk(
-            step, carry, k=k, gain=gain, shift=shift,
-            x_ref=x_ref, upstream_ref=upstream_ref, summed_ref=summed_ref,
+            step, carry, k=k, gain=gain, shift=shift, x_ref=x_ref, upstream_ref=upstream_ref
         ):
             first, second = carry
             at = pl.multiple_of(step * CHUNK, CHUNK)
@@ -556,9 +566,9 @@
             real = (spot < limit).astype(F32)
             before = out_ref[k, here, :]
             summed = x_ref[here, :].astype(F32) + (before * gain + shift)
-            summed_ref[here, :] = summed.astype(BF16)
             share = logistic(summed)
-            grad = upstream_ref[here, :].astype(F32) * real * (share * (1.0 + summed * (1.0 - share)))
+            grad = upstream_ref[here, :].astype(F32) * real
+            grad = grad * (share * (1.0 + summed * (1.0 - share)))
             grad_ref[k, here, :] = grad
             return first + fold(grad), second + fold(grad * before)
 
@@ -569,22 +579,38 @@
         first = total_of(first)
         for t, row in enumerate((first, r * (total_of(second) - mu * first))):
             msg_ref[t * blocks + k : t * blocks + k + 1, :] = row
-
-
-def finish_owned(counts_ref, summed_ref, swapped_ref, cot_ref, result_ref, grad_ref):
+    shared_ref[0:rows, :] = weighted_ref[...]
+    exact = jnp.concatenate([map_ref[n] for n in range(2 * blocks)], axis=0)
+    high = exact.astype(BF16).astype(F32)
+    middle = (exact - high).astype(BF16).astype(F32)
+    shared_ref[rows : rows + 16, :] = jnp.concatenate([high, middle], axis=0).astype(BF16)
+    rest = jnp.concatenate([exact - high - middle, jnp.zeros_like(exact)], axis=0)
+    shared_ref[rows + 16 : rows + 32, :] = rest.astype(BF16)
+
+
+def finish_owned(
+    counts_ref, near_ref, swapped_ref, far_ref, w_ref, x_ref, cot_ref, result_ref, grad_ref, out_ref
+):
     chan, group = lax.axis_index("chan"), lax.axis_index("dp")
-    pieces = summed_ref.at[0], swapped_ref.at[0], summed_ref.at[2], swapped_ref.at[1]
     rows = cot_ref.shape[1]
-    for s, piece in enumerate(pieces):
+    blocks = len(SLOTS)
+    for s, piece in enumerate((near_ref, swapped_ref.at[0], far_ref, swapped_ref.at[1])):
         batch = chan ^ s
         limit = counts_ref[batch, group] * PIXELS
-
-        def chunk(step, carry, piece=piece, batch=batch, limit=limit):
+        out_ref[...] = dot_nn(piece[0:rows, :], w_ref[chan])
+        exact = piece[rows : rows + 32, :].astype(F32)
+        exact = exact[0:8] + exact[8:16] + exact[16:24]
+        gain, shift = exact[0:1], exact[blocks : blocks + 1]
+        for k in range(1, blocks):
+            gain = jnp.where(chan == k, exact[k : k + 1], gain)
+            shift = jnp.where(chan == k, exact[blocks + k : blocks + k + 1], shift)
+
+        def chunk(step, carry, batch=batch, limit=limit, gain=gain, shift=shift):
             at = pl.multiple_of(step * CHUNK, CHUNK)
             here = pl.ds(at, CHUNK)
             spot = lax.broadcasted_iota(jnp.int32, (CHUNK, 1), 0) + at
             real = (spot < limit).astype(F32)
-            summed = piece[here, :].astype(F32)
+            summed = x_ref[batch, here, :].astype(F32) + (out_ref[here, :] * gain + shift)
             share = logistic(summed)
             held = share * real
             result_ref[batch, here, :] = (summed * held).astype(BF16)
@@ -842,8 +868,7 @@
     for turn, s in enumerate(ORDER):
         target = keep_ref if turn < 2 else send_ref
         held = place.batch ^ place.chan ^ s
-        term = dot_tn(weighted_ref[...], low_ref[held])
-        term = (term - outer(center, row_sums(low_ref[held]), True)).astype(BF16)
+        term = centred_dot(weighted_ref[...], center, low_ref[held]).astype(BF16)
         target[turn % 2, 0:width, :] = term[:, :lanes]
         target[turn % 2, width : 2 * width, :] = term[:, lanes:]
     wide_ref[...] = dot_tn(logits_ref[...], gate_ref[0], HIGHEST)
@@ -887,7 +912,7 @@
         )
         low = low_ref[WIDE : WIDE + rows, r * width : (r + 1) * width]
         offset = jnp.concatenate([center[:, r * half : (r + 1) * half]] * 9, axis=1)
-        wide_ref[...] = dot_tn(low, right) - outer(row_sums(low), offset)
+        wide_ref[...] = dot_centred(low, right, offset)
         for turn, s in enumerate(ORDER):
             target = keep_ref if turn < 2 else send_ref
             here = pl.ds(pl.multiple_of((place.chan ^ s) * own, own), own)
@@ -946,9 +971,10 @@
             flat_ref[at : at + SIDE, :] = value[:SIDE]
     low_ref[...] = flat_ref[...].astype(BF16)
     lanes = keep_ref.shape[2]
-    low_sums = row_sums(low_ref[...])
+    low = jnp.concatenate([low_ref[...], sum_rows(low_ref[...])], axis=0)
     for k, x in enumerate((x0, x1, x2, x3)):
-        wide_ref[...] = dot_tn(low_ref[...], x[...]) - outer(low_sums, sums[2 + k : 3 + k] / total)
+        center = same_rows(-sums[2 + k : 3 + k] / total)
+        wide_ref[...] = dot_tn(low, jnp.concatenate([x[...], center], axis=0))
         for turn, s in enumerate(ORDER):
             target = keep_ref if turn < 2 else send_ref
             here = pl.ds(pl.multiple_of((chan ^ s) * own, own), own)
@@ -1060,17 +1086,6 @@
     sum_ref[...] = value.astype(BF16)
 
 
-def join_depth(
-    counts_ref,
-    piece_refs,
-    whole_ref,
-):
-    place = Place(counts_ref)
-    rows = piece_refs[0].shape[0]
-    for t, ref in enumerate(piece_refs):
-        whole_ref[pl.ds(pl.multiple_of((place.depth ^ t) * rows, 16), rows), :] = ref[...]
-
-
 def unpack(
     joined,
     counts_ref,
@@ -1111,13 +1126,14 @@
         mid_ref[...] = term_refs[0][...].astype(F32)
         write(term_refs[1][...].astype(F32), 0)
     else:
-        even = Place(counts_ref).parity == 0
+        place = Place(counts_ref)
+        even = place.parity == 0
         piece = term_refs[0].shape[0] // len(SLOTS)
         rows = mid_ref.shape[0] // 2 // len(SLOTS)
         for half in range(2):
             mine, other = term_refs[half], term_refs[1 - half]
             for z in range(len(SLOTS)):
-                here = slice(z * piece, (z + 1) * piece)
+                here = pl.ds(pl.multiple_of((place.depth ^ z) * piece, 16), piece)
                 value = jnp.where(even, mine[here, :].astype(F32), other[here, :].astype(F32))
                 at = (half * len(SLOTS) + z) * rows
                 mid_ref[at : at + rows, :] = value[:rows]
@@ -1235,7 +1251,7 @@
     def kernel(body, outs, *args, smem=1):
         return call(body, outs, [], 0, *args, smem=smem)
 
-    def add_over_all(first, second, low, summed, finish_own):
+    def add_over_all(first, second, low, shared, finish_own):
         first_rows, second_rows = first[0].shape[1], sum(k.shape[1] for k in second[0])
         if groups != 8:
             rows = padded(first_rows + second_rows)
@@ -1251,7 +1267,7 @@
             (terms,) = kernel(add_groups, [shape(terms.shape, BF16)], terms, smem=0)
             terms = lax.all_to_all(terms, "dp", 0, 0).reshape(rows, -1)
             terms = terms[:first_rows], terms[first_rows : first_rows + second_rows]
-            return (terms, low, across(low)) + tuple(finish_own(summed))
+            return (terms, low, across(low)) + tuple(finish_own(*shared))
         second_rows = padded(second_rows)
         halves = (first_rows // 2, second_rows // 2)
         pieces = (first_rows // groups, second_rows // groups)
@@ -1271,7 +1287,7 @@
             *first,
         )
         first_arrived = parity(send)
-        arrived = after(arrived, summed, low)
+        arrived = after(arrived, shared[1])
         keep, send = call(
             add_chip,
             [rows(halves[1]), rows(halves[1], BF16)],
@@ -1300,22 +1316,23 @@
             (first_keep, keep),
             (first_arrived, arrived),
         )
-        low_other = across(after(low, keep))
-        result, grad_summed = finish_own(after(summed, keep))
+        low = away_plane(after(low, keep))
+        result, grad_summed = finish_own(*after_all(shared, keep))
         arrived = tuple(along(send[t - 1], t) for t in range(1, depth))
         arrived = after_all(arrived, result)
+        low_other = across(after(low, *arrived))
         (mine,) = kernel(add_depth, [rows(sum(pieces), BF16)], keep, arrived, smem=0)
         mine = (mine,) + tuple(along(mine, t) for t in range(1, depth))
         low, low_other = after_all((low, low_other), *mine)
-        (mine,) = kernel(join_depth, [rows(sum(halves), BF16)], counts, mine)
+        mine = jnp.concatenate(mine)
         return (mine, parity(mine)), low, low_other, result, grad_summed
 
     def slots_of(tensor, *which):
         return [lax.dynamic_index_in_dim(tensor, chan ^ s, 0, keepdims=False) for s in which]
 
+    first = weight_in.T
+    other, near = across(first), core(first)
     far = slots_of(activations, 2, 3)
-    first = after(weight_in.T, *far)
-    other, near = across(first), core(first)
     x = slots_of(after(activations, near), 0, 1) + far
     x = tuple(home(piece, s) for s, piece in enumerate(x))
 
@@ -1445,23 +1462,26 @@
         w_out,
     )
     out_sums = exchange(2 * parts, 0)(msg)
-    *summed, grad, msg = call(
+    shared, grad, msg = call(
         finish,
-        [shape((2, rows, lanes), BF16)] * 2
-        + [shape((parts, rows, lanes)), shape((2 * parts, lanes))],
-        [],
+        [
+            shape((rows + 32, width), BF16),
+            shape((parts, rows, lanes)),
+            shape((2 * parts, lanes)),
+        ],
+        [pltpu.VMEM((2 * parts, 1, lanes), F32)],
         0,
         counts,
         out,
         out_sums,
         out_affine,
+        weighted,
         x,
         *cot,
     )
     out_back = exchange(2 * parts, 0)(msg)
 
-    near, far = summed
-    far = across(far)
+    shared = away_plane(shared)
 
     sums_rows = 2 * 2 * width // inter
     low_out, grad_weighted, grad_logits, msg = call(
@@ -1502,8 +1522,9 @@
         grad_logits,
         mid_affine,
     )
-    mid_back = after_all(mid_back, keep, far)
-    summed = away_plane(after(jnp.concatenate([near, far]), mid_back[0]))
+    mid_back = after_all(mid_back, keep, shared)
+    shared = after(shared, mid_back[0])
+    shared = (shared, across(shared))
     out_keep, out_arrived = keep, core(after(send, mid_back[0]))
     low_mid, grad_hidden, grad_squeeze, vectors, msg = call(
         back_mid,
@@ -1543,7 +1564,7 @@
         low_mid,
         in_affine,
     )
-    in_back = after_all(in_back, keep)
+    in_back = after_all(in_back, keep, shared[1])
     in_rows = parts * lanes // (2 * own) * own
     low_in, in_keep, in_send = call(
         functools.partial(back_in, 1.0 / groups),
@@ -1570,17 +1591,28 @@
     )
     owned = shape((batches, rows, lanes), BF16)
 
-    def finish_own(summed):
-        swapped = core(jnp.stack([summed[1], summed[3]]))
-        return call(finish_owned, [owned, owned], [], 0, counts, summed, swapped, cotangent)
+    def finish_own(near, far):
+        swapped = core(jnp.stack([near, far]))
+        return call(
+            finish_owned,
+            [owned, owned],
+            [pltpu.VMEM((rows, lanes), F32)],
+            product,
+            counts,
+            near,
+            swapped,
+            far,
+            w_out,
+            activations,
+            cotangent,
+        )
 
     send = after(send, low_in)
-    low_in = away_plane(low_in)
     terms, low_in, low_other, result, grad_summed = add_over_all(
         (keep, core(send)),
         ((out_keep, in_keep), (out_arrived, core(in_send))),
         low_in,
-        summed,
+        shared,
         finish_own,
     )
     lows = (low_in, core(low_in), low_other, core(low_other))

time: 173 us -> 169 us (0.977)
    pallas_call x23 -> x22, Pallas kernels: 35.2 us -> 34 us  [call(): pl.pallas_call(body, out_shape=outs, in_specs=specs, out_specs=[pl.BlockS...]
  transfers between devices with their start and end apart: 62 -> 62, of which waited for: 31 -> 33; matrix products, arithmetic and copies ran while one was open for 1% -> 2% of each run, Pallas kernels for 18% -> 16%
where the time goes in v6:
time: 169 us
  waiting for transfers between devices  67.8 us (40%)
  starting transfers between devices  63.1 us (37%)
  Pallas kernels  34 us (20%)
  local copies, waits for them, and re-layouts  2.55 us (2%)
    ppermute x62, waiting for transfers between devices, permute(): return lax.ppermute(tensor, ('dp', 'chan'), pairs)  67.8 us
    ppermute x62, starting transfers between devices, permute(): return lax.ppermute(tensor, ('dp', 'chan'), pairs)  63.1 us
    pallas_call x22, Pallas kernels, call(): pl.pallas_call(body, out_shape=outs, in_specs=specs, out_specs=[pl.BlockS...  34 us
  transfers between devices with their start and end apart: 62, of which 33 were waited for; matrix products, arithmetic and copies ran while one was open for 2% of the time, Pallas kernels for 16%

profile of v6, /device:TPU:0, one launch (start us, length us, event | category | flops | bytes accessed | tf_op | source)
XLA Modules:
  0.0 169.2 jit_solution(17358439074136337292)
XLA Ops:
  0.7 3.0 %collective-permute-start.5 = (bf16[64,1024]{1,0:T(8,128)(2,1)}, bf16[64,1024]{1,0:T(8,128)(2,1)S(1)}, u32[]{:S(2)}, u32[]{:S(2)}) collective-permute-start(bf16[64,1024]{1,0:T(8,128)(2,1)} %bitcast.37), channel_id=1, source_target_pairs={{0,2},{1,3},{2,0},{3,1},{4,6},{5,7},{6,4},{7,5},{8,10},{9,11},{10,... | collective-permute-start | bytes 393224 | tf_op jit(solution)/shard_map/ppermute | solution.py:1197
  3.8 2.2 %dynamic-slice_bitcast_fusion = (bf16[784,256]{1,0:T(8,128)(2,1)}, bf16[784,256]{1,0:T(8,128)(2,1)}) fusion(bf16[4,784,256]{2,1,0:T(8,128)(2,1)} %x_ref.1, s32[]{:T(128)S(6)} %select_n.20, s32[]{:T(128)S(6)} %select_n.19), kind=kLoop, calls=%fused_computation.4 | loop fusion | bytes 1605640 | tf_op jit(solution)/shard_map/jit(dynamic_index_in_dim)/squeeze | solution.py:1331
  6.0 1.4 collective-permute-start.4
  7.4 1.5 collective-permute-start.3
  10.4 1.5 collective-permute-start.6
  11.9 1.0 collective-permute-done.6.a3
  13.3 12.1 %collective-permute-done.4.x3.x_refs_3_ = bf16[784,256]{1,0:T(8,128)(2,1)S(1)} collective-permute-done((bf16[784,256]{1,0:T(8,128)(2,1)}, bf16[784,256]{1,0:T(8,128)(2,1)S(1)}, u32[]{:S(2)}, u32[]{:S(2)}) %collective-permute-start.4) | collective-permute-done | bytes 401440 | tf_op jit(solution)/shard_map/ppermute | solution.py:1197
  25.4 1.5 collective-permute-done.3.x2.x_refs_2_
  26.9 1.6 reduce_in.1
  28.8 1.2 collective-permute-done.8
  29.9 3.7 %collective-permute-start.11 = (f32[6,256]{1,0:T(8,128)S(1)}, f32[6,256]{1,0:T(8,128)S(1)}, u32[]{:S(2)}, u32[]{:S(2)}) collective-permute-start(f32[6,256]{1,0:T(8,128)S(1)} %add.39.sums_refs_0_), channel_id=1, source_target_pairs={{0,24},{1,25},{2,26},{3,27},{4,28},{5,29},{6,30},{7,31},{8,16},{9,... | collective-permute-start | bytes 18440 | tf_op jit(solution)/shard_map/ppermute | solution.py:1197
  35.4 2.8 %collective-permute-done.10.sums_refs_2_ = f32[6,256]{1,0:T(8,128)S(1)} collective-permute-done((f32[6,256]{1,0:T(8,128)S(1)}, f32[6,256]{1,0:T(8,128)S(1)}, u32[]{:S(2)}, u32[]{:S(2)}) %collective-permute-start.10) | collective-permute-done | bytes 6176 | tf_op jit(solution)/shard_map/ppermute | solution.py:1197
  38.2 1.6 collective-permute-start.27
  39.7 1.8 %collective-permute-done.13.b3 = bf16[1872,128]{1,0:T(8,128)(2,1)S(1)} collective-permute-done((bf16[1872,128]{1,0:T(8,128)(2,1)S(1)}, bf16[1872,128]{1,0:T(8,128)(2,1)S(1)}, u32[]{:S(2)}, u32[]{:S(2)}) %collective-permute-start.13) | collective-permute-done | bytes 479264 | tf_op jit(solution)/shard_map/ppermute | solution.py:1197
  42.5 2.3 %conv_mid.1 = (bf16[3,976,256]{2,1,0:T(8,128)(2,1)S(1)}, f32[896,512]{1,0:T(8,128)S(1)}, f32[2,512]{1,0:T(2,128)S(1)}) custom-call(s32[4,8]{1,0:T(4,128)S(1)} %copy-done.2, f32[896,256]{1,0:T(8,128)S(1)} %get-tuple-element.125.pre_ref, f32[6,256]{1,0:T(8,128)S(1)} %add.39.sums_refs_0_, f32[6,256]{1,0:T(8,128)S(1)} %collective-permute-done.9.sums_refs_1_, ...), custom_call_target="tpu_custom_call" | custom-call | flops 1056964608 | bytes 5462144 | tf_op jit(solution)/shard_map/conv_mid/pallas_call | solution.py:192
  45.0 1.0 collective-permute-done.14
  46.0 2.6 %collective-permute-start.17 = (f32[2,512]{1,0:T(2,128)S(1)}, f32[2,512]{1,0:T(2,128)S(1)}, u32[]{:S(2)}, u32[]{:S(2)}) collective-permute-start(f32[2,512]{1,0:T(2,128)S(1)} %add.40.sums_refs_0_.mid_sums_refs_0_), channel_id=1, source_target_pairs={{0,24},{1,25},{2,26},{3,27},{4,28},{5,29},{6,30},{7,31},{8,16},{9,... | collective-permute-start | bytes 12296 | tf_op jit(solution)/shard_map/ppermute | solution.py:1197
  48.6 1.8 %collective-permute-start.15 = (f32[2,512]{1,0:T(2,128)S(1)}, f32[2,512]{1,0:T(2,128)S(1)}, u32[]{:S(2)}, u32[]{:S(2)}) collective-permute-start(f32[2,512]{1,0:T(2,128)S(1)} %add.40.sums_refs_0_.mid_sums_refs_0_), channel_id=1, source_target_pairs={{0,8},{1,9},{2,10},{3,11},{4,12},{5,13},{6,14},{7,15},{8,0},{9,1},... | collective-permute-start | bytes 12296 | tf_op jit(solution)/shard_map/ppermute | solution.py:1197
  50.4 1.0 collective-permute-done.17.sums_refs_3_.mid_sums_refs_3_
  51.4 1.7 %collective-permute-done.16.sums_refs_2_.mid_sums_refs_2_ = f32[2,512]{1,0:T(2,128)S(1)} collective-permute-done((f32[2,512]{1,0:T(2,128)S(1)}, f32[2,512]{1,0:T(2,128)S(1)}, u32[]{:S(2)}, u32[]{:S(2)}) %collective-permute-start.16) | collective-permute-done | bytes 4128 | tf_op jit(solution)/shard_map/ppermute | solution.py:1197
  53.2 1.7 %pool.1 = (f32[4,256]{1,0:T(4,128)S(1)}, f32[40,128]{1,0:T(8,128)S(1)}) custom-call(s32[4,8]{1,0:T(4,128)S(1)} %copy-done.2, f32[896,512]{1,0:T(8,128)S(1)} %get-tuple-element.133.mid_ref, f32[2,512]{1,0:T(2,128)S(1)} %add.40.sums_refs_0_.mid_sums_refs_0_, f32[2,512]{1,0:T(2,128)S(1)} %collective-permute-done.15.sums_refs_1_.mid_sums_refs_1_, ...), custom_call_target="tpu_custom_call" | custom-call | bytes 1945728 | tf_op jit(solution)/shard_map/pool/pallas_call | solution.py:192
  55.8 1.5 collective-permute-start.28
  58.7 3.6 %collective-permute-start.21 = (f32[80,128]{1,0:T(8,128)S(1)}, f32[80,128]{1,0:T(8,128)S(1)}, u32[]{:S(2)}, u32[]{:S(2)}) collective-permute-start(f32[80,128]{1,0:T(8,128)S(1)} %constant_dynamic-update-slice_fusion.gathered_refs_0_), channel_id=1, source_target_pairs={{0,24},{1,25},{2,26},{3,27},{4,28},{5,29},{6,30},{7,31},{8,16},{9,... | collective-permute-start | bytes 122888 | tf_op jit(solution)/shard_map/ppermute | solution.py:1197
  64.6 2.6 %collective-permute-done.20.gathered_refs_2_ = f32[80,128]{1,0:T(8,128)S(1)} collective-permute-done((f32[80,128]{1,0:T(8,128)S(1)}, f32[80,128]{1,0:T(8,128)S(1)}, u32[]{:S(2)}, u32[]{:S(2)}) %collective-permute-start.20) | collective-permute-done | bytes 40992 | tf_op jit(solution)/shard_map/ppermute | solution.py:1197
  67.2 1.9 %attend.1 = (f32[2,4,128]{2,1,0:T(4,128)S(1)}, f32[4,512]{1,0:T(4,128)S(1)}, bf16[784,256]{1,0:T(8,128)(2,1)S(1)}, f32[4,784,256]{2,1,0:T(8,128)S(1)}, f32[8,256]{1,0:T(8,128)S(1)}) custom-call(s32[4,8]{1,0:T(4,128)S(1)} %copy-done.2, f32[80,128]{1,0:T(8,128)S(1)} %constant_dynamic-update-slice_fusion.gathered_refs_0_, ...), custom_call_target="tpu_custom_call" | custom-call | flops 411041792 | bytes 6327424 | tf_op jit(solution)/shard_map/attend/pallas_call | solution.py:192
  69.3 1.2 collective-permute-done.22
  70.4 2.0 %collective-permute-start.25 = (f32[8,256]{1,0:T(8,128)S(1)}, f32[8,256]{1,0:T(8,128)S(1)}, u32[]{:S(2)}, u32[]{:S(2)}) collective-permute-start(f32[8,256]{1,0:T(8,128)S(1)} %add.41.sums_refs_0_), channel_id=1, source_target_pairs={{0,24},{1,25},{2,26},{3,27},{4,28},{5,29},{6,30},{7,31},{8,16},{9,... | collective-permute-start | bytes 24584 | tf_op jit(solution)/shard_map/ppermute | solution.py:1197
  72.6 2.2 %collective-permute-start.23 = (f32[8,256]{1,0:T(8,128)S(1)}, f32[8,256]{1,0:T(8,128)S(1)}, u32[]{:S(2)}, u32[]{:S(2)}) collective-permute-start(f32[8,256]{1,0:T(8,128)S(1)} %add.41.sums_refs_0_), channel_id=1, source_target_pairs={{0,8},{1,9},{2,10},{3,11},{4,12},{5,13},{6,14},{7,15},{8,0},{9,1},... | collective-permute-start | bytes 24584 | tf_op jit(solution)/shard_map/ppermute | solution.py:1197
  74.8 1.2 collective-permute-done.25.sums_refs_3_
  76.0 1.0 collective-permute-done.24.sums_refs_2_
  77.0 2.6 %finish.1 = (bf16[816,256]{1,0:T(8,128)(2,1)S(1)}, f32[4,784,256]{2,1,0:T(8,128)S(1)}, f32[8,256]{1,0:T(8,128)S(1)}) custom-call(s32[4,8]{1,0:T(4,128)S(1)} %copy-done.2, f32[4,784,256]{2,1,0:T(8,128)S(1)} %get-tuple-element.142.out_ref, f32[8,256]{1,0:T(8,128)S(1)} %add.41.sums_refs_0_, f32[8,256]{1,0:T(8,128)S(1)} %collective-permute-done.23.sums_refs_1_, ...), custom_call_target="tpu_custom_call" | custom-call | bytes 11305088 | tf_op jit(solution)/shard_map/finish/pallas_call | solution.py:192
  79.7 1.2 collective-permute-done.30
  80.8 3.1 %collective-permute-start.33 = (f32[8,256]{1,0:T(8,128)S(1)}, f32[8,256]{1,0:T(8,128)S(1)}, u32[]{:S(2)}, u32[]{:S(2)}) collective-permute-start(f32[8,256]{1,0:T(8,128)S(1)} %add.42.back_refs_0_.out_back_refs_0_), channel_id=1, source_target_pairs={{0,24},{1,25},{2,26},{3,27},{4,28},{5,29},{6,30},{7,31},{8,16},{9,... | collective-permute-start | bytes 24584 | tf_op jit(solution)/shard_map/ppermute | solution.py:1197
  84.0 1.2 collective-permute-start.31
  86.3 2.2 %collective-permute-done.32.back_refs_2_.out_back_refs_2_ = f32[8,256]{1,0:T(8,128)S(1)} collective-permute-done((f32[8,256]{1,0:T(8,128)S(1)}, f32[8,256]{1,0:T(8,128)S(1)}, u32[]{:S(2)}, u32[]{:S(2)}) %collective-permute-start.32) | collective-permute-done | bytes 8224 | tf_op jit(solution)/shard_map/ppermute | solution.py:1197
  88.5 2.8 %back_out.1 = (bf16[4,784,256]{2,1,0:T(8,128)(2,1)S(1)}, f32[896,256]{1,0:T(8,128)S(1)}, f32[4,512]{1,0:T(4,128)S(1)}, f32[12,128]{1,0:T(8,128)S(1)}) custom-call(s32[4,8]{1,0:T(4,128)S(1)} %copy-done.2, f32[4,784,256]{2,1,0:T(8,128)S(1)} %get-tuple-element.151.grad_ref, f32[4,784,256]{2,1,0:T(8,128)S(1)} %get-tuple-element.142.out_ref, ...), custom_call_target="tpu_custom_call" | custom-call | flops 411041792 | bytes 11556992 | tf_op jit(solution)/shard_map/back_out/pallas_call | solution.py:192
  91.3 1.1 collective-permute-start.34
  93.2 2.3 %collective-permute-start.37 = (f32[16,128]{1,0:T(8,128)S(1)}, f32[16,128]{1,0:T(8,128)S(1)}, u32[]{:S(2)}, u32[]{:S(2)}) collective-permute-start(f32[16,128]{1,0:T(8,128)S(1)} %pad_maximum_fusion.5.back_refs_0_), channel_id=1, source_target_pairs={{0,24},{1,25},{2,26},{3,27},{4,28},{5,29},{6,30},{7,31},{8,16},{9,... | collective-permute-start | bytes 24584 | tf_op jit(solution)/shard_map/ppermute | solution.py:1197
  95.5 2.2 %collective-permute-start.35 = (f32[16,128]{1,0:T(8,128)S(1)}, f32[16,128]{1,0:T(8,128)S(1)}, u32[]{:S(2)}, u32[]{:S(2)}) collective-permute-start(f32[16,128]{1,0:T(8,128)S(1)} %pad_maximum_fusion.5.back_refs_0_), channel_id=1, source_target_pairs={{0,8},{1,9},{2,10},{3,11},{4,12},{5,13},{6,14},{7,15},{8,0},{9,1},... | collective-permute-start | bytes 24584 | tf_op jit(solution)/shard_map/ppermute | solution.py:1197
  97.7 1.8 %weight_out_term.1 = (bf16[2,656,128]{2,1,0:T(8,128)(2,1)S(1)}, bf16[2,656,128]{2,1,0:T(8,128)(2,1)S(1)}) custom-call(s32[4,8]{1,0:T(4,128)S(1)} %copy-done.2, bf16[784,256]{1,0:T(8,128)(2,1)S(1)} %get-tuple-element.156.weighted_ref, bf16[4,784,256]{2,1,0:T(8,128)(2,1)S(1)} %get-tuple-element.157.low_ref, f32[2,4,128]{2,1,0:T(4,128)S(1)} %get-tuple-element.154.gate_ref, ...), custom_call_target="tpu_custom_call" | custom-call | flops 411041792 | bytes 2695296 | tf_op jit(solution)/shard_map/weight_out_term/pallas_call | solution.py:192
  100.8 3.6 %back_mid.1 = (bf16[976,512]{1,0:T(8,128)(2,1)S(1)}, f32[896,256]{1,0:T(8,128)S(1)}, f32[4,128]{1,0:T(4,128)S(1)}, f32[8,512]{1,0:T(8,128)S(1)}, f32[2,256]{1,0:T(2,128)S(1)}) custom-call(s32[4,8]{1,0:T(4,128)S(1)} %copy-done.2, f32[16,128]{1,0:T(8,128)S(1)} %pad_maximum_fusion.5.back_refs_0_, f32[16,128]{1,0:T(8,128)S(1)} %collective-permute-done.35.back_refs_1_, ...), custom_call_target="tpu_custom_call" | custom-call | flops 1056964608 | bytes 7122048 | tf_op jit(solution)/shard_map/back_mid/pallas_call | solution.py:192
  104.6 1.0 collective-permute-done.40
  105.6 1.9 %collective-permute-start.43 = (f32[2,256]{1,0:T(2,128)S(1)}, f32[2,256]{1,0:T(2,128)S(1)}, u32[]{:S(2)}, u32[]{:S(2)}) collective-permute-start(f32[2,256]{1,0:T(2,128)S(1)} %add.44.back_refs_0_), channel_id=1, source_target_pairs={{0,24},{1,25},{2,26},{3,27},{4,28},{5,29},{6,30},{7,31},{8,16},{9,... | collective-permute-start | bytes 6152 | tf_op jit(solution)/shard_map/ppermute | solution.py:1197
  108.4 1.6 collective-permute-start.41
  110.0 2.4 %weight_mid_term.1 = (bf16[2,1152,128]{2,1,0:T(8,128)(2,1)S(1)}, bf16[2,1152,128]{2,1,0:T(8,128)(2,1)S(1)}) custom-call(s32[4,8]{1,0:T(4,128)S(1)} %copy-done.2, bf16[3,976,256]{2,1,0:T(8,128)(2,1)S(1)} %get-tuple-element.172.taps_ref, bf16[976,512]{1,0:T(8,128)(2,1)S(1)} %get-tuple-element.173.low_ref, f32[2,256]{1,0:T(2,128)S(1)} %get-tuple-element.131.affine_ref), custom_call_target="tpu_custom_call" | custom-call | flops 1056964608 | bytes 3680384 | tf_op jit(solution)/shard_map/weight_mid_term/pallas_call | solution.py:192
  112.5 1.9 %back_in.1 = (bf16[784,256]{1,0:T(8,128)(2,1)S(1)}, bf16[2,592,128]{2,1,0:T(8,128)(2,1)S(1)}, bf16[2,592,128]{2,1,0:T(8,128)(2,1)S(1)}) custom-call(s32[4,8]{1,0:T(4,128)S(1)} %copy-done.2, f32[896,256]{1,0:T(8,128)S(1)} %get-tuple-element.176.grad_ref, f32[896,256]{1,0:T(8,128)S(1)} %get-tuple-element.125.pre_ref, f32[6,256]{1,0:T(8,128)S(1)} %add.39.sums_refs_0_, ...), custom_call_target="tpu_custom_call" | custom-call | flops 411041792 | bytes 4702336 | tf_op jit(solution)/shard_map/back_in/pallas_call | solution.py:192
  115.0 1.9 %collective-permute-done.46.arrived_refs_1_ = bf16[2,592,128]{2,1,0:T(8,128)(2,1)S(1)} collective-permute-done((bf16[2,592,128]{2,1,0:T(8,128)(2,1)S(1)}, bf16[2,592,128]{2,1,0:T(8,128)(2,1)S(1)}, u32[]{:S(2)}, u32[]{:S(2)}) %collective-permute-start.46) | collective-permute-done | bytes 303136 | tf_op jit(solution)/shard_map/ppermute | solution.py:1197
  117.1 1.4 collective-permute-start.47
  119.5 7.3 %collective-permute-done.47.arrived_ref = bf16[1280,128]{1,0:T(8,128)(2,1)S(1)} collective-permute-done((bf16[1280,128]{1,0:T(8,128)(2,1)S(1)}, bf16[1280,128]{1,0:T(8,128)(2,1)S(1)}, u32[]{:S(2)}, u32[]{:S(2)}) %collective-permute-start.47) | collective-permute-done | bytes 327712 | tf_op jit(solution)/shard_map/ppermute | solution.py:1197
  129.4 3.7 %collective-permute-done.49.arrived_refs_1_ = bf16[640,128]{1,0:T(8,128)(2,1)S(1)} collective-permute-done((bf16[640,128]{1,0:T(8,128)(2,1)S(1)}, bf16[640,128]{1,0:T(8,128)(2,1)S(1)}, u32[]{:S(2)}, u32[]{:S(2)}) %collective-permute-start.49) | collective-permute-done | bytes 163872 | tf_op jit(solution)/shard_map/ppermute | solution.py:1197
  135.4 1.1 collective-permute-start.52
  136.5 1.2 collective-permute-start.53
  137.8 2.1 %collective-permute-start.54 = (bf16[304,128]{1,0:T(8,128)(2,1)S(1)}, bf16[304,128]{1,0:T(8,128)(2,1)S(1)}, u32[]{:S(2)}, u32[]{:S(2)}) collective-permute-start(bf16[304,128]{1,0:T(8,128)(2,1)S(1)} %get-tuple-element.205), channel_id=1, source_target_pairs={{0,24},{1,25},{2,26},{3,27},{4,28},{5,29},{6,30},{7,31},{8,16},{9,... | collective-permute-start | bytes 233480 | tf_op jit(solution)/shard_map/ppermute | solution.py:1197
  139.9 3.9 %finish_owned.1 = (bf16[4,784,256]{2,1,0:T(8,128)(2,1)}, bf16[4,784,256]{2,1,0:T(8,128)(2,1)S(1)}) custom-call(s32[4,8]{1,0:T(4,128)S(1)} %copy-done.2, bf16[816,256]{1,0:T(8,128)(2,1)S(1)} %collective-permute-done.29.near_ref, bf16[2,816,256]{2,1,0:T(8,128)(2,1)S(1)} %collective-permute-done.50.swapped_ref, ...), custom_call_target="tpu_custom_call" | custom-call | flops 411041792 | bytes 8618112 | tf_op jit(solution)/shard_map/finish_owned/pallas_call | solution.py:192
  143.8 1.1 collective-permute-done.54.arrived_refs_2_
  144.9 1.1 collective-permute-start.55
  146.0 1.7 %collective-permute-start.58 = (bf16[304,128]{1,0:T(8,128)(2,1)S(1)}, bf16[304,128]{1,0:T(8,128)(2,1)S(1)}, u32[]{:S(2)}, u32[]{:S(2)}) collective-permute-start(bf16[304,128]{1,0:T(8,128)(2,1)S(1)} %add_depth.1), channel_id=1, source_target_pairs={{0,24},{1,25},{2,26},{3,27},{4,28},{5,29},{6,30},{7,31},{8,16},{9,... | collective-permute-start | bytes 233480 | tf_op jit(solution)/shard_map/ppermute | solution.py:1197
  147.8 1.8 %collective-permute-start.57 = (bf16[304,128]{1,0:T(8,128)(2,1)S(1)}, bf16[304,128]{1,0:T(8,128)(2,1)S(1)}, u32[]{:S(2)}, u32[]{:S(2)}) collective-permute-start(bf16[304,128]{1,0:T(8,128)(2,1)S(1)} %add_depth.1), channel_id=1, source_target_pairs={{0,16},{1,17},{2,18},{3,19},{4,20},{5,21},{6,22},{7,23},{8,24},{9,... | collective-permute-start | bytes 233480 | tf_op jit(solution)/shard_map/ppermute | solution.py:1197
  150.5 2.6 %collective-permute-done.58 = bf16[304,128]{1,0:T(8,128)(2,1)S(1)} collective-permute-done((bf16[304,128]{1,0:T(8,128)(2,1)S(1)}, bf16[304,128]{1,0:T(8,128)(2,1)S(1)}, u32[]{:S(2)}, u32[]{:S(2)}) %collective-permute-start.58) | collective-permute-done | bytes 77856 | tf_op jit(solution)/shard_map/ppermute | solution.py:1197
  153.0 4.4 %collective-permute-done.57 = bf16[304,128]{1,0:T(8,128)(2,1)S(1)} collective-permute-done((bf16[304,128]{1,0:T(8,128)(2,1)S(1)}, bf16[304,128]{1,0:T(8,128)(2,1)S(1)}, u32[]{:S(2)}, u32[]{:S(2)}) %collective-permute-start.57) | collective-permute-done | bytes 77856 | tf_op jit(solution)/shard_map/ppermute | solution.py:1197
  158.0 1.1 collective-permute-done.59.low_refs_1_
  159.7 1.8 %grad_owned.1 = bf16[4,784,256]{2,1,0:T(8,128)(2,1)} custom-call(bf16[784,256]{1,0:T(8,128)(2,1)S(1)} %collective-permute-done.51.low_refs_0_, bf16[784,256]{1,0:T(8,128)(2,1)S(1)} %collective-permute-done.59.low_refs_1_, bf16[784,256]{1,0:T(8,128)(2,1)S(1)} %collective-permute-done.55.low_refs_2_, bf16[784,256]{1,0:T(8,128)(2,1)S(1)} %collective-permute-done.60.low_refs_3_, ...), custom_call_target="tpu_custom_call" | custom-call | flops 411041792 | bytes 5341184 | tf_op jit(solution)/shard_map/grad_owned/pallas_call | solution.py:192
  161.6 5.8 %collective-permute-done.61.term_refs_1_ = bf16[1216,128]{1,0:T(8,128)(2,1)S(1)} collective-permute-done((bf16[1216,128]{1,0:T(8,128)(2,1)S(1)}, bf16[1216,128]{1,0:T(8,128)(2,1)S(1)}, u32[]{:S(2)}, u32[]{:S(2)}) %collective-permute-start.61) | collective-permute-done | bytes 311328 | tf_op jit(solution)/shard_map/ppermute | solution.py:1197
  167.4 1.7 unpack.1
  (140 shorter events, 22.9 us)
Async XLA Ops:
  0.7 9.7 %collective-permute-start.5 = (bf16[64,1024]{1,0:T(8,128)(2,1)}, bf16[64,1024]{1,0:T(8,128)(2,1)S(1)}, u32[]{:S(2)}, u32[]{:S(2)}) collective-permute-start(bf16[64,1024]{1,0:T(8,128)(2,1)} %bitcast.37), channel_id=1, source_target_pairs={{0,2},{1,3},{2,0},{3,1},{4,6},{5,7},{6,4},{7,5},{8,10},{9,11},{10,... | collective-permute-start | bytes 393224 | tf_op jit(solution)/shard_map/ppermute | solution.py:1197
  3.7 5.3 %collective-permute-start = (bf16[64,1024]{1,0:T(8,128)(2,1)}, bf16[64,1024]{1,0:T(8,128)(2,1)S(1)}, u32[]{:S(2)}, u32[]{:S(2)}) collective-permute-start(bf16[64,1024]{1,0:T(8,128)(2,1)} %bitcast.38), channel_id=1, source_target_pairs={{0,1},{1,0},{2,3},{3,2},{4,5},{5,4},{6,7},{7,6},{8,9},{9,8},{10,11... | collective-permute-start | bytes 393224 | tf_op jit(solution)/shard_map/ppermute | solution.py:1197
  6.0 20.8 %copy-start.2 = (s32[4,8]{1,0:T(4,128)S(1)}, s32[4,8]{1,0:T(4,128)}, u32[]{:S(2)}) copy-start(s32[4,8]{1,0:T(4,128)} %counts_ref.33) | copy-start | bytes 388
  6.0 20.8 %copy-start.5 = (bf16[1024,64]{0,1:T(8,128)(2,1)S(1)}, bf16[1024,64]{0,1:T(8,128)(2,1)}, u32[]{:S(2)}) copy-start(bf16[1024,64]{0,1:T(8,128)(2,1)} %param.19) | copy-start | bytes 393220
  6.0 19.3 %collective-permute-start.4 = (bf16[784,256]{1,0:T(8,128)(2,1)}, bf16[784,256]{1,0:T(8,128)(2,1)S(1)}, u32[]{:S(2)}, u32[]{:S(2)}) collective-permute-start(bf16[784,256]{1,0:T(8,128)(2,1)} %get-tuple-element.234), channel_id=1, source_target_pairs={{0,6},{1,2},{2,4},{3,0},{4,7},{5,3},{6,5},{7,1},{8,14},{9,10},{10,... | collective-permute-start | bytes 1204232 | tf_op jit(solution)/shard_map/ppermute | solution.py:1197
  7.4 19.4 %collective-permute-start.3 = (bf16[784,256]{1,0:T(8,128)(2,1)}, bf16[784,256]{1,0:T(8,128)(2,1)S(1)}, u32[]{:S(2)}, u32[]{:S(2)}) collective-permute-start(bf16[784,256]{1,0:T(8,128)(2,1)} %get-tuple-element.235), channel_id=1, source_target_pairs={{0,2},{1,6},{2,0},{3,4},{4,3},{5,7},{6,1},{7,5},{8,10},{9,14},{10,... | collective-permute-start | bytes 1204232 | tf_op jit(solution)/shard_map/ppermute | solution.py:1197
  9.1 17.8 %collective-permute-start.2 = (bf16[784,256]{1,0:T(8,128)(2,1)S(1)}, bf16[784,256]{1,0:T(8,128)(2,1)S(1)}, u32[]{:S(2)}, u32[]{:S(2)}) collective-permute-start(bf16[784,256]{1,0:T(8,128)(2,1)S(1)} %get-tuple-element.236), channel_id=1, source_target_pairs={{0,4},{1,0},{2,6},{3,2},{4,5},{5,1},{6,7},{7,3},{8,12},{9,8},{10,1... | collective-permute-start | bytes 1204232 | tf_op jit(solution)/shard_map/ppermute | solution.py:1197
  9.3 17.5 %collective-permute-start.1 = (bf16[784,256]{1,0:T(8,128)(2,1)S(1)}, bf16[784,256]{1,0:T(8,128)(2,1)S(1)}, u32[]{:S(2)}, u32[]{:S(2)}) collective-permute-start(bf16[784,256]{1,0:T(8,128)(2,1)S(1)} %get-tuple-element.237), channel_id=1, source_target_pairs={{0,0},{1,4},{2,2},{3,6},{4,1},{5,5},{6,3},{7,7},{8,8},{9,12},{10,1... | collective-permute-start | bytes 1204232 | tf_op jit(solution)/shard_map/ppermute | solution.py:1197
  10.4 2.5 %collective-permute-start.6 = (bf16[64,1024]{1,0:T(8,128)(2,1)S(1)}, bf16[64,1024]{1,0:T(8,128)(2,1)S(1)}, u32[]{:S(2)}, u32[]{:S(2)}) collective-permute-start(bf16[64,1024]{1,0:T(8,128)(2,1)S(1)} %collective-permute-done.5.a2), channel_id=1, source_target_pairs={{0,1},{1,0},{2,3},{3,2},{4,5},{5,4},{6,7},{7,6},{8,9},{9,8},{10,11... | collective-permute-start | bytes 393224 | tf_op jit(solution)/shard_map/ppermute | solution.py:1197
  12.9 15.8 %collective-permute-start.7 = (bf16[1872,128]{1,0:T(8,128)(2,1)S(1)}, bf16[1872,128]{1,0:T(8,128)(2,1)S(1)}, u32[]{:S(2)}, u32[]{:S(2)}) collective-permute-start(bf16[1872,128]{1,0:T(8,128)(2,1)S(1)} %pack.1.b0), channel_id=1, source_target_pairs={{0,1},{1,0},{2,3},{3,2},{4,5},{5,4},{6,7},{7,6},{8,9},{9,8},{10,11... | collective-permute-start | bytes 1437704 | tf_op jit(solution)/shard_map/ppermute | solution.py:1197
  26.8 12.9 %collective-permute-start.12 = (bf16[1872,128]{1,0:T(8,128)(2,1)S(1)}, bf16[1872,128]{1,0:T(8,128)(2,1)S(1)}, u32[]{:S(2)}, u32[]{:S(2)}) collective-permute-start(bf16[1872,128]{1,0:T(8,128)(2,1)S(1)} %pack.1.b0), channel_id=1, source_target_pairs={{0,2},{1,3},{2,0},{3,1},{4,6},{5,7},{6,4},{7,5},{8,10},{9,11},{10,... | collective-permute-start | bytes 1437704 | tf_op jit(solution)/shard_map/ppermute | solution.py:1197
  28.7 1.2 collective-permute-start.8
  29.9 5.4 %collective-permute-start.11 = (f32[6,256]{1,0:T(8,128)S(1)}, f32[6,256]{1,0:T(8,128)S(1)}, u32[]{:S(2)}, u32[]{:S(2)}) collective-permute-start(f32[6,256]{1,0:T(8,128)S(1)} %add.39.sums_refs_0_), channel_id=1, source_target_pairs={{0,24},{1,25},{2,26},{3,27},{4,28},{5,29},{6,30},{7,31},{8,16},{9,... | collective-permute-start | bytes 18440 | tf_op jit(solution)/shard_map/ppermute | solution.py:1197
  33.6 4.5 %collective-permute-start.10 = (f32[6,256]{1,0:T(8,128)S(1)}, f32[6,256]{1,0:T(8,128)S(1)}, u32[]{:S(2)}, u32[]{:S(2)}) collective-permute-start(f32[6,256]{1,0:T(8,128)S(1)} %add.39.sums_refs_0_), channel_id=1, source_target_pairs={{0,16},{1,17},{2,18},{3,19},{4,20},{5,21},{6,22},{7,23},{8,24},{9,... | collective-permute-start | bytes 18440 | tf_op jit(solution)/shard_map/ppermute | solution.py:1197
  33.6 4.5 %collective-permute-start.9 = (f32[6,256]{1,0:T(8,128)S(1)}, f32[6,256]{1,0:T(8,128)S(1)}, u32[]{:S(2)}, u32[]{:S(2)}) collective-permute-start(f32[6,256]{1,0:T(8,128)S(1)} %add.39.sums_refs_0_), channel_id=1, source_target_pairs={{0,8},{1,9},{2,10},{3,11},{4,12},{5,13},{6,14},{7,15},{8,0},{9,1},... | collective-permute-start | bytes 18440 | tf_op jit(solution)/shard_map/ppermute | solution.py:1197
  34.4 20.5 %collective-permute-start.26 = (bf16[2,784,256]{2,1,0:T(8,128)(2,1)S(1)}, bf16[2,784,256]{2,1,0:T(8,128)(2,1)S(1)}, u32[]{:S(2)}, u32[]{:S(2)}) collective-permute-start(bf16[2,784,256]{2,1,0:T(8,128)(2,1)S(1)} %pad_maximum_fusion.2), channel_id=1, source_target_pairs={{0,0},{1,4},{2,2},{3,6},{4,1},{5,5},{6,3},{7,7},{8,8},{9,12},{10,1... | collective-permute-start | bytes 2408456 | tf_op jit(solution)/shard_map/ppermute | solution.py:1197
  38.2 17.5 %collective-permute-start.27 = (bf16[2,784,256]{2,1,0:T(8,128)(2,1)S(1)}, bf16[2,784,256]{2,1,0:T(8,128)(2,1)S(1)}, u32[]{:S(2)}, u32[]{:S(2)}) collective-permute-start(bf16[2,784,256]{2,1,0:T(8,128)(2,1)S(1)} %pad_maximum_fusion.1), channel_id=1, source_target_pairs={{0,4},{1,0},{2,6},{3,2},{4,5},{5,1},{6,7},{7,3},{8,12},{9,8},{10,1... | collective-permute-start | bytes 2408456 | tf_op jit(solution)/shard_map/ppermute | solution.py:1197
  39.7 1.8 %collective-permute-start.13 = (bf16[1872,128]{1,0:T(8,128)(2,1)S(1)}, bf16[1872,128]{1,0:T(8,128)(2,1)S(1)}, u32[]{:S(2)}, u32[]{:S(2)}) collective-permute-start(bf16[1872,128]{1,0:T(8,128)(2,1)S(1)} %collective-permute-done.12.b2), channel_id=1, source_target_pairs={{0,1},{1,0},{2,3},{3,2},{4,5},{5,4},{6,7},{7,6},{8,9},{9,8},{10,11... | collective-permute-start | bytes 1437704 | tf_op jit(solution)/shard_map/ppermute | solution.py:1197
  44.8 1.2 collective-permute-start.14
  46.0 5.4 %collective-permute-start.17 = (f32[2,512]{1,0:T(2,128)S(1)}, f32[2,512]{1,0:T(2,128)S(1)}, u32[]{:S(2)}, u32[]{:S(2)}) collective-permute-start(f32[2,512]{1,0:T(2,128)S(1)} %add.40.sums_refs_0_.mid_sums_refs_0_), channel_id=1, source_target_pairs={{0,24},{1,25},{2,26},{3,27},{4,28},{5,29},{6,30},{7,31},{8,16},{9,... | collective-permute-start | bytes 12296 | tf_op jit(solution)/shard_map/ppermute | solution.py:1197
  48.6 4.5 %collective-permute-start.16 = (f32[2,512]{1,0:T(2,128)S(1)}, f32[2,512]{1,0:T(2,128)S(1)}, u32[]{:S(2)}, u32[]{:S(2)}) collective-permute-start(f32[2,512]{1,0:T(2,128)S(1)} %add.40.sums_refs_0_.mid_sums_refs_0_), channel_id=1, source_target_pairs={{0,16},{1,17},{2,18},{3,19},{4,20},{5,21},{6,22},{7,23},{8,24},{9,... | collective-permute-start | bytes 12296 | tf_op jit(solution)/shard_map/ppermute | solution.py:1197
  48.6 4.5 %collective-permute-start.15 = (f32[2,512]{1,0:T(2,128)S(1)}, f32[2,512]{1,0:T(2,128)S(1)}, u32[]{:S(2)}, u32[]{:S(2)}) collective-permute-start(f32[2,512]{1,0:T(2,128)S(1)} %add.40.sums_refs_0_.mid_sums_refs_0_), channel_id=1, source_target_pairs={{0,8},{1,9},{2,10},{3,11},{4,12},{5,13},{6,14},{7,15},{8,0},{9,1},... | collective-permute-start | bytes 12296 | tf_op jit(solution)/shard_map/ppermute | solution.py:1197
  55.8 21.2 %collective-permute-start.28 = (bf16[2,784,256]{2,1,0:T(8,128)(2,1)S(1)}, bf16[2,784,256]{2,1,0:T(8,128)(2,1)S(1)}, u32[]{:S(2)}, u32[]{:S(2)}) collective-permute-start(bf16[2,784,256]{2,1,0:T(8,128)(2,1)S(1)} %pad_maximum_fusion.3), channel_id=1, source_target_pairs={{0,2},{1,3},{2,0},{3,1},{4,6},{5,7},{6,4},{7,5},{8,10},{9,11},{10,... | collective-permute-start | bytes 2408456 | tf_op jit(solution)/shard_map/ppermute | solution.py:1197
  57.3 1.4 collective-permute-start.18
  58.7 5.9 %collective-permute-start.21 = (f32[80,128]{1,0:T(8,128)S(1)}, f32[80,128]{1,0:T(8,128)S(1)}, u32[]{:S(2)}, u32[]{:S(2)}) collective-permute-start(f32[80,128]{1,0:T(8,128)S(1)} %constant_dynamic-update-slice_fusion.gathered_refs_0_), channel_id=1, source_target_pairs={{0,24},{1,25},{2,26},{3,27},{4,28},{5,29},{6,30},{7,31},{8,16},{9,... | collective-permute-start | bytes 122888 | tf_op jit(solution)/shard_map/ppermute | solution.py:1197
  62.3 4.9 %collective-permute-start.20 = (f32[80,128]{1,0:T(8,128)S(1)}, f32[80,128]{1,0:T(8,128)S(1)}, u32[]{:S(2)}, u32[]{:S(2)}) collective-permute-start(f32[80,128]{1,0:T(8,128)S(1)} %constant_dynamic-update-slice_fusion.gathered_refs_0_), channel_id=1, source_target_pairs={{0,16},{1,17},{2,18},{3,19},{4,20},{5,21},{6,22},{7,23},{8,24},{9,... | collective-permute-start | bytes 122888 | tf_op jit(solution)/shard_map/ppermute | solution.py:1197
  62.3 4.9 %collective-permute-start.19 = (f32[80,128]{1,0:T(8,128)S(1)}, f32[80,128]{1,0:T(8,128)S(1)}, u32[]{:S(2)}, u32[]{:S(2)}) collective-permute-start(f32[80,128]{1,0:T(8,128)S(1)} %constant_dynamic-update-slice_fusion.gathered_refs_0_), channel_id=1, source_target_pairs={{0,8},{1,9},{2,10},{3,11},{4,12},{5,13},{6,14},{7,15},{8,0},{9,1},... | collective-permute-start | bytes 122888 | tf_op jit(solution)/shard_map/ppermute | solution.py:1197
  69.2 1.2 collective-permute-start.22
  70.4 5.6 %collective-permute-start.25 = (f32[8,256]{1,0:T(8,128)S(1)}, f32[8,256]{1,0:T(8,128)S(1)}, u32[]{:S(2)}, u32[]{:S(2)}) collective-permute-start(f32[8,256]{1,0:T(8,128)S(1)} %add.41.sums_refs_0_), channel_id=1, source_target_pairs={{0,24},{1,25},{2,26},{3,27},{4,28},{5,29},{6,30},{7,31},{8,16},{9,... | collective-permute-start | bytes 24584 | tf_op jit(solution)/shard_map/ppermute | solution.py:1197
  72.4 4.6 %collective-permute-start.24 = (f32[8,256]{1,0:T(8,128)S(1)}, f32[8,256]{1,0:T(8,128)S(1)}, u32[]{:S(2)}, u32[]{:S(2)}) collective-permute-start(f32[8,256]{1,0:T(8,128)S(1)} %add.41.sums_refs_0_), channel_id=1, source_target_pairs={{0,16},{1,17},{2,18},{3,19},{4,20},{5,21},{6,22},{7,23},{8,24},{9,... | collective-permute-start | bytes 24584 | tf_op jit(solution)/shard_map/ppermute | solution.py:1197
  72.6 4.4 %collective-permute-start.23 = (f32[8,256]{1,0:T(8,128)S(1)}, f32[8,256]{1,0:T(8,128)S(1)}, u32[]{:S(2)}, u32[]{:S(2)}) collective-permute-start(f32[8,256]{1,0:T(8,128)S(1)} %add.41.sums_refs_0_), channel_id=1, source_target_pairs={{0,8},{1,9},{2,10},{3,11},{4,12},{5,13},{6,14},{7,15},{8,0},{9,1},... | collective-permute-start | bytes 24584 | tf_op jit(solution)/shard_map/ppermute | solution.py:1197
  79.6 1.2 collective-permute-start.30
  80.8 5.5 %collective-permute-start.33 = (f32[8,256]{1,0:T(8,128)S(1)}, f32[8,256]{1,0:T(8,128)S(1)}, u32[]{:S(2)}, u32[]{:S(2)}) collective-permute-start(f32[8,256]{1,0:T(8,128)S(1)} %add.42.back_refs_0_.out_back_refs_0_), channel_id=1, source_target_pairs={{0,24},{1,25},{2,26},{3,27},{4,28},{5,29},{6,30},{7,31},{8,16},{9,... | collective-permute-start | bytes 24584 | tf_op jit(solution)/shard_map/ppermute | solution.py:1197
  84.0 4.5 %collective-permute-start.32 = (f32[8,256]{1,0:T(8,128)S(1)}, f32[8,256]{1,0:T(8,128)S(1)}, u32[]{:S(2)}, u32[]{:S(2)}) collective-permute-start(f32[8,256]{1,0:T(8,128)S(1)} %add.42.back_refs_0_.out_back_refs_0_), channel_id=1, source_target_pairs={{0,16},{1,17},{2,18},{3,19},{4,20},{5,21},{6,22},{7,23},{8,24},{9,... | collective-permute-start | bytes 24584 | tf_op jit(solution)/shard_map/ppermute | solution.py:1197
  84.0 4.5 %collective-permute-start.31 = (f32[8,256]{1,0:T(8,128)S(1)}, f32[8,256]{1,0:T(8,128)S(1)}, u32[]{:S(2)}, u32[]{:S(2)}) collective-permute-start(f32[8,256]{1,0:T(8,128)S(1)} %add.42.back_refs_0_.out_back_refs_0_), channel_id=1, source_target_pairs={{0,8},{1,9},{2,10},{3,11},{4,12},{5,13},{6,14},{7,15},{8,0},{9,1},... | collective-permute-start | bytes 24584 | tf_op jit(solution)/shard_map/ppermute | solution.py:1197
  85.2 14.8 %collective-permute-start.29 = (bf16[816,256]{1,0:T(8,128)(2,1)S(1)}, bf16[816,256]{1,0:T(8,128)(2,1)S(1)}, u32[]{:S(2)}, u32[]{:S(2)}) collective-permute-start(bf16[816,256]{1,0:T(8,128)(2,1)S(1)} %get-tuple-element.150), channel_id=1, source_target_pairs={{0,0},{1,4},{2,2},{3,6},{4,1},{5,5},{6,3},{7,7},{8,8},{9,12},{10,1... | collective-permute-start | bytes 1253384 | tf_op jit(solution)/shard_map/ppermute | solution.py:1197
  91.3 1.9 %collective-permute-start.34 = (f32[12,128]{1,0:T(8,128)S(1)}, f32[12,128]{1,0:T(8,128)S(1)}, u32[]{:S(2)}, u32[]{:S(2)}) collective-permute-start(f32[12,128]{1,0:T(8,128)S(1)} %get-tuple-element.155), channel_id=1, source_target_pairs={{0,1},{1,0},{2,3},{3,2},{4,5},{5,4},{6,7},{7,6},{8,9},{9,8},{10,11... | collective-permute-start | bytes 18440 | tf_op jit(solution)/shard_map/ppermute | solution.py:1197
  93.2 6.3 %collective-permute-start.37 = (f32[16,128]{1,0:T(8,128)S(1)}, f32[16,128]{1,0:T(8,128)S(1)}, u32[]{:S(2)}, u32[]{:S(2)}) collective-permute-start(f32[16,128]{1,0:T(8,128)S(1)} %pad_maximum_fusion.5.back_refs_0_), channel_id=1, source_target_pairs={{0,24},{1,25},{2,26},{3,27},{4,28},{5,29},{6,30},{7,31},{8,16},{9,... | collective-permute-start | bytes 24584 | tf_op jit(solution)/shard_map/ppermute | solution.py:1197
  95.5 4.5 %collective-permute-start.36 = (f32[16,128]{1,0:T(8,128)S(1)}, f32[16,128]{1,0:T(8,128)S(1)}, u32[]{:S(2)}, u32[]{:S(2)}) collective-permute-start(f32[16,128]{1,0:T(8,128)S(1)} %pad_maximum_fusion.5.back_refs_0_), channel_id=1, source_target_pairs={{0,16},{1,17},{2,18},{3,19},{4,20},{5,21},{6,22},{7,23},{8,24},{9,... | collective-permute-start | bytes 24584 | tf_op jit(solution)/shard_map/ppermute | solution.py:1197
  95.5 4.5 %collective-permute-start.35 = (f32[16,128]{1,0:T(8,128)S(1)}, f32[16,128]{1,0:T(8,128)S(1)}, u32[]{:S(2)}, u32[]{:S(2)}) collective-permute-start(f32[16,128]{1,0:T(8,128)S(1)} %pad_maximum_fusion.5.back_refs_0_), channel_id=1, source_target_pairs={{0,8},{1,9},{2,10},{3,11},{4,12},{5,13},{6,14},{7,15},{8,0},{9,1},... | collective-permute-start | bytes 24584 | tf_op jit(solution)/shard_map/ppermute | solution.py:1197
  100.1 4.3 %collective-permute-start.39 = (bf16[2,656,128]{2,1,0:T(8,128)(2,1)S(1)}, bf16[2,656,128]{2,1,0:T(8,128)(2,1)S(1)}, u32[]{:S(2)}, u32[]{:S(2)}) collective-permute-start(bf16[2,656,128]{2,1,0:T(8,128)(2,1)S(1)} %get-tuple-element.170), channel_id=1, source_target_pairs={{0,1},{1,0},{2,3},{3,2},{4,5},{5,4},{6,7},{7,6},{8,9},{9,8},{10,11... | collective-permute-start | bytes 1007624 | tf_op jit(solution)/shard_map/ppermute | solution.py:1197
  100.1 12.4 %collective-permute-start.38 = (bf16[816,256]{1,0:T(8,128)(2,1)S(1)}, bf16[816,256]{1,0:T(8,128)(2,1)S(1)}, u32[]{:S(2)}, u32[]{:S(2)}) collective-permute-start(bf16[816,256]{1,0:T(8,128)(2,1)S(1)} %collective-permute-done.29.near_ref), channel_id=1, source_target_pairs={{0,2},{1,3},{2,0},{3,1},{4,6},{5,7},{6,4},{7,5},{8,10},{9,11},{10,... | collective-permute-start | bytes 1253384 | tf_op jit(solution)/shard_map/ppermute | solution.py:1197
  104.4 1.2 collective-permute-start.40
  105.6 6.8 %collective-permute-start.43 = (f32[2,256]{1,0:T(2,128)S(1)}, f32[2,256]{1,0:T(2,128)S(1)}, u32[]{:S(2)}, u32[]{:S(2)}) collective-permute-start(f32[2,256]{1,0:T(2,128)S(1)} %add.44.back_refs_0_), channel_id=1, source_target_pairs={{0,24},{1,25},{2,26},{3,27},{4,28},{5,29},{6,30},{7,31},{8,16},{9,... | collective-permute-start | bytes 6152 | tf_op jit(solution)/shard_map/ppermute | solution.py:1197
  107.5 5.0 %collective-permute-start.42 = (f32[2,256]{1,0:T(2,128)S(1)}, f32[2,256]{1,0:T(2,128)S(1)}, u32[]{:S(2)}, u32[]{:S(2)}) collective-permute-start(f32[2,256]{1,0:T(2,128)S(1)} %add.44.back_refs_0_), channel_id=1, source_target_pairs={{0,16},{1,17},{2,18},{3,19},{4,20},{5,21},{6,22},{7,23},{8,24},{9,... | collective-permute-start | bytes 6152 | tf_op jit(solution)/shard_map/ppermute | solution.py:1197
  108.4 4.1 %collective-permute-start.41 = (f32[2,256]{1,0:T(2,128)S(1)}, f32[2,256]{1,0:T(2,128)S(1)}, u32[]{:S(2)}, u32[]{:S(2)}) collective-permute-start(f32[2,256]{1,0:T(2,128)S(1)} %add.44.back_refs_0_), channel_id=1, source_target_pairs={{0,8},{1,9},{2,10},{3,11},{4,12},{5,13},{6,14},{7,15},{8,0},{9,1},... | collective-permute-start | bytes 6152 | tf_op jit(solution)/shard_map/ppermute | solution.py:1197
  114.4 4.1 %collective-permute-start.44 = (bf16[2,1152,128]{2,1,0:T(8,128)(2,1)S(1)}, bf16[2,1152,128]{2,1,0:T(8,128)(2,1)S(1)}, u32[]{:S(2)}, u32[]{:S(2)}) collective-permute-start(bf16[2,1152,128]{2,1,0:T(8,128)(2,1)S(1)} %get-tuple-element.185), channel_id=1, source_target_pairs={{0,1},{1,0},{2,3},{3,2},{4,5},{5,4},{6,7},{7,6},{8,9},{9,8},{10,11... | collective-permute-start | bytes 1769480 | tf_op jit(solution)/shard_map/ppermute | solution.py:1197
  114.5 2.4 %collective-permute-start.46 = (bf16[2,592,128]{2,1,0:T(8,128)(2,1)S(1)}, bf16[2,592,128]{2,1,0:T(8,128)(2,1)S(1)}, u32[]{:S(2)}, u32[]{:S(2)}) collective-permute-start(bf16[2,592,128]{2,1,0:T(8,128)(2,1)S(1)} %get-tuple-element.190), channel_id=1, source_target_pairs={{0,1},{1,0},{2,3},{3,2},{4,5},{5,4},{6,7},{7,6},{8,9},{9,8},{10,11... | collective-permute-start | bytes 909320 | tf_op jit(solution)/shard_map/ppermute | solution.py:1197
  117.1 9.8 %collective-permute-start.47 = (bf16[1280,128]{1,0:T(8,128)(2,1)S(1)}, bf16[1280,128]{1,0:T(8,128)(2,1)S(1)}, u32[]{:S(2)}, u32[]{:S(2)}) collective-permute-start(bf16[1280,128]{1,0:T(8,128)(2,1)S(1)} %get-tuple-element.192), channel_id=1, source_target_pairs={{0,2},{1,3},{2,0},{3,1},{4,6},{5,7},{6,4},{7,5},{8,10},{9,11},{10,... | collective-permute-start | bytes 983048 | tf_op jit(solution)/shard_map/ppermute | solution.py:1197
  119.2 9.2 %collective-permute-start.45 = (bf16[2,576,128]{2,1,0:T(8,128)(2,1)S(1)}, bf16[2,576,128]{2,1,0:T(8,128)(2,1)S(1)}, u32[]{:S(2)}, u32[]{:S(2)}) collective-permute-start(bf16[2,576,128]{2,1,0:T(8,128)(2,1)S(1)} %get-tuple-element.187), channel_id=1, source_target_pairs={{0,4},{1,5},{2,6},{3,7},{4,0},{5,1},{6,2},{7,3},{8,12},{9,13},{10,... | collective-permute-start | bytes 884744 | tf_op jit(solution)/shard_map/ppermute | solution.py:1197
  127.5 5.5 %collective-permute-start.49 = (bf16[640,128]{1,0:T(8,128)(2,1)S(1)}, bf16[640,128]{1,0:T(8,128)(2,1)S(1)}, u32[]{:S(2)}, u32[]{:S(2)}) collective-permute-start(bf16[640,128]{1,0:T(8,128)(2,1)S(1)} %get-tuple-element.196), channel_id=1, source_target_pairs={{0,4},{1,5},{2,6},{3,7},{4,0},{5,1},{6,2},{7,3},{8,12},{9,13},{10,... | collective-permute-start | bytes 491528 | tf_op jit(solution)/shard_map/ppermute | solution.py:1197
  128.5 5.2 %collective-permute-start.48 = (bf16[576,128]{1,0:T(8,128)(2,1)S(1)}, bf16[576,128]{1,0:T(8,128)(2,1)S(1)}, u32[]{:S(2)}, u32[]{:S(2)}) collective-permute-start(bf16[576,128]{1,0:T(8,128)(2,1)S(1)} %get-tuple-element.195), channel_id=1, source_target_pairs={{0,2},{1,3},{2,0},{3,1},{4,6},{5,7},{6,4},{7,5},{8,10},{9,11},{10,... | collective-permute-start | bytes 442376 | tf_op jit(solution)/shard_map/ppermute | solution.py:1197
  134.4 5.5 %collective-permute-start.50 = (bf16[2,816,256]{2,1,0:T(8,128)(2,1)S(1)}, bf16[2,816,256]{2,1,0:T(8,128)(2,1)S(1)}, u32[]{:S(2)}, u32[]{:S(2)}) collective-permute-start(bf16[2,816,256]{2,1,0:T(8,128)(2,1)S(1)} %pad_maximum_fusion), channel_id=1, source_target_pairs={{0,1},{1,0},{2,3},{3,2},{4,5},{5,4},{6,7},{7,6},{8,9},{9,8},{10,11... | collective-permute-start | bytes 2506760 | tf_op jit(solution)/shard_map/ppermute | solution.py:1197
  134.5 10.4 %collective-permute-start.51 = (bf16[784,256]{1,0:T(8,128)(2,1)S(1)}, bf16[784,256]{1,0:T(8,128)(2,1)S(1)}, u32[]{:S(2)}, u32[]{:S(2)}) collective-permute-start(bf16[784,256]{1,0:T(8,128)(2,1)S(1)} %get-tuple-element.202), channel_id=1, source_target_pairs={{0,0},{1,4},{2,2},{3,6},{4,1},{5,5},{6,3},{7,7},{8,8},{9,12},{10,1... | collective-permute-start | bytes 1204232 | tf_op jit(solution)/shard_map/ppermute | solution.py:1197
  135.4 8.4 %collective-permute-start.52 = (bf16[304,128]{1,0:T(8,128)(2,1)S(1)}, bf16[304,128]{1,0:T(8,128)(2,1)S(1)}, u32[]{:S(2)}, u32[]{:S(2)}) collective-permute-start(bf16[304,128]{1,0:T(8,128)(2,1)S(1)} %get-tuple-element.203), channel_id=1, source_target_pairs={{0,8},{1,9},{2,10},{3,11},{4,12},{5,13},{6,14},{7,15},{8,0},{9,1},... | collective-permute-start | bytes 233480 | tf_op jit(solution)/shard_map/ppermute | solution.py:1197
  136.5 7.3 %collective-permute-start.53 = (bf16[304,128]{1,0:T(8,128)(2,1)S(1)}, bf16[304,128]{1,0:T(8,128)(2,1)S(1)}, u32[]{:S(2)}, u32[]{:S(2)}) collective-permute-start(bf16[304,128]{1,0:T(8,128)(2,1)S(1)} %get-tuple-element.204), channel_id=1, source_target_pairs={{0,16},{1,17},{2,18},{3,19},{4,20},{5,21},{6,22},{7,23},{8,24},{9,... | collective-permute-start | bytes 233480 | tf_op jit(solution)/shard_map/ppermute | solution.py:1197
  137.8 7.1 %collective-permute-start.54 = (bf16[304,128]{1,0:T(8,128)(2,1)S(1)}, bf16[304,128]{1,0:T(8,128)(2,1)S(1)}, u32[]{:S(2)}, u32[]{:S(2)}) collective-permute-start(bf16[304,128]{1,0:T(8,128)(2,1)S(1)} %get-tuple-element.205), channel_id=1, source_target_pairs={{0,24},{1,25},{2,26},{3,27},{4,28},{5,29},{6,30},{7,31},{8,16},{9,... | collective-permute-start | bytes 233480 | tf_op jit(solution)/shard_map/ppermute | solution.py:1197
  144.9 12.5 %collective-permute-start.55 = (bf16[784,256]{1,0:T(8,128)(2,1)S(1)}, bf16[784,256]{1,0:T(8,128)(2,1)S(1)}, u32[]{:S(2)}, u32[]{:S(2)}) collective-permute-start(bf16[784,256]{1,0:T(8,128)(2,1)S(1)} %collective-permute-done.51.low_refs_0_), channel_id=1, source_target_pairs={{0,2},{1,3},{2,0},{3,1},{4,6},{5,7},{6,4},{7,5},{8,10},{9,11},{10,... | collective-permute-start | bytes 1204232 | tf_op jit(solution)/shard_map/ppermute | solution.py:1197
  146.0 7.0 %collective-permute-start.58 = (bf16[304,128]{1,0:T(8,128)(2,1)S(1)}, bf16[304,128]{1,0:T(8,128)(2,1)S(1)}, u32[]{:S(2)}, u32[]{:S(2)}) collective-permute-start(bf16[304,128]{1,0:T(8,128)(2,1)S(1)} %add_depth.1), channel_id=1, source_target_pairs={{0,24},{1,25},{2,26},{3,27},{4,28},{5,29},{6,30},{7,31},{8,16},{9,... | collective-permute-start | bytes 233480 | tf_op jit(solution)/shard_map/ppermute | solution.py:1197
  147.8 9.7 %collective-permute-start.57 = (bf16[304,128]{1,0:T(8,128)(2,1)S(1)}, bf16[304,128]{1,0:T(8,128)(2,1)S(1)}, u32[]{:S(2)}, u32[]{:S(2)}) collective-permute-start(bf16[304,128]{1,0:T(8,128)(2,1)S(1)} %add_depth.1), channel_id=1, source_target_pairs={{0,16},{1,17},{2,18},{3,19},{4,20},{5,21},{6,22},{7,23},{8,24},{9,... | collective-permute-start | bytes 233480 | tf_op jit(solution)/shard_map/ppermute | solution.py:1197
  149.6 7.9 %collective-permute-start.56 = (bf16[304,128]{1,0:T(8,128)(2,1)S(1)}, bf16[304,128]{1,0:T(8,128)(2,1)S(1)}, u32[]{:S(2)}, u32[]{:S(2)}) collective-permute-start(bf16[304,128]{1,0:T(8,128)(2,1)S(1)} %add_depth.1), channel_id=1, source_target_pairs={{0,8},{1,9},{2,10},{3,11},{4,12},{5,13},{6,14},{7,15},{8,0},{9,1},... | collective-permute-start | bytes 233480 | tf_op jit(solution)/shard_map/ppermute | solution.py:1197
  157.4 1.7 %collective-permute-start.59 = (bf16[784,256]{1,0:T(8,128)(2,1)S(1)}, bf16[784,256]{1,0:T(8,128)(2,1)S(1)}, u32[]{:S(2)}, u32[]{:S(2)}) collective-permute-start(bf16[784,256]{1,0:T(8,128)(2,1)S(1)} %collective-permute-done.51.low_refs_0_), channel_id=1, source_target_pairs={{0,1},{1,0},{2,3},{3,2},{4,5},{5,4},{6,7},{7,6},{8,9},{9,8},{10,11... | collective-permute-start | bytes 1204232 | tf_op jit(solution)/shard_map/ppermute | solution.py:1197
  157.4 2.3 %collective-permute-start.60 = (bf16[784,256]{1,0:T(8,128)(2,1)S(1)}, bf16[784,256]{1,0:T(8,128)(2,1)S(1)}, u32[]{:S(2)}, u32[]{:S(2)}) collective-permute-start(bf16[784,256]{1,0:T(8,128)(2,1)S(1)} %collective-permute-done.55.low_refs_2_), channel_id=1, source_target_pairs={{0,1},{1,0},{2,3},{3,2},{4,5},{5,4},{6,7},{7,6},{8,9},{9,8},{10,11... | collective-permute-start | bytes 1204232 | tf_op jit(solution)/shard_map/ppermute | solution.py:1197
  158.0 9.4 %collective-permute-start.61 = (bf16[1216,128]{1,0:T(8,128)(2,1)S(1)}, bf16[1216,128]{1,0:T(8,128)(2,1)S(1)}, u32[]{:S(2)}, u32[]{:S(2)}) collective-permute-start(bf16[1216,128]{1,0:T(8,128)(2,1)S(1)} %pad_maximum_fusion.4.term_refs_0_), channel_id=1, source_target_pairs={{0,4},{1,5},{2,6},{3,7},{4,0},{5,1},{6,2},{7,3},{8,12},{9,13},{10,... | collective-permute-start | bytes 933896 | tf_op jit(solution)/shard_map/ppermute | solution.py:1197
  (15 other events, 114.1 us)

commit v7 on v6

--- a/solution.py
+++ b/solution.py
@@ -1267,6 +1267,7 @@
             (terms,) = kernel(add_groups, [shape(terms.shape, BF16)], terms, smem=0)
             terms = lax.all_to_all(terms, "dp", 0, 0).reshape(rows, -1)
             terms = terms[:first_rows], terms[first_rows : first_rows + second_rows]
+            low = away_plane(low)
             return (terms, low, across(low)) + tuple(finish_own(*shared))
         second_rows = padded(second_rows)
         halves = (first_rows // 2, second_rows // 2)

time: 169 us -> 169 us (level)
  no operation moved by 1% of the time
where the time goes in v7:
time: 169 us
  waiting for transfers between devices  67.8 us (40%)
  starting transfers between devices  63.1 us (37%)
  Pallas kernels  34 us (20%)
  local copies, waits for them, and re-layouts  2.55 us (2%)
    ppermute x62, waiting for transfers between devices, permute(): return lax.ppermute(tensor, ('dp', 'chan'), pairs)  67.8 us
    ppermute x62, starting transfers between devices, permute(): return lax.ppermute(tensor, ('dp', 'chan'), pairs)  63.1 us
    pallas_call x22, Pallas kernels, call(): pl.pallas_call(body, out_shape=outs, in_specs=specs, out_specs=[pl.BlockS...  34 us
  transfers between devices with their start and end apart: 62, of which 33 were waited for; matrix products, arithmetic and copies ran while one was open for 2% of the time, Pallas kernels for 16%

profile of v7, /device:TPU:0, one launch (start us, length us, event | category | flops | bytes accessed | tf_op | source)
XLA Modules:
  0.0 169.2 jit_solution(17358439074136337292)
XLA Ops:
  0.7 3.0 %collective-permute-start.5 = (bf16[64,1024]{1,0:T(8,128)(2,1)}, bf16[64,1024]{1,0:T(8,128)(2,1)S(1)}, u32[]{:S(2)}, u32[]{:S(2)}) collective-permute-start(bf16[64,1024]{1,0:T(8,128)(2,1)} %bitcast.37), channel_id=1, source_target_pairs={{0,2},{1,3},{2,0},{3,1},{4,6},{5,7},{6,4},{7,5},{8,10},{9,11},{10,... | collective-permute-start | bytes 393224 | tf_op jit(solution)/shard_map/ppermute | solution.py:1197
  3.8 2.2 %dynamic-slice_bitcast_fusion = (bf16[784,256]{1,0:T(8,128)(2,1)}, bf16[784,256]{1,0:T(8,128)(2,1)}) fusion(bf16[4,784,256]{2,1,0:T(8,128)(2,1)} %x_ref.1, s32[]{:T(128)S(6)} %select_n.20, s32[]{:T(128)S(6)} %select_n.19), kind=kLoop, calls=%fused_computation.4 | loop fusion | bytes 1605640 | tf_op jit(solution)/shard_map/jit(dynamic_index_in_dim)/squeeze | solution.py:1332
  6.0 1.4 collective-permute-start.4
  7.4 1.5 collective-permute-start.3
  10.4 1.5 collective-permute-start.6
  11.9 1.0 collective-permute-done.6.a3
  13.3 12.1 %collective-permute-done.4.x3.x_refs_3_ = bf16[784,256]{1,0:T(8,128)(2,1)S(1)} collective-permute-done((bf16[784,256]{1,0:T(8,128)(2,1)}, bf16[784,256]{1,0:T(8,128)(2,1)S(1)}, u32[]{:S(2)}, u32[]{:S(2)}) %collective-permute-start.4) | collective-permute-done | bytes 401440 | tf_op jit(solution)/shard_map/ppermute | solution.py:1197
  25.4 1.5 collective-permute-done.3.x2.x_refs_2_
  26.9 1.6 reduce_in.1
  28.8 1.2 collective-permute-done.8
  29.9 3.7 %collective-permute-start.11 = (f32[6,256]{1,0:T(8,128)S(1)}, f32[6,256]{1,0:T(8,128)S(1)}, u32[]{:S(2)}, u32[]{:S(2)}) collective-permute-start(f32[6,256]{1,0:T(8,128)S(1)} %add.39.sums_refs_0_), channel_id=1, source_target_pairs={{0,24},{1,25},{2,26},{3,27},{4,28},{5,29},{6,30},{7,31},{8,16},{9,... | collective-permute-start | bytes 18440 | tf_op jit(solution)/shard_map/ppermute | solution.py:1197
  35.4 2.8 %collective-permute-done.10.sums_refs_2_ = f32[6,256]{1,0:T(8,128)S(1)} collective-permute-done((f32[6,256]{1,0:T(8,128)S(1)}, f32[6,256]{1,0:T(8,128)S(1)}, u32[]{:S(2)}, u32[]{:S(2)}) %collective-permute-start.10) | collective-permute-done | bytes 6176 | tf_op jit(solution)/shard_map/ppermute | solution.py:1197
  38.2 1.6 collective-permute-start.27
  39.7 1.8 %collective-permute-done.13.b3 = bf16[1872,128]{1,0:T(8,128)(2,1)S(1)} collective-permute-done((bf16[1872,128]{1,0:T(8,128)(2,1)S(1)}, bf16[1872,128]{1,0:T(8,128)(2,1)S(1)}, u32[]{:S(2)}, u32[]{:S(2)}) %collective-permute-start.13) | collective-permute-done | bytes 479264 | tf_op jit(solution)/shard_map/ppermute | solution.py:1197
  42.5 2.3 %conv_mid.1 = (bf16[3,976,256]{2,1,0:T(8,128)(2,1)S(1)}, f32[896,512]{1,0:T(8,128)S(1)}, f32[2,512]{1,0:T(2,128)S(1)}) custom-call(s32[4,8]{1,0:T(4,128)S(1)} %copy-done.2, f32[896,256]{1,0:T(8,128)S(1)} %get-tuple-element.125.pre_ref, f32[6,256]{1,0:T(8,128)S(1)} %add.39.sums_refs_0_, f32[6,256]{1,0:T(8,128)S(1)} %collective-permute-done.9.sums_refs_1_, ...), custom_call_target="tpu_custom_call" | custom-call | flops 1056964608 | bytes 5462144 | tf_op jit(solution)/shard_map/conv_mid/pallas_call | solution.py:192
  45.0 1.0 collective-permute-done.14
  46.0 2.6 %collective-permute-start.17 = (f32[2,512]{1,0:T(2,128)S(1)}, f32[2,512]{1,0:T(2,128)S(1)}, u32[]{:S(2)}, u32[]{:S(2)}) collective-permute-start(f32[2,512]{1,0:T(2,128)S(1)} %add.40.sums_refs_0_.mid_sums_refs_0_), channel_id=1, source_target_pairs={{0,24},{1,25},{2,26},{3,27},{4,28},{5,29},{6,30},{7,31},{8,16},{9,... | collective-permute-start | bytes 12296 | tf_op jit(solution)/shard_map/ppermute | solution.py:1197
  48.6 1.8 %collective-permute-start.15 = (f32[2,512]{1,0:T(2,128)S(1)}, f32[2,512]{1,0:T(2,128)S(1)}, u32[]{:S(2)}, u32[]{:S(2)}) collective-permute-start(f32[2,512]{1,0:T(2,128)S(1)} %add.40.sums_refs_0_.mid_sums_refs_0_), channel_id=1, source_target_pairs={{0,8},{1,9},{2,10},{3,11},{4,12},{5,13},{6,14},{7,15},{8,0},{9,1},... | collective-permute-start | bytes 12296 | tf_op jit(solution)/shard_map/ppermute | solution.py:1197
  50.4 1.0 collective-permute-done.17.sums_refs_3_.mid_sums_refs_3_
  51.4 1.7 %collective-permute-done.16.sums_refs_2_.mid_sums_refs_2_ = f32[2,512]{1,0:T(2,128)S(1)} collective-permute-done((f32[2,512]{1,0:T(2,128)S(1)}, f32[2,512]{1,0:T(2,128)S(1)}, u32[]{:S(2)}, u32[]{:S(2)}) %collective-permute-start.16) | collective-permute-done | bytes 4128 | tf_op jit(solution)/shard_map/ppermute | solution.py:1197
  53.2 1.7 %pool.1 = (f32[4,256]{1,0:T(4,128)S(1)}, f32[40,128]{1,0:T(8,128)S(1)}) custom-call(s32[4,8]{1,0:T(4,128)S(1)} %copy-done.2, f32[896,512]{1,0:T(8,128)S(1)} %get-tuple-element.133.mid_ref, f32[2,512]{1,0:T(2,128)S(1)} %add.40.sums_refs_0_.mid_sums_refs_0_, f32[2,512]{1,0:T(2,128)S(1)} %collective-permute-done.15.sums_refs_1_.mid_sums_refs_1_, ...), custom_call_target="tpu_custom_call" | custom-call | bytes 1945728 | tf_op jit(solution)/shard_map/pool/pallas_call | solution.py:192
  55.8 1.5 collective-permute-start.28
  58.7 3.6 %collective-permute-start.21 = (f32[80,128]{1,0:T(8,128)S(1)}, f32[80,128]{1,0:T(8,128)S(1)}, u32[]{:S(2)}, u32[]{:S(2)}) collective-permute-start(f32[80,128]{1,0:T(8,128)S(1)} %constant_dynamic-update-slice_fusion.gathered_refs_0_), channel_id=1, source_target_pairs={{0,24},{1,25},{2,26},{3,27},{4,28},{5,29},{6,30},{7,31},{8,16},{9,... | collective-permute-start | bytes 122888 | tf_op jit(solution)/shard_map/ppermute | solution.py:1197
  64.6 2.6 %collective-permute-done.20.gathered_refs_2_ = f32[80,128]{1,0:T(8,128)S(1)} collective-permute-done((f32[80,128]{1,0:T(8,128)S(1)}, f32[80,128]{1,0:T(8,128)S(1)}, u32[]{:S(2)}, u32[]{:S(2)}) %collective-permute-start.20) | collective-permute-done | bytes 40992 | tf_op jit(solution)/shard_map/ppermute | solution.py:1197
  67.2 1.9 %attend.1 = (f32[2,4,128]{2,1,0:T(4,128)S(1)}, f32[4,512]{1,0:T(4,128)S(1)}, bf16[784,256]{1,0:T(8,128)(2,1)S(1)}, f32[4,784,256]{2,1,0:T(8,128)S(1)}, f32[8,256]{1,0:T(8,128)S(1)}) custom-call(s32[4,8]{1,0:T(4,128)S(1)} %copy-done.2, f32[80,128]{1,0:T(8,128)S(1)} %constant_dynamic-update-slice_fusion.gathered_refs_0_, ...), custom_call_target="tpu_custom_call" | custom-call | flops 411041792 | bytes 6327424 | tf_op jit(solution)/shard_map/attend/pallas_call | solution.py:192
  69.3 1.2 collective-permute-done.22
  70.4 2.0 %collective-permute-start.25 = (f32[8,256]{1,0:T(8,128)S(1)}, f32[8,256]{1,0:T(8,128)S(1)}, u32[]{:S(2)}, u32[]{:S(2)}) collective-permute-start(f32[8,256]{1,0:T(8,128)S(1)} %add.41.sums_refs_0_), channel_id=1, source_target_pairs={{0,24},{1,25},{2,26},{3,27},{4,28},{5,29},{6,30},{7,31},{8,16},{9,... | collective-permute-start | bytes 24584 | tf_op jit(solution)/shard_map/ppermute | solution.py:1197
  72.6 2.2 %collective-permute-start.23 = (f32[8,256]{1,0:T(8,128)S(1)}, f32[8,256]{1,0:T(8,128)S(1)}, u32[]{:S(2)}, u32[]{:S(2)}) collective-permute-start(f32[8,256]{1,0:T(8,128)S(1)} %add.41.sums_refs_0_), channel_id=1, source_target_pairs={{0,8},{1,9},{2,10},{3,11},{4,12},{5,13},{6,14},{7,15},{8,0},{9,1},... | collective-permute-start | bytes 24584 | tf_op jit(solution)/shard_map/ppermute | solution.py:1197
  74.8 1.2 collective-permute-done.25.sums_refs_3_
  76.0 1.0 collective-permute-done.24.sums_refs_2_
  77.0 2.6 %finish.1 = (bf16[816,256]{1,0:T(8,128)(2,1)S(1)}, f32[4,784,256]{2,1,0:T(8,128)S(1)}, f32[8,256]{1,0:T(8,128)S(1)}) custom-call(s32[4,8]{1,0:T(4,128)S(1)} %copy-done.2, f32[4,784,256]{2,1,0:T(8,128)S(1)} %get-tuple-element.142.out_ref, f32[8,256]{1,0:T(8,128)S(1)} %add.41.sums_refs_0_, f32[8,256]{1,0:T(8,128)S(1)} %collective-permute-done.23.sums_refs_1_, ...), custom_call_target="tpu_custom_call" | custom-call | bytes 11305088 | tf_op jit(solution)/shard_map/finish/pallas_call | solution.py:192
  79.7 1.2 collective-permute-done.30
  80.8 3.1 %collective-permute-start.33 = (f32[8,256]{1,0:T(8,128)S(1)}, f32[8,256]{1,0:T(8,128)S(1)}, u32[]{:S(2)}, u32[]{:S(2)}) collective-permute-start(f32[8,256]{1,0:T(8,128)S(1)} %add.42.back_refs_0_.out_back_refs_0_), channel_id=1, source_target_pairs={{0,24},{1,25},{2,26},{3,27},{4,28},{5,29},{6,30},{7,31},{8,16},{9,... | collective-permute-start | bytes 24584 | tf_op jit(solution)/shard_map/ppermute | solution.py:1197
  84.0 1.2 collective-permute-start.31
  86.3 2.2 %collective-permute-done.32.back_refs_2_.out_back_refs_2_ = f32[8,256]{1,0:T(8,128)S(1)} collective-permute-done((f32[8,256]{1,0:T(8,128)S(1)}, f32[8,256]{1,0:T(8,128)S(1)}, u32[]{:S(2)}, u32[]{:S(2)}) %collective-permute-start.32) | collective-permute-done | bytes 8224 | tf_op jit(solution)/shard_map/ppermute | solution.py:1197
  88.5 2.8 %back_out.1 = (bf16[4,784,256]{2,1,0:T(8,128)(2,1)S(1)}, f32[896,256]{1,0:T(8,128)S(1)}, f32[4,512]{1,0:T(4,128)S(1)}, f32[12,128]{1,0:T(8,128)S(1)}) custom-call(s32[4,8]{1,0:T(4,128)S(1)} %copy-done.2, f32[4,784,256]{2,1,0:T(8,128)S(1)} %get-tuple-element.151.grad_ref, f32[4,784,256]{2,1,0:T(8,128)S(1)} %get-tuple-element.142.out_ref, ...), custom_call_target="tpu_custom_call" | custom-call | flops 411041792 | bytes 11556992 | tf_op jit(solution)/shard_map/back_out/pallas_call | solution.py:192
  91.3 1.1 collective-permute-start.34
  93.2 2.3 %collective-permute-start.37 = (f32[16,128]{1,0:T(8,128)S(1)}, f32[16,128]{1,0:T(8,128)S(1)}, u32[]{:S(2)}, u32[]{:S(2)}) collective-permute-start(f32[16,128]{1,0:T(8,128)S(1)} %pad_maximum_fusion.5.back_refs_0_), channel_id=1, source_target_pairs={{0,24},{1,25},{2,26},{3,27},{4,28},{5,29},{6,30},{7,31},{8,16},{9,... | collective-permute-start | bytes 24584 | tf_op jit(solution)/shard_map/ppermute | solution.py:1197
  95.5 2.2 %collective-permute-start.35 = (f32[16,128]{1,0:T(8,128)S(1)}, f32[16,128]{1,0:T(8,128)S(1)}, u32[]{:S(2)}, u32[]{:S(2)}) collective-permute-start(f32[16,128]{1,0:T(8,128)S(1)} %pad_maximum_fusion.5.back_refs_0_), channel_id=1, source_target_pairs={{0,8},{1,9},{2,10},{3,11},{4,12},{5,13},{6,14},{7,15},{8,0},{9,1},... | collective-permute-start | bytes 24584 | tf_op jit(solution)/shard_map/ppermute | solution.py:1197
  97.7 1.8 %weight_out_term.1 = (bf16[2,656,128]{2,1,0:T(8,128)(2,1)S(1)}, bf16[2,656,128]{2,1,0:T(8,128)(2,1)S(1)}) custom-call(s32[4,8]{1,0:T(4,128)S(1)} %copy-done.2, bf16[784,256]{1,0:T(8,128)(2,1)S(1)} %get-tuple-element.156.weighted_ref, bf16[4,784,256]{2,1,0:T(8,128)(2,1)S(1)} %get-tuple-element.157.low_ref, f32[2,4,128]{2,1,0:T(4,128)S(1)} %get-tuple-element.154.gate_ref, ...), custom_call_target="tpu_custom_call" | custom-call | flops 411041792 | bytes 2695296 | tf_op jit(solution)/shard_map/weight_out_term/pallas_call | solution.py:192
  100.8 3.6 %back_mid.1 = (bf16[976,512]{1,0:T(8,128)(2,1)S(1)}, f32[896,256]{1,0:T(8,128)S(1)}, f32[4,128]{1,0:T(4,128)S(1)}, f32[8,512]{1,0:T(8,128)S(1)}, f32[2,256]{1,0:T(2,128)S(1)}) custom-call(s32[4,8]{1,0:T(4,128)S(1)} %copy-done.2, f32[16,128]{1,0:T(8,128)S(1)} %pad_maximum_fusion.5.back_refs_0_, f32[16,128]{1,0:T(8,128)S(1)} %collective-permute-done.35.back_refs_1_, ...), custom_call_target="tpu_custom_call" | custom-call | flops 1056964608 | bytes 7122048 | tf_op jit(solution)/shard_map/back_mid/pallas_call | solution.py:192
  104.6 1.0 collective-permute-done.40
  105.6 1.9 %collective-permute-start.43 = (f32[2,256]{1,0:T(2,128)S(1)}, f32[2,256]{1,0:T(2,128)S(1)}, u32[]{:S(2)}, u32[]{:S(2)}) collective-permute-start(f32[2,256]{1,0:T(2,128)S(1)} %add.44.back_refs_0_), channel_id=1, source_target_pairs={{0,24},{1,25},{2,26},{3,27},{4,28},{5,29},{6,30},{7,31},{8,16},{9,... | collective-permute-start | bytes 6152 | tf_op jit(solution)/shard_map/ppermute | solution.py:1197
  108.4 1.6 collective-permute-start.41
  110.0 2.4 %weight_mid_term.1 = (bf16[2,1152,128]{2,1,0:T(8,128)(2,1)S(1)}, bf16[2,1152,128]{2,1,0:T(8,128)(2,1)S(1)}) custom-call(s32[4,8]{1,0:T(4,128)S(1)} %copy-done.2, bf16[3,976,256]{2,1,0:T(8,128)(2,1)S(1)} %get-tuple-element.172.taps_ref, bf16[976,512]{1,0:T(8,128)(2,1)S(1)} %get-tuple-element.173.low_ref, f32[2,256]{1,0:T(2,128)S(1)} %get-tuple-element.131.affine_ref), custom_call_target="tpu_custom_call" | custom-call | flops 1056964608 | bytes 3680384 | tf_op jit(solution)/shard_map/weight_mid_term/pallas_call | solution.py:192
  112.5 1.9 %back_in.1 = (bf16[784,256]{1,0:T(8,128)(2,1)S(1)}, bf16[2,592,128]{2,1,0:T(8,128)(2,1)S(1)}, bf16[2,592,128]{2,1,0:T(8,128)(2,1)S(1)}) custom-call(s32[4,8]{1,0:T(4,128)S(1)} %copy-done.2, f32[896,256]{1,0:T(8,128)S(1)} %get-tuple-element.176.grad_ref, f32[896,256]{1,0:T(8,128)S(1)} %get-tuple-element.125.pre_ref, f32[6,256]{1,0:T(8,128)S(1)} %add.39.sums_refs_0_, ...), custom_call_target="tpu_custom_call" | custom-call | flops 411041792 | bytes 4702336 | tf_op jit(solution)/shard_map/back_in/pallas_call | solution.py:192
  115.0 1.9 %collective-permute-done.46.arrived_refs_1_ = bf16[2,592,128]{2,1,0:T(8,128)(2,1)S(1)} collective-permute-done((bf16[2,592,128]{2,1,0:T(8,128)(2,1)S(1)}, bf16[2,592,128]{2,1,0:T(8,128)(2,1)S(1)}, u32[]{:S(2)}, u32[]{:S(2)}) %collective-permute-start.46) | collective-permute-done | bytes 303136 | tf_op jit(solution)/shard_map/ppermute | solution.py:1197
  117.1 1.4 collective-permute-start.47
  119.5 7.3 %collective-permute-done.47.arrived_ref = bf16[1280,128]{1,0:T(8,128)(2,1)S(1)} collective-permute-done((bf16[1280,128]{1,0:T(8,128)(2,1)S(1)}, bf16[1280,128]{1,0:T(8,128)(2,1)S(1)}, u32[]{:S(2)}, u32[]{:S(2)}) %collective-permute-start.47) | collective-permute-done | bytes 327712 | tf_op jit(solution)/shard_map/ppermute | solution.py:1197
  129.4 3.7 %collective-permute-done.49.arrived_refs_1_ = bf16[640,128]{1,0:T(8,128)(2,1)S(1)} collective-permute-done((bf16[640,128]{1,0:T(8,128)(2,1)S(1)}, bf16[640,128]{1,0:T(8,128)(2,1)S(1)}, u32[]{:S(2)}, u32[]{:S(2)}) %collective-permute-start.49) | collective-permute-done | bytes 163872 | tf_op jit(solution)/shard_map/ppermute | solution.py:1197
  135.4 1.1 collective-permute-start.52
  136.5 1.2 collective-permute-start.53
  137.8 2.1 %collective-permute-start.54 = (bf16[304,128]{1,0:T(8,128)(2,1)S(1)}, bf16[304,128]{1,0:T(8,128)(2,1)S(1)}, u32[]{:S(2)}, u32[]{:S(2)}) collective-permute-start(bf16[304,128]{1,0:T(8,128)(2,1)S(1)} %get-tuple-element.205), channel_id=1, source_target_pairs={{0,24},{1,25},{2,26},{3,27},{4,28},{5,29},{6,30},{7,31},{8,16},{9,... | collective-permute-start | bytes 233480 | tf_op jit(solution)/shard_map/ppermute | solution.py:1197
  139.9 3.9 %finish_owned.1 = (bf16[4,784,256]{2,1,0:T(8,128)(2,1)}, bf16[4,784,256]{2,1,0:T(8,128)(2,1)S(1)}) custom-call(s32[4,8]{1,0:T(4,128)S(1)} %copy-done.2, bf16[816,256]{1,0:T(8,128)(2,1)S(1)} %collective-permute-done.29.near_ref, bf16[2,816,256]{2,1,0:T(8,128)(2,1)S(1)} %collective-permute-done.50.swapped_ref, ...), custom_call_target="tpu_custom_call" | custom-call | flops 411041792 | bytes 8618112 | tf_op jit(solution)/shard_map/finish_owned/pallas_call | solution.py:192
  143.8 1.1 collective-permute-done.54.arrived_refs_2_
  144.9 1.1 collective-permute-start.55
  146.0 1.7 %collective-permute-start.58 = (bf16[304,128]{1,0:T(8,128)(2,1)S(1)}, bf16[304,128]{1,0:T(8,128)(2,1)S(1)}, u32[]{:S(2)}, u32[]{:S(2)}) collective-permute-start(bf16[304,128]{1,0:T(8,128)(2,1)S(1)} %add_depth.1), channel_id=1, source_target_pairs={{0,24},{1,25},{2,26},{3,27},{4,28},{5,29},{6,30},{7,31},{8,16},{9,... | collective-permute-start | bytes 233480 | tf_op jit(solution)/shard_map/ppermute | solution.py:1197
  147.8 1.8 %collective-permute-start.57 = (bf16[304,128]{1,0:T(8,128)(2,1)S(1)}, bf16[304,128]{1,0:T(8,128)(2,1)S(1)}, u32[]{:S(2)}, u32[]{:S(2)}) collective-permute-start(bf16[304,128]{1,0:T(8,128)(2,1)S(1)} %add_depth.1), channel_id=1, source_target_pairs={{0,16},{1,17},{2,18},{3,19},{4,20},{5,21},{6,22},{7,23},{8,24},{9,... | collective-permute-start | bytes 233480 | tf_op jit(solution)/shard_map/ppermute | solution.py:1197
  150.5 2.6 %collective-permute-done.58 = bf16[304,128]{1,0:T(8,128)(2,1)S(1)} collective-permute-done((bf16[304,128]{1,0:T(8,128)(2,1)S(1)}, bf16[304,128]{1,0:T(8,128)(2,1)S(1)}, u32[]{:S(2)}, u32[]{:S(2)}) %collective-permute-start.58) | collective-permute-done | bytes 77856 | tf_op jit(solution)/shard_map/ppermute | solution.py:1197
  153.0 4.4 %collective-permute-done.57 = bf16[304,128]{1,0:T(8,128)(2,1)S(1)} collective-permute-done((bf16[304,128]{1,0:T(8,128)(2,1)S(1)}, bf16[304,128]{1,0:T(8,128)(2,1)S(1)}, u32[]{:S(2)}, u32[]{:S(2)}) %collective-permute-start.57) | collective-permute-done | bytes 77856 | tf_op jit(solution)/shard_map/ppermute | solution.py:1197
  158.0 1.1 collective-permute-done.59.low_refs_1_
  159.7 1.8 %grad_owned.1 = bf16[4,784,256]{2,1,0:T(8,128)(2,1)} custom-call(bf16[784,256]{1,0:T(8,128)(2,1)S(1)} %collective-permute-done.51.low_refs_0_, bf16[784,256]{1,0:T(8,128)(2,1)S(1)} %collective-permute-done.59.low_refs_1_, bf16[784,256]{1,0:T(8,128)(2,1)S(1)} %collective-permute-done.55.low_refs_2_, bf16[784,256]{1,0:T(8,128)(2,1)S(1)} %collective-permute-done.60.low_refs_3_, ...), custom_call_target="tpu_custom_call" | custom-call | flops 411041792 | bytes 5341184 | tf_op jit(solution)/shard_map/grad_owned/pallas_call | solution.py:192
  161.6 5.8 %collective-permute-done.61.term_refs_1_ = bf16[1216,128]{1,0:T(8,128)(2,1)S(1)} collective-permute-done((bf16[1216,128]{1,0:T(8,128)(2,1)S(1)}, bf16[1216,128]{1,0:T(8,128)(2,1)S(1)}, u32[]{:S(2)}, u32[]{:S(2)}) %collective-permute-start.61) | collective-permute-done | bytes 311328 | tf_op jit(solution)/shard_map/ppermute | solution.py:1197
  167.4 1.7 unpack.1
  (140 shorter events, 22.9 us)
Async XLA Ops:
  0.7 9.7 %collective-permute-start.5 = (bf16[64,1024]{1,0:T(8,128)(2,1)}, bf16[64,1024]{1,0:T(8,128)(2,1)S(1)}, u32[]{:S(2)}, u32[]{:S(2)}) collective-permute-start(bf16[64,1024]{1,0:T(8,128)(2,1)} %bitcast.37), channel_id=1, source_target_pairs={{0,2},{1,3},{2,0},{3,1},{4,6},{5,7},{6,4},{7,5},{8,10},{9,11},{10,... | collective-permute-start | bytes 393224 | tf_op jit(solution)/shard_map/ppermute | solution.py:1197
  3.7 5.3 %collective-permute-start = (bf16[64,1024]{1,0:T(8,128)(2,1)}, bf16[64,1024]{1,0:T(8,128)(2,1)S(1)}, u32[]{:S(2)}, u32[]{:S(2)}) collective-permute-start(bf16[64,1024]{1,0:T(8,128)(2,1)} %bitcast.38), channel_id=1, source_target_pairs={{0,1},{1,0},{2,3},{3,2},{4,5},{5,4},{6,7},{7,6},{8,9},{9,8},{10,11... | collective-permute-start | bytes 393224 | tf_op jit(solution)/shard_map/ppermute | solution.py:1197
  6.0 20.8 %copy-start.2 = (s32[4,8]{1,0:T(4,128)S(1)}, s32[4,8]{1,0:T(4,128)}, u32[]{:S(2)}) copy-start(s32[4,8]{1,0:T(4,128)} %counts_ref.33) | copy-start | bytes 388
  6.0 20.8 %copy-start.5 = (bf16[1024,64]{0,1:T(8,128)(2,1)S(1)}, bf16[1024,64]{0,1:T(8,128)(2,1)}, u32[]{:S(2)}) copy-start(bf16[1024,64]{0,1:T(8,128)(2,1)} %param.19) | copy-start | bytes 393220
  6.0 19.3 %collective-permute-start.4 = (bf16[784,256]{1,0:T(8,128)(2,1)}, bf16[784,256]{1,0:T(8,128)(2,1)S(1)}, u32[]{:S(2)}, u32[]{:S(2)}) collective-permute-start(bf16[784,256]{1,0:T(8,128)(2,1)} %get-tuple-element.234), channel_id=1, source_target_pairs={{0,6},{1,2},{2,4},{3,0},{4,7},{5,3},{6,5},{7,1},{8,14},{9,10},{10,... | collective-permute-start | bytes 1204232 | tf_op jit(solution)/shard_map/ppermute | solution.py:1197
  7.4 19.4 %collective-permute-start.3 = (bf16[784,256]{1,0:T(8,128)(2,1)}, bf16[784,256]{1,0:T(8,128)(2,1)S(1)}, u32[]{:S(2)}, u32[]{:S(2)}) collective-permute-start(bf16[784,256]{1,0:T(8,128)(2,1)} %get-tuple-element.235), channel_id=1, source_target_pairs={{0,2},{1,6},{2,0},{3,4},{4,3},{5,7},{6,1},{7,5},{8,10},{9,14},{10,... | collective-permute-start | bytes 1204232 | tf_op jit(solution)/shard_map/ppermute | solution.py:1197
  9.1 17.8 %collective-permute-start.2 = (bf16[784,256]{1,0:T(8,128)(2,1)S(1)}, bf16[784,256]{1,0:T(8,128)(2,1)S(1)}, u32[]{:S(2)}, u32[]{:S(2)}) collective-permute-start(bf16[784,256]{1,0:T(8,128)(2,1)S(1)} %get-tuple-element.236), channel_id=1, source_target_pairs={{0,4},{1,0},{2,6},{3,2},{4,5},{5,1},{6,7},{7,3},{8,12},{9,8},{10,1... | collective-permute-start | bytes 1204232 | tf_op jit(solution)/shard_map/ppermute | solution.py:1197
  9.3 17.5 %collective-permute-start.1 = (bf16[784,256]{1,0:T(8,128)(2,1)S(1)}, bf16[784,256]{1,0:T(8,128)(2,1)S(1)}, u32[]{:S(2)}, u32[]{:S(2)}) collective-permute-start(bf16[784,256]{1,0:T(8,128)(2,1)S(1)} %get-tuple-element.237), channel_id=1, source_target_pairs={{0,0},{1,4},{2,2},{3,6},{4,1},{5,5},{6,3},{7,7},{8,8},{9,12},{10,1... | collective-permute-start | bytes 1204232 | tf_op jit(solution)/shard_map/ppermute | solution.py:1197
  10.4 2.5 %collective-permute-start.6 = (bf16[64,1024]{1,0:T(8,128)(2,1)S(1)}, bf16[64,1024]{1,0:T(8,128)(2,1)S(1)}, u32[]{:S(2)}, u32[]{:S(2)}) collective-permute-start(bf16[64,1024]{1,0:T(8,128)(2,1)S(1)} %collective-permute-done.5.a2), channel_id=1, source_target_pairs={{0,1},{1,0},{2,3},{3,2},{4,5},{5,4},{6,7},{7,6},{8,9},{9,8},{10,11... | collective-permute-start | bytes 393224 | tf_op jit(solution)/shard_map/ppermute | solution.py:1197
  12.9 15.8 %collective-permute-start.7 = (bf16[1872,128]{1,0:T(8,128)(2,1)S(1)}, bf16[1872,128]{1,0:T(8,128)(2,1)S(1)}, u32[]{:S(2)}, u32[]{:S(2)}) collective-permute-start(bf16[1872,128]{1,0:T(8,128)(2,1)S(1)} %pack.1.b0), channel_id=1, source_target_pairs={{0,1},{1,0},{2,3},{3,2},{4,5},{5,4},{6,7},{7,6},{8,9},{9,8},{10,11... | collective-permute-start | bytes 1437704 | tf_op jit(solution)/shard_map/ppermute | solution.py:1197
  26.8 12.9 %collective-permute-start.12 = (bf16[1872,128]{1,0:T(8,128)(2,1)S(1)}, bf16[1872,128]{1,0:T(8,128)(2,1)S(1)}, u32[]{:S(2)}, u32[]{:S(2)}) collective-permute-start(bf16[1872,128]{1,0:T(8,128)(2,1)S(1)} %pack.1.b0), channel_id=1, source_target_pairs={{0,2},{1,3},{2,0},{3,1},{4,6},{5,7},{6,4},{7,5},{8,10},{9,11},{10,... | collective-permute-start | bytes 1437704 | tf_op jit(solution)/shard_map/ppermute | solution.py:1197
  28.7 1.2 collective-permute-start.8
  29.9 5.4 %collective-permute-start.11 = (f32[6,256]{1,0:T(8,128)S(1)}, f32[6,256]{1,0:T(8,128)S(1)}, u32[]{:S(2)}, u32[]{:S(2)}) collective-permute-start(f32[6,256]{1,0:T(8,128)S(1)} %add.39.sums_refs_0_), channel_id=1, source_target_pairs={{0,24},{1,25},{2,26},{3,27},{4,28},{5,29},{6,30},{7,31},{8,16},{9,... | collective-permute-start | bytes 18440 | tf_op jit(solution)/shard_map/ppermute | solution.py:1197
  33.6 4.5 %collective-permute-start.10 = (f32[6,256]{1,0:T(8,128)S(1)}, f32[6,256]{1,0:T(8,128)S(1)}, u32[]{:S(2)}, u32[]{:S(2)}) collective-permute-start(f32[6,256]{1,0:T(8,128)S(1)} %add.39.sums_refs_0_), channel_id=1, source_target_pairs={{0,16},{1,17},{2,18},{3,19},{4,20},{5,21},{6,22},{7,23},{8,24},{9,... | collective-permute-start | bytes 18440 | tf_op jit(solution)/shard_map/ppermute | solution.py:1197
  33.6 4.5 %collective-permute-start.9 = (f32[6,256]{1,0:T(8,128)S(1)}, f32[6,256]{1,0:T(8,128)S(1)}, u32[]{:S(2)}, u32[]{:S(2)}) collective-permute-start(f32[6,256]{1,0:T(8,128)S(1)} %add.39.sums_refs_0_), channel_id=1, source_target_pairs={{0,8},{1,9},{2,10},{3,11},{4,12},{5,13},{6,14},{7,15},{8,0},{9,1},... | collective-permute-start | bytes 18440 | tf_op jit(solution)/shard_map/ppermute | solution.py:1197
  34.4 20.5 %collective-permute-start.26 = (bf16[2,784,256]{2,1,0:T(8,128)(2,1)S(1)}, bf16[2,784,256]{2,1,0:T(8,128)(2,1)S(1)}, u32[]{:S(2)}, u32[]{:S(2)}) collective-permute-start(bf16[2,784,256]{2,1,0:T(8,128)(2,1)S(1)} %pad_maximum_fusion.2), channel_id=1, source_target_pairs={{0,0},{1,4},{2,2},{3,6},{4,1},{5,5},{6,3},{7,7},{8,8},{9,12},{10,1... | collective-permute-start | bytes 2408456 | tf_op jit(solution)/shard_map/ppermute | solution.py:1197
  38.2 17.5 %collective-permute-start.27 = (bf16[2,784,256]{2,1,0:T(8,128)(2,1)S(1)}, bf16[2,784,256]{2,1,0:T(8,128)(2,1)S(1)}, u32[]{:S(2)}, u32[]{:S(2)}) collective-permute-start(bf16[2,784,256]{2,1,0:T(8,128)(2,1)S(1)} %pad_maximum_fusion.1), channel_id=1, source_target_pairs={{0,4},{1,0},{2,6},{3,2},{4,5},{5,1},{6,7},{7,3},{8,12},{9,8},{10,1... | collective-permute-start | bytes 2408456 | tf_op jit(solution)/shard_map/ppermute | solution.py:1197
  39.7 1.8 %collective-permute-start.13 = (bf16[1872,128]{1,0:T(8,128)(2,1)S(1)}, bf16[1872,128]{1,0:T(8,128)(2,1)S(1)}, u32[]{:S(2)}, u32[]{:S(2)}) collective-permute-start(bf16[1872,128]{1,0:T(8,128)(2,1)S(1)} %collective-permute-done.12.b2), channel_id=1, source_target_pairs={{0,1},{1,0},{2,3},{3,2},{4,5},{5,4},{6,7},{7,6},{8,9},{9,8},{10,11... | collective-permute-start | bytes 1437704 | tf_op jit(solution)/shard_map/ppermute | solution.py:1197
  44.8 1.2 collective-permute-start.14
  46.0 5.4 %collective-permute-start.17 = (f32[2,512]{1,0:T(2,128)S(1)}, f32[2,512]{1,0:T(2,128)S(1)}, u32[]{:S(2)}, u32[]{:S(2)}) collective-permute-start(f32[2,512]{1,0:T(2,128)S(1)} %add.40.sums_refs_0_.mid_sums_refs_0_), channel_id=1, source_target_pairs={{0,24},{1,25},{2,26},{3,27},{4,28},{5,29},{6,30},{7,31},{8,16},{9,... | collective-permute-start | bytes 12296 | tf_op jit(solution)/shard_map/ppermute | solution.py:1197
  48.6 4.5 %collective-permute-start.16 = (f32[2,512]{1,0:T(2,128)S(1)}, f32[2,512]{1,0:T(2,128)S(1)}, u32[]{:S(2)}, u32[]{:S(2)}) collective-permute-start(f32[2,512]{1,0:T(2,128)S(1)} %add.40.sums_refs_0_.mid_sums_refs_0_), channel_id=1, source_target_pairs={{0,16},{1,17},{2,18},{3,19},{4,20},{5,21},{6,22},{7,23},{8,24},{9,... | collective-permute-start | bytes 12296 | tf_op jit(solution)/shard_map/ppermute | solution.py:1197
  48.6 4.5 %collective-permute-start.15 = (f32[2,512]{1,0:T(2,128)S(1)}, f32[2,512]{1,0:T(2,128)S(1)}, u32[]{:S(2)}, u32[]{:S(2)}) collective-permute-start(f32[2,512]{1,0:T(2,128)S(1)} %add.40.sums_refs_0_.mid_sums_refs_0_), channel_id=1, source_target_pairs={{0,8},{1,9},{2,10},{3,11},{4,12},{5,13},{6,14},{7,15},{8,0},{9,1},... | collective-permute-start | bytes 12296 | tf_op jit(solution)/shard_map/ppermute | solution.py:1197
  55.8 21.2 %collective-permute-start.28 = (bf16[2,784,256]{2,1,0:T(8,128)(2,1)S(1)}, bf16[2,784,256]{2,1,0:T(8,128)(2,1)S(1)}, u32[]{:S(2)}, u32[]{:S(2)}) collective-permute-start(bf16[2,784,256]{2,1,0:T(8,128)(2,1)S(1)} %pad_maximum_fusion.3), channel_id=1, source_target_pairs={{0,2},{1,3},{2,0},{3,1},{4,6},{5,7},{6,4},{7,5},{8,10},{9,11},{10,... | collective-permute-start | bytes 2408456 | tf_op jit(solution)/shard_map/ppermute | solution.py:1197
  57.3 1.4 collective-permute-start.18
  58.7 5.9 %collective-permute-start.21 = (f32[80,128]{1,0:T(8,128)S(1)}, f32[80,128]{1,0:T(8,128)S(1)}, u32[]{:S(2)}, u32[]{:S(2)}) collective-permute-start(f32[80,128]{1,0:T(8,128)S(1)} %constant_dynamic-update-slice_fusion.gathered_refs_0_), channel_id=1, source_target_pairs={{0,24},{1,25},{2,26},{3,27},{4,28},{5,29},{6,30},{7,31},{8,16},{9,... | collective-permute-start | bytes 122888 | tf_op jit(solution)/shard_map/ppermute | solution.py:1197
  62.3 4.9 %collective-permute-start.20 = (f32[80,128]{1,0:T(8,128)S(1)}, f32[80,128]{1,0:T(8,128)S(1)}, u32[]{:S(2)}, u32[]{:S(2)}) collective-permute-start(f32[80,128]{1,0:T(8,128)S(1)} %constant_dynamic-update-slice_fusion.gathered_refs_0_), channel_id=1, source_target_pairs={{0,16},{1,17},{2,18},{3,19},{4,20},{5,21},{6,22},{7,23},{8,24},{9,... | collective-permute-start | bytes 122888 | tf_op jit(solution)/shard_map/ppermute | solution.py:1197
  62.3 4.9 %collective-permute-start.19 = (f32[80,128]{1,0:T(8,128)S(1)}, f32[80,128]{1,0:T(8,128)S(1)}, u32[]{:S(2)}, u32[]{:S(2)}) collective-permute-start(f32[80,128]{1,0:T(8,128)S(1)} %constant_dynamic-update-slice_fusion.gathered_refs_0_), channel_id=1, source_target_pairs={{0,8},{1,9},{2,10},{3,11},{4,12},{5,13},{6,14},{7,15},{8,0},{9,1},... | collective-permute-start | bytes 122888 | tf_op jit(solution)/shard_map/ppermute | solution.py:1197
  69.2 1.2 collective-permute-start.22
  70.4 5.6 %collective-permute-start.25 = (f32[8,256]{1,0:T(8,128)S(1)}, f32[8,256]{1,0:T(8,128)S(1)}, u32[]{:S(2)}, u32[]{:S(2)}) collective-permute-start(f32[8,256]{1,0:T(8,128)S(1)} %add.41.sums_refs_0_), channel_id=1, source_target_pairs={{0,24},{1,25},{2,26},{3,27},{4,28},{5,29},{6,30},{7,31},{8,16},{9,... | collective-permute-start | bytes 24584 | tf_op jit(solution)/shard_map/ppermute | solution.py:1197
  72.4 4.6 %collective-permute-start.24 = (f32[8,256]{1,0:T(8,128)S(1)}, f32[8,256]{1,0:T(8,128)S(1)}, u32[]{:S(2)}, u32[]{:S(2)}) collective-permute-start(f32[8,256]{1,0:T(8,128)S(1)} %add.41.sums_refs_0_), channel_id=1, source_target_pairs={{0,16},{1,17},{2,18},{3,19},{4,20},{5,21},{6,22},{7,23},{8,24},{9,... | collective-permute-start | bytes 24584 | tf_op jit(solution)/shard_map/ppermute | solution.py:1197
  72.6 4.4 %collective-permute-start.23 = (f32[8,256]{1,0:T(8,128)S(1)}, f32[8,256]{1,0:T(8,128)S(1)}, u32[]{:S(2)}, u32[]{:S(2)}) collective-permute-start(f32[8,256]{1,0:T(8,128)S(1)} %add.41.sums_refs_0_), channel_id=1, source_target_pairs={{0,8},{1,9},{2,10},{3,11},{4,12},{5,13},{6,14},{7,15},{8,0},{9,1},... | collective-permute-start | bytes 24584 | tf_op jit(solution)/shard_map/ppermute | solution.py:1197
  79.6 1.2 collective-permute-start.30
  80.8 5.5 %collective-permute-start.33 = (f32[8,256]{1,0:T(8,128)S(1)}, f32[8,256]{1,0:T(8,128)S(1)}, u32[]{:S(2)}, u32[]{:S(2)}) collective-permute-start(f32[8,256]{1,0:T(8,128)S(1)} %add.42.back_refs_0_.out_back_refs_0_), channel_id=1, source_target_pairs={{0,24},{1,25},{2,26},{3,27},{4,28},{5,29},{6,30},{7,31},{8,16},{9,... | collective-permute-start | bytes 24584 | tf_op jit(solution)/shard_map/ppermute | solution.py:1197
  84.0 4.5 %collective-permute-start.32 = (f32[8,256]{1,0:T(8,128)S(1)}, f32[8,256]{1,0:T(8,128)S(1)}, u32[]{:S(2)}, u32[]{:S(2)}) collective-permute-start(f32[8,256]{1,0:T(8,128)S(1)} %add.42.back_refs_0_.out_back_refs_0_), channel_id=1, source_target_pairs={{0,16},{1,17},{2,18},{3,19},{4,20},{5,21},{6,22},{7,23},{8,24},{9,... | collective-permute-start | bytes 24584 | tf_op jit(solution)/shard_map/ppermute | solution.py:1197
  84.0 4.5 %collective-permute-start.31 = (f32[8,256]{1,0:T(8,128)S(1)}, f32[8,256]{1,0:T(8,128)S(1)}, u32[]{:S(2)}, u32[]{:S(2)}) collective-permute-start(f32[8,256]{1,0:T(8,128)S(1)} %add.42.back_refs_0_.out_back_refs_0_), channel_id=1, source_target_pairs={{0,8},{1,9},{2,10},{3,11},{4,12},{5,13},{6,14},{7,15},{8,0},{9,1},... | collective-permute-start | bytes 24584 | tf_op jit(solution)/shard_map/ppermute | solution.py:1197
  85.2 14.8 %collective-permute-start.29 = (bf16[816,256]{1,0:T(8,128)(2,1)S(1)}, bf16[816,256]{1,0:T(8,128)(2,1)S(1)}, u32[]{:S(2)}, u32[]{:S(2)}) collective-permute-start(bf16[816,256]{1,0:T(8,128)(2,1)S(1)} %get-tuple-element.150), channel_id=1, source_target_pairs={{0,0},{1,4},{2,2},{3,6},{4,1},{5,5},{6,3},{7,7},{8,8},{9,12},{10,1... | collective-permute-start | bytes 1253384 | tf_op jit(solution)/shard_map/ppermute | solution.py:1197
  91.3 1.9 %collective-permute-start.34 = (f32[12,128]{1,0:T(8,128)S(1)}, f32[12,128]{1,0:T(8,128)S(1)}, u32[]{:S(2)}, u32[]{:S(2)}) collective-permute-start(f32[12,128]{1,0:T(8,128)S(1)} %get-tuple-element.155), channel_id=1, source_target_pairs={{0,1},{1,0},{2,3},{3,2},{4,5},{5,4},{6,7},{7,6},{8,9},{9,8},{10,11... | collective-permute-start | bytes 18440 | tf_op jit(solution)/shard_map/ppermute | solution.py:1197
  93.2 6.3 %collective-permute-start.37 = (f32[16,128]{1,0:T(8,128)S(1)}, f32[16,128]{1,0:T(8,128)S(1)}, u32[]{:S(2)}, u32[]{:S(2)}) collective-permute-start(f32[16,128]{1,0:T(8,128)S(1)} %pad_maximum_fusion.5.back_refs_0_), channel_id=1, source_target_pairs={{0,24},{1,25},{2,26},{3,27},{4,28},{5,29},{6,30},{7,31},{8,16},{9,... | collective-permute-start | bytes 24584 | tf_op jit(solution)/shard_map/ppermute | solution.py:1197
  95.5 4.5 %collective-permute-start.36 = (f32[16,128]{1,0:T(8,128)S(1)}, f32[16,128]{1,0:T(8,128)S(1)}, u32[]{:S(2)}, u32[]{:S(2)}) collective-permute-start(f32[16,128]{1,0:T(8,128)S(1)} %pad_maximum_fusion.5.back_refs_0_), channel_id=1, source_target_pairs={{0,16},{1,17},{2,18},{3,19},{4,20},{5,21},{6,22},{7,23},{8,24},{9,... | collective-permute-start | bytes 24584 | tf_op jit(solution)/shard_map/ppermute | solution.py:1197
  95.5 4.5 %collective-permute-start.35 = (f32[16,128]{1,0:T(8,128)S(1)}, f32[16,128]{1,0:T(8,128)S(1)}, u32[]{:S(2)}, u32[]{:S(2)}) collective-permute-start(f32[16,128]{1,0:T(8,128)S(1)} %pad_maximum_fusion.5.back_refs_0_), channel_id=1, source_target_pairs={{0,8},{1,9},{2,10},{3,11},{4,12},{5,13},{6,14},{7,15},{8,0},{9,1},... | collective-permute-start | bytes 24584 | tf_op jit(solution)/shard_map/ppermute | solution.py:1197
  100.1 4.3 %collective-permute-start.39 = (bf16[2,656,128]{2,1,0:T(8,128)(2,1)S(1)}, bf16[2,656,128]{2,1,0:T(8,128)(2,1)S(1)}, u32[]{:S(2)}, u32[]{:S(2)}) collective-permute-start(bf16[2,656,128]{2,1,0:T(8,128)(2,1)S(1)} %get-tuple-element.170), channel_id=1, source_target_pairs={{0,1},{1,0},{2,3},{3,2},{4,5},{5,4},{6,7},{7,6},{8,9},{9,8},{10,11... | collective-permute-start | bytes 1007624 | tf_op jit(solution)/shard_map/ppermute | solution.py:1197
  100.1 12.4 %collective-permute-start.38 = (bf16[816,256]{1,0:T(8,128)(2,1)S(1)}, bf16[816,256]{1,0:T(8,128)(2,1)S(1)}, u32[]{:S(2)}, u32[]{:S(2)}) collective-permute-start(bf16[816,256]{1,0:T(8,128)(2,1)S(1)} %collective-permute-done.29.near_ref), channel_id=1, source_target_pairs={{0,2},{1,3},{2,0},{3,1},{4,6},{5,7},{6,4},{7,5},{8,10},{9,11},{10,... | collective-permute-start | bytes 1253384 | tf_op jit(solution)/shard_map/ppermute | solution.py:1197
  104.4 1.2 collective-permute-start.40
  105.6 6.8 %collective-permute-start.43 = (f32[2,256]{1,0:T(2,128)S(1)}, f32[2,256]{1,0:T(2,128)S(1)}, u32[]{:S(2)}, u32[]{:S(2)}) collective-permute-start(f32[2,256]{1,0:T(2,128)S(1)} %add.44.back_refs_0_), channel_id=1, source_target_pairs={{0,24},{1,25},{2,26},{3,27},{4,28},{5,29},{6,30},{7,31},{8,16},{9,... | collective-permute-start | bytes 6152 | tf_op jit(solution)/shard_map/ppermute | solution.py:1197
  107.5 5.0 %collective-permute-start.42 = (f32[2,256]{1,0:T(2,128)S(1)}, f32[2,256]{1,0:T(2,128)S(1)}, u32[]{:S(2)}, u32[]{:S(2)}) collective-permute-start(f32[2,256]{1,0:T(2,128)S(1)} %add.44.back_refs_0_), channel_id=1, source_target_pairs={{0,16},{1,17},{2,18},{3,19},{4,20},{5,21},{6,22},{7,23},{8,24},{9,... | collective-permute-start | bytes 6152 | tf_op jit(solution)/shard_map/ppermute | solution.py:1197
  108.4 4.1 %collective-permute-start.41 = (f32[2,256]{1,0:T(2,128)S(1)}, f32[2,256]{1,0:T(2,128)S(1)}, u32[]{:S(2)}, u32[]{:S(2)}) collective-permute-start(f32[2,256]{1,0:T(2,128)S(1)} %add.44.back_refs_0_), channel_id=1, source_target_pairs={{0,8},{1,9},{2,10},{3,11},{4,12},{5,13},{6,14},{7,15},{8,0},{9,1},... | collective-permute-start | bytes 6152 | tf_op jit(solution)/shard_map/ppermute | solution.py:1197
  114.4 4.1 %collective-permute-start.44 = (bf16[2,1152,128]{2,1,0:T(8,128)(2,1)S(1)}, bf16[2,1152,128]{2,1,0:T(8,128)(2,1)S(1)}, u32[]{:S(2)}, u32[]{:S(2)}) collective-permute-start(bf16[2,1152,128]{2,1,0:T(8,128)(2,1)S(1)} %get-tuple-element.185), channel_id=1, source_target_pairs={{0,1},{1,0},{2,3},{3,2},{4,5},{5,4},{6,7},{7,6},{8,9},{9,8},{10,11... | collective-permute-start | bytes 1769480 | tf_op jit(solution)/shard_map/ppermute | solution.py:1197
  114.5 2.4 %collective-permute-start.46 = (bf16[2,592,128]{2,1,0:T(8,128)(2,1)S(1)}, bf16[2,592,128]{2,1,0:T(8,128)(2,1)S(1)}, u32[]{:S(2)}, u32[]{:S(2)}) collective-permute-start(bf16[2,592,128]{2,1,0:T(8,128)(2,1)S(1)} %get-tuple-element.190), channel_id=1, source_target_pairs={{0,1},{1,0},{2,3},{3,2},{4,5},{5,4},{6,7},{7,6},{8,9},{9,8},{10,11... | collective-permute-start | bytes 909320 | tf_op jit(solution)/shard_map/ppermute | solution.py:1197
  117.1 9.8 %collective-permute-start.47 = (bf16[1280,128]{1,0:T(8,128)(2,1)S(1)}, bf16[1280,128]{1,0:T(8,128)(2,1)S(1)}, u32[]{:S(2)}, u32[]{:S(2)}) collective-permute-start(bf16[1280,128]{1,0:T(8,128)(2,1)S(1)} %get-tuple-element.192), channel_id=1, source_target_pairs={{0,2},{1,3},{2,0},{3,1},{4,6},{5,7},{6,4},{7,5},{8,10},{9,11},{10,... | collective-permute-start | bytes 983048 | tf_op jit(solution)/shard_map/ppermute | solution.py:1197
  119.2 9.2 %collective-permute-start.45 = (bf16[2,576,128]{2,1,0:T(8,128)(2,1)S(1)}, bf16[2,576,128]{2,1,0:T(8,128)(2,1)S(1)}, u32[]{:S(2)}, u32[]{:S(2)}) collective-permute-start(bf16[2,576,128]{2,1,0:T(8,128)(2,1)S(1)} %get-tuple-element.187), channel_id=1, source_target_pairs={{0,4},{1,5},{2,6},{3,7},{4,0},{5,1},{6,2},{7,3},{8,12},{9,13},{10,... | collective-permute-start | bytes 884744 | tf_op jit(solution)/shard_map/ppermute | solution.py:1197
  127.5 5.5 %collective-permute-start.49 = (bf16[640,128]{1,0:T(8,128)(2,1)S(1)}, bf16[640,128]{1,0:T(8,128)(2,1)S(1)}, u32[]{:S(2)}, u32[]{:S(2)}) collective-permute-start(bf16[640,128]{1,0:T(8,128)(2,1)S(1)} %get-tuple-element.196), channel_id=1, source_target_pairs={{0,4},{1,5},{2,6},{3,7},{4,0},{5,1},{6,2},{7,3},{8,12},{9,13},{10,... | collective-permute-start | bytes 491528 | tf_op jit(solution)/shard_map/ppermute | solution.py:1197
  128.5 5.2 %collective-permute-start.48 = (bf16[576,128]{1,0:T(8,128)(2,1)S(1)}, bf16[576,128]{1,0:T(8,128)(2,1)S(1)}, u32[]{:S(2)}, u32[]{:S(2)}) collective-permute-start(bf16[576,128]{1,0:T(8,128)(2,1)S(1)} %get-tuple-element.195), channel_id=1, source_target_pairs={{0,2},{1,3},{2,0},{3,1},{4,6},{5,7},{6,4},{7,5},{8,10},{9,11},{10,... | collective-permute-start | bytes 442376 | tf_op jit(solution)/shard_map/ppermute | solution.py:1197
  134.4 5.5 %collective-permute-start.50 = (bf16[2,816,256]{2,1,0:T(8,128)(2,1)S(1)}, bf16[2,816,256]{2,1,0:T(8,128)(2,1)S(1)}, u32[]{:S(2)}, u32[]{:S(2)}) collective-permute-start(bf16[2,816,256]{2,1,0:T(8,128)(2,1)S(1)} %pad_maximum_fusion), channel_id=1, source_target_pairs={{0,1},{1,0},{2,3},{3,2},{4,5},{5,4},{6,7},{7,6},{8,9},{9,8},{10,11... | collective-permute-start | bytes 2506760 | tf_op jit(solution)/shard_map/ppermute | solution.py:1197
  134.5 10.4 %collective-permute-start.51 = (bf16[784,256]{1,0:T(8,128)(2,1)S(1)}, bf16[784,256]{1,0:T(8,128)(2,1)S(1)}, u32[]{:S(2)}, u32[]{:S(2)}) collective-permute-start(bf16[784,256]{1,0:T(8,128)(2,1)S(1)} %get-tuple-element.202), channel_id=1, source_target_pairs={{0,0},{1,4},{2,2},{3,6},{4,1},{5,5},{6,3},{7,7},{8,8},{9,12},{10,1... | collective-permute-start | bytes 1204232 | tf_op jit(solution)/shard_map/ppermute | solution.py:1197
  135.4 8.4 %collective-permute-start.52 = (bf16[304,128]{1,0:T(8,128)(2,1)S(1)}, bf16[304,128]{1,0:T(8,128)(2,1)S(1)}, u32[]{:S(2)}, u32[]{:S(2)}) collective-permute-start(bf16[304,128]{1,0:T(8,128)(2,1)S(1)} %get-tuple-element.203), channel_id=1, source_target_pairs={{0,8},{1,9},{2,10},{3,11},{4,12},{5,13},{6,14},{7,15},{8,0},{9,1},... | collective-permute-start | bytes 233480 | tf_op jit(solution)/shard_map/ppermute | solution.py:1197
  136.5 7.3 %collective-permute-start.53 = (bf16[304,128]{1,0:T(8,128)(2,1)S(1)}, bf16[304,128]{1,0:T(8,128)(2,1)S(1)}, u32[]{:S(2)}, u32[]{:S(2)}) collective-permute-start(bf16[304,128]{1,0:T(8,128)(2,1)S(1)} %get-tuple-element.204), channel_id=1, source_target_pairs={{0,16},{1,17},{2,18},{3,19},{4,20},{5,21},{6,22},{7,23},{8,24},{9,... | collective-permute-start | bytes 233480 | tf_op jit(solution)/shard_map/ppermute | solution.py:1197
  137.8 7.1 %collective-permute-start.54 = (bf16[304,128]{1,0:T(8,128)(2,1)S(1)}, bf16[304,128]{1,0:T(8,128)(2,1)S(1)}, u32[]{:S(2)}, u32[]{:S(2)}) collective-permute-start(bf16[304,128]{1,0:T(8,128)(2,1)S(1)} %get-tuple-element.205), channel_id=1, source_target_pairs={{0,24},{1,25},{2,26},{3,27},{4,28},{5,29},{6,30},{7,31},{8,16},{9,... | collective-permute-start | bytes 233480 | tf_op jit(solution)/shard_map/ppermute | solution.py:1197
  144.9 12.5 %collective-permute-start.55 = (bf16[784,256]{1,0:T(8,128)(2,1)S(1)}, bf16[784,256]{1,0:T(8,128)(2,1)S(1)}, u32[]{:S(2)}, u32[]{:S(2)}) collective-permute-start(bf16[784,256]{1,0:T(8,128)(2,1)S(1)} %collective-permute-done.51.low_refs_0_), channel_id=1, source_target_pairs={{0,2},{1,3},{2,0},{3,1},{4,6},{5,7},{6,4},{7,5},{8,10},{9,11},{10,... | collective-permute-start | bytes 1204232 | tf_op jit(solution)/shard_map/ppermute | solution.py:1197
  146.0 7.0 %collective-permute-start.58 = (bf16[304,128]{1,0:T(8,128)(2,1)S(1)}, bf16[304,128]{1,0:T(8,128)(2,1)S(1)}, u32[]{:S(2)}, u32[]{:S(2)}) collective-permute-start(bf16[304,128]{1,0:T(8,128)(2,1)S(1)} %add_depth.1), channel_id=1, source_target_pairs={{0,24},{1,25},{2,26},{3,27},{4,28},{5,29},{6,30},{7,31},{8,16},{9,... | collective-permute-start | bytes 233480 | tf_op jit(solution)/shard_map/ppermute | solution.py:1197
  147.8 9.7 %collective-permute-start.57 = (bf16[304,128]{1,0:T(8,128)(2,1)S(1)}, bf16[304,128]{1,0:T(8,128)(2,1)S(1)}, u32[]{:S(2)}, u32[]{:S(2)}) collective-permute-start(bf16[304,128]{1,0:T(8,128)(2,1)S(1)} %add_depth.1), channel_id=1, source_target_pairs={{0,16},{1,17},{2,18},{3,19},{4,20},{5,21},{6,22},{7,23},{8,24},{9,... | collective-permute-start | bytes 233480 | tf_op jit(solution)/shard_map/ppermute | solution.py:1197
  149.6 7.9 %collective-permute-start.56 = (bf16[304,128]{1,0:T(8,128)(2,1)S(1)}, bf16[304,128]{1,0:T(8,128)(2,1)S(1)}, u32[]{:S(2)}, u32[]{:S(2)}) collective-permute-start(bf16[304,128]{1,0:T(8,128)(2,1)S(1)} %add_depth.1), channel_id=1, source_target_pairs={{0,8},{1,9},{2,10},{3,11},{4,12},{5,13},{6,14},{7,15},{8,0},{9,1},... | collective-permute-start | bytes 233480 | tf_op jit(solution)/shard_map/ppermute | solution.py:1197
  157.4 1.7 %collective-permute-start.59 = (bf16[784,256]{1,0:T(8,128)(2,1)S(1)}, bf16[784,256]{1,0:T(8,128)(2,1)S(1)}, u32[]{:S(2)}, u32[]{:S(2)}) collective-permute-start(bf16[784,256]{1,0:T(8,128)(2,1)S(1)} %collective-permute-done.51.low_refs_0_), channel_id=1, source_target_pairs={{0,1},{1,0},{2,3},{3,2},{4,5},{5,4},{6,7},{7,6},{8,9},{9,8},{10,11... | collective-permute-start | bytes 1204232 | tf_op jit(solution)/shard_map/ppermute | solution.py:1197
  157.4 2.3 %collective-permute-start.60 = (bf16[784,256]{1,0:T(8,128)(2,1)S(1)}, bf16[784,256]{1,0:T(8,128)(2,1)S(1)}, u32[]{:S(2)}, u32[]{:S(2)}) collective-permute-start(bf16[784,256]{1,0:T(8,128)(2,1)S(1)} %collective-permute-done.55.low_refs_2_), channel_id=1, source_target_pairs={{0,1},{1,0},{2,3},{3,2},{4,5},{5,4},{6,7},{7,6},{8,9},{9,8},{10,11... | collective-permute-start | bytes 1204232 | tf_op jit(solution)/shard_map/ppermute | solution.py:1197
  158.0 9.4 %collective-permute-start.61 = (bf16[1216,128]{1,0:T(8,128)(2,1)S(1)}, bf16[1216,128]{1,0:T(8,128)(2,1)S(1)}, u32[]{:S(2)}, u32[]{:S(2)}) collective-permute-start(bf16[1216,128]{1,0:T(8,128)(2,1)S(1)} %pad_maximum_fusion.4.term_refs_0_), channel_id=1, source_target_pairs={{0,4},{1,5},{2,6},{3,7},{4,0},{5,1},{6,2},{7,3},{8,12},{9,13},{10,... | collective-permute-start | bytes 933896 | tf_op jit(solution)/shard_map/ppermute | solution.py:1197
  (15 other events, 114.1 us)

commit v8 on v7

--- a/solution.py
+++ b/solution.py
@@ -1268,7 +1268,9 @@
             terms = lax.all_to_all(terms, "dp", 0, 0).reshape(rows, -1)
             terms = terms[:first_rows], terms[first_rows : first_rows + second_rows]
             low = away_plane(low)
-            return (terms, low, across(low)) + tuple(finish_own(*shared))
+            near, far = shared
+            owned = finish_own(near, core(jnp.stack([near, far])), far)
+            return (terms, low, across(low)) + tuple(owned)
         second_rows = padded(second_rows)
         halves = (first_rows // 2, second_rows // 2)
         pieces = (first_rows // groups, second_rows // groups)
@@ -1288,7 +1290,10 @@
             *first,
         )
         first_arrived = parity(send)
-        arrived = after(arrived, shared[1])
+        near, far = after_all(shared, send, second_send)
+        swapped = core(jnp.stack([near, far]))
+        arrived = after(arrived, swapped)
+        low = away_plane(after(low, send))
         keep, send = call(
             add_chip,
             [rows(halves[1]), rows(halves[1], BF16)],
@@ -1307,7 +1312,7 @@
             smem=0,
         )
         first_arrived = across(send)
-        arrived = after(arrived, first_arrived)
+        arrived = after(arrived, first_arrived, low)
         keep, *send = call(
             add_last,
             [rows(sum(pieces))] + [rows(sum(pieces), BF16)] * (depth - 1),
@@ -1317,8 +1322,7 @@
             (first_keep, keep),
             (first_arrived, arrived),
         )
-        low = away_plane(after(low, keep))
-        result, grad_summed = finish_own(*after_all(shared, keep))
+        result, grad_summed = finish_own(*after_all((near, swapped, far), keep))
         arrived = tuple(along(send[t - 1], t) for t in range(1, depth))
         arrived = after_all(arrived, result)
         low_other = across(after(low, *arrived))
@@ -1592,8 +1596,7 @@
     )
     owned = shape((batches, rows, lanes), BF16)
 
-    def finish_own(near, far):
-        swapped = core(jnp.stack([near, far]))
+    def finish_own(near, swapped, far):
         return call(
             finish_owned,
             [owned, owned],

time: 169 us -> 167 us (0.988)
  waiting for transfers between devices: 67.8 us -> 63.7 us
  starting transfers between devices: 63.1 us -> 65 us
    ppermute x62, waiting for transfers between devices: 67.8 us -> 63.7 us  [permute(): return lax.ppermute(tensor, ('dp', 'chan'), pairs)]
    ppermute x62, starting transfers between devices: 63.1 us -> 65 us  [permute(): return lax.ppermute(tensor, ('dp', 'chan'), pairs)]
  transfers between devices with their start and end apart: 62 -> 62, of which waited for: 33 -> 31; matrix products, arithmetic and copies ran while one was open for 2% -> 2% of each run, Pallas kernels for 16% -> 16%
where the time goes in v8:
time: 167 us
  starting transfers between devices  65 us (39%)
  waiting for transfers between devices  63.7 us (38%)
  Pallas kernels  34 us (20%)
  local copies, waits for them, and re-layouts  2.55 us (2%)
    ppermute x62, starting transfers between devices, permute(): return lax.ppermute(tensor, ('dp', 'chan'), pairs)  65 us
    ppermute x62, waiting for transfers between devices, permute(): return lax.ppermute(tensor, ('dp', 'chan'), pairs)  63.7 us
    pallas_call x22, Pallas kernels, call(): pl.pallas_call(body, out_shape=outs, in_specs=specs, out_specs=[pl.BlockS...  34 us
  transfers between devices with their start and end apart: 62, of which 31 were waited for; matrix products, arithmetic and copies ran while one was open for 2% of the time, Pallas kernels for 16%

profile of v8, /device:TPU:0, one launch (start us, length us, event | category | flops | bytes accessed | tf_op | source)
XLA Modules:
  0.0 167.0 jit_solution(2736452327879680086)
XLA Ops:
  0.7 3.0 %collective-permute-start.5 = (bf16[64,1024]{1,0:T(8,128)(2,1)}, bf16[64,1024]{1,0:T(8,128)(2,1)S(1)}, u32[]{:S(2)}, u32[]{:S(2)}) collective-permute-start(bf16[64,1024]{1,0:T(8,128)(2,1)} %bitcast.37), channel_id=1, source_target_pairs={{0,2},{1,3},{2,0},{3,1},{4,6},{5,7},{6,4},{7,5},{8,10},{9,11},{10,... | collective-permute-start | bytes 393224 | tf_op jit(solution)/shard_map/ppermute | solution.py:1197
  3.8 2.2 %dynamic-slice_bitcast_fusion = (bf16[784,256]{1,0:T(8,128)(2,1)}, bf16[784,256]{1,0:T(8,128)(2,1)}) fusion(bf16[4,784,256]{2,1,0:T(8,128)(2,1)} %x_ref.1, s32[]{:T(128)S(6)} %select_n.20, s32[]{:T(128)S(6)} %select_n.19), kind=kLoop, calls=%fused_computation.4 | loop fusion | bytes 1605640 | tf_op jit(solution)/shard_map/jit(dynamic_index_in_dim)/squeeze | solution.py:1336
  6.0 1.4 collective-permute-start.4
  7.4 1.5 collective-permute-start.3
  10.4 1.5 collective-permute-start.6
  11.9 1.0 collective-permute-done.6.a3
  13.3 12.1 %collective-permute-done.4.x3.x_refs_3_ = bf16[784,256]{1,0:T(8,128)(2,1)S(1)} collective-permute-done((bf16[784,256]{1,0:T(8,128)(2,1)}, bf16[784,256]{1,0:T(8,128)(2,1)S(1)}, u32[]{:S(2)}, u32[]{:S(2)}) %collective-permute-start.4) | collective-permute-done | bytes 401440 | tf_op jit(solution)/shard_map/ppermute | solution.py:1197
  25.4 1.5 collective-permute-done.3.x2.x_refs_2_
  26.9 1.6 reduce_in.1
  28.8 1.2 collective-permute-done.8
  29.9 3.7 %collective-permute-start.11 = (f32[6,256]{1,0:T(8,128)S(1)}, f32[6,256]{1,0:T(8,128)S(1)}, u32[]{:S(2)}, u32[]{:S(2)}) collective-permute-start(f32[6,256]{1,0:T(8,128)S(1)} %add.39.sums_refs_0_), channel_id=1, source_target_pairs={{0,24},{1,25},{2,26},{3,27},{4,28},{5,29},{6,30},{7,31},{8,16},{9,... | collective-permute-start | bytes 18440 | tf_op jit(solution)/shard_map/ppermute | solution.py:1197
  35.4 2.8 %collective-permute-done.10.sums_refs_2_ = f32[6,256]{1,0:T(8,128)S(1)} collective-permute-done((f32[6,256]{1,0:T(8,128)S(1)}, f32[6,256]{1,0:T(8,128)S(1)}, u32[]{:S(2)}, u32[]{:S(2)}) %collective-permute-start.10) | collective-permute-done | bytes 6176 | tf_op jit(solution)/shard_map/ppermute | solution.py:1197
  38.2 1.6 collective-permute-start.27
  39.7 1.8 %collective-permute-done.13.b3 = bf16[1872,128]{1,0:T(8,128)(2,1)S(1)} collective-permute-done((bf16[1872,128]{1,0:T(8,128)(2,1)S(1)}, bf16[1872,128]{1,0:T(8,128)(2,1)S(1)}, u32[]{:S(2)}, u32[]{:S(2)}) %collective-permute-start.13) | collective-permute-done | bytes 479264 | tf_op jit(solution)/shard_map/ppermute | solution.py:1197
  42.5 2.3 %conv_mid.1 = (bf16[3,976,256]{2,1,0:T(8,128)(2,1)S(1)}, f32[896,512]{1,0:T(8,128)S(1)}, f32[2,512]{1,0:T(2,128)S(1)}) custom-call(s32[4,8]{1,0:T(4,128)S(1)} %copy-done.2, f32[896,256]{1,0:T(8,128)S(1)} %get-tuple-element.128.pre_ref, f32[6,256]{1,0:T(8,128)S(1)} %add.39.sums_refs_0_, f32[6,256]{1,0:T(8,128)S(1)} %collective-permute-done.9.sums_refs_1_, ...), custom_call_target="tpu_custom_call" | custom-call | flops 1056964608 | bytes 5462144 | tf_op jit(solution)/shard_map/conv_mid/pallas_call | solution.py:192
  45.0 1.0 collective-permute-done.14
  46.0 2.6 %collective-permute-start.17 = (f32[2,512]{1,0:T(2,128)S(1)}, f32[2,512]{1,0:T(2,128)S(1)}, u32[]{:S(2)}, u32[]{:S(2)}) collective-permute-start(f32[2,512]{1,0:T(2,128)S(1)} %add.40.sums_refs_0_.mid_sums_refs_0_), channel_id=1, source_target_pairs={{0,24},{1,25},{2,26},{3,27},{4,28},{5,29},{6,30},{7,31},{8,16},{9,... | collective-permute-start | bytes 12296 | tf_op jit(solution)/shard_map/ppermute | solution.py:1197
  48.6 1.8 %collective-permute-start.15 = (f32[2,512]{1,0:T(2,128)S(1)}, f32[2,512]{1,0:T(2,128)S(1)}, u32[]{:S(2)}, u32[]{:S(2)}) collective-permute-start(f32[2,512]{1,0:T(2,128)S(1)} %add.40.sums_refs_0_.mid_sums_refs_0_), channel_id=1, source_target_pairs={{0,8},{1,9},{2,10},{3,11},{4,12},{5,13},{6,14},{7,15},{8,0},{9,1},... | collective-permute-start | bytes 12296 | tf_op jit(solution)/shard_map/ppermute | solution.py:1197
  50.4 1.0 collective-permute-done.17.sums_refs_3_.mid_sums_refs_3_
  51.4 1.7 %collective-permute-done.16.sums_refs_2_.mid_sums_refs_2_ = f32[2,512]{1,0:T(2,128)S(1)} collective-permute-done((f32[2,512]{1,0:T(2,128)S(1)}, f32[2,512]{1,0:T(2,128)S(1)}, u32[]{:S(2)}, u32[]{:S(2)}) %collective-permute-start.16) | collective-permute-done | bytes 4128 | tf_op jit(solution)/shard_map/ppermute | solution.py:1197
  53.2 1.7 %pool.1 = (f32[4,256]{1,0:T(4,128)S(1)}, f32[40,128]{1,0:T(8,128)S(1)}) custom-call(s32[4,8]{1,0:T(4,128)S(1)} %copy-done.2, f32[896,512]{1,0:T(8,128)S(1)} %get-tuple-element.136.mid_ref, f32[2,512]{1,0:T(2,128)S(1)} %add.40.sums_refs_0_.mid_sums_refs_0_, f32[2,512]{1,0:T(2,128)S(1)} %collective-permute-done.15.sums_refs_1_.mid_sums_refs_1_, ...), custom_call_target="tpu_custom_call" | custom-call | bytes 1945728 | tf_op jit(solution)/shard_map/pool/pallas_call | solution.py:192
  55.8 1.5 collective-permute-start.28
  58.7 3.6 %collective-permute-start.21 = (f32[80,128]{1,0:T(8,128)S(1)}, f32[80,128]{1,0:T(8,128)S(1)}, u32[]{:S(2)}, u32[]{:S(2)}) collective-permute-start(f32[80,128]{1,0:T(8,128)S(1)} %constant_dynamic-update-slice_fusion.gathered_refs_0_), channel_id=1, source_target_pairs={{0,24},{1,25},{2,26},{3,27},{4,28},{5,29},{6,30},{7,31},{8,16},{9,... | collective-permute-start | bytes 122888 | tf_op jit(solution)/shard_map/ppermute | solution.py:1197
  64.6 2.6 %collective-permute-done.20.gathered_refs_2_ = f32[80,128]{1,0:T(8,128)S(1)} collective-permute-done((f32[80,128]{1,0:T(8,128)S(1)}, f32[80,128]{1,0:T(8,128)S(1)}, u32[]{:S(2)}, u32[]{:S(2)}) %collective-permute-start.20) | collective-permute-done | bytes 40992 | tf_op jit(solution)/shard_map/ppermute | solution.py:1197
  67.2 1.9 %attend.1 = (f32[2,4,128]{2,1,0:T(4,128)S(1)}, f32[4,512]{1,0:T(4,128)S(1)}, bf16[784,256]{1,0:T(8,128)(2,1)S(1)}, f32[4,784,256]{2,1,0:T(8,128)S(1)}, f32[8,256]{1,0:T(8,128)S(1)}) custom-call(s32[4,8]{1,0:T(4,128)S(1)} %copy-done.2, f32[80,128]{1,0:T(8,128)S(1)} %constant_dynamic-update-slice_fusion.gathered_refs_0_, ...), custom_call_target="tpu_custom_call" | custom-call | flops 411041792 | bytes 6327424 | tf_op jit(solution)/shard_map/attend/pallas_call | solution.py:192
  69.3 1.2 collective-permute-done.22
  70.4 2.0 %collective-permute-start.25 = (f32[8,256]{1,0:T(8,128)S(1)}, f32[8,256]{1,0:T(8,128)S(1)}, u32[]{:S(2)}, u32[]{:S(2)}) collective-permute-start(f32[8,256]{1,0:T(8,128)S(1)} %add.41.sums_refs_0_), channel_id=1, source_target_pairs={{0,24},{1,25},{2,26},{3,27},{4,28},{5,29},{6,30},{7,31},{8,16},{9,... | collective-permute-start | bytes 24584 | tf_op jit(solution)/shard_map/ppermute | solution.py:1197
  72.6 2.2 %collective-permute-start.23 = (f32[8,256]{1,0:T(8,128)S(1)}, f32[8,256]{1,0:T(8,128)S(1)}, u32[]{:S(2)}, u32[]{:S(2)}) collective-permute-start(f32[8,256]{1,0:T(8,128)S(1)} %add.41.sums_refs_0_), channel_id=1, source_target_pairs={{0,8},{1,9},{2,10},{3,11},{4,12},{5,13},{6,14},{7,15},{8,0},{9,1},... | collective-permute-start | bytes 24584 | tf_op jit(solution)/shard_map/ppermute | solution.py:1197
  74.8 1.2 collective-permute-done.25.sums_refs_3_
  77.0 2.6 %finish.1 = (bf16[816,256]{1,0:T(8,128)(2,1)S(1)}, f32[4,784,256]{2,1,0:T(8,128)S(1)}, f32[8,256]{1,0:T(8,128)S(1)}) custom-call(s32[4,8]{1,0:T(4,128)S(1)} %copy-done.2, f32[4,784,256]{2,1,0:T(8,128)S(1)} %get-tuple-element.145.out_ref, f32[8,256]{1,0:T(8,128)S(1)} %add.41.sums_refs_0_, f32[8,256]{1,0:T(8,128)S(1)} %collective-permute-done.23.sums_refs_1_, ...), custom_call_target="tpu_custom_call" | custom-call | bytes 11305088 | tf_op jit(solution)/shard_map/finish/pallas_call | solution.py:192
  79.7 1.2 collective-permute-done.30
  80.8 3.1 %collective-permute-start.33 = (f32[8,256]{1,0:T(8,128)S(1)}, f32[8,256]{1,0:T(8,128)S(1)}, u32[]{:S(2)}, u32[]{:S(2)}) collective-permute-start(f32[8,256]{1,0:T(8,128)S(1)} %add.42.back_refs_0_.out_back_refs_0_), channel_id=1, source_target_pairs={{0,24},{1,25},{2,26},{3,27},{4,28},{5,29},{6,30},{7,31},{8,16},{9,... | collective-permute-start | bytes 24584 | tf_op jit(solution)/shard_map/ppermute | solution.py:1197
  84.0 1.2 collective-permute-start.31
  86.3 2.2 %collective-permute-done.32.back_refs_2_.out_back_refs_2_ = f32[8,256]{1,0:T(8,128)S(1)} collective-permute-done((f32[8,256]{1,0:T(8,128)S(1)}, f32[8,256]{1,0:T(8,128)S(1)}, u32[]{:S(2)}, u32[]{:S(2)}) %collective-permute-start.32) | collective-permute-done | bytes 8224 | tf_op jit(solution)/shard_map/ppermute | solution.py:1197
  88.5 2.8 %back_out.1 = (bf16[4,784,256]{2,1,0:T(8,128)(2,1)S(1)}, f32[896,256]{1,0:T(8,128)S(1)}, f32[4,512]{1,0:T(4,128)S(1)}, f32[12,128]{1,0:T(8,128)S(1)}) custom-call(s32[4,8]{1,0:T(4,128)S(1)} %copy-done.2, f32[4,784,256]{2,1,0:T(8,128)S(1)} %get-tuple-element.154.grad_ref, f32[4,784,256]{2,1,0:T(8,128)S(1)} %get-tuple-element.145.out_ref, ...), custom_call_target="tpu_custom_call" | custom-call | flops 411041792 | bytes 11556992 | tf_op jit(solution)/shard_map/back_out/pallas_call | solution.py:192
  91.3 1.1 collective-permute-start.34
  93.2 2.3 %collective-permute-start.37 = (f32[16,128]{1,0:T(8,128)S(1)}, f32[16,128]{1,0:T(8,128)S(1)}, u32[]{:S(2)}, u32[]{:S(2)}) collective-permute-start(f32[16,128]{1,0:T(8,128)S(1)} %pad_maximum_fusion.5.back_refs_0_), channel_id=1, source_target_pairs={{0,24},{1,25},{2,26},{3,27},{4,28},{5,29},{6,30},{7,31},{8,16},{9,... | collective-permute-start | bytes 24584 | tf_op jit(solution)/shard_map/ppermute | solution.py:1197
  95.5 2.2 %collective-permute-start.35 = (f32[16,128]{1,0:T(8,128)S(1)}, f32[16,128]{1,0:T(8,128)S(1)}, u32[]{:S(2)}, u32[]{:S(2)}) collective-permute-start(f32[16,128]{1,0:T(8,128)S(1)} %pad_maximum_fusion.5.back_refs_0_), channel_id=1, source_target_pairs={{0,8},{1,9},{2,10},{3,11},{4,12},{5,13},{6,14},{7,15},{8,0},{9,1},... | collective-permute-start | bytes 24584 | tf_op jit(solution)/shard_map/ppermute | solution.py:1197
  97.7 1.8 %weight_out_term.1 = (bf16[2,656,128]{2,1,0:T(8,128)(2,1)S(1)}, bf16[2,656,128]{2,1,0:T(8,128)(2,1)S(1)}) custom-call(s32[4,8]{1,0:T(4,128)S(1)} %copy-done.2, bf16[784,256]{1,0:T(8,128)(2,1)S(1)} %get-tuple-element.159.weighted_ref, bf16[4,784,256]{2,1,0:T(8,128)(2,1)S(1)} %get-tuple-element.160.low_ref, f32[2,4,128]{2,1,0:T(4,128)S(1)} %get-tuple-element.157.gate_ref, ...), custom_call_target="tpu_custom_call" | custom-call | flops 411041792 | bytes 2695296 | tf_op jit(solution)/shard_map/weight_out_term/pallas_call | solution.py:192
  100.8 3.6 %back_mid.1 = (bf16[976,512]{1,0:T(8,128)(2,1)S(1)}, f32[896,256]{1,0:T(8,128)S(1)}, f32[4,128]{1,0:T(4,128)S(1)}, f32[8,512]{1,0:T(8,128)S(1)}, f32[2,256]{1,0:T(2,128)S(1)}) custom-call(s32[4,8]{1,0:T(4,128)S(1)} %copy-done.2, f32[16,128]{1,0:T(8,128)S(1)} %pad_maximum_fusion.5.back_refs_0_, f32[16,128]{1,0:T(8,128)S(1)} %collective-permute-done.35.back_refs_1_, ...), custom_call_target="tpu_custom_call" | custom-call | flops 1056964608 | bytes 7122048 | tf_op jit(solution)/shard_map/back_mid/pallas_call | solution.py:192
  104.6 1.0 collective-permute-done.40
  105.6 1.9 %collective-permute-start.43 = (f32[2,256]{1,0:T(2,128)S(1)}, f32[2,256]{1,0:T(2,128)S(1)}, u32[]{:S(2)}, u32[]{:S(2)}) collective-permute-start(f32[2,256]{1,0:T(2,128)S(1)} %add.44.back_refs_0_), channel_id=1, source_target_pairs={{0,24},{1,25},{2,26},{3,27},{4,28},{5,29},{6,30},{7,31},{8,16},{9,... | collective-permute-start | bytes 6152 | tf_op jit(solution)/shard_map/ppermute | solution.py:1197
  108.4 1.6 collective-permute-start.41
  110.0 2.4 %weight_mid_term.1 = (bf16[2,1152,128]{2,1,0:T(8,128)(2,1)S(1)}, bf16[2,1152,128]{2,1,0:T(8,128)(2,1)S(1)}) custom-call(s32[4,8]{1,0:T(4,128)S(1)} %copy-done.2, bf16[3,976,256]{2,1,0:T(8,128)(2,1)S(1)} %get-tuple-element.175.taps_ref, bf16[976,512]{1,0:T(8,128)(2,1)S(1)} %get-tuple-element.176.low_ref, f32[2,256]{1,0:T(2,128)S(1)} %get-tuple-element.134.affine_ref), custom_call_target="tpu_custom_call" | custom-call | flops 1056964608 | bytes 3680384 | tf_op jit(solution)/shard_map/weight_mid_term/pallas_call | solution.py:192
  112.5 1.9 %back_in.1 = (bf16[784,256]{1,0:T(8,128)(2,1)S(1)}, bf16[2,592,128]{2,1,0:T(8,128)(2,1)S(1)}, bf16[2,592,128]{2,1,0:T(8,128)(2,1)S(1)}) custom-call(s32[4,8]{1,0:T(4,128)S(1)} %copy-done.2, f32[896,256]{1,0:T(8,128)S(1)} %get-tuple-element.179.grad_ref, f32[896,256]{1,0:T(8,128)S(1)} %get-tuple-element.128.pre_ref, f32[6,256]{1,0:T(8,128)S(1)} %add.39.sums_refs_0_, ...), custom_call_target="tpu_custom_call" | custom-call | flops 411041792 | bytes 4702336 | tf_op jit(solution)/shard_map/back_in/pallas_call | solution.py:192
  115.0 1.9 %collective-permute-done.45.arrived_refs_1_ = bf16[2,592,128]{2,1,0:T(8,128)(2,1)S(1)} collective-permute-done((bf16[2,592,128]{2,1,0:T(8,128)(2,1)S(1)}, bf16[2,592,128]{2,1,0:T(8,128)(2,1)S(1)}, u32[]{:S(2)}, u32[]{:S(2)}) %collective-permute-start.45) | collective-permute-done | bytes 303136 | tf_op jit(solution)/shard_map/ppermute | solution.py:1197
  118.1 1.4 collective-permute-start.48
  120.6 7.4 %collective-permute-done.48.arrived_ref = bf16[1280,128]{1,0:T(8,128)(2,1)S(1)} collective-permute-done((bf16[1280,128]{1,0:T(8,128)(2,1)S(1)}, bf16[1280,128]{1,0:T(8,128)(2,1)S(1)}, u32[]{:S(2)}, u32[]{:S(2)}) %collective-permute-start.48) | collective-permute-done | bytes 327712 | tf_op jit(solution)/shard_map/ppermute | solution.py:1197
  130.6 4.3 %collective-permute-done.49.arrived_refs_0_ = bf16[576,128]{1,0:T(8,128)(2,1)S(1)} collective-permute-done((bf16[576,128]{1,0:T(8,128)(2,1)S(1)}, bf16[576,128]{1,0:T(8,128)(2,1)S(1)}, u32[]{:S(2)}, u32[]{:S(2)}) %collective-permute-start.49) | collective-permute-done | bytes 147488 | tf_op jit(solution)/shard_map/ppermute | solution.py:1197
  134.9 1.4 collective-permute-done.50.arrived_refs_1_
  136.9 1.1 collective-permute-start.52
  138.0 1.3 collective-permute-start.53
  139.3 2.1 %collective-permute-start.54 = (bf16[304,128]{1,0:T(8,128)(2,1)S(1)}, bf16[304,128]{1,0:T(8,128)(2,1)S(1)}, u32[]{:S(2)}, u32[]{:S(2)}) collective-permute-start(bf16[304,128]{1,0:T(8,128)(2,1)S(1)} %get-tuple-element.211), channel_id=1, source_target_pairs={{0,24},{1,25},{2,26},{3,27},{4,28},{5,29},{6,30},{7,31},{8,16},{9,... | collective-permute-start | bytes 233480 | tf_op jit(solution)/shard_map/ppermute | solution.py:1197
  141.4 3.9 %finish_owned.1 = (bf16[4,784,256]{2,1,0:T(8,128)(2,1)}, bf16[4,784,256]{2,1,0:T(8,128)(2,1)S(1)}) custom-call(s32[4,8]{1,0:T(4,128)S(1)} %copy-done.2, bf16[816,256]{1,0:T(8,128)(2,1)S(1)} %collective-permute-done.29.near_ref, bf16[2,816,256]{2,1,0:T(8,128)(2,1)S(1)} %collective-permute-done.46.swapped_ref, ...), custom_call_target="tpu_custom_call" | custom-call | flops 411041792 | bytes 8618112 | tf_op jit(solution)/shard_map/finish_owned/pallas_call | solution.py:192
  145.6 1.2 collective-permute-start.55
  146.9 1.8 %collective-permute-start.58 = (bf16[304,128]{1,0:T(8,128)(2,1)S(1)}, bf16[304,128]{1,0:T(8,128)(2,1)S(1)}, u32[]{:S(2)}, u32[]{:S(2)}) collective-permute-start(bf16[304,128]{1,0:T(8,128)(2,1)S(1)} %add_depth.1), channel_id=1, source_target_pairs={{0,24},{1,25},{2,26},{3,27},{4,28},{5,29},{6,30},{7,31},{8,16},{9,... | collective-permute-start | bytes 233480 | tf_op jit(solution)/shard_map/ppermute | solution.py:1197
  148.7 1.1 collective-permute-start.57
  149.8 1.5 collective-permute-start.56
  151.3 1.9 %collective-permute-done.58 = bf16[304,128]{1,0:T(8,128)(2,1)S(1)} collective-permute-done((bf16[304,128]{1,0:T(8,128)(2,1)S(1)}, bf16[304,128]{1,0:T(8,128)(2,1)S(1)}, u32[]{:S(2)}, u32[]{:S(2)}) %collective-permute-start.58) | collective-permute-done | bytes 77856 | tf_op jit(solution)/shard_map/ppermute | solution.py:1197
  153.2 1.9 %collective-permute-done.57 = bf16[304,128]{1,0:T(8,128)(2,1)S(1)} collective-permute-done((bf16[304,128]{1,0:T(8,128)(2,1)S(1)}, bf16[304,128]{1,0:T(8,128)(2,1)S(1)}, u32[]{:S(2)}, u32[]{:S(2)}) %collective-permute-start.57) | collective-permute-done | bytes 77856 | tf_op jit(solution)/shard_map/ppermute | solution.py:1197
  155.7 1.8 %collective-permute-start.61 = (bf16[1216,128]{1,0:T(8,128)(2,1)S(1)}, bf16[1216,128]{1,0:T(8,128)(2,1)S(1)}, u32[]{:S(2)}, u32[]{:S(2)}) collective-permute-start(bf16[1216,128]{1,0:T(8,128)(2,1)S(1)} %pad_maximum_fusion.4.term_refs_0_), channel_id=1, source_target_pairs={{0,4},{1,5},{2,6},{3,7},{4,0},{5,1},{6,2},{7,3},{8,12},{9,13},{10,... | collective-permute-start | bytes 933896 | tf_op jit(solution)/shard_map/ppermute | solution.py:1197
  157.6 1.8 %grad_owned.1 = bf16[4,784,256]{2,1,0:T(8,128)(2,1)} custom-call(bf16[784,256]{1,0:T(8,128)(2,1)S(1)} %collective-permute-done.51.low_refs_0_, bf16[784,256]{1,0:T(8,128)(2,1)S(1)} %collective-permute-done.59.low_refs_1_, bf16[784,256]{1,0:T(8,128)(2,1)S(1)} %collective-permute-done.55.low_refs_2_, bf16[784,256]{1,0:T(8,128)(2,1)S(1)} %collective-permute-done.60.low_refs_3_, ...), custom_call_target="tpu_custom_call" | custom-call | flops 411041792 | bytes 5341184 | tf_op jit(solution)/shard_map/grad_owned/pallas_call | solution.py:192
  159.4 5.8 %collective-permute-done.61.term_refs_1_ = bf16[1216,128]{1,0:T(8,128)(2,1)S(1)} collective-permute-done((bf16[1216,128]{1,0:T(8,128)(2,1)S(1)}, bf16[1216,128]{1,0:T(8,128)(2,1)S(1)}, u32[]{:S(2)}, u32[]{:S(2)}) %collective-permute-start.61) | collective-permute-done | bytes 311328 | tf_op jit(solution)/shard_map/ppermute | solution.py:1197
  165.2 1.7 unpack.1
  (140 shorter events, 22.0 us)
Async XLA Ops:
  0.7 9.7 %collective-permute-start.5 = (bf16[64,1024]{1,0:T(8,128)(2,1)}, bf16[64,1024]{1,0:T(8,128)(2,1)S(1)}, u32[]{:S(2)}, u32[]{:S(2)}) collective-permute-start(bf16[64,1024]{1,0:T(8,128)(2,1)} %bitcast.37), channel_id=1, source_target_pairs={{0,2},{1,3},{2,0},{3,1},{4,6},{5,7},{6,4},{7,5},{8,10},{9,11},{10,... | collective-permute-start | bytes 393224 | tf_op jit(solution)/shard_map/ppermute | solution.py:1197
  3.7 5.3 %collective-permute-start = (bf16[64,1024]{1,0:T(8,128)(2,1)}, bf16[64,1024]{1,0:T(8,128)(2,1)S(1)}, u32[]{:S(2)}, u32[]{:S(2)}) collective-permute-start(bf16[64,1024]{1,0:T(8,128)(2,1)} %bitcast.38), channel_id=1, source_target_pairs={{0,1},{1,0},{2,3},{3,2},{4,5},{5,4},{6,7},{7,6},{8,9},{9,8},{10,11... | collective-permute-start | bytes 393224 | tf_op jit(solution)/shard_map/ppermute | solution.py:1197
  6.0 20.8 %copy-start.2 = (s32[4,8]{1,0:T(4,128)S(1)}, s32[4,8]{1,0:T(4,128)}, u32[]{:S(2)}) copy-start(s32[4,8]{1,0:T(4,128)} %counts_ref.33) | copy-start | bytes 388
  6.0 20.8 %copy-start.5 = (bf16[1024,64]{0,1:T(8,128)(2,1)S(1)}, bf16[1024,64]{0,1:T(8,128)(2,1)}, u32[]{:S(2)}) copy-start(bf16[1024,64]{0,1:T(8,128)(2,1)} %param.19) | copy-start | bytes 393220
  6.0 19.3 %collective-permute-start.4 = (bf16[784,256]{1,0:T(8,128)(2,1)}, bf16[784,256]{1,0:T(8,128)(2,1)S(1)}, u32[]{:S(2)}, u32[]{:S(2)}) collective-permute-start(bf16[784,256]{1,0:T(8,128)(2,1)} %get-tuple-element.240), channel_id=1, source_target_pairs={{0,6},{1,2},{2,4},{3,0},{4,7},{5,3},{6,5},{7,1},{8,14},{9,10},{10,... | collective-permute-start | bytes 1204232 | tf_op jit(solution)/shard_map/ppermute | solution.py:1197
  7.4 19.4 %collective-permute-start.3 = (bf16[784,256]{1,0:T(8,128)(2,1)}, bf16[784,256]{1,0:T(8,128)(2,1)S(1)}, u32[]{:S(2)}, u32[]{:S(2)}) collective-permute-start(bf16[784,256]{1,0:T(8,128)(2,1)} %get-tuple-element.241), channel_id=1, source_target_pairs={{0,2},{1,6},{2,0},{3,4},{4,3},{5,7},{6,1},{7,5},{8,10},{9,14},{10,... | collective-permute-start | bytes 1204232 | tf_op jit(solution)/shard_map/ppermute | solution.py:1197
  9.1 17.8 %collective-permute-start.2 = (bf16[784,256]{1,0:T(8,128)(2,1)S(1)}, bf16[784,256]{1,0:T(8,128)(2,1)S(1)}, u32[]{:S(2)}, u32[]{:S(2)}) collective-permute-start(bf16[784,256]{1,0:T(8,128)(2,1)S(1)} %get-tuple-element.242), channel_id=1, source_target_pairs={{0,4},{1,0},{2,6},{3,2},{4,5},{5,1},{6,7},{7,3},{8,12},{9,8},{10,1... | collective-permute-start | bytes 1204232 | tf_op jit(solution)/shard_map/ppermute | solution.py:1197
  9.3 17.5 %collective-permute-start.1 = (bf16[784,256]{1,0:T(8,128)(2,1)S(1)}, bf16[784,256]{1,0:T(8,128)(2,1)S(1)}, u32[]{:S(2)}, u32[]{:S(2)}) collective-permute-start(bf16[784,256]{1,0:T(8,128)(2,1)S(1)} %get-tuple-element.243), channel_id=1, source_target_pairs={{0,0},{1,4},{2,2},{3,6},{4,1},{5,5},{6,3},{7,7},{8,8},{9,12},{10,1... | collective-permute-start | bytes 1204232 | tf_op jit(solution)/shard_map/ppermute | solution.py:1197
  10.4 2.5 %collective-permute-start.6 = (bf16[64,1024]{1,0:T(8,128)(2,1)S(1)}, bf16[64,1024]{1,0:T(8,128)(2,1)S(1)}, u32[]{:S(2)}, u32[]{:S(2)}) collective-permute-start(bf16[64,1024]{1,0:T(8,128)(2,1)S(1)} %collective-permute-done.5.a2), channel_id=1, source_target_pairs={{0,1},{1,0},{2,3},{3,2},{4,5},{5,4},{6,7},{7,6},{8,9},{9,8},{10,11... | collective-permute-start | bytes 393224 | tf_op jit(solution)/shard_map/ppermute | solution.py:1197
  12.9 15.8 %collective-permute-start.7 = (bf16[1872,128]{1,0:T(8,128)(2,1)S(1)}, bf16[1872,128]{1,0:T(8,128)(2,1)S(1)}, u32[]{:S(2)}, u32[]{:S(2)}) collective-permute-start(bf16[1872,128]{1,0:T(8,128)(2,1)S(1)} %pack.1.b0), channel_id=1, source_target_pairs={{0,1},{1,0},{2,3},{3,2},{4,5},{5,4},{6,7},{7,6},{8,9},{9,8},{10,11... | collective-permute-start | bytes 1437704 | tf_op jit(solution)/shard_map/ppermute | solution.py:1197
  26.8 12.9 %collective-permute-start.12 = (bf16[1872,128]{1,0:T(8,128)(2,1)S(1)}, bf16[1872,128]{1,0:T(8,128)(2,1)S(1)}, u32[]{:S(2)}, u32[]{:S(2)}) collective-permute-start(bf16[1872,128]{1,0:T(8,128)(2,1)S(1)} %pack.1.b0), channel_id=1, source_target_pairs={{0,2},{1,3},{2,0},{3,1},{4,6},{5,7},{6,4},{7,5},{8,10},{9,11},{10,... | collective-permute-start | bytes 1437704 | tf_op jit(solution)/shard_map/ppermute | solution.py:1197
  28.7 1.2 collective-permute-start.8
  29.9 5.4 %collective-permute-start.11 = (f32[6,256]{1,0:T(8,128)S(1)}, f32[6,256]{1,0:T(8,128)S(1)}, u32[]{:S(2)}, u32[]{:S(2)}) collective-permute-start(f32[6,256]{1,0:T(8,128)S(1)} %add.39.sums_refs_0_), channel_id=1, source_target_pairs={{0,24},{1,25},{2,26},{3,27},{4,28},{5,29},{6,30},{7,31},{8,16},{9,... | collective-permute-start | bytes 18440 | tf_op jit(solution)/shard_map/ppermute | solution.py:1197
  33.6 4.5 %collective-permute-start.10 = (f32[6,256]{1,0:T(8,128)S(1)}, f32[6,256]{1,0:T(8,128)S(1)}, u32[]{:S(2)}, u32[]{:S(2)}) collective-permute-start(f32[6,256]{1,0:T(8,128)S(1)} %add.39.sums_refs_0_), channel_id=1, source_target_pairs={{0,16},{1,17},{2,18},{3,19},{4,20},{5,21},{6,22},{7,23},{8,24},{9,... | collective-permute-start | bytes 18440 | tf_op jit(solution)/shard_map/ppermute | solution.py:1197
  33.6 4.5 %collective-permute-start.9 = (f32[6,256]{1,0:T(8,128)S(1)}, f32[6,256]{1,0:T(8,128)S(1)}, u32[]{:S(2)}, u32[]{:S(2)}) collective-permute-start(f32[6,256]{1,0:T(8,128)S(1)} %add.39.sums_refs_0_), channel_id=1, source_target_pairs={{0,8},{1,9},{2,10},{3,11},{4,12},{5,13},{6,14},{7,15},{8,0},{9,1},... | collective-permute-start | bytes 18440 | tf_op jit(solution)/shard_map/ppermute | solution.py:1197
  34.4 20.5 %collective-permute-start.26 = (bf16[2,784,256]{2,1,0:T(8,128)(2,1)S(1)}, bf16[2,784,256]{2,1,0:T(8,128)(2,1)S(1)}, u32[]{:S(2)}, u32[]{:S(2)}) collective-permute-start(bf16[2,784,256]{2,1,0:T(8,128)(2,1)S(1)} %pad_maximum_fusion.2), channel_id=1, source_target_pairs={{0,0},{1,4},{2,2},{3,6},{4,1},{5,5},{6,3},{7,7},{8,8},{9,12},{10,1... | collective-permute-start | bytes 2408456 | tf_op jit(solution)/shard_map/ppermute | solution.py:1197
  38.2 17.5 %collective-permute-start.27 = (bf16[2,784,256]{2,1,0:T(8,128)(2,1)S(1)}, bf16[2,784,256]{2,1,0:T(8,128)(2,1)S(1)}, u32[]{:S(2)}, u32[]{:S(2)}) collective-permute-start(bf16[2,784,256]{2,1,0:T(8,128)(2,1)S(1)} %pad_maximum_fusion.1), channel_id=1, source_target_pairs={{0,4},{1,0},{2,6},{3,2},{4,5},{5,1},{6,7},{7,3},{8,12},{9,8},{10,1... | collective-permute-start | bytes 2408456 | tf_op jit(solution)/shard_map/ppermute | solution.py:1197
  39.7 1.8 %collective-permute-start.13 = (bf16[1872,128]{1,0:T(8,128)(2,1)S(1)}, bf16[1872,128]{1,0:T(8,128)(2,1)S(1)}, u32[]{:S(2)}, u32[]{:S(2)}) collective-permute-start(bf16[1872,128]{1,0:T(8,128)(2,1)S(1)} %collective-permute-done.12.b2), channel_id=1, source_target_pairs={{0,1},{1,0},{2,3},{3,2},{4,5},{5,4},{6,7},{7,6},{8,9},{9,8},{10,11... | collective-permute-start | bytes 1437704 | tf_op jit(solution)/shard_map/ppermute | solution.py:1197
  44.8 1.2 collective-permute-start.14
  46.0 5.4 %collective-permute-start.17 = (f32[2,512]{1,0:T(2,128)S(1)}, f32[2,512]{1,0:T(2,128)S(1)}, u32[]{:S(2)}, u32[]{:S(2)}) collective-permute-start(f32[2,512]{1,0:T(2,128)S(1)} %add.40.sums_refs_0_.mid_sums_refs_0_), channel_id=1, source_target_pairs={{0,24},{1,25},{2,26},{3,27},{4,28},{5,29},{6,30},{7,31},{8,16},{9,... | collective-permute-start | bytes 12296 | tf_op jit(solution)/shard_map/ppermute | solution.py:1197
  48.6 4.5 %collective-permute-start.16 = (f32[2,512]{1,0:T(2,128)S(1)}, f32[2,512]{1,0:T(2,128)S(1)}, u32[]{:S(2)}, u32[]{:S(2)}) collective-permute-start(f32[2,512]{1,0:T(2,128)S(1)} %add.40.sums_refs_0_.mid_sums_refs_0_), channel_id=1, source_target_pairs={{0,16},{1,17},{2,18},{3,19},{4,20},{5,21},{6,22},{7,23},{8,24},{9,... | collective-permute-start | bytes 12296 | tf_op jit(solution)/shard_map/ppermute | solution.py:1197
  48.6 4.5 %collective-permute-start.15 = (f32[2,512]{1,0:T(2,128)S(1)}, f32[2,512]{1,0:T(2,128)S(1)}, u32[]{:S(2)}, u32[]{:S(2)}) collective-permute-start(f32[2,512]{1,0:T(2,128)S(1)} %add.40.sums_refs_0_.mid_sums_refs_0_), channel_id=1, source_target_pairs={{0,8},{1,9},{2,10},{3,11},{4,12},{5,13},{6,14},{7,15},{8,0},{9,1},... | collective-permute-start | bytes 12296 | tf_op jit(solution)/shard_map/ppermute | solution.py:1197
  55.8 21.2 %collective-permute-start.28 = (bf16[2,784,256]{2,1,0:T(8,128)(2,1)S(1)}, bf16[2,784,256]{2,1,0:T(8,128)(2,1)S(1)}, u32[]{:S(2)}, u32[]{:S(2)}) collective-permute-start(bf16[2,784,256]{2,1,0:T(8,128)(2,1)S(1)} %pad_maximum_fusion.3), channel_id=1, source_target_pairs={{0,2},{1,3},{2,0},{3,1},{4,6},{5,7},{6,4},{7,5},{8,10},{9,11},{10,... | collective-permute-start | bytes 2408456 | tf_op jit(solution)/shard_map/ppermute | solution.py:1197
  57.3 1.4 collective-permute-start.18
  58.7 5.9 %collective-permute-start.21 = (f32[80,128]{1,0:T(8,128)S(1)}, f32[80,128]{1,0:T(8,128)S(1)}, u32[]{:S(2)}, u32[]{:S(2)}) collective-permute-start(f32[80,128]{1,0:T(8,128)S(1)} %constant_dynamic-update-slice_fusion.gathered_refs_0_), channel_id=1, source_target_pairs={{0,24},{1,25},{2,26},{3,27},{4,28},{5,29},{6,30},{7,31},{8,16},{9,... | collective-permute-start | bytes 122888 | tf_op jit(solution)/shard_map/ppermute | solution.py:1197
  62.3 4.9 %collective-permute-start.20 = (f32[80,128]{1,0:T(8,128)S(1)}, f32[80,128]{1,0:T(8,128)S(1)}, u32[]{:S(2)}, u32[]{:S(2)}) collective-permute-start(f32[80,128]{1,0:T(8,128)S(1)} %constant_dynamic-update-slice_fusion.gathered_refs_0_), channel_id=1, source_target_pairs={{0,16},{1,17},{2,18},{3,19},{4,20},{5,21},{6,22},{7,23},{8,24},{9,... | collective-permute-start | bytes 122888 | tf_op jit(solution)/shard_map/ppermute | solution.py:1197
  62.3 4.9 %collective-permute-start.19 = (f32[80,128]{1,0:T(8,128)S(1)}, f32[80,128]{1,0:T(8,128)S(1)}, u32[]{:S(2)}, u32[]{:S(2)}) collective-permute-start(f32[80,128]{1,0:T(8,128)S(1)} %constant_dynamic-update-slice_fusion.gathered_refs_0_), channel_id=1, source_target_pairs={{0,8},{1,9},{2,10},{3,11},{4,12},{5,13},{6,14},{7,15},{8,0},{9,1},... | collective-permute-start | bytes 122888 | tf_op jit(solution)/shard_map/ppermute | solution.py:1197
  69.2 1.2 collective-permute-start.22
  70.4 5.6 %collective-permute-start.25 = (f32[8,256]{1,0:T(8,128)S(1)}, f32[8,256]{1,0:T(8,128)S(1)}, u32[]{:S(2)}, u32[]{:S(2)}) collective-permute-start(f32[8,256]{1,0:T(8,128)S(1)} %add.41.sums_refs_0_), channel_id=1, source_target_pairs={{0,24},{1,25},{2,26},{3,27},{4,28},{5,29},{6,30},{7,31},{8,16},{9,... | collective-permute-start | bytes 24584 | tf_op jit(solution)/shard_map/ppermute | solution.py:1197
  72.4 4.6 %collective-permute-start.24 = (f32[8,256]{1,0:T(8,128)S(1)}, f32[8,256]{1,0:T(8,128)S(1)}, u32[]{:S(2)}, u32[]{:S(2)}) collective-permute-start(f32[8,256]{1,0:T(8,128)S(1)} %add.41.sums_refs_0_), channel_id=1, source_target_pairs={{0,16},{1,17},{2,18},{3,19},{4,20},{5,21},{6,22},{7,23},{8,24},{9,... | collective-permute-start | bytes 24584 | tf_op jit(solution)/shard_map/ppermute | solution.py:1197
  72.6 4.4 %collective-permute-start.23 = (f32[8,256]{1,0:T(8,128)S(1)}, f32[8,256]{1,0:T(8,128)S(1)}, u32[]{:S(2)}, u32[]{:S(2)}) collective-permute-start(f32[8,256]{1,0:T(8,128)S(1)} %add.41.sums_refs_0_), channel_id=1, source_target_pairs={{0,8},{1,9},{2,10},{3,11},{4,12},{5,13},{6,14},{7,15},{8,0},{9,1},... | collective-permute-start | bytes 24584 | tf_op jit(solution)/shard_map/ppermute | solution.py:1197
  79.6 1.2 collective-permute-start.30
  80.8 5.5 %collective-permute-start.33 = (f32[8,256]{1,0:T(8,128)S(1)}, f32[8,256]{1,0:T(8,128)S(1)}, u32[]{:S(2)}, u32[]{:S(2)}) collective-permute-start(f32[8,256]{1,0:T(8,128)S(1)} %add.42.back_refs_0_.out_back_refs_0_), channel_id=1, source_target_pairs={{0,24},{1,25},{2,26},{3,27},{4,28},{5,29},{6,30},{7,31},{8,16},{9,... | collective-permute-start | bytes 24584 | tf_op jit(solution)/shard_map/ppermute | solution.py:1197
  84.0 4.5 %collective-permute-start.32 = (f32[8,256]{1,0:T(8,128)S(1)}, f32[8,256]{1,0:T(8,128)S(1)}, u32[]{:S(2)}, u32[]{:S(2)}) collective-permute-start(f32[8,256]{1,0:T(8,128)S(1)} %add.42.back_refs_0_.out_back_refs_0_), channel_id=1, source_target_pairs={{0,16},{1,17},{2,18},{3,19},{4,20},{5,21},{6,22},{7,23},{8,24},{9,... | collective-permute-start | bytes 24584 | tf_op jit(solution)/shard_map/ppermute | solution.py:1197
  84.0 4.5 %collective-permute-start.31 = (f32[8,256]{1,0:T(8,128)S(1)}, f32[8,256]{1,0:T(8,128)S(1)}, u32[]{:S(2)}, u32[]{:S(2)}) collective-permute-start(f32[8,256]{1,0:T(8,128)S(1)} %add.42.back_refs_0_.out_back_refs_0_), channel_id=1, source_target_pairs={{0,8},{1,9},{2,10},{3,11},{4,12},{5,13},{6,14},{7,15},{8,0},{9,1},... | collective-permute-start | bytes 24584 | tf_op jit(solution)/shard_map/ppermute | solution.py:1197
  85.2 14.8 %collective-permute-start.29 = (bf16[816,256]{1,0:T(8,128)(2,1)S(1)}, bf16[816,256]{1,0:T(8,128)(2,1)S(1)}, u32[]{:S(2)}, u32[]{:S(2)}) collective-permute-start(bf16[816,256]{1,0:T(8,128)(2,1)S(1)} %get-tuple-element.153), channel_id=1, source_target_pairs={{0,0},{1,4},{2,2},{3,6},{4,1},{5,5},{6,3},{7,7},{8,8},{9,12},{10,1... | collective-permute-start | bytes 1253384 | tf_op jit(solution)/shard_map/ppermute | solution.py:1197
  91.3 1.9 %collective-permute-start.34 = (f32[12,128]{1,0:T(8,128)S(1)}, f32[12,128]{1,0:T(8,128)S(1)}, u32[]{:S(2)}, u32[]{:S(2)}) collective-permute-start(f32[12,128]{1,0:T(8,128)S(1)} %get-tuple-element.158), channel_id=1, source_target_pairs={{0,1},{1,0},{2,3},{3,2},{4,5},{5,4},{6,7},{7,6},{8,9},{9,8},{10,11... | collective-permute-start | bytes 18440 | tf_op jit(solution)/shard_map/ppermute | solution.py:1197
  93.2 6.3 %collective-permute-start.37 = (f32[16,128]{1,0:T(8,128)S(1)}, f32[16,128]{1,0:T(8,128)S(1)}, u32[]{:S(2)}, u32[]{:S(2)}) collective-permute-start(f32[16,128]{1,0:T(8,128)S(1)} %pad_maximum_fusion.5.back_refs_0_), channel_id=1, source_target_pairs={{0,24},{1,25},{2,26},{3,27},{4,28},{5,29},{6,30},{7,31},{8,16},{9,... | collective-permute-start | bytes 24584 | tf_op jit(solution)/shard_map/ppermute | solution.py:1197
  95.5 4.5 %collective-permute-start.36 = (f32[16,128]{1,0:T(8,128)S(1)}, f32[16,128]{1,0:T(8,128)S(1)}, u32[]{:S(2)}, u32[]{:S(2)}) collective-permute-start(f32[16,128]{1,0:T(8,128)S(1)} %pad_maximum_fusion.5.back_refs_0_), channel_id=1, source_target_pairs={{0,16},{1,17},{2,18},{3,19},{4,20},{5,21},{6,22},{7,23},{8,24},{9,... | collective-permute-start | bytes 24584 | tf_op jit(solution)/shard_map/ppermute | solution.py:1197
  95.5 4.5 %collective-permute-start.35 = (f32[16,128]{1,0:T(8,128)S(1)}, f32[16,128]{1,0:T(8,128)S(1)}, u32[]{:S(2)}, u32[]{:S(2)}) collective-permute-start(f32[16,128]{1,0:T(8,128)S(1)} %pad_maximum_fusion.5.back_refs_0_), channel_id=1, source_target_pairs={{0,8},{1,9},{2,10},{3,11},{4,12},{5,13},{6,14},{7,15},{8,0},{9,1},... | collective-permute-start | bytes 24584 | tf_op jit(solution)/shard_map/ppermute | solution.py:1197
  100.1 4.3 %collective-permute-start.39 = (bf16[2,656,128]{2,1,0:T(8,128)(2,1)S(1)}, bf16[2,656,128]{2,1,0:T(8,128)(2,1)S(1)}, u32[]{:S(2)}, u32[]{:S(2)}) collective-permute-start(bf16[2,656,128]{2,1,0:T(8,128)(2,1)S(1)} %get-tuple-element.173), channel_id=1, source_target_pairs={{0,1},{1,0},{2,3},{3,2},{4,5},{5,4},{6,7},{7,6},{8,9},{9,8},{10,11... | collective-permute-start | bytes 1007624 | tf_op jit(solution)/shard_map/ppermute | solution.py:1197
  100.1 12.4 %collective-permute-start.38 = (bf16[816,256]{1,0:T(8,128)(2,1)S(1)}, bf16[816,256]{1,0:T(8,128)(2,1)S(1)}, u32[]{:S(2)}, u32[]{:S(2)}) collective-permute-start(bf16[816,256]{1,0:T(8,128)(2,1)S(1)} %collective-permute-done.29.near_ref), channel_id=1, source_target_pairs={{0,2},{1,3},{2,0},{3,1},{4,6},{5,7},{6,4},{7,5},{8,10},{9,11},{10,... | collective-permute-start | bytes 1253384 | tf_op jit(solution)/shard_map/ppermute | solution.py:1197
  104.4 1.2 collective-permute-start.40
  105.6 6.8 %collective-permute-start.43 = (f32[2,256]{1,0:T(2,128)S(1)}, f32[2,256]{1,0:T(2,128)S(1)}, u32[]{:S(2)}, u32[]{:S(2)}) collective-permute-start(f32[2,256]{1,0:T(2,128)S(1)} %add.44.back_refs_0_), channel_id=1, source_target_pairs={{0,24},{1,25},{2,26},{3,27},{4,28},{5,29},{6,30},{7,31},{8,16},{9,... | collective-permute-start | bytes 6152 | tf_op jit(solution)/shard_map/ppermute | solution.py:1197
  107.5 5.0 %collective-permute-start.42 = (f32[2,256]{1,0:T(2,128)S(1)}, f32[2,256]{1,0:T(2,128)S(1)}, u32[]{:S(2)}, u32[]{:S(2)}) collective-permute-start(f32[2,256]{1,0:T(2,128)S(1)} %add.44.back_refs_0_), channel_id=1, source_target_pairs={{0,16},{1,17},{2,18},{3,19},{4,20},{5,21},{6,22},{7,23},{8,24},{9,... | collective-permute-start | bytes 6152 | tf_op jit(solution)/shard_map/ppermute | solution.py:1197
  108.4 4.1 %collective-permute-start.41 = (f32[2,256]{1,0:T(2,128)S(1)}, f32[2,256]{1,0:T(2,128)S(1)}, u32[]{:S(2)}, u32[]{:S(2)}) collective-permute-start(f32[2,256]{1,0:T(2,128)S(1)} %add.44.back_refs_0_), channel_id=1, source_target_pairs={{0,8},{1,9},{2,10},{3,11},{4,12},{5,13},{6,14},{7,15},{8,0},{9,1},... | collective-permute-start | bytes 6152 | tf_op jit(solution)/shard_map/ppermute | solution.py:1197
  114.4 2.7 %collective-permute-start.44 = (bf16[2,1152,128]{2,1,0:T(8,128)(2,1)S(1)}, bf16[2,1152,128]{2,1,0:T(8,128)(2,1)S(1)}, u32[]{:S(2)}, u32[]{:S(2)}) collective-permute-start(bf16[2,1152,128]{2,1,0:T(8,128)(2,1)S(1)} %get-tuple-element.188), channel_id=1, source_target_pairs={{0,1},{1,0},{2,3},{3,2},{4,5},{5,4},{6,7},{7,6},{8,9},{9,8},{10,11... | collective-permute-start | bytes 1769480 | tf_op jit(solution)/shard_map/ppermute | solution.py:1197
  114.5 2.4 %collective-permute-start.45 = (bf16[2,592,128]{2,1,0:T(8,128)(2,1)S(1)}, bf16[2,592,128]{2,1,0:T(8,128)(2,1)S(1)}, u32[]{:S(2)}, u32[]{:S(2)}) collective-permute-start(bf16[2,592,128]{2,1,0:T(8,128)(2,1)S(1)} %get-tuple-element.191), channel_id=1, source_target_pairs={{0,1},{1,0},{2,3},{3,2},{4,5},{5,4},{6,7},{7,6},{8,9},{9,8},{10,11... | collective-permute-start | bytes 909320 | tf_op jit(solution)/shard_map/ppermute | solution.py:1197
  117.9 10.2 %collective-permute-start.46 = (bf16[2,816,256]{2,1,0:T(8,128)(2,1)S(1)}, bf16[2,816,256]{2,1,0:T(8,128)(2,1)S(1)}, u32[]{:S(2)}, u32[]{:S(2)}) collective-permute-start(bf16[2,816,256]{2,1,0:T(8,128)(2,1)S(1)} %pad_maximum_fusion), channel_id=1, source_target_pairs={{0,1},{1,0},{2,3},{3,2},{4,5},{5,4},{6,7},{7,6},{8,9},{9,8},{10,11... | collective-permute-start | bytes 2506760 | tf_op jit(solution)/shard_map/ppermute | solution.py:1197
  118.1 10.0 %collective-permute-start.48 = (bf16[1280,128]{1,0:T(8,128)(2,1)S(1)}, bf16[1280,128]{1,0:T(8,128)(2,1)S(1)}, u32[]{:S(2)}, u32[]{:S(2)}) collective-permute-start(bf16[1280,128]{1,0:T(8,128)(2,1)S(1)} %get-tuple-element.192), channel_id=1, source_target_pairs={{0,2},{1,3},{2,0},{3,1},{4,6},{5,7},{6,4},{7,5},{8,10},{9,11},{10,... | collective-permute-start | bytes 983048 | tf_op jit(solution)/shard_map/ppermute | solution.py:1197
  119.5 10.2 %collective-permute-start.47 = (bf16[2,576,128]{2,1,0:T(8,128)(2,1)S(1)}, bf16[2,576,128]{2,1,0:T(8,128)(2,1)S(1)}, u32[]{:S(2)}, u32[]{:S(2)}) collective-permute-start(bf16[2,576,128]{2,1,0:T(8,128)(2,1)S(1)} %get-tuple-element.189), channel_id=1, source_target_pairs={{0,4},{1,5},{2,6},{3,7},{4,0},{5,1},{6,2},{7,3},{8,12},{9,13},{10,... | collective-permute-start | bytes 884744 | tf_op jit(solution)/shard_map/ppermute | solution.py:1197
  119.7 10.9 %collective-permute-start.51 = (bf16[784,256]{1,0:T(8,128)(2,1)S(1)}, bf16[784,256]{1,0:T(8,128)(2,1)S(1)}, u32[]{:S(2)}, u32[]{:S(2)}) collective-permute-start(bf16[784,256]{1,0:T(8,128)(2,1)S(1)} %get-tuple-element.202), channel_id=1, source_target_pairs={{0,0},{1,4},{2,2},{3,6},{4,1},{5,5},{6,3},{7,7},{8,8},{9,12},{10,1... | collective-permute-start | bytes 1204232 | tf_op jit(solution)/shard_map/ppermute | solution.py:1197
  128.7 7.5 %collective-permute-start.50 = (bf16[640,128]{1,0:T(8,128)(2,1)S(1)}, bf16[640,128]{1,0:T(8,128)(2,1)S(1)}, u32[]{:S(2)}, u32[]{:S(2)}) collective-permute-start(bf16[640,128]{1,0:T(8,128)(2,1)S(1)} %get-tuple-element.201), channel_id=1, source_target_pairs={{0,4},{1,5},{2,6},{3,7},{4,0},{5,1},{6,2},{7,3},{8,12},{9,13},{10,... | collective-permute-start | bytes 491528 | tf_op jit(solution)/shard_map/ppermute | solution.py:1197
  129.7 5.2 %collective-permute-start.49 = (bf16[576,128]{1,0:T(8,128)(2,1)S(1)}, bf16[576,128]{1,0:T(8,128)(2,1)S(1)}, u32[]{:S(2)}, u32[]{:S(2)}) collective-permute-start(bf16[576,128]{1,0:T(8,128)(2,1)S(1)} %get-tuple-element.200), channel_id=1, source_target_pairs={{0,2},{1,3},{2,0},{3,1},{4,6},{5,7},{6,4},{7,5},{8,10},{9,11},{10,... | collective-permute-start | bytes 442376 | tf_op jit(solution)/shard_map/ppermute | solution.py:1197
  136.9 8.4 %collective-permute-start.52 = (bf16[304,128]{1,0:T(8,128)(2,1)S(1)}, bf16[304,128]{1,0:T(8,128)(2,1)S(1)}, u32[]{:S(2)}, u32[]{:S(2)}) collective-permute-start(bf16[304,128]{1,0:T(8,128)(2,1)S(1)} %get-tuple-element.209), channel_id=1, source_target_pairs={{0,8},{1,9},{2,10},{3,11},{4,12},{5,13},{6,14},{7,15},{8,0},{9,1},... | collective-permute-start | bytes 233480 | tf_op jit(solution)/shard_map/ppermute | solution.py:1197
  138.0 7.3 %collective-permute-start.53 = (bf16[304,128]{1,0:T(8,128)(2,1)S(1)}, bf16[304,128]{1,0:T(8,128)(2,1)S(1)}, u32[]{:S(2)}, u32[]{:S(2)}) collective-permute-start(bf16[304,128]{1,0:T(8,128)(2,1)S(1)} %get-tuple-element.210), channel_id=1, source_target_pairs={{0,16},{1,17},{2,18},{3,19},{4,20},{5,21},{6,22},{7,23},{8,24},{9,... | collective-permute-start | bytes 233480 | tf_op jit(solution)/shard_map/ppermute | solution.py:1197
  139.3 6.3 %collective-permute-start.54 = (bf16[304,128]{1,0:T(8,128)(2,1)S(1)}, bf16[304,128]{1,0:T(8,128)(2,1)S(1)}, u32[]{:S(2)}, u32[]{:S(2)}) collective-permute-start(bf16[304,128]{1,0:T(8,128)(2,1)S(1)} %get-tuple-element.211), channel_id=1, source_target_pairs={{0,24},{1,25},{2,26},{3,27},{4,28},{5,29},{6,30},{7,31},{8,16},{9,... | collective-permute-start | bytes 233480 | tf_op jit(solution)/shard_map/ppermute | solution.py:1197
  145.6 9.6 %collective-permute-start.55 = (bf16[784,256]{1,0:T(8,128)(2,1)S(1)}, bf16[784,256]{1,0:T(8,128)(2,1)S(1)}, u32[]{:S(2)}, u32[]{:S(2)}) collective-permute-start(bf16[784,256]{1,0:T(8,128)(2,1)S(1)} %collective-permute-done.51.low_refs_0_), channel_id=1, source_target_pairs={{0,2},{1,3},{2,0},{3,1},{4,6},{5,7},{6,4},{7,5},{8,10},{9,11},{10,... | collective-permute-start | bytes 1204232 | tf_op jit(solution)/shard_map/ppermute | solution.py:1197
  146.9 6.4 %collective-permute-start.58 = (bf16[304,128]{1,0:T(8,128)(2,1)S(1)}, bf16[304,128]{1,0:T(8,128)(2,1)S(1)}, u32[]{:S(2)}, u32[]{:S(2)}) collective-permute-start(bf16[304,128]{1,0:T(8,128)(2,1)S(1)} %add_depth.1), channel_id=1, source_target_pairs={{0,24},{1,25},{2,26},{3,27},{4,28},{5,29},{6,30},{7,31},{8,16},{9,... | collective-permute-start | bytes 233480 | tf_op jit(solution)/shard_map/ppermute | solution.py:1197
  148.7 6.5 %collective-permute-start.57 = (bf16[304,128]{1,0:T(8,128)(2,1)S(1)}, bf16[304,128]{1,0:T(8,128)(2,1)S(1)}, u32[]{:S(2)}, u32[]{:S(2)}) collective-permute-start(bf16[304,128]{1,0:T(8,128)(2,1)S(1)} %add_depth.1), channel_id=1, source_target_pairs={{0,16},{1,17},{2,18},{3,19},{4,20},{5,21},{6,22},{7,23},{8,24},{9,... | collective-permute-start | bytes 233480 | tf_op jit(solution)/shard_map/ppermute | solution.py:1197
  149.8 5.4 %collective-permute-start.56 = (bf16[304,128]{1,0:T(8,128)(2,1)S(1)}, bf16[304,128]{1,0:T(8,128)(2,1)S(1)}, u32[]{:S(2)}, u32[]{:S(2)}) collective-permute-start(bf16[304,128]{1,0:T(8,128)(2,1)S(1)} %add_depth.1), channel_id=1, source_target_pairs={{0,8},{1,9},{2,10},{3,11},{4,12},{5,13},{6,14},{7,15},{8,0},{9,1},... | collective-permute-start | bytes 233480 | tf_op jit(solution)/shard_map/ppermute | solution.py:1197
  155.2 2.4 %collective-permute-start.59 = (bf16[784,256]{1,0:T(8,128)(2,1)S(1)}, bf16[784,256]{1,0:T(8,128)(2,1)S(1)}, u32[]{:S(2)}, u32[]{:S(2)}) collective-permute-start(bf16[784,256]{1,0:T(8,128)(2,1)S(1)} %collective-permute-done.51.low_refs_0_), channel_id=1, source_target_pairs={{0,1},{1,0},{2,3},{3,2},{4,5},{5,4},{6,7},{7,6},{8,9},{9,8},{10,11... | collective-permute-start | bytes 1204232 | tf_op jit(solution)/shard_map/ppermute | solution.py:1197
  155.2 2.4 %collective-permute-start.60 = (bf16[784,256]{1,0:T(8,128)(2,1)S(1)}, bf16[784,256]{1,0:T(8,128)(2,1)S(1)}, u32[]{:S(2)}, u32[]{:S(2)}) collective-permute-start(bf16[784,256]{1,0:T(8,128)(2,1)S(1)} %collective-permute-done.55.low_refs_2_), channel_id=1, source_target_pairs={{0,1},{1,0},{2,3},{3,2},{4,5},{5,4},{6,7},{7,6},{8,9},{9,8},{10,11... | collective-permute-start | bytes 1204232 | tf_op jit(solution)/shard_map/ppermute | solution.py:1197
  155.7 9.4 %collective-permute-start.61 = (bf16[1216,128]{1,0:T(8,128)(2,1)S(1)}, bf16[1216,128]{1,0:T(8,128)(2,1)S(1)}, u32[]{:S(2)}, u32[]{:S(2)}) collective-permute-start(bf16[1216,128]{1,0:T(8,128)(2,1)S(1)} %pad_maximum_fusion.4.term_refs_0_), channel_id=1, source_target_pairs={{0,4},{1,5},{2,6},{3,7},{4,0},{5,1},{6,2},{7,3},{8,12},{9,13},{10,... | collective-permute-start | bytes 933896 | tf_op jit(solution)/shard_map/ppermute | solution.py:1197
  (15 other events, 114.1 us)

commit v9 on v8

--- a/solution.py
+++ b/solution.py
@@ -1530,7 +1530,7 @@
     mid_back = after_all(mid_back, keep, shared)
     shared = after(shared, mid_back[0])
     shared = (shared, across(shared))
-    out_keep, out_arrived = keep, core(after(send, mid_back[0]))
+    out_keep, out_send = keep, send
     low_mid, grad_hidden, grad_squeeze, vectors, msg = call(
         back_mid,
         [
@@ -1558,7 +1558,8 @@
         in_affine,
         w_mid_back,
     )
-    in_back = exchange(2, 0)(after(msg, out_arrived))
+    out_arrived = core(after(out_send, msg))
+    in_back = exchange(2, 0)(msg)
     keep, send = call(
         weight_mid_term,
         [shape((2, 18 * own, 2 * own), BF16)] * 2,

time: 167 us -> 168 us (level)
  transfers between devices with their start and end apart: 62 -> 62, of which waited for: 31 -> 32; matrix products, arithmetic and copies ran while one was open for 2% -> 2% of each run, Pallas kernels for 16% -> 16%
where the time goes in v9:
time: 168 us; the launch traced here: 167 us
  starting transfers between devices  64.9 us (39%)
  waiting for transfers between devices  64.2 us (38%)
  Pallas kernels  34 us (20%)
  local copies, waits for them, and re-layouts  2.55 us (2%)
    ppermute x62, starting transfers between devices, permute(): return lax.ppermute(tensor, ('dp', 'chan'), pairs)  64.9 us
    ppermute x62, waiting for transfers between devices, permute(): return lax.ppermute(tensor, ('dp', 'chan'), pairs)  64.2 us
    pallas_call x22, Pallas kernels, call(): pl.pallas_call(body, out_shape=outs, in_specs=specs, out_specs=[pl.BlockS...  34 us
  transfers between devices with their start and end apart: 62, of which 32 were waited for; matrix products, arithmetic and copies ran while one was open for 2% of the time, Pallas kernels for 16%

profile of v9, /device:TPU:0, one launch (start us, length us, event | category | flops | bytes accessed | tf_op | source)
XLA Modules:
  0.0 167.4 jit_solution(9490744872147980710)
XLA Ops:
  0.7 3.0 %collective-permute-start.5 = (bf16[64,1024]{1,0:T(8,128)(2,1)}, bf16[64,1024]{1,0:T(8,128)(2,1)S(1)}, u32[]{:S(2)}, u32[]{:S(2)}) collective-permute-start(bf16[64,1024]{1,0:T(8,128)(2,1)} %bitcast.37), channel_id=1, source_target_pairs={{0,2},{1,3},{2,0},{3,1},{4,6},{5,7},{6,4},{7,5},{8,10},{9,11},{10,... | collective-permute-start | bytes 393224 | tf_op jit(solution)/shard_map/ppermute | solution.py:1197
  3.8 2.2 %dynamic-slice_bitcast_fusion = (bf16[784,256]{1,0:T(8,128)(2,1)}, bf16[784,256]{1,0:T(8,128)(2,1)}) fusion(bf16[4,784,256]{2,1,0:T(8,128)(2,1)} %x_ref.1, s32[]{:T(128)S(6)} %select_n.20, s32[]{:T(128)S(6)} %select_n.19), kind=kLoop, calls=%fused_computation.4 | loop fusion | bytes 1605640 | tf_op jit(solution)/shard_map/jit(dynamic_index_in_dim)/squeeze | solution.py:1336
  6.0 1.4 collective-permute-start.4
  7.4 1.5 collective-permute-start.3
  10.4 1.5 collective-permute-start.6
  11.9 1.0 collective-permute-done.6.a3
  13.3 12.1 %collective-permute-done.4.x3.x_refs_3_ = bf16[784,256]{1,0:T(8,128)(2,1)S(1)} collective-permute-done((bf16[784,256]{1,0:T(8,128)(2,1)}, bf16[784,256]{1,0:T(8,128)(2,1)S(1)}, u32[]{:S(2)}, u32[]{:S(2)}) %collective-permute-start.4) | collective-permute-done | bytes 401440 | tf_op jit(solution)/shard_map/ppermute | solution.py:1197
  25.4 1.5 collective-permute-done.3.x2.x_refs_2_
  26.9 1.6 reduce_in.1
  28.8 1.2 collective-permute-done.8
  29.9 3.7 %collective-permute-start.11 = (f32[6,256]{1,0:T(8,128)S(1)}, f32[6,256]{1,0:T(8,128)S(1)}, u32[]{:S(2)}, u32[]{:S(2)}) collective-permute-start(f32[6,256]{1,0:T(8,128)S(1)} %add.39.sums_refs_0_), channel_id=1, source_target_pairs={{0,24},{1,25},{2,26},{3,27},{4,28},{5,29},{6,30},{7,31},{8,16},{9,... | collective-permute-start | bytes 18440 | tf_op jit(solution)/shard_map/ppermute | solution.py:1197
  35.4 2.8 %collective-permute-done.10.sums_refs_2_ = f32[6,256]{1,0:T(8,128)S(1)} collective-permute-done((f32[6,256]{1,0:T(8,128)S(1)}, f32[6,256]{1,0:T(8,128)S(1)}, u32[]{:S(2)}, u32[]{:S(2)}) %collective-permute-start.10) | collective-permute-done | bytes 6176 | tf_op jit(solution)/shard_map/ppermute | solution.py:1197
  38.2 1.6 collective-permute-start.27
  39.7 1.8 %collective-permute-done.13.b3 = bf16[1872,128]{1,0:T(8,128)(2,1)S(1)} collective-permute-done((bf16[1872,128]{1,0:T(8,128)(2,1)S(1)}, bf16[1872,128]{1,0:T(8,128)(2,1)S(1)}, u32[]{:S(2)}, u32[]{:S(2)}) %collective-permute-start.13) | collective-permute-done | bytes 479264 | tf_op jit(solution)/shard_map/ppermute | solution.py:1197
  42.5 2.3 %conv_mid.1 = (bf16[3,976,256]{2,1,0:T(8,128)(2,1)S(1)}, f32[896,512]{1,0:T(8,128)S(1)}, f32[2,512]{1,0:T(2,128)S(1)}) custom-call(s32[4,8]{1,0:T(4,128)S(1)} %copy-done.2, f32[896,256]{1,0:T(8,128)S(1)} %get-tuple-element.127.pre_ref, f32[6,256]{1,0:T(8,128)S(1)} %add.39.sums_refs_0_, f32[6,256]{1,0:T(8,128)S(1)} %collective-permute-done.9.sums_refs_1_, ...), custom_call_target="tpu_custom_call" | custom-call | flops 1056964608 | bytes 5462144 | tf_op jit(solution)/shard_map/conv_mid/pallas_call | solution.py:192
  45.0 1.0 collective-permute-done.14
  46.0 2.6 %collective-permute-start.17 = (f32[2,512]{1,0:T(2,128)S(1)}, f32[2,512]{1,0:T(2,128)S(1)}, u32[]{:S(2)}, u32[]{:S(2)}) collective-permute-start(f32[2,512]{1,0:T(2,128)S(1)} %add.40.sums_refs_0_.mid_sums_refs_0_), channel_id=1, source_target_pairs={{0,24},{1,25},{2,26},{3,27},{4,28},{5,29},{6,30},{7,31},{8,16},{9,... | collective-permute-start | bytes 12296 | tf_op jit(solution)/shard_map/ppermute | solution.py:1197
  48.6 1.8 %collective-permute-start.15 = (f32[2,512]{1,0:T(2,128)S(1)}, f32[2,512]{1,0:T(2,128)S(1)}, u32[]{:S(2)}, u32[]{:S(2)}) collective-permute-start(f32[2,512]{1,0:T(2,128)S(1)} %add.40.sums_refs_0_.mid_sums_refs_0_), channel_id=1, source_target_pairs={{0,8},{1,9},{2,10},{3,11},{4,12},{5,13},{6,14},{7,15},{8,0},{9,1},... | collective-permute-start | bytes 12296 | tf_op jit(solution)/shard_map/ppermute | solution.py:1197
  50.4 1.0 collective-permute-done.17.sums_refs_3_.mid_sums_refs_3_
  51.4 1.7 %collective-permute-done.16.sums_refs_2_.mid_sums_refs_2_ = f32[2,512]{1,0:T(2,128)S(1)} collective-permute-done((f32[2,512]{1,0:T(2,128)S(1)}, f32[2,512]{1,0:T(2,128)S(1)}, u32[]{:S(2)}, u32[]{:S(2)}) %collective-permute-start.16) | collective-permute-done | bytes 4128 | tf_op jit(solution)/shard_map/ppermute | solution.py:1197
  53.2 1.7 %pool.1 = (f32[4,256]{1,0:T(4,128)S(1)}, f32[40,128]{1,0:T(8,128)S(1)}) custom-call(s32[4,8]{1,0:T(4,128)S(1)} %copy-done.2, f32[896,512]{1,0:T(8,128)S(1)} %get-tuple-element.135.mid_ref, f32[2,512]{1,0:T(2,128)S(1)} %add.40.sums_refs_0_.mid_sums_refs_0_, f32[2,512]{1,0:T(2,128)S(1)} %collective-permute-done.15.sums_refs_1_.mid_sums_refs_1_, ...), custom_call_target="tpu_custom_call" | custom-call | bytes 1945728 | tf_op jit(solution)/shard_map/pool/pallas_call | solution.py:192
  55.8 1.5 collective-permute-start.28
  58.7 3.6 %collective-permute-start.21 = (f32[80,128]{1,0:T(8,128)S(1)}, f32[80,128]{1,0:T(8,128)S(1)}, u32[]{:S(2)}, u32[]{:S(2)}) collective-permute-start(f32[80,128]{1,0:T(8,128)S(1)} %constant_dynamic-update-slice_fusion.gathered_refs_0_), channel_id=1, source_target_pairs={{0,24},{1,25},{2,26},{3,27},{4,28},{5,29},{6,30},{7,31},{8,16},{9,... | collective-permute-start | bytes 122888 | tf_op jit(solution)/shard_map/ppermute | solution.py:1197
  64.6 2.6 %collective-permute-done.20.gathered_refs_2_ = f32[80,128]{1,0:T(8,128)S(1)} collective-permute-done((f32[80,128]{1,0:T(8,128)S(1)}, f32[80,128]{1,0:T(8,128)S(1)}, u32[]{:S(2)}, u32[]{:S(2)}) %collective-permute-start.20) | collective-permute-done | bytes 40992 | tf_op jit(solution)/shard_map/ppermute | solution.py:1197
  67.2 1.9 %attend.1 = (f32[2,4,128]{2,1,0:T(4,128)S(1)}, f32[4,512]{1,0:T(4,128)S(1)}, bf16[784,256]{1,0:T(8,128)(2,1)S(1)}, f32[4,784,256]{2,1,0:T(8,128)S(1)}, f32[8,256]{1,0:T(8,128)S(1)}) custom-call(s32[4,8]{1,0:T(4,128)S(1)} %copy-done.2, f32[80,128]{1,0:T(8,128)S(1)} %constant_dynamic-update-slice_fusion.gathered_refs_0_, ...), custom_call_target="tpu_custom_call" | custom-call | flops 411041792 | bytes 6327424 | tf_op jit(solution)/shard_map/attend/pallas_call | solution.py:192
  69.3 1.2 collective-permute-done.22
  70.4 2.0 %collective-permute-start.25 = (f32[8,256]{1,0:T(8,128)S(1)}, f32[8,256]{1,0:T(8,128)S(1)}, u32[]{:S(2)}, u32[]{:S(2)}) collective-permute-start(f32[8,256]{1,0:T(8,128)S(1)} %add.41.sums_refs_0_), channel_id=1, source_target_pairs={{0,24},{1,25},{2,26},{3,27},{4,28},{5,29},{6,30},{7,31},{8,16},{9,... | collective-permute-start | bytes 24584 | tf_op jit(solution)/shard_map/ppermute | solution.py:1197
  72.6 2.2 %collective-permute-start.23 = (f32[8,256]{1,0:T(8,128)S(1)}, f32[8,256]{1,0:T(8,128)S(1)}, u32[]{:S(2)}, u32[]{:S(2)}) collective-permute-start(f32[8,256]{1,0:T(8,128)S(1)} %add.41.sums_refs_0_), channel_id=1, source_target_pairs={{0,8},{1,9},{2,10},{3,11},{4,12},{5,13},{6,14},{7,15},{8,0},{9,1},... | collective-permute-start | bytes 24584 | tf_op jit(solution)/shard_map/ppermute | solution.py:1197
  74.8 1.2 collective-permute-done.25.sums_refs_3_
  77.0 2.6 %finish.1 = (bf16[816,256]{1,0:T(8,128)(2,1)S(1)}, f32[4,784,256]{2,1,0:T(8,128)S(1)}, f32[8,256]{1,0:T(8,128)S(1)}) custom-call(s32[4,8]{1,0:T(4,128)S(1)} %copy-done.2, f32[4,784,256]{2,1,0:T(8,128)S(1)} %get-tuple-element.144.out_ref, f32[8,256]{1,0:T(8,128)S(1)} %add.41.sums_refs_0_, f32[8,256]{1,0:T(8,128)S(1)} %collective-permute-done.23.sums_refs_1_, ...), custom_call_target="tpu_custom_call" | custom-call | bytes 11305088 | tf_op jit(solution)/shard_map/finish/pallas_call | solution.py:192
  79.7 1.2 collective-permute-done.30
  80.8 3.1 %collective-permute-start.33 = (f32[8,256]{1,0:T(8,128)S(1)}, f32[8,256]{1,0:T(8,128)S(1)}, u32[]{:S(2)}, u32[]{:S(2)}) collective-permute-start(f32[8,256]{1,0:T(8,128)S(1)} %add.42.back_refs_0_.out_back_refs_0_), channel_id=1, source_target_pairs={{0,24},{1,25},{2,26},{3,27},{4,28},{5,29},{6,30},{7,31},{8,16},{9,... | collective-permute-start | bytes 24584 | tf_op jit(solution)/shard_map/ppermute | solution.py:1197
  84.0 1.2 collective-permute-start.31
  86.3 2.2 %collective-permute-done.32.back_refs_2_.out_back_refs_2_ = f32[8,256]{1,0:T(8,128)S(1)} collective-permute-done((f32[8,256]{1,0:T(8,128)S(1)}, f32[8,256]{1,0:T(8,128)S(1)}, u32[]{:S(2)}, u32[]{:S(2)}) %collective-permute-start.32) | collective-permute-done | bytes 8224 | tf_op jit(solution)/shard_map/ppermute | solution.py:1197
  88.5 2.8 %back_out.1 = (bf16[4,784,256]{2,1,0:T(8,128)(2,1)S(1)}, f32[896,256]{1,0:T(8,128)S(1)}, f32[4,512]{1,0:T(4,128)S(1)}, f32[12,128]{1,0:T(8,128)S(1)}) custom-call(s32[4,8]{1,0:T(4,128)S(1)} %copy-done.2, f32[4,784,256]{2,1,0:T(8,128)S(1)} %get-tuple-element.153.grad_ref, f32[4,784,256]{2,1,0:T(8,128)S(1)} %get-tuple-element.144.out_ref, ...), custom_call_target="tpu_custom_call" | custom-call | flops 411041792 | bytes 11556992 | tf_op jit(solution)/shard_map/back_out/pallas_call | solution.py:192
  91.3 1.1 collective-permute-start.34
  93.2 2.3 %collective-permute-start.37 = (f32[16,128]{1,0:T(8,128)S(1)}, f32[16,128]{1,0:T(8,128)S(1)}, u32[]{:S(2)}, u32[]{:S(2)}) collective-permute-start(f32[16,128]{1,0:T(8,128)S(1)} %pad_maximum_fusion.5.back_refs_0_), channel_id=1, source_target_pairs={{0,24},{1,25},{2,26},{3,27},{4,28},{5,29},{6,30},{7,31},{8,16},{9,... | collective-permute-start | bytes 24584 | tf_op jit(solution)/shard_map/ppermute | solution.py:1197
  95.5 2.2 %collective-permute-start.35 = (f32[16,128]{1,0:T(8,128)S(1)}, f32[16,128]{1,0:T(8,128)S(1)}, u32[]{:S(2)}, u32[]{:S(2)}) collective-permute-start(f32[16,128]{1,0:T(8,128)S(1)} %pad_maximum_fusion.5.back_refs_0_), channel_id=1, source_target_pairs={{0,8},{1,9},{2,10},{3,11},{4,12},{5,13},{6,14},{7,15},{8,0},{9,1},... | collective-permute-start | bytes 24584 | tf_op jit(solution)/shard_map/ppermute | solution.py:1197
  97.7 1.8 %weight_out_term.1 = (bf16[2,656,128]{2,1,0:T(8,128)(2,1)S(1)}, bf16[2,656,128]{2,1,0:T(8,128)(2,1)S(1)}) custom-call(s32[4,8]{1,0:T(4,128)S(1)} %copy-done.2, bf16[784,256]{1,0:T(8,128)(2,1)S(1)} %get-tuple-element.158.weighted_ref, bf16[4,784,256]{2,1,0:T(8,128)(2,1)S(1)} %get-tuple-element.159.low_ref, f32[2,4,128]{2,1,0:T(4,128)S(1)} %get-tuple-element.156.gate_ref, ...), custom_call_target="tpu_custom_call" | custom-call | flops 411041792 | bytes 2695296 | tf_op jit(solution)/shard_map/weight_out_term/pallas_call | solution.py:192
  100.7 3.6 %back_mid.1 = (bf16[976,512]{1,0:T(8,128)(2,1)S(1)}, f32[896,256]{1,0:T(8,128)S(1)}, f32[4,128]{1,0:T(4,128)S(1)}, f32[8,512]{1,0:T(8,128)S(1)}, f32[2,256]{1,0:T(2,128)S(1)}) custom-call(s32[4,8]{1,0:T(4,128)S(1)} %copy-done.2, f32[16,128]{1,0:T(8,128)S(1)} %pad_maximum_fusion.5.back_refs_0_, f32[16,128]{1,0:T(8,128)S(1)} %collective-permute-done.35.back_refs_1_, ...), custom_call_target="tpu_custom_call" | custom-call | flops 1056964608 | bytes 7122048 | tf_op jit(solution)/shard_map/back_mid/pallas_call | solution.py:192
  104.4 1.1 collective-permute-done.39
  105.5 1.9 %collective-permute-start.42 = (f32[2,256]{1,0:T(2,128)S(1)}, f32[2,256]{1,0:T(2,128)S(1)}, u32[]{:S(2)}, u32[]{:S(2)}) collective-permute-start(f32[2,256]{1,0:T(2,128)S(1)} %add.44.back_refs_0_), channel_id=1, source_target_pairs={{0,24},{1,25},{2,26},{3,27},{4,28},{5,29},{6,30},{7,31},{8,16},{9,... | collective-permute-start | bytes 6152 | tf_op jit(solution)/shard_map/ppermute | solution.py:1197
  108.4 1.6 collective-permute-start.40
  109.9 2.4 %weight_mid_term.1 = (bf16[2,1152,128]{2,1,0:T(8,128)(2,1)S(1)}, bf16[2,1152,128]{2,1,0:T(8,128)(2,1)S(1)}) custom-call(s32[4,8]{1,0:T(4,128)S(1)} %copy-done.2, bf16[3,976,256]{2,1,0:T(8,128)(2,1)S(1)} %get-tuple-element.171.taps_ref, bf16[976,512]{1,0:T(8,128)(2,1)S(1)} %get-tuple-element.172.low_ref, f32[2,256]{1,0:T(2,128)S(1)} %get-tuple-element.133.affine_ref), custom_call_target="tpu_custom_call" | custom-call | flops 1056964608 | bytes 3680384 | tf_op jit(solution)/shard_map/weight_mid_term/pallas_call | solution.py:192
  112.4 1.9 %back_in.1 = (bf16[784,256]{1,0:T(8,128)(2,1)S(1)}, bf16[2,592,128]{2,1,0:T(8,128)(2,1)S(1)}, bf16[2,592,128]{2,1,0:T(8,128)(2,1)S(1)}) custom-call(s32[4,8]{1,0:T(4,128)S(1)} %copy-done.2, f32[896,256]{1,0:T(8,128)S(1)} %get-tuple-element.175.grad_ref, f32[896,256]{1,0:T(8,128)S(1)} %get-tuple-element.127.pre_ref, f32[6,256]{1,0:T(8,128)S(1)} %add.39.sums_refs_0_, ...), custom_call_target="tpu_custom_call" | custom-call | flops 411041792 | bytes 4702336 | tf_op jit(solution)/shard_map/back_in/pallas_call | solution.py:192
  115.0 1.9 %collective-permute-done.44.arrived_refs_0_ = bf16[2,656,128]{2,1,0:T(8,128)(2,1)S(1)} collective-permute-done((bf16[2,656,128]{2,1,0:T(8,128)(2,1)S(1)}, bf16[2,656,128]{2,1,0:T(8,128)(2,1)S(1)}, u32[]{:S(2)}, u32[]{:S(2)}) %collective-permute-start.44) | collective-permute-done | bytes 335904 | tf_op jit(solution)/shard_map/ppermute | solution.py:1197
  118.5 1.4 collective-permute-start.48
  121.0 7.4 %collective-permute-done.48.arrived_ref = bf16[1280,128]{1,0:T(8,128)(2,1)S(1)} collective-permute-done((bf16[1280,128]{1,0:T(8,128)(2,1)S(1)}, bf16[1280,128]{1,0:T(8,128)(2,1)S(1)}, u32[]{:S(2)}, u32[]{:S(2)}) %collective-permute-start.48) | collective-permute-done | bytes 327712 | tf_op jit(solution)/shard_map/ppermute | solution.py:1197
  131.0 4.3 %collective-permute-done.49.arrived_refs_0_ = bf16[576,128]{1,0:T(8,128)(2,1)S(1)} collective-permute-done((bf16[576,128]{1,0:T(8,128)(2,1)S(1)}, bf16[576,128]{1,0:T(8,128)(2,1)S(1)}, u32[]{:S(2)}, u32[]{:S(2)}) %collective-permute-start.49) | collective-permute-done | bytes 147488 | tf_op jit(solution)/shard_map/ppermute | solution.py:1197
  135.3 1.4 collective-permute-done.50.arrived_refs_1_
  137.3 1.1 collective-permute-start.52
  138.4 1.2 collective-permute-start.53
  139.7 2.1 %collective-permute-start.54 = (bf16[304,128]{1,0:T(8,128)(2,1)S(1)}, bf16[304,128]{1,0:T(8,128)(2,1)S(1)}, u32[]{:S(2)}, u32[]{:S(2)}) collective-permute-start(bf16[304,128]{1,0:T(8,128)(2,1)S(1)} %get-tuple-element.209), channel_id=1, source_target_pairs={{0,24},{1,25},{2,26},{3,27},{4,28},{5,29},{6,30},{7,31},{8,16},{9,... | collective-permute-start | bytes 233480 | tf_op jit(solution)/shard_map/ppermute | solution.py:1197
  141.8 3.9 %finish_owned.1 = (bf16[4,784,256]{2,1,0:T(8,128)(2,1)}, bf16[4,784,256]{2,1,0:T(8,128)(2,1)S(1)}) custom-call(s32[4,8]{1,0:T(4,128)S(1)} %copy-done.2, bf16[816,256]{1,0:T(8,128)(2,1)S(1)} %collective-permute-done.29.near_ref, bf16[2,816,256]{2,1,0:T(8,128)(2,1)S(1)} %collective-permute-done.46.swapped_ref, ...), custom_call_target="tpu_custom_call" | custom-call | flops 411041792 | bytes 8618112 | tf_op jit(solution)/shard_map/finish_owned/pallas_call | solution.py:192
  146.0 1.3 collective-permute-start.55
  147.3 1.8 %collective-permute-start.58 = (bf16[304,128]{1,0:T(8,128)(2,1)S(1)}, bf16[304,128]{1,0:T(8,128)(2,1)S(1)}, u32[]{:S(2)}, u32[]{:S(2)}) collective-permute-start(bf16[304,128]{1,0:T(8,128)(2,1)S(1)} %add_depth.1), channel_id=1, source_target_pairs={{0,24},{1,25},{2,26},{3,27},{4,28},{5,29},{6,30},{7,31},{8,16},{9,... | collective-permute-start | bytes 233480 | tf_op jit(solution)/shard_map/ppermute | solution.py:1197
  149.1 1.1 collective-permute-start.57
  150.2 1.5 collective-permute-start.56
  151.7 1.9 %collective-permute-done.58 = bf16[304,128]{1,0:T(8,128)(2,1)S(1)} collective-permute-done((bf16[304,128]{1,0:T(8,128)(2,1)S(1)}, bf16[304,128]{1,0:T(8,128)(2,1)S(1)}, u32[]{:S(2)}, u32[]{:S(2)}) %collective-permute-start.58) | collective-permute-done | bytes 77856 | tf_op jit(solution)/shard_map/ppermute | solution.py:1197
  153.7 1.9 %collective-permute-done.57 = bf16[304,128]{1,0:T(8,128)(2,1)S(1)} collective-permute-done((bf16[304,128]{1,0:T(8,128)(2,1)S(1)}, bf16[304,128]{1,0:T(8,128)(2,1)S(1)}, u32[]{:S(2)}, u32[]{:S(2)}) %collective-permute-start.57) | collective-permute-done | bytes 77856 | tf_op jit(solution)/shard_map/ppermute | solution.py:1197
  156.1 1.8 %collective-permute-start.61 = (bf16[1216,128]{1,0:T(8,128)(2,1)S(1)}, bf16[1216,128]{1,0:T(8,128)(2,1)S(1)}, u32[]{:S(2)}, u32[]{:S(2)}) collective-permute-start(bf16[1216,128]{1,0:T(8,128)(2,1)S(1)} %pad_maximum_fusion.4.term_refs_0_), channel_id=1, source_target_pairs={{0,4},{1,5},{2,6},{3,7},{4,0},{5,1},{6,2},{7,3},{8,12},{9,13},{10,... | collective-permute-start | bytes 933896 | tf_op jit(solution)/shard_map/ppermute | solution.py:1197
  158.0 1.8 %grad_owned.1 = bf16[4,784,256]{2,1,0:T(8,128)(2,1)} custom-call(bf16[784,256]{1,0:T(8,128)(2,1)S(1)} %collective-permute-done.51.low_refs_0_, bf16[784,256]{1,0:T(8,128)(2,1)S(1)} %collective-permute-done.59.low_refs_1_, bf16[784,256]{1,0:T(8,128)(2,1)S(1)} %collective-permute-done.55.low_refs_2_, bf16[784,256]{1,0:T(8,128)(2,1)S(1)} %collective-permute-done.60.low_refs_3_, ...), custom_call_target="tpu_custom_call" | custom-call | flops 411041792 | bytes 5341184 | tf_op jit(solution)/shard_map/grad_owned/pallas_call | solution.py:192
  159.8 5.8 %collective-permute-done.61.term_refs_1_ = bf16[1216,128]{1,0:T(8,128)(2,1)S(1)} collective-permute-done((bf16[1216,128]{1,0:T(8,128)(2,1)S(1)}, bf16[1216,128]{1,0:T(8,128)(2,1)S(1)}, u32[]{:S(2)}, u32[]{:S(2)}) %collective-permute-start.61) | collective-permute-done | bytes 311328 | tf_op jit(solution)/shard_map/ppermute | solution.py:1197
  165.5 1.7 unpack.1
  (140 shorter events, 22.3 us)
Async XLA Ops:
  0.7 9.7 %collective-permute-start.5 = (bf16[64,1024]{1,0:T(8,128)(2,1)}, bf16[64,1024]{1,0:T(8,128)(2,1)S(1)}, u32[]{:S(2)}, u32[]{:S(2)}) collective-permute-start(bf16[64,1024]{1,0:T(8,128)(2,1)} %bitcast.37), channel_id=1, source_target_pairs={{0,2},{1,3},{2,0},{3,1},{4,6},{5,7},{6,4},{7,5},{8,10},{9,11},{10,... | collective-permute-start | bytes 393224 | tf_op jit(solution)/shard_map/ppermute | solution.py:1197
  3.7 5.3 %collective-permute-start = (bf16[64,1024]{1,0:T(8,128)(2,1)}, bf16[64,1024]{1,0:T(8,128)(2,1)S(1)}, u32[]{:S(2)}, u32[]{:S(2)}) collective-permute-start(bf16[64,1024]{1,0:T(8,128)(2,1)} %bitcast.38), channel_id=1, source_target_pairs={{0,1},{1,0},{2,3},{3,2},{4,5},{5,4},{6,7},{7,6},{8,9},{9,8},{10,11... | collective-permute-start | bytes 393224 | tf_op jit(solution)/shard_map/ppermute | solution.py:1197
  6.0 20.8 %copy-start.2 = (s32[4,8]{1,0:T(4,128)S(1)}, s32[4,8]{1,0:T(4,128)}, u32[]{:S(2)}) copy-start(s32[4,8]{1,0:T(4,128)} %counts_ref.33) | copy-start | bytes 388
  6.0 20.8 %copy-start.5 = (bf16[1024,64]{0,1:T(8,128)(2,1)S(1)}, bf16[1024,64]{0,1:T(8,128)(2,1)}, u32[]{:S(2)}) copy-start(bf16[1024,64]{0,1:T(8,128)(2,1)} %param.19) | copy-start | bytes 393220
  6.0 19.3 %collective-permute-start.4 = (bf16[784,256]{1,0:T(8,128)(2,1)}, bf16[784,256]{1,0:T(8,128)(2,1)S(1)}, u32[]{:S(2)}, u32[]{:S(2)}) collective-permute-start(bf16[784,256]{1,0:T(8,128)(2,1)} %get-tuple-element.238), channel_id=1, source_target_pairs={{0,6},{1,2},{2,4},{3,0},{4,7},{5,3},{6,5},{7,1},{8,14},{9,10},{10,... | collective-permute-start | bytes 1204232 | tf_op jit(solution)/shard_map/ppermute | solution.py:1197
  7.4 19.4 %collective-permute-start.3 = (bf16[784,256]{1,0:T(8,128)(2,1)}, bf16[784,256]{1,0:T(8,128)(2,1)S(1)}, u32[]{:S(2)}, u32[]{:S(2)}) collective-permute-start(bf16[784,256]{1,0:T(8,128)(2,1)} %get-tuple-element.239), channel_id=1, source_target_pairs={{0,2},{1,6},{2,0},{3,4},{4,3},{5,7},{6,1},{7,5},{8,10},{9,14},{10,... | collective-permute-start | bytes 1204232 | tf_op jit(solution)/shard_map/ppermute | solution.py:1197
  9.1 17.8 %collective-permute-start.2 = (bf16[784,256]{1,0:T(8,128)(2,1)S(1)}, bf16[784,256]{1,0:T(8,128)(2,1)S(1)}, u32[]{:S(2)}, u32[]{:S(2)}) collective-permute-start(bf16[784,256]{1,0:T(8,128)(2,1)S(1)} %get-tuple-element.240), channel_id=1, source_target_pairs={{0,4},{1,0},{2,6},{3,2},{4,5},{5,1},{6,7},{7,3},{8,12},{9,8},{10,1... | collective-permute-start | bytes 1204232 | tf_op jit(solution)/shard_map/ppermute | solution.py:1197
  9.3 17.5 %collective-permute-start.1 = (bf16[784,256]{1,0:T(8,128)(2,1)S(1)}, bf16[784,256]{1,0:T(8,128)(2,1)S(1)}, u32[]{:S(2)}, u32[]{:S(2)}) collective-permute-start(bf16[784,256]{1,0:T(8,128)(2,1)S(1)} %get-tuple-element.241), channel_id=1, source_target_pairs={{0,0},{1,4},{2,2},{3,6},{4,1},{5,5},{6,3},{7,7},{8,8},{9,12},{10,1... | collective-permute-start | bytes 1204232 | tf_op jit(solution)/shard_map/ppermute | solution.py:1197
  10.4 2.5 %collective-permute-start.6 = (bf16[64,1024]{1,0:T(8,128)(2,1)S(1)}, bf16[64,1024]{1,0:T(8,128)(2,1)S(1)}, u32[]{:S(2)}, u32[]{:S(2)}) collective-permute-start(bf16[64,1024]{1,0:T(8,128)(2,1)S(1)} %collective-permute-done.5.a2), channel_id=1, source_target_pairs={{0,1},{1,0},{2,3},{3,2},{4,5},{5,4},{6,7},{7,6},{8,9},{9,8},{10,11... | collective-permute-start | bytes 393224 | tf_op jit(solution)/shard_map/ppermute | solution.py:1197
  12.9 15.8 %collective-permute-start.7 = (bf16[1872,128]{1,0:T(8,128)(2,1)S(1)}, bf16[1872,128]{1,0:T(8,128)(2,1)S(1)}, u32[]{:S(2)}, u32[]{:S(2)}) collective-permute-start(bf16[1872,128]{1,0:T(8,128)(2,1)S(1)} %pack.1.b0), channel_id=1, source_target_pairs={{0,1},{1,0},{2,3},{3,2},{4,5},{5,4},{6,7},{7,6},{8,9},{9,8},{10,11... | collective-permute-start | bytes 1437704 | tf_op jit(solution)/shard_map/ppermute | solution.py:1197
  26.8 12.9 %collective-permute-start.12 = (bf16[1872,128]{1,0:T(8,128)(2,1)S(1)}, bf16[1872,128]{1,0:T(8,128)(2,1)S(1)}, u32[]{:S(2)}, u32[]{:S(2)}) collective-permute-start(bf16[1872,128]{1,0:T(8,128)(2,1)S(1)} %pack.1.b0), channel_id=1, source_target_pairs={{0,2},{1,3},{2,0},{3,1},{4,6},{5,7},{6,4},{7,5},{8,10},{9,11},{10,... | collective-permute-start | bytes 1437704 | tf_op jit(solution)/shard_map/ppermute | solution.py:1197
  28.7 1.2 collective-permute-start.8
  29.9 5.4 %collective-permute-start.11 = (f32[6,256]{1,0:T(8,128)S(1)}, f32[6,256]{1,0:T(8,128)S(1)}, u32[]{:S(2)}, u32[]{:S(2)}) collective-permute-start(f32[6,256]{1,0:T(8,128)S(1)} %add.39.sums_refs_0_), channel_id=1, source_target_pairs={{0,24},{1,25},{2,26},{3,27},{4,28},{5,29},{6,30},{7,31},{8,16},{9,... | collective-permute-start | bytes 18440 | tf_op jit(solution)/shard_map/ppermute | solution.py:1197
  33.6 4.5 %collective-permute-start.10 = (f32[6,256]{1,0:T(8,128)S(1)}, f32[6,256]{1,0:T(8,128)S(1)}, u32[]{:S(2)}, u32[]{:S(2)}) collective-permute-start(f32[6,256]{1,0:T(8,128)S(1)} %add.39.sums_refs_0_), channel_id=1, source_target_pairs={{0,16},{1,17},{2,18},{3,19},{4,20},{5,21},{6,22},{7,23},{8,24},{9,... | collective-permute-start | bytes 18440 | tf_op jit(solution)/shard_map/ppermute | solution.py:1197
  33.6 4.5 %collective-permute-start.9 = (f32[6,256]{1,0:T(8,128)S(1)}, f32[6,256]{1,0:T(8,128)S(1)}, u32[]{:S(2)}, u32[]{:S(2)}) collective-permute-start(f32[6,256]{1,0:T(8,128)S(1)} %add.39.sums_refs_0_), channel_id=1, source_target_pairs={{0,8},{1,9},{2,10},{3,11},{4,12},{5,13},{6,14},{7,15},{8,0},{9,1},... | collective-permute-start | bytes 18440 | tf_op jit(solution)/shard_map/ppermute | solution.py:1197
  34.4 20.5 %collective-permute-start.26 = (bf16[2,784,256]{2,1,0:T(8,128)(2,1)S(1)}, bf16[2,784,256]{2,1,0:T(8,128)(2,1)S(1)}, u32[]{:S(2)}, u32[]{:S(2)}) collective-permute-start(bf16[2,784,256]{2,1,0:T(8,128)(2,1)S(1)} %pad_maximum_fusion.2), channel_id=1, source_target_pairs={{0,0},{1,4},{2,2},{3,6},{4,1},{5,5},{6,3},{7,7},{8,8},{9,12},{10,1... | collective-permute-start | bytes 2408456 | tf_op jit(solution)/shard_map/ppermute | solution.py:1197
  38.2 17.5 %collective-permute-start.27 = (bf16[2,784,256]{2,1,0:T(8,128)(2,1)S(1)}, bf16[2,784,256]{2,1,0:T(8,128)(2,1)S(1)}, u32[]{:S(2)}, u32[]{:S(2)}) collective-permute-start(bf16[2,784,256]{2,1,0:T(8,128)(2,1)S(1)} %pad_maximum_fusion.1), channel_id=1, source_target_pairs={{0,4},{1,0},{2,6},{3,2},{4,5},{5,1},{6,7},{7,3},{8,12},{9,8},{10,1... | collective-permute-start | bytes 2408456 | tf_op jit(solution)/shard_map/ppermute | solution.py:1197
  39.7 1.8 %collective-permute-start.13 = (bf16[1872,128]{1,0:T(8,128)(2,1)S(1)}, bf16[1872,128]{1,0:T(8,128)(2,1)S(1)}, u32[]{:S(2)}, u32[]{:S(2)}) collective-permute-start(bf16[1872,128]{1,0:T(8,128)(2,1)S(1)} %collective-permute-done.12.b2), channel_id=1, source_target_pairs={{0,1},{1,0},{2,3},{3,2},{4,5},{5,4},{6,7},{7,6},{8,9},{9,8},{10,11... | collective-permute-start | bytes 1437704 | tf_op jit(solution)/shard_map/ppermute | solution.py:1197
  44.8 1.2 collective-permute-start.14
  46.0 5.4 %collective-permute-start.17 = (f32[2,512]{1,0:T(2,128)S(1)}, f32[2,512]{1,0:T(2,128)S(1)}, u32[]{:S(2)}, u32[]{:S(2)}) collective-permute-start(f32[2,512]{1,0:T(2,128)S(1)} %add.40.sums_refs_0_.mid_sums_refs_0_), channel_id=1, source_target_pairs={{0,24},{1,25},{2,26},{3,27},{4,28},{5,29},{6,30},{7,31},{8,16},{9,... | collective-permute-start | bytes 12296 | tf_op jit(solution)/shard_map/ppermute | solution.py:1197
  48.6 4.5 %collective-permute-start.16 = (f32[2,512]{1,0:T(2,128)S(1)}, f32[2,512]{1,0:T(2,128)S(1)}, u32[]{:S(2)}, u32[]{:S(2)}) collective-permute-start(f32[2,512]{1,0:T(2,128)S(1)} %add.40.sums_refs_0_.mid_sums_refs_0_), channel_id=1, source_target_pairs={{0,16},{1,17},{2,18},{3,19},{4,20},{5,21},{6,22},{7,23},{8,24},{9,... | collective-permute-start | bytes 12296 | tf_op jit(solution)/shard_map/ppermute | solution.py:1197
  48.6 4.5 %collective-permute-start.15 = (f32[2,512]{1,0:T(2,128)S(1)}, f32[2,512]{1,0:T(2,128)S(1)}, u32[]{:S(2)}, u32[]{:S(2)}) collective-permute-start(f32[2,512]{1,0:T(2,128)S(1)} %add.40.sums_refs_0_.mid_sums_refs_0_), channel_id=1, source_target_pairs={{0,8},{1,9},{2,10},{3,11},{4,12},{5,13},{6,14},{7,15},{8,0},{9,1},... | collective-permute-start | bytes 12296 | tf_op jit(solution)/shard_map/ppermute | solution.py:1197
  55.8 21.2 %collective-permute-start.28 = (bf16[2,784,256]{2,1,0:T(8,128)(2,1)S(1)}, bf16[2,784,256]{2,1,0:T(8,128)(2,1)S(1)}, u32[]{:S(2)}, u32[]{:S(2)}) collective-permute-start(bf16[2,784,256]{2,1,0:T(8,128)(2,1)S(1)} %pad_maximum_fusion.3), channel_id=1, source_target_pairs={{0,2},{1,3},{2,0},{3,1},{4,6},{5,7},{6,4},{7,5},{8,10},{9,11},{10,... | collective-permute-start | bytes 2408456 | tf_op jit(solution)/shard_map/ppermute | solution.py:1197
  57.3 1.4 collective-permute-start.18
  58.7 5.9 %collective-permute-start.21 = (f32[80,128]{1,0:T(8,128)S(1)}, f32[80,128]{1,0:T(8,128)S(1)}, u32[]{:S(2)}, u32[]{:S(2)}) collective-permute-start(f32[80,128]{1,0:T(8,128)S(1)} %constant_dynamic-update-slice_fusion.gathered_refs_0_), channel_id=1, source_target_pairs={{0,24},{1,25},{2,26},{3,27},{4,28},{5,29},{6,30},{7,31},{8,16},{9,... | collective-permute-start | bytes 122888 | tf_op jit(solution)/shard_map/ppermute | solution.py:1197
  62.3 4.9 %collective-permute-start.20 = (f32[80,128]{1,0:T(8,128)S(1)}, f32[80,128]{1,0:T(8,128)S(1)}, u32[]{:S(2)}, u32[]{:S(2)}) collective-permute-start(f32[80,128]{1,0:T(8,128)S(1)} %constant_dynamic-update-slice_fusion.gathered_refs_0_), channel_id=1, source_target_pairs={{0,16},{1,17},{2,18},{3,19},{4,20},{5,21},{6,22},{7,23},{8,24},{9,... | collective-permute-start | bytes 122888 | tf_op jit(solution)/shard_map/ppermute | solution.py:1197
  62.3 4.9 %collective-permute-start.19 = (f32[80,128]{1,0:T(8,128)S(1)}, f32[80,128]{1,0:T(8,128)S(1)}, u32[]{:S(2)}, u32[]{:S(2)}) collective-permute-start(f32[80,128]{1,0:T(8,128)S(1)} %constant_dynamic-update-slice_fusion.gathered_refs_0_), channel_id=1, source_target_pairs={{0,8},{1,9},{2,10},{3,11},{4,12},{5,13},{6,14},{7,15},{8,0},{9,1},... | collective-permute-start | bytes 122888 | tf_op jit(solution)/shard_map/ppermute | solution.py:1197
  69.2 1.2 collective-permute-start.22
  70.4 5.6 %collective-permute-start.25 = (f32[8,256]{1,0:T(8,128)S(1)}, f32[8,256]{1,0:T(8,128)S(1)}, u32[]{:S(2)}, u32[]{:S(2)}) collective-permute-start(f32[8,256]{1,0:T(8,128)S(1)} %add.41.sums_refs_0_), channel_id=1, source_target_pairs={{0,24},{1,25},{2,26},{3,27},{4,28},{5,29},{6,30},{7,31},{8,16},{9,... | collective-permute-start | bytes 24584 | tf_op jit(solution)/shard_map/ppermute | solution.py:1197
  72.4 4.6 %collective-permute-start.24 = (f32[8,256]{1,0:T(8,128)S(1)}, f32[8,256]{1,0:T(8,128)S(1)}, u32[]{:S(2)}, u32[]{:S(2)}) collective-permute-start(f32[8,256]{1,0:T(8,128)S(1)} %add.41.sums_refs_0_), channel_id=1, source_target_pairs={{0,16},{1,17},{2,18},{3,19},{4,20},{5,21},{6,22},{7,23},{8,24},{9,... | collective-permute-start | bytes 24584 | tf_op jit(solution)/shard_map/ppermute | solution.py:1197
  72.6 4.4 %collective-permute-start.23 = (f32[8,256]{1,0:T(8,128)S(1)}, f32[8,256]{1,0:T(8,128)S(1)}, u32[]{:S(2)}, u32[]{:S(2)}) collective-permute-start(f32[8,256]{1,0:T(8,128)S(1)} %add.41.sums_refs_0_), channel_id=1, source_target_pairs={{0,8},{1,9},{2,10},{3,11},{4,12},{5,13},{6,14},{7,15},{8,0},{9,1},... | collective-permute-start | bytes 24584 | tf_op jit(solution)/shard_map/ppermute | solution.py:1197
  79.6 1.2 collective-permute-start.30
  80.8 5.5 %collective-permute-start.33 = (f32[8,256]{1,0:T(8,128)S(1)}, f32[8,256]{1,0:T(8,128)S(1)}, u32[]{:S(2)}, u32[]{:S(2)}) collective-permute-start(f32[8,256]{1,0:T(8,128)S(1)} %add.42.back_refs_0_.out_back_refs_0_), channel_id=1, source_target_pairs={{0,24},{1,25},{2,26},{3,27},{4,28},{5,29},{6,30},{7,31},{8,16},{9,... | collective-permute-start | bytes 24584 | tf_op jit(solution)/shard_map/ppermute | solution.py:1197
  84.0 4.5 %collective-permute-start.32 = (f32[8,256]{1,0:T(8,128)S(1)}, f32[8,256]{1,0:T(8,128)S(1)}, u32[]{:S(2)}, u32[]{:S(2)}) collective-permute-start(f32[8,256]{1,0:T(8,128)S(1)} %add.42.back_refs_0_.out_back_refs_0_), channel_id=1, source_target_pairs={{0,16},{1,17},{2,18},{3,19},{4,20},{5,21},{6,22},{7,23},{8,24},{9,... | collective-permute-start | bytes 24584 | tf_op jit(solution)/shard_map/ppermute | solution.py:1197
  84.0 4.5 %collective-permute-start.31 = (f32[8,256]{1,0:T(8,128)S(1)}, f32[8,256]{1,0:T(8,128)S(1)}, u32[]{:S(2)}, u32[]{:S(2)}) collective-permute-start(f32[8,256]{1,0:T(8,128)S(1)} %add.42.back_refs_0_.out_back_refs_0_), channel_id=1, source_target_pairs={{0,8},{1,9},{2,10},{3,11},{4,12},{5,13},{6,14},{7,15},{8,0},{9,1},... | collective-permute-start | bytes 24584 | tf_op jit(solution)/shard_map/ppermute | solution.py:1197
  85.2 14.8 %collective-permute-start.29 = (bf16[816,256]{1,0:T(8,128)(2,1)S(1)}, bf16[816,256]{1,0:T(8,128)(2,1)S(1)}, u32[]{:S(2)}, u32[]{:S(2)}) collective-permute-start(bf16[816,256]{1,0:T(8,128)(2,1)S(1)} %get-tuple-element.152), channel_id=1, source_target_pairs={{0,0},{1,4},{2,2},{3,6},{4,1},{5,5},{6,3},{7,7},{8,8},{9,12},{10,1... | collective-permute-start | bytes 1253384 | tf_op jit(solution)/shard_map/ppermute | solution.py:1197
  91.3 1.9 %collective-permute-start.34 = (f32[12,128]{1,0:T(8,128)S(1)}, f32[12,128]{1,0:T(8,128)S(1)}, u32[]{:S(2)}, u32[]{:S(2)}) collective-permute-start(f32[12,128]{1,0:T(8,128)S(1)} %get-tuple-element.157), channel_id=1, source_target_pairs={{0,1},{1,0},{2,3},{3,2},{4,5},{5,4},{6,7},{7,6},{8,9},{9,8},{10,11... | collective-permute-start | bytes 18440 | tf_op jit(solution)/shard_map/ppermute | solution.py:1197
  93.2 6.3 %collective-permute-start.37 = (f32[16,128]{1,0:T(8,128)S(1)}, f32[16,128]{1,0:T(8,128)S(1)}, u32[]{:S(2)}, u32[]{:S(2)}) collective-permute-start(f32[16,128]{1,0:T(8,128)S(1)} %pad_maximum_fusion.5.back_refs_0_), channel_id=1, source_target_pairs={{0,24},{1,25},{2,26},{3,27},{4,28},{5,29},{6,30},{7,31},{8,16},{9,... | collective-permute-start | bytes 24584 | tf_op jit(solution)/shard_map/ppermute | solution.py:1197
  95.5 4.5 %collective-permute-start.36 = (f32[16,128]{1,0:T(8,128)S(1)}, f32[16,128]{1,0:T(8,128)S(1)}, u32[]{:S(2)}, u32[]{:S(2)}) collective-permute-start(f32[16,128]{1,0:T(8,128)S(1)} %pad_maximum_fusion.5.back_refs_0_), channel_id=1, source_target_pairs={{0,16},{1,17},{2,18},{3,19},{4,20},{5,21},{6,22},{7,23},{8,24},{9,... | collective-permute-start | bytes 24584 | tf_op jit(solution)/shard_map/ppermute | solution.py:1197
  95.5 4.5 %collective-permute-start.35 = (f32[16,128]{1,0:T(8,128)S(1)}, f32[16,128]{1,0:T(8,128)S(1)}, u32[]{:S(2)}, u32[]{:S(2)}) collective-permute-start(f32[16,128]{1,0:T(8,128)S(1)} %pad_maximum_fusion.5.back_refs_0_), channel_id=1, source_target_pairs={{0,8},{1,9},{2,10},{3,11},{4,12},{5,13},{6,14},{7,15},{8,0},{9,1},... | collective-permute-start | bytes 24584 | tf_op jit(solution)/shard_map/ppermute | solution.py:1197
  100.1 12.3 %collective-permute-start.38 = (bf16[816,256]{1,0:T(8,128)(2,1)S(1)}, bf16[816,256]{1,0:T(8,128)(2,1)S(1)}, u32[]{:S(2)}, u32[]{:S(2)}) collective-permute-start(bf16[816,256]{1,0:T(8,128)(2,1)S(1)} %collective-permute-done.29.near_ref), channel_id=1, source_target_pairs={{0,2},{1,3},{2,0},{3,1},{4,6},{5,7},{6,4},{7,5},{8,10},{9,11},{10,... | collective-permute-start | bytes 1253384 | tf_op jit(solution)/shard_map/ppermute | solution.py:1197
  104.3 1.2 collective-permute-start.39
  105.5 6.8 %collective-permute-start.42 = (f32[2,256]{1,0:T(2,128)S(1)}, f32[2,256]{1,0:T(2,128)S(1)}, u32[]{:S(2)}, u32[]{:S(2)}) collective-permute-start(f32[2,256]{1,0:T(2,128)S(1)} %add.44.back_refs_0_), channel_id=1, source_target_pairs={{0,24},{1,25},{2,26},{3,27},{4,28},{5,29},{6,30},{7,31},{8,16},{9,... | collective-permute-start | bytes 6152 | tf_op jit(solution)/shard_map/ppermute | solution.py:1197
  107.5 4.9 %collective-permute-start.41 = (f32[2,256]{1,0:T(2,128)S(1)}, f32[2,256]{1,0:T(2,128)S(1)}, u32[]{:S(2)}, u32[]{:S(2)}) collective-permute-start(f32[2,256]{1,0:T(2,128)S(1)} %add.44.back_refs_0_), channel_id=1, source_target_pairs={{0,16},{1,17},{2,18},{3,19},{4,20},{5,21},{6,22},{7,23},{8,24},{9,... | collective-permute-start | bytes 6152 | tf_op jit(solution)/shard_map/ppermute | solution.py:1197
  108.4 4.0 %collective-permute-start.40 = (f32[2,256]{1,0:T(2,128)S(1)}, f32[2,256]{1,0:T(2,128)S(1)}, u32[]{:S(2)}, u32[]{:S(2)}) collective-permute-start(f32[2,256]{1,0:T(2,128)S(1)} %add.44.back_refs_0_), channel_id=1, source_target_pairs={{0,8},{1,9},{2,10},{3,11},{4,12},{5,13},{6,14},{7,15},{8,0},{9,1},... | collective-permute-start | bytes 6152 | tf_op jit(solution)/shard_map/ppermute | solution.py:1197
  114.3 3.1 %collective-permute-start.43 = (bf16[2,1152,128]{2,1,0:T(8,128)(2,1)S(1)}, bf16[2,1152,128]{2,1,0:T(8,128)(2,1)S(1)}, u32[]{:S(2)}, u32[]{:S(2)}) collective-permute-start(bf16[2,1152,128]{2,1,0:T(8,128)(2,1)S(1)} %get-tuple-element.184), channel_id=1, source_target_pairs={{0,1},{1,0},{2,3},{3,2},{4,5},{5,4},{6,7},{7,6},{8,9},{9,8},{10,11... | collective-permute-start | bytes 1769480 | tf_op jit(solution)/shard_map/ppermute | solution.py:1197
  114.4 2.5 %collective-permute-start.44 = (bf16[2,656,128]{2,1,0:T(8,128)(2,1)S(1)}, bf16[2,656,128]{2,1,0:T(8,128)(2,1)S(1)}, u32[]{:S(2)}, u32[]{:S(2)}) collective-permute-start(bf16[2,656,128]{2,1,0:T(8,128)(2,1)S(1)} %get-tuple-element.188), channel_id=1, source_target_pairs={{0,1},{1,0},{2,3},{3,2},{4,5},{5,4},{6,7},{7,6},{8,9},{9,8},{10,11... | collective-permute-start | bytes 1007624 | tf_op jit(solution)/shard_map/ppermute | solution.py:1197
  114.9 2.4 %collective-permute-start.45 = (bf16[2,592,128]{2,1,0:T(8,128)(2,1)S(1)}, bf16[2,592,128]{2,1,0:T(8,128)(2,1)S(1)}, u32[]{:S(2)}, u32[]{:S(2)}) collective-permute-start(bf16[2,592,128]{2,1,0:T(8,128)(2,1)S(1)} %get-tuple-element.189), channel_id=1, source_target_pairs={{0,1},{1,0},{2,3},{3,2},{4,5},{5,4},{6,7},{7,6},{8,9},{9,8},{10,11... | collective-permute-start | bytes 909320 | tf_op jit(solution)/shard_map/ppermute | solution.py:1197
  118.3 10.2 %collective-permute-start.46 = (bf16[2,816,256]{2,1,0:T(8,128)(2,1)S(1)}, bf16[2,816,256]{2,1,0:T(8,128)(2,1)S(1)}, u32[]{:S(2)}, u32[]{:S(2)}) collective-permute-start(bf16[2,816,256]{2,1,0:T(8,128)(2,1)S(1)} %pad_maximum_fusion), channel_id=1, source_target_pairs={{0,1},{1,0},{2,3},{3,2},{4,5},{5,4},{6,7},{7,6},{8,9},{9,8},{10,11... | collective-permute-start | bytes 2506760 | tf_op jit(solution)/shard_map/ppermute | solution.py:1197
  118.5 10.0 %collective-permute-start.48 = (bf16[1280,128]{1,0:T(8,128)(2,1)S(1)}, bf16[1280,128]{1,0:T(8,128)(2,1)S(1)}, u32[]{:S(2)}, u32[]{:S(2)}) collective-permute-start(bf16[1280,128]{1,0:T(8,128)(2,1)S(1)} %get-tuple-element.190), channel_id=1, source_target_pairs={{0,2},{1,3},{2,0},{3,1},{4,6},{5,7},{6,4},{7,5},{8,10},{9,11},{10,... | collective-permute-start | bytes 983048 | tf_op jit(solution)/shard_map/ppermute | solution.py:1197
  119.9 10.2 %collective-permute-start.47 = (bf16[2,576,128]{2,1,0:T(8,128)(2,1)S(1)}, bf16[2,576,128]{2,1,0:T(8,128)(2,1)S(1)}, u32[]{:S(2)}, u32[]{:S(2)}) collective-permute-start(bf16[2,576,128]{2,1,0:T(8,128)(2,1)S(1)} %get-tuple-element.185), channel_id=1, source_target_pairs={{0,4},{1,5},{2,6},{3,7},{4,0},{5,1},{6,2},{7,3},{8,12},{9,13},{10,... | collective-permute-start | bytes 884744 | tf_op jit(solution)/shard_map/ppermute | solution.py:1197
  120.1 10.9 %collective-permute-start.51 = (bf16[784,256]{1,0:T(8,128)(2,1)S(1)}, bf16[784,256]{1,0:T(8,128)(2,1)S(1)}, u32[]{:S(2)}, u32[]{:S(2)}) collective-permute-start(bf16[784,256]{1,0:T(8,128)(2,1)S(1)} %get-tuple-element.200), channel_id=1, source_target_pairs={{0,0},{1,4},{2,2},{3,6},{4,1},{5,5},{6,3},{7,7},{8,8},{9,12},{10,1... | collective-permute-start | bytes 1204232 | tf_op jit(solution)/shard_map/ppermute | solution.py:1197
  129.1 7.5 %collective-permute-start.50 = (bf16[640,128]{1,0:T(8,128)(2,1)S(1)}, bf16[640,128]{1,0:T(8,128)(2,1)S(1)}, u32[]{:S(2)}, u32[]{:S(2)}) collective-permute-start(bf16[640,128]{1,0:T(8,128)(2,1)S(1)} %get-tuple-element.199), channel_id=1, source_target_pairs={{0,4},{1,5},{2,6},{3,7},{4,0},{5,1},{6,2},{7,3},{8,12},{9,13},{10,... | collective-permute-start | bytes 491528 | tf_op jit(solution)/shard_map/ppermute | solution.py:1197
  130.1 5.2 %collective-permute-start.49 = (bf16[576,128]{1,0:T(8,128)(2,1)S(1)}, bf16[576,128]{1,0:T(8,128)(2,1)S(1)}, u32[]{:S(2)}, u32[]{:S(2)}) collective-permute-start(bf16[576,128]{1,0:T(8,128)(2,1)S(1)} %get-tuple-element.198), channel_id=1, source_target_pairs={{0,2},{1,3},{2,0},{3,1},{4,6},{5,7},{6,4},{7,5},{8,10},{9,11},{10,... | collective-permute-start | bytes 442376 | tf_op jit(solution)/shard_map/ppermute | solution.py:1197
  137.3 8.4 %collective-permute-start.52 = (bf16[304,128]{1,0:T(8,128)(2,1)S(1)}, bf16[304,128]{1,0:T(8,128)(2,1)S(1)}, u32[]{:S(2)}, u32[]{:S(2)}) collective-permute-start(bf16[304,128]{1,0:T(8,128)(2,1)S(1)} %get-tuple-element.207), channel_id=1, source_target_pairs={{0,8},{1,9},{2,10},{3,11},{4,12},{5,13},{6,14},{7,15},{8,0},{9,1},... | collective-permute-start | bytes 233480 | tf_op jit(solution)/shard_map/ppermute | solution.py:1197
  138.4 7.3 %collective-permute-start.53 = (bf16[304,128]{1,0:T(8,128)(2,1)S(1)}, bf16[304,128]{1,0:T(8,128)(2,1)S(1)}, u32[]{:S(2)}, u32[]{:S(2)}) collective-permute-start(bf16[304,128]{1,0:T(8,128)(2,1)S(1)} %get-tuple-element.208), channel_id=1, source_target_pairs={{0,16},{1,17},{2,18},{3,19},{4,20},{5,21},{6,22},{7,23},{8,24},{9,... | collective-permute-start | bytes 233480 | tf_op jit(solution)/shard_map/ppermute | solution.py:1197
  139.7 6.3 %collective-permute-start.54 = (bf16[304,128]{1,0:T(8,128)(2,1)S(1)}, bf16[304,128]{1,0:T(8,128)(2,1)S(1)}, u32[]{:S(2)}, u32[]{:S(2)}) collective-permute-start(bf16[304,128]{1,0:T(8,128)(2,1)S(1)} %get-tuple-element.209), channel_id=1, source_target_pairs={{0,24},{1,25},{2,26},{3,27},{4,28},{5,29},{6,30},{7,31},{8,16},{9,... | collective-permute-start | bytes 233480 | tf_op jit(solution)/shard_map/ppermute | solution.py:1197
  146.0 9.6 %collective-permute-start.55 = (bf16[784,256]{1,0:T(8,128)(2,1)S(1)}, bf16[784,256]{1,0:T(8,128)(2,1)S(1)}, u32[]{:S(2)}, u32[]{:S(2)}) collective-permute-start(bf16[784,256]{1,0:T(8,128)(2,1)S(1)} %collective-permute-done.51.low_refs_0_), channel_id=1, source_target_pairs={{0,2},{1,3},{2,0},{3,1},{4,6},{5,7},{6,4},{7,5},{8,10},{9,11},{10,... | collective-permute-start | bytes 1204232 | tf_op jit(solution)/shard_map/ppermute | solution.py:1197
  147.3 6.4 %collective-permute-start.58 = (bf16[304,128]{1,0:T(8,128)(2,1)S(1)}, bf16[304,128]{1,0:T(8,128)(2,1)S(1)}, u32[]{:S(2)}, u32[]{:S(2)}) collective-permute-start(bf16[304,128]{1,0:T(8,128)(2,1)S(1)} %add_depth.1), channel_id=1, source_target_pairs={{0,24},{1,25},{2,26},{3,27},{4,28},{5,29},{6,30},{7,31},{8,16},{9,... | collective-permute-start | bytes 233480 | tf_op jit(solution)/shard_map/ppermute | solution.py:1197
  149.1 6.5 %collective-permute-start.57 = (bf16[304,128]{1,0:T(8,128)(2,1)S(1)}, bf16[304,128]{1,0:T(8,128)(2,1)S(1)}, u32[]{:S(2)}, u32[]{:S(2)}) collective-permute-start(bf16[304,128]{1,0:T(8,128)(2,1)S(1)} %add_depth.1), channel_id=1, source_target_pairs={{0,16},{1,17},{2,18},{3,19},{4,20},{5,21},{6,22},{7,23},{8,24},{9,... | collective-permute-start | bytes 233480 | tf_op jit(solution)/shard_map/ppermute | solution.py:1197
  150.2 5.4 %collective-permute-start.56 = (bf16[304,128]{1,0:T(8,128)(2,1)S(1)}, bf16[304,128]{1,0:T(8,128)(2,1)S(1)}, u32[]{:S(2)}, u32[]{:S(2)}) collective-permute-start(bf16[304,128]{1,0:T(8,128)(2,1)S(1)} %add_depth.1), channel_id=1, source_target_pairs={{0,8},{1,9},{2,10},{3,11},{4,12},{5,13},{6,14},{7,15},{8,0},{9,1},... | collective-permute-start | bytes 233480 | tf_op jit(solution)/shard_map/ppermute | solution.py:1197
  155.6 2.4 %collective-permute-start.59 = (bf16[784,256]{1,0:T(8,128)(2,1)S(1)}, bf16[784,256]{1,0:T(8,128)(2,1)S(1)}, u32[]{:S(2)}, u32[]{:S(2)}) collective-permute-start(bf16[784,256]{1,0:T(8,128)(2,1)S(1)} %collective-permute-done.51.low_refs_0_), channel_id=1, source_target_pairs={{0,1},{1,0},{2,3},{3,2},{4,5},{5,4},{6,7},{7,6},{8,9},{9,8},{10,11... | collective-permute-start | bytes 1204232 | tf_op jit(solution)/shard_map/ppermute | solution.py:1197
  155.6 2.4 %collective-permute-start.60 = (bf16[784,256]{1,0:T(8,128)(2,1)S(1)}, bf16[784,256]{1,0:T(8,128)(2,1)S(1)}, u32[]{:S(2)}, u32[]{:S(2)}) collective-permute-start(bf16[784,256]{1,0:T(8,128)(2,1)S(1)} %collective-permute-done.55.low_refs_2_), channel_id=1, source_target_pairs={{0,1},{1,0},{2,3},{3,2},{4,5},{5,4},{6,7},{7,6},{8,9},{9,8},{10,11... | collective-permute-start | bytes 1204232 | tf_op jit(solution)/shard_map/ppermute | solution.py:1197
  156.1 9.4 %collective-permute-start.61 = (bf16[1216,128]{1,0:T(8,128)(2,1)S(1)}, bf16[1216,128]{1,0:T(8,128)(2,1)S(1)}, u32[]{:S(2)}, u32[]{:S(2)}) collective-permute-start(bf16[1216,128]{1,0:T(8,128)(2,1)S(1)} %pad_maximum_fusion.4.term_refs_0_), channel_id=1, source_target_pairs={{0,4},{1,5},{2,6},{3,7},{4,0},{5,1},{6,2},{7,3},{8,12},{9,13},{10,... | collective-permute-start | bytes 933896 | tf_op jit(solution)/shard_map/ppermute | solution.py:1197
  (15 other events, 114.1 us)
